TPU v7x, 128 devices: a whole 4x4x4 slice. The times are simulated.
128 devices in a mesh: heads: 4 (over x_hi, core), seq: 32 (over z, y, x_lo).
Axes of the slice: x: 4 (x_hi: 2, x_lo: 2; x = x_hi * 2 + x_lo), y: 4, z: 4, core: 2. Of those that a mesh axis runs over, the one named last changes fastest.
Arguments:
- decoder_states: bfloat16 [8192, 4096], P('seq', 'heads'), may hold values from -6 to 6
- query_weight: bfloat16 [4096, 4096], P(None, 'heads'), may hold values from -1 to 1
- output_weight: bfloat16 [4096, 4096], P('heads'), may hold values from -0.09375 to 0.09375
- context_keys: bfloat16 [1024, 4096], P(('heads', 'seq')), may hold values from -512 to 512
- context_values: bfloat16 [1024, 4096], P(('heads', 'seq')), may hold values from -6 to 6
- lengths: int32 [4], replicated, may hold values from 1 to 256, 704 in all
- slot_passage: int32 [4], replicated, may hold values from 0 to 3, each once
- output_cotangent: bfloat16 [8192, 4096], P('seq', 'heads'), may hold values from -6 to 6
Outputs:
- attended: bfloat16 [8192, 4096], P('seq', 'heads')
- query_weight_grad: float32 [4096, 4096], P('seq', 'heads')
- output_weight_grad: float32 [4096, 4096], P('heads', 'seq')
- context_keys_grad: float32 [1024, 4096], P(('heads', 'seq'))
- context_values_grad: float32 [1024, 4096], P(('heads', 'seq'))
Inputs may be any that keep to these rules, and one draw needn't show every extreme that they name: `lengths`: the valid tokens of all passages add up to 704. `slot_passage`: each passage stands in exactly one slot.
All inputs are finite; a program needn't handle non-finite values.
Results may differ from a plain program's by a relative error of at most 0.035.
Values may be sent and summed in bfloat16 or wider, within the bound.
No kernel may reach another device: no remote copies, remote signals or barrier semaphores. Data moves between devices by JAX's collectives and lax.ppermute only.
A program may use at most 128 MiB of HBM per device.

v0:
```python
import math

import jax
import jax.numpy as jnp
from jax import lax
from jax.sharding import PartitionSpec as P

HEAD = 128


def key_validity(lengths, slot_passage, seq_count, head_count, owned_rows, slot_tokens):
    passage_count = lengths.shape[0]
    passage_ids = jnp.arange(passage_count, dtype=jnp.int32)
    slot_lengths = jnp.sum(
        jnp.where(slot_passage[:, None] == passage_ids[None, :], lengths[None, :], 0), axis=1
    )
    seq_index = jnp.arange(seq_count, dtype=jnp.int32)[:, None, None]
    head_index = jnp.arange(head_count, dtype=jnp.int32)[None, :, None]
    token_index = jnp.arange(owned_rows, dtype=jnp.int32)[None, None, :]
    position = ((head_index * seq_count + seq_index) * owned_rows + token_index).reshape(-1)
    slot_limit = jnp.sum(
        jnp.where(
            (position // slot_tokens)[:, None] == passage_ids[None, :], slot_lengths[None, :], 0
        ),
        axis=1,
    )
    return position % slot_tokens < slot_limit


def on_device(
    decoder_states,
    query_weight,
    output_weight,
    context_keys,
    context_values,
    lengths,
    slot_passage,
    output_cotangent,
):
    seq_count = lax.axis_size("seq")
    head_count = lax.axis_size("heads")
    owned_rows = context_keys.shape[0]
    slot_tokens = min(256, owned_rows * seq_count * head_count // 2)
    local_cols = query_weight.shape[1]
    local_heads = local_cols // HEAD
    score_scale = 1.0 / math.sqrt(HEAD)
    wide_states, wide_grad = (
        lax.all_gather(decoder_states, "heads", axis=1, tiled=True),
        lax.all_gather(output_cotangent, "heads", axis=1, tiled=True),
    )
    token_count = wide_states.shape[0]
    queries = jnp.dot(wide_states, query_weight, preferred_element_type=jnp.float32).astype(
        jnp.bfloat16
    )
    block_keys, block_values = (
        lax.all_to_all(context_keys, "heads", split_axis=1, concat_axis=0, tiled=True),
        lax.all_to_all(context_values, "heads", split_axis=1, concat_axis=0, tiled=True),
    )
    every_key, every_value = (
        lax.all_gather(block_keys, "seq", axis=0, tiled=True),
        lax.all_gather(block_values, "seq", axis=0, tiled=True),
    )
    query_heads = queries.reshape(token_count, local_heads, HEAD)
    key_heads = every_key.reshape(-1, local_heads, HEAD)
    value_heads = every_value.reshape(-1, local_heads, HEAD)
    key_valid = key_validity(lengths, slot_passage, seq_count, head_count, owned_rows, slot_tokens)
    scores = (
        jnp.einsum("qnd,knd->nqk", query_heads, key_heads, preferred_element_type=jnp.float32)
        * score_scale
    )
    masked = jnp.where(key_valid[None, None, :], scores, -jnp.inf)
    row_max = jnp.max(masked, axis=2, keepdims=True)
    weights = jnp.exp(masked - row_max)
    probabilities = weights / jnp.sum(weights, axis=2, keepdims=True)
    probs_low = probabilities.astype(jnp.bfloat16)
    mixed_heads = jnp.einsum(
        "nqk,knd->qnd", probs_low, value_heads, preferred_element_type=jnp.float32
    ).astype(jnp.bfloat16)
    heads_out = mixed_heads.reshape(token_count, local_cols)
    output_terms = jnp.dot(heads_out, output_weight, preferred_element_type=jnp.float32)
    attended = lax.psum_scatter(output_terms, "heads", scatter_dimension=1, tiled=True).astype(
        jnp.bfloat16
    )
    heads_grad = lax.dot_general(
        wide_grad, output_weight, (((1,), (1,)), ((), ())), preferred_element_type=jnp.float32
    ).astype(jnp.bfloat16)
    output_weight_terms = lax.dot_general(
        heads_out, wide_grad, (((0,), (0,)), ((), ())), preferred_element_type=jnp.float32
    )
    output_weight_grad = lax.psum_scatter(
        output_weight_terms.astype(jnp.bfloat16), "seq", scatter_dimension=1, tiled=True
    ).astype(jnp.float32)
    grad_heads = heads_grad.reshape(token_count, local_heads, HEAD)
    value_dots = jnp.einsum(
        "qnd,knd->nqk", grad_heads, value_heads, preferred_element_type=jnp.float32
    )
    row_delta = jnp.sum(grad_heads.astype(jnp.float32) * mixed_heads.astype(jnp.float32), axis=2).T[
        :, :, None
    ]
    score_grad = (probabilities * (value_dots - row_delta) * score_scale).astype(jnp.bfloat16)
    query_grad = jnp.einsum(
        "nqk,knd->qnd", score_grad, key_heads, preferred_element_type=jnp.float32
    )
    query_grad = query_grad.astype(jnp.bfloat16).reshape(token_count, local_cols)
    query_weight_grad = lax.psum_scatter(
        lax.dot_general(
            wide_states, query_grad, (((0,), (0,)), ((), ())), preferred_element_type=jnp.float32
        ).astype(jnp.bfloat16),
        "seq",
        scatter_dimension=0,
        tiled=True,
    ).astype(jnp.float32)
    score_source = score_grad.reshape(local_heads, token_count, seq_count, head_count, owned_rows)
    prob_source = probs_low.reshape(local_heads, token_count, seq_count, head_count, owned_rows)
    key_terms = jnp.einsum(
        "nqsht,qnd->hstnd", score_source, query_heads, preferred_element_type=jnp.float32
    ).astype(jnp.bfloat16)
    value_terms = jnp.einsum(
        "nqsht,qnd->hstnd", prob_source, grad_heads, preferred_element_type=jnp.float32
    ).astype(jnp.bfloat16)
    sent_shape = (seq_count * head_count, 1, owned_rows, local_cols)
    key_moved, value_moved = (
        lax.all_to_all(
            key_terms.reshape(sent_shape), ("heads", "seq"), split_axis=0, concat_axis=1, tiled=True
        ),
        lax.all_to_all(
            value_terms.reshape(sent_shape),
            ("heads", "seq"),
            split_axis=0,
            concat_axis=1,
            tiled=True,
        ),
    )

    def owner_total(moved):
        summed = jnp.sum(
            moved.reshape(head_count, seq_count, owned_rows, local_cols).astype(jnp.float32), axis=1
        )
        return summed.transpose(1, 0, 2).reshape(owned_rows, head_count * local_cols)

    context_keys_grad = owner_total(key_moved)
    context_values_grad = owner_total(value_moved)
    return (attended, query_weight_grad, output_weight_grad, context_keys_grad, context_values_grad)


def solution(mesh):
    placed = (
        P("seq", "heads"),
        P(None, "heads"),
        P("heads", None),
        P(("heads", "seq"), None),
        P(("heads", "seq"), None),
        P(),
        P(),
        P("seq", "heads"),
    )
    return jax.shard_map(
        on_device,
        mesh=mesh,
        in_specs=placed,
        out_specs=(
            P("seq", "heads"),
            P("seq", "heads"),
            P("heads", "seq"),
            P(("heads", "seq"), None),
            P(("heads", "seq"), None),
        ),
        check_vma=False,
    )
```

profile of v0, /device:TPU:0, one launch (start us, length us, event | category | flops | bytes accessed | tf_op | source)
XLA Modules:
  0.0 896.1 jit_solution(5695328665669162410)
XLA Ops:
  8.7 10.1 %all_to_all.56 = bf16[8,4,1024]{2,0,1:T(8,128)(2,1)} all-to-all(bf16[8,4,1024]{2,0,1:T(8,128)(2,1)} %bitcast.121), channel_id=1, replica_groups=mesh['heads'=4,'seq'=32] {'heads'}, dimensions={1} | all-to-all | bytes 131072 | tf_op jit(solution)/shard_map/all_to_all | solution.py:56
  22.2 6.1 all-to-all-done.1
  30.2 9.3 %all-gather.11.cloned.1.call-done = bf16[256,4096]{1,0:T(8,128)(2,1)} async-done(((bf16[256,1024]{1,0:T(8,128)(2,1)}), bf16[256,4096]{1,0:T(8,128)(2,1)}) %all-gather.11.cloned.1.call-update) | async-done | bytes 2097168 | tf_op jit(solution)/shard_map/all_gather | solution.py:49
  39.5 6.4 convolution_convert_fusion.2
  46.1 21.2 %all-gather.5.cloned.1.call-done = bf16[256,4096]{1,0:T(8,128)(2,1)} async-done(((bf16[256,1024]{1,0:T(8,128)(2,1)}), bf16[256,4096]{1,0:T(8,128)(2,1)}) %all-gather.5.cloned.1.call-update) | async-done | bytes 2097168 | tf_op jit(solution)/shard_map/all_gather | solution.py:48
  67.2 6.3 convolution_convert_fusion.4
  73.6 149.9 %all-gather.7.cloned.1.call-done = bf16[1024,1024]{1,0:T(8,128)(2,1)} async-done(((bf16[32,1024]{1,0:T(8,128)(2,1)}), bf16[1024,1024]{1,0:T(8,128)(2,1)}) %all-gather.7.cloned.1.call-update) | async-done | bytes 2097168 | tf_op jit(solution)/shard_map/all_gather | solution.py:60
  226.4 5.1 fusion.33
  231.5 5.4 fusion.9
  236.9 144.0 %all-gather.9.cloned.1.call-done = bf16[1024,1024]{1,0:T(8,128)(2,1)} async-done(((bf16[32,1024]{1,0:T(8,128)(2,1)}), bf16[1024,1024]{1,0:T(8,128)(2,1)}) %all-gather.9.cloned.1.call-update) | async-done | bytes 2097168 | tf_op jit(solution)/shard_map/all_gather | solution.py:61
  389.3 7.7 fusion.38
  397.2 7.3 convolution_convert_fusion
  404.5 12.3 %copy.103 = bf16[1024,4096]{0,1:T(8,128)(2,1)} copy(bf16[1024,4096]{1,0:T(8,128)(2,1)} %convolution_convert_fusion) | data formatting | bytes 16777216
  416.9 5.2 multiply_convert_fusion
  425.8 5.7 convert_bitcast_fusion
  431.5 12.0 %copy.101 = bf16[4096,1024]{1,0:T(8,128)(2,1)} copy(bf16[4096,1024]{0,1:T(8,128)(2,1)} %convert_bitcast_fusion) | data formatting | bytes 16777216
  444.6 6.4 copy.81
  459.8 8.8 all-to-all-start.2
  468.6 6.5 copy.86
  487.0 34.9 %all-to-all-done.2 = bf16[128,1,8,1024]{3,2,1,0:T(8,128)(2,1)S(1)} async-done(((bf16[128,1,8,1024]{3,2,1,0:T(8,128)(2,1)}), bf16[128,1,8,1024]{3,2,1,0:T(8,128)(2,1)S(1)}, u32[]{:S(2)}, u32[]{:S(2)}) %all-to-all-start.2) | async-done | bytes 2097184 | tf_op jit(solution)/shard_map/all_to_all | solution.py:123
  521.9 5.8 all-to-all-start.3
  528.7 51.9 %all-to-all-done.3 = bf16[128,1,8,1024]{3,2,1,0:T(8,128)(2,1)} async-done(((bf16[128,1,8,1024]{3,2,1,0:T(8,128)(2,1)}), bf16[128,1,8,1024]{3,2,1,0:T(8,128)(2,1)}, u32[]{:S(2)}, u32[]{:S(2)}) %all-to-all-start.3) | async-done | bytes 2097184 | tf_op jit(solution)/shard_map/all_to_all | solution.py:126
  585.3 105.3 %reduce-scatter.12.cloned.1.call-done = bf16[128,1024]{1,0:T(8,128)(2,1)} async-done(((bf16[4096,1024]{1,0:T(8,128)(2,1)}), bf16[128,1024]{1,0:T(8,128)(2,1)}) %reduce-scatter.12.cloned.1.call-update) | async-done | bytes 262160
  692.6 194.6 %reduce-scatter.10.cloned.1.call-done = bf16[128,1024]{1,0:T(8,128)(2,1)} async-done(((bf16[4096,1024]{1,0:T(8,128)(2,1)}), bf16[128,1024]{1,0:T(8,128)(2,1)}) %reduce-scatter.10.cloned.1.call-update) | async-done | bytes 262160
  (53 shorter events, 53.5 us)
Async XLA Ops:
  7.2 32.3 %all-gather.11.cloned.1.call-start = ((), (), s32[]{:S(2)}) async-start(), calls=%async_computation.11 | async-start | bytes 2621440 | tf_op jit(solution)/shard_map/all_gather | solution.py:49
  7.9 59.3 %all-gather.5.cloned.1.call-start = ((), (), s32[]{:S(2)}) async-start(), calls=%async_computation.7 | async-start | bytes 2621440 | tf_op jit(solution)/shard_map/all_gather | solution.py:48
  8.6 214.9 %all-gather.7.cloned.1.call-start = ((), (), s32[]{:S(2)}) async-start(), calls=%async_computation.8 | async-start | bytes 2162688 | tf_op jit(solution)/shard_map/all_gather | solution.py:60
  18.8 9.4 %all-to-all-start.1 = ((bf16[8,4,1024]{2,0,1:T(8,128)(2,1)}), bf16[8,4,1024]{2,0,1:T(8,128)(2,1)S(1)}, u32[]{:S(2)}, u32[]{:S(2)}) async-start(bf16[8,4,1024]{2,0,1:T(8,128)(2,1)} %bitcast.122), calls=%async_computation.1 | async-start | bytes 131072 | tf_op jit(solution)/shard_map/all_to_all | solution.py:57
  22.1 358.7 %all-gather.9.cloned.1.call-start = ((), (), s32[]{:S(2)}) async-start(), calls=%async_computation.9 | async-start | bytes 2162688 | tf_op jit(solution)/shard_map/all_gather | solution.py:61
  28.3 0.6 copy-start.4
  28.9 554.3 %reduce-scatter.8.cloned.1.call-start = ((), (), s32[]{:S(2)}) async-start(), calls=%async_computation.10 | async-start | bytes 5242880 | tf_op jit(solution)/shard_map/reduce_scatter | solution.py:81
  73.6 157.9 %copy-start.2 = (bf16[256,1024]{1,0:T(8,128)(2,1)}, bf16[256,1024]{1,0:T(8,128)(2,1)S(1)}, u32[]{:S(2)}) copy-start(bf16[256,1024]{1,0:T(8,128)(2,1)S(1)} %convolution_convert_fusion.4) | copy-start | bytes 1572868
  397.0 293.6 %reduce-scatter.12.cloned.1.call-start = ((), (), s32[]{:S(2)}) async-start(), calls=%async_computation.13 | async-start | bytes 8650752
  416.9 470.3 %reduce-scatter.10.cloned.1.call-start = ((), (), s32[]{:S(2)}) async-start(), calls=%async_computation.12 | async-start | bytes 8650752
  422.1 2.1 copy-start
  424.2 1.6 copy-start.1
  443.5 1.0 copy-start.3
  459.8 62.2 %all-to-all-start.2 = ((bf16[128,1,8,1024]{3,2,1,0:T(8,128)(2,1)}), bf16[128,1,8,1024]{3,2,1,0:T(8,128)(2,1)S(1)}, u32[]{:S(2)}, u32[]{:S(2)}) async-start(bf16[128,1,8,1024]{3,2,1,0:T(8,128)(2,1)} %bitcast.101), calls=%async_computation.3 | async-start | bytes 4194304 | tf_op jit(solution)/shard_map/all_to_all | solution.py:123
  521.9 58.7 %all-to-all-start.3 = ((bf16[128,1,8,1024]{3,2,1,0:T(8,128)(2,1)}), bf16[128,1,8,1024]{3,2,1,0:T(8,128)(2,1)}, u32[]{:S(2)}, u32[]{:S(2)}) async-start(bf16[128,1,8,1024]{3,2,1,0:T(8,128)(2,1)} %bitcast.102), calls=%async_computation.4 | async-start | bytes 4194304 | tf_op jit(solution)/shard_map/all_to_all | solution.py:126
Sparse Core Ops, SparseCore 0:
  9.7 29.7 all-gather.10
  41.1 26.0 all-gather.4
  68.9 154.6 all-gather.6
  225.6 155.2 all-gather.8
  397.1 51.4 reduce-scatter.7
  451.0 239.5 reduce-scatter.11
  693.1 193.9 reduce-scatter.9
where the time goes:
time: 898 us; the launch traced here: 896 us
  waiting for transfers between devices  719 us (80%)
  local copies, waits for them, and re-layouts  62 us (7%)
  matrix products  59.7 us (7%)
  starting transfers between devices  18.4 us (2%)
  between operations  14.3 us (2%)
  other arithmetic  13 us (1%)
  blocking collectives  10.1 us (1%)
    unnamed x9, waiting for transfers between devices  301 us
    all_gather x1, waiting for transfers between devices, on_device(): lax.all_gather(block_keys, 'seq', axis=0, tiled=True)  150 us
    all_gather x1, waiting for transfers between devices, on_device(): lax.all_gather(block_values, 'seq', axis=0, tiled=True)  144 us
    all_to_all x1, waiting for transfers between devices, on_device(): lax.all_to_all(value_terms.reshape(sent_shape), ('heads', 'seq'), split_a...  51.9 us
    all_to_all x1, waiting for transfers between devices, on_device(): lax.all_to_all(key_terms.reshape(sent_shape), ('heads', 'seq'), split_axi...  34.9 us
    unnamed x16, local copies, waits for them, and re-layouts  31.4 us
    all_gather x1, waiting for transfers between devices, on_device(): lax.all_gather(decoder_states, 'heads', axis=1, tiled=True)  21.2 us
  transfers between devices with their start and end apart: 10, of which 9 were waited for; matrix products, arithmetic and copies ran while one was open for 13% of the time, Pallas kernels for 0%

commit v1 on v0

v1 whole, which is shorter than its diff:
```python
import math

import jax
import jax.numpy as jnp
from jax import lax
from jax.experimental import pallas as pl
from jax.experimental.pallas import tpu as pltpu
from jax.sharding import Mesh
from jax.sharding import PartitionSpec as P

HEAD = 128
SCALE = 1.0 / math.sqrt(HEAD)
F32 = jnp.float32
BF16 = jnp.bfloat16
AXES = (("xh", 2), ("core", 2), ("z", 4), ("y", 4), ("xl", 2))
HEADS = ("xh", "core")
SEQ = ("z", "y", "xl")
SWAP = [(0, 1), (1, 0)]
VMEM = 56 * 1024 * 1024


def context_bias(lengths, slot_passage, slot_tokens):
    slot_lengths = jnp.sum(
        jnp.where(slot_passage[:, None] == jnp.arange(4)[None, :], lengths[None, :], 0), axis=1
    )
    token = jnp.arange(4 * slot_tokens, dtype=jnp.int32)
    plane, slot, layer, row = token // 128, (token // 32) % 4, (token // 8) % 4, token % 8
    position = (layer * 8 + plane) * 8 + row
    limit = jnp.sum(jnp.where(slot[:, None] == jnp.arange(4)[None, :], slot_lengths[None, :], 0), axis=1)
    return jnp.where(position < limit, 0.0, -jnp.inf).astype(F32)[None, :]


def dot(a, b, contract):
    return lax.dot_general(a, b, (contract, ((), ())), preferred_element_type=F32)


def attention_kernel(bias, q_ref, g_ref, k_ref, v_ref, ho_ref, dq_ref, dk_ref, dv_ref, dk_sum, dv_sum):
    step = pl.program_id(1)

    @pl.when(step == 0)
    def _():
        dk_sum[...] = jnp.zeros_like(dk_sum)
        dv_sum[...] = jnp.zeros_like(dv_sum)

    q, g, k, v = q_ref[...], g_ref[...], k_ref[...], v_ref[...]
    scores = dot(q, k, ((1,), (1,))) + bias[...]
    top = jnp.max(scores, axis=1, keepdims=True)
    weights = jnp.exp((scores - top) * SCALE)
    probs = weights * (1.0 / jnp.sum(weights, axis=1, keepdims=True))
    probs_low = probs.astype(BF16)
    heads_out = dot(probs_low, v, ((1,), (0,))).astype(BF16)
    ho_ref[...] = heads_out
    value_dots = dot(g, v, ((1,), (1,)))
    delta = jnp.sum(g.astype(F32) * heads_out.astype(F32), axis=1, keepdims=True)
    score_grad = (probs * (value_dots - delta) * SCALE).astype(BF16)
    dq_ref[...] = dot(score_grad, k, ((1,), (0,))).astype(BF16)
    dk_sum[...] += dot(q, score_grad, ((0,), (0,)))
    dv_sum[...] += dot(g, probs_low, ((0,), (0,)))

    @pl.when(step == pl.num_programs(1) - 1)
    def _():
        dk_ref[...] = dk_sum[...].T.astype(BF16)
        dv_ref[...] = dv_sum[...].T.astype(BF16)


def attention(bias, q, g, k, v, rows=256):
    tokens, cols = q.shape
    context = k.shape[0]
    token_block = pl.BlockSpec((rows, HEAD), lambda h, t: (t, h))
    context_block = pl.BlockSpec((context, HEAD), lambda h, t: (0, h))
    return pl.pallas_call(
        attention_kernel,
        grid=(cols // HEAD, tokens // rows),
        in_specs=[
            pl.BlockSpec((1, context), lambda h, t: (0, 0)),
            token_block,
            token_block,
            context_block,
            context_block,
        ],
        out_specs=[token_block, token_block, context_block, context_block],
        out_shape=[
            jax.ShapeDtypeStruct((tokens, cols), BF16),
            jax.ShapeDtypeStruct((tokens, cols), BF16),
            jax.ShapeDtypeStruct((context, cols), BF16),
            jax.ShapeDtypeStruct((context, cols), BF16),
        ],
        scratch_shapes=[pltpu.VMEM((HEAD, context), F32), pltpu.VMEM((HEAD, context), F32)],
        compiler_params=pltpu.CompilerParams(vmem_limit_bytes=VMEM),
        cost_estimate=pl.CostEstimate(
            flops=12 * tokens * cols * context,
            bytes_accessed=2 * (4 * tokens * cols + 4 * context * cols),
            transcendentals=tokens * context * cols // HEAD,
        ),
        name="attention",
    )(bias, q, g, k, v)


def output_grad_kernel(ho_ref, g_ref, out_ref):
    product = dot(ho_ref[0], g_ref[...], ((0,), (0,))).astype(BF16)
    for part in range(out_ref.shape[0]):
        out_ref[part] = product[:, part * 128 : (part + 1) * 128]


def output_weight_terms(heads_out, cotangent):
    layers, tokens, cols = heads_out.shape
    wide = cotangent.shape[1]
    return pl.pallas_call(
        output_grad_kernel,
        grid=(layers,),
        in_specs=[
            pl.BlockSpec((1, tokens, cols), lambda i: (i, 0, 0)),
            pl.BlockSpec((tokens, wide), lambda i: (0, 0)),
        ],
        out_specs=pl.BlockSpec((wide // 128, cols, 128), lambda i: (0, i, 0)),
        out_shape=jax.ShapeDtypeStruct((wide // 128, layers * cols, 128), BF16),
        compiler_params=pltpu.CompilerParams(vmem_limit_bytes=VMEM),
        cost_estimate=pl.CostEstimate(
            flops=2 * tokens * layers * cols * wide,
            bytes_accessed=2 * (tokens * layers * cols + tokens * wide + layers * cols * wide),
            transcendentals=0,
        ),
        name="output_weight_terms",
    )(heads_out, cotangent)


def query_grad_kernel(x_ref, dq_ref, out_ref):
    left = x_ref[...].T
    cols = dq_ref.shape[2]
    for layer in range(dq_ref.shape[0]):
        out_ref[:, layer * cols : (layer + 1) * cols] = dot(left, dq_ref[layer], ((1,), (0,))).astype(BF16)


def query_weight_terms(states, query_grad):
    layers, tokens, cols = query_grad.shape
    wide = states.shape[1]
    rows = 256
    return pl.pallas_call(
        query_grad_kernel,
        grid=(wide // rows,),
        in_specs=[
            pl.BlockSpec((tokens, rows), lambda i: (0, i)),
            pl.BlockSpec((layers, tokens, cols), lambda i: (0, 0, 0)),
        ],
        out_specs=pl.BlockSpec((rows, layers * cols), lambda i: (i, 0)),
        out_shape=jax.ShapeDtypeStruct((wide, layers * cols), BF16),
        compiler_params=pltpu.CompilerParams(vmem_limit_bytes=VMEM),
        cost_estimate=pl.CostEstimate(
            flops=2 * tokens * layers * cols * wide,
            bytes_accessed=2 * (tokens * layers * cols + tokens * wide + layers * cols * wide),
            transcendentals=0,
        ),
        name="query_weight_terms",
    )(states, query_grad)


def ordered(mine, other, index, axis):
    return jnp.where(
        index == 0, jnp.concatenate([mine, other], axis), jnp.concatenate([other, mine], axis)
    )


def on_device(
    decoder_states,
    query_weight,
    output_weight,
    context_keys,
    context_values,
    lengths,
    slot_passage,
    output_cotangent,
):
    xh, core, z = lax.axis_index("xh"), lax.axis_index("core"), lax.axis_index("z")
    tokens, cols = decoder_states.shape
    layers = lax.axis_size("z")
    piece = cols // layers

    def all_features(local):
        over_x = ordered(local[:, None], lax.ppermute(local, "xh", SWAP)[:, None], xh, 1)
        other = lax.ppermute(over_x, "core", SWAP)
        full = ordered(over_x[:, :, None], other[:, :, None], core, 2)
        return full.reshape(tokens, 4 * cols)

    own = jnp.stack([context_keys, context_values]).reshape(2, 8, 16, piece).transpose(2, 0, 1, 3)
    parts = lax.all_to_all(own, HEADS + ("z",), 0, 0, tiled=True)
    parts = parts.transpose(1, 0, 2, 3).reshape(1, 2, 128, piece)
    context = lax.all_to_all(
        jnp.broadcast_to(parts, (8, 2, 128, piece)), ("y", "xl"), 0, 0, tiled=True
    )
    keys = context[:, 0].reshape(1024, piece)
    values = context[:, 1].reshape(1024, piece)
    bias = context_bias(lengths, slot_passage, 256)

    wide_states = all_features(decoder_states)
    wide_grad = all_features(output_cotangent)
    queries = jnp.dot(wide_states, query_weight, preferred_element_type=F32).astype(BF16)
    heads_grad = dot(wide_grad, output_weight, ((1,), (1,))).astype(BF16)

    def by_heads(rows):
        split = rows.reshape(tokens, layers, piece).transpose(1, 0, 2)
        return lax.all_to_all(split, "z", 0, 0, tiled=True).reshape(layers * tokens, piece)

    group_queries = by_heads(queries)
    group_grad = by_heads(heads_grad)

    def column_block(full):
        half = lax.dynamic_index_in_dim(full.reshape(tokens, layers, 2, cols // 2), core, 2, False)
        mine = lax.all_to_all(half.transpose(1, 0, 2), "z", 0, 0, tiled=True)
        mine = mine.reshape(layers * tokens, cols // 2)
        return ordered(mine, lax.ppermute(mine, "core", SWAP), core, 1)

    group_cotangent = column_block(wide_grad)
    group_states = column_block(wide_states)

    heads_out, query_grad, key_terms, value_terms = attention(
        bias, group_queries, group_grad, keys, values
    )

    def along_z(local):
        copies = jnp.broadcast_to(local[None], (layers,) + local.shape)
        return lax.all_to_all(copies, "z", 0, 0, tiled=True)

    every_out = along_z(heads_out)

    def plane_sum(terms):
        moved = lax.all_to_all(terms, ("y", "xl"), 0, 0, tiled=True)
        return jnp.sum(moved.astype(F32), axis=0)

    output_weight_grad = plane_sum(output_weight_terms(every_out, group_cotangent))

    own_out = lax.dynamic_slice_in_dim(every_out, z * tokens, tokens, 1)
    own_out = own_out.transpose(1, 0, 2).reshape(tokens, cols)
    partial = jnp.dot(own_out, output_weight, preferred_element_type=F32)
    partial = partial.reshape(tokens, 2, 2, cols)
    kept = lax.dynamic_index_in_dim(partial, core, 2, False)
    given = lax.dynamic_index_in_dim(partial, 1 - core, 2, False).astype(BF16)
    pair = kept + lax.ppermute(given, "core", SWAP).astype(F32)
    kept = lax.dynamic_index_in_dim(pair, xh, 1, False)
    given = lax.dynamic_index_in_dim(pair, 1 - xh, 1, False).astype(BF16)
    attended = (kept + lax.ppermute(given, "xh", SWAP).astype(F32)).astype(BF16)

    every_query_grad = along_z(query_grad)
    query_weight_grad = plane_sum(
        query_weight_terms(group_states, every_query_grad).reshape(8, 128, cols)
    )

    terms = jnp.stack([key_terms.reshape(8, 128, piece), value_terms.reshape(8, 128, piece)], 1)
    sums = plane_sum(terms).astype(BF16)
    owned = lax.all_to_all(
        sums.reshape(2, 16, 8, piece).transpose(1, 0, 2, 3), HEADS + ("z",), 0, 0, tiled=True
    )
    owned = owned.transpose(1, 2, 0, 3).reshape(2, 8, 16 * piece).astype(F32)
    return attended, query_weight_grad, output_weight_grad, owned[0], owned[1]


def solution(mesh):
    devices = mesh.devices.reshape([size for _, size in AXES])
    split = Mesh(devices, [name for name, _ in AXES])
    return jax.shard_map(
        on_device,
        mesh=split,
        in_specs=(
            P(SEQ, HEADS),
            P(None, HEADS),
            P(HEADS, None),
            P(HEADS + SEQ, None),
            P(HEADS + SEQ, None),
            P(),
            P(),
            P(SEQ, HEADS),
        ),
        out_specs=(
            P(SEQ, HEADS),
            P(SEQ, HEADS),
            P(HEADS, SEQ),
            P(HEADS + SEQ, None),
            P(HEADS + SEQ, None),
        ),
        check_vma=False,
    )
```

time: 898 us -> 309 us (0.34)
  waiting for transfers between devices: 719 us -> 106 us
  matrix products: 59.7 us -> 18.2 us
  starting transfers between devices: 18.4 us -> 54.4 us
  blocking collectives: 10.1 us -> 42.8 us
  local copies, waits for them, and re-layouts: 62 us -> 35.2 us
  Pallas kernels: 0 us -> 25.3 us
  between operations: 14.3 us -> 0.99 us
  other arithmetic: 13 us -> 23.1 us
    all_gather x4 -> x0, waiting for transfers between devices: 324 us -> none  [the longest x1 150 us: on_device(): lax.all_gather(block_keys, 'seq', axis=0, tiled=True)]
    unnamed x9 -> x0, waiting for transfers between devices: 301 us -> none
    ppermute x0 -> x8, waiting for transfers between devices: none -> 45.4 us  [the longest x1 30.8 us: on_device(): attended = (kept + lax.ppermute(given, 'xh', SWAP).astype(F32)).astype(BF16)]
    dot_general x10 -> x3, matrix products: 54.6 us -> 18.2 us  [the longest x1 6.52 us: dot(): lax.dot_general(a, b, (contract, ((), ())), preferred_element_type=F32)]
    all_to_all x1 -> x2, blocking collectives: 10.1 us -> 42.8 us  [the longest x1 30.3 us: along_z(): return lax.all_to_all(copies, 'z', 0, 0, tiled=True)]
    all_to_all x3 -> x10, waiting for transfers between devices: 92.8 us -> 60.8 us  [the longest x1 15.2 us: along_z(): return lax.all_to_all(copies, 'z', 0, 0, tiled=True)]
    unnamed x16 -> x26, local copies, waits for them, and re-layouts: 31.4 us -> 3.4 us
    all_to_all x3 -> x10, starting transfers between devices: 17.9 us -> 45.7 us  [the longest x3 14 us: plane_sum(): moved = lax.all_to_all(terms, ('y', 'xl'), 0, 0, tiled=True)]
  transfers between devices with their start and end apart: 10 -> 18, of which waited for: 9 -> 10; matrix products, arithmetic and copies ran while one was open for 13% -> 22% of each run, Pallas kernels for 0% -> 8%
where the time goes in v1:
time: 309 us; the launch traced here: 306 us
  waiting for transfers between devices  106 us (34%)
  starting transfers between devices  54.4 us (18%)
  blocking collectives  42.8 us (14%)
  local copies, waits for them, and re-layouts  35.2 us (11%)
  Pallas kernels  25.3 us (8%)
  other arithmetic  23.1 us (7%)
  matrix products  18.2 us (6%)
    ppermute x1, waiting for transfers between devices, on_device(): attended = (kept + lax.ppermute(given, 'xh', SWAP).astype(F32)).astype(BF16)  30.8 us
    all_to_all x1, blocking collectives, along_z(): return lax.all_to_all(copies, 'z', 0, 0, tiled=True)  30.3 us
    all_to_all x1, waiting for transfers between devices, along_z(): return lax.all_to_all(copies, 'z', 0, 0, tiled=True)  15.2 us
    all_to_all x3, starting transfers between devices, plane_sum(): moved = lax.all_to_all(terms, ('y', 'xl'), 0, 0, tiled=True)  14 us
    pallas_call x1, Pallas kernels, attention(): pl.pallas_call(attention_kernel, grid=(cols // HEAD, tokens // rows), in_...  13.1 us
    all_to_all x1, blocking collectives, on_device(): lax.all_to_all(sums.reshape(2, 16, 8, piece).transpose(1, 0, 2, 3), HEADS...  12.5 us
    dot_general x1, local copies, waits for them, and re-layouts, on_device(): partial = jnp.dot(own_out, output_weight, preferred_element_type=F32)  12 us
    ppermute x2, waiting for transfers between devices, all_features(): lax.ppermute(local, 'xh', SWAP)[:, None]  11.9 us
  transfers between devices with their start and end apart: 18, of which 10 were waited for; matrix products, arithmetic and copies ran while one was open for 22% of the time, Pallas kernels for 8%

profile of v1, /device:TPU:0, one launch (start us, length us, event | category | flops | bytes accessed | tf_op | source)
XLA Modules:
  0.0 306.2 jit_solution(7127016638552931029)
XLA Ops:
  5.2 11.9 %collective-permute-done.2 = bf16[256,1024]{0,1:T(8,128)(2,1)S(1)} collective-permute-done((bf16[256,1024]{0,1:T(8,128)(2,1)S(1)}, bf16[256,1024]{0,1:T(8,128)(2,1)S(1)}, u32[]{:S(2)}, u32[]{:S(2)}) %collective-permute-start.2) | collective-permute-done | bytes 524320 | tf_op jit(solution)/shard_map/ppermute | solution.py:179
  22.5 5.4 %all-to-all-start.2 = ((bf16[16,2,8,256]{3,2,1,0:T(8,128)(2,1)}), bf16[16,2,8,256]{3,2,1,0:T(8,128)(2,1)S(1)}, u32[]{:S(2)}, u32[]{:S(2)}) async-start(bf16[16,2,8,256]{3,2,1,0:T(8,128)(2,1)} %maximum_bitcast_fusion), calls=%async_computation.2 | async-start | bytes 262144 | tf_op jit(solution)/shard_map/all_to_all | solution.py:185
  27.9 11.3 %all-to-all-done.2 = bf16[16,2,8,256]{3,2,1,0:T(8,128)(2,1)S(1)} async-done(((bf16[16,2,8,256]{3,2,1,0:T(8,128)(2,1)}), bf16[16,2,8,256]{3,2,1,0:T(8,128)(2,1)S(1)}, u32[]{:S(2)}, u32[]{:S(2)}) %all-to-all-start.2) | async-done | bytes 131104 | tf_op jit(solution)/shard_map/all_to_all | solution.py:185
  40.3 5.4 %all-to-all-start.3 = ((bf16[8,2,128,256]{3,2,1,0:T(8,128)(2,1)}), bf16[8,2,128,256]{3,2,1,0:T(8,128)(2,1)S(1)}, u32[]{:S(2)}, u32[]{:S(2)}) async-start(bf16[8,2,128,256]{3,2,1,0:T(8,128)(2,1)} %broadcast_in_dim.91), calls=%async_computation.3 | async-start | bytes 2097152 | tf_op jit(solution)/shard_map/all_to_all | solution.py:187
  48.4 6.5 %convolution_convert_fusion = bf16[256,1024]{1,0:T(8,128)(2,1)S(1)} fusion(bf16[256,4096]{0,1:T(8,128)(2,1)S(1)} %bitcast.97, bf16[1024,4096]{1,0:T(8,128)(2,1)} %param.10), kind=kOutput, calls=%fused_computation.9 | convolution fusion | flops 2147745792 | bytes 11010048 | tf_op jit(solution)/shard_map/dot_general | solution.py:34
  56.1 5.6 %all-to-all-done.3 = bf16[8,2,128,256]{3,2,1,0:T(8,128)(2,1)S(1)} async-done(((bf16[8,2,128,256]{3,2,1,0:T(8,128)(2,1)}), bf16[8,2,128,256]{3,2,1,0:T(8,128)(2,1)S(1)}, u32[]{:S(2)}, u32[]{:S(2)}) %all-to-all-start.3) | async-done | bytes 1048608 | tf_op jit(solution)/shard_map/all_to_all | solution.py:187
  61.8 4.1 %all-to-all-start.1 = ((bf16[4,256,256]{2,1,0:T(8,128)(2,1)}), bf16[4,256,256]{2,1,0:T(8,128)(2,1)}, u32[]{:S(2)}, u32[]{:S(2)}) async-start(bf16[4,256,256]{2,1,0:T(8,128)(2,1)} %bitcast.110), calls=%async_computation.1 | async-start | bytes 1048576 | tf_op jit(solution)/shard_map/all_to_all | solution.py:201
  65.9 5.7 %convolution_convert_fusion.1 = bf16[256,1024]{1,0:T(8,128)(2,1)S(1)} fusion(bf16[256,4096]{0,1:T(8,128)(2,1)S(1)} %bitcast.89, bf16[4096,1024]{1,0:T(8,128)(2,1)} %param.9), kind=kOutput, calls=%fused_computation.10 | convolution fusion | flops 2147745792 | bytes 11010048 | tf_op jit(solution)/shard_map/dot_general | solution.py:196
  81.9 5.2 %all-to-all-done = bf16[4,256,256]{2,1,0:T(8,128)(2,1)} async-done(((bf16[4,256,256]{2,1,0:T(8,128)(2,1)}), bf16[4,256,256]{2,1,0:T(8,128)(2,1)}, u32[]{:S(2)}, u32[]{:S(2)}) %all-to-all-start) | async-done | bytes 524320 | tf_op jit(solution)/shard_map/all_to_all | solution.py:201
  93.5 13.1 %attention.1 = (bf16[1024,256]{1,0:T(8,128)(2,1)}, bf16[1024,256]{1,0:T(8,128)(2,1)}, bf16[1024,256]{1,0:T(8,128)(2,1)}, bf16[1024,256]{1,0:T(8,128)(2,1)}) custom-call(f32[1,1024]{1,0:T(1,128)} %compare_select_fusion.2.bias, bf16[1024,256]{1,0:T(8,128)(2,1)} %bitcast.9.q_ref, bf16[1024,256]{1,0:T(8,128)(2,1)} %bitcast.17.g_ref, ...), custom_call_target="tpu_custom_call" | custom-call | flops 3221225472 | bytes 4194304 | tf_op jit(solution)/shard_map/attention/pallas_call | solution.py:71
  108.9 4.8 %all-to-all-start.10 = ((bf16[8,2,128,256]{3,2,1,0:T(8,128)(2,1)}), bf16[8,2,128,256]{3,2,1,0:T(8,128)(2,1)}, u32[]{:S(2)}, u32[]{:S(2)}) async-start(bf16[8,2,128,256]{3,2,1,0:T(8,128)(2,1)} %pad_maximum_fusion), calls=%async_computation.10 | async-start | bytes 2097152 | tf_op jit(solution)/shard_map/all_to_all | solution.py:226
  116.9 10.7 %all-to-all-done.10 = bf16[8,2,128,256]{3,2,1,0:T(8,128)(2,1)} async-done(((bf16[8,2,128,256]{3,2,1,0:T(8,128)(2,1)}), bf16[8,2,128,256]{3,2,1,0:T(8,128)(2,1)}, u32[]{:S(2)}, u32[]{:S(2)}) %all-to-all-start.10) | async-done | bytes 1048608 | tf_op jit(solution)/shard_map/all_to_all | solution.py:226
  127.6 4.5 %all-to-all-start.5 = ((bf16[4,256,512]{2,1,0:T(8,128)(2,1)}), bf16[4,256,512]{2,1,0:T(8,128)(2,1)S(1)}, u32[]{:S(2)}, u32[]{:S(2)}) async-start(bf16[4,256,512]{2,1,0:T(8,128)(2,1)} %bitcast.36), calls=%async_computation.5 | async-start | bytes 2097152 | tf_op jit(solution)/shard_map/all_to_all | solution.py:208
  133.5 10.3 %all-to-all-done.5 = bf16[4,256,512]{2,1,0:T(8,128)(2,1)S(1)} async-done(((bf16[4,256,512]{2,1,0:T(8,128)(2,1)}), bf16[4,256,512]{2,1,0:T(8,128)(2,1)S(1)}, u32[]{:S(2)}, u32[]{:S(2)}) %all-to-all-start.5) | async-done | bytes 1048608 | tf_op jit(solution)/shard_map/all_to_all | solution.py:208
  143.8 12.5 %all_to_all.60 = bf16[16,2,8,256]{3,2,1,0:T(8,128)(2,1)S(1)} all-to-all(bf16[16,2,8,256]{3,2,1,0:T(8,128)(2,1)S(1)} %copy.109), channel_id=1, replica_groups=mesh['xh'=2,'core'=2,'z'=4,'y'=4,'xl'=2] {'xh','core','z'}, dimensions={0} | all-to-all | bytes 262144 | tf_op jit(solution)/shard_map/all_to_all | solution.py:249
  157.6 30.3 %all_to_all.61.ho_ref = bf16[4,1024,256]{2,1,0:T(8,128)(2,1)} all-to-all(bf16[4,1024,256]{2,1,0:T(8,128)(2,1)S(1)} %broadcast_in_dim.92), channel_id=1, replica_groups=mesh['xh'=2,'core'=2,'z'=4,'y'=4,'xl'=2] {'z'}, dimensions={0} | all-to-all | bytes 4194304 | tf_op jit(solution)/shard_map/all_to_all | solution.py:221
  189.3 4.6 %all-to-all-start.6 = ((bf16[4,1024,256]{2,1,0:T(8,128)(2,1)}), bf16[4,1024,256]{2,1,0:T(8,128)(2,1)}, u32[]{:S(2)}, u32[]{:S(2)}) async-start(bf16[4,1024,256]{2,1,0:T(8,128)(2,1)} %broadcast_in_dim.93), calls=%async_computation.6 | async-start | bytes 4194304 | tf_op jit(solution)/shard_map/all_to_all | solution.py:221
  198.7 6.1 %output_weight_terms.1 = bf16[8,1024,128]{2,1,0:T(8,128)(2,1)} custom-call(bf16[4,1024,256]{2,1,0:T(8,128)(2,1)} %all_to_all.61.ho_ref, bf16[1024,1024]{1,0:T(8,128)(2,1)} %maximum_select_fusion.3.g_ref), custom_call_target="tpu_custom_call" | custom-call | flops 2147483648 | bytes 6291456 | tf_op jit(solution)/shard_map/output_weight_terms/pallas_call | solution.py:108
  204.8 15.2 %all-to-all-done.6.dq_ref = bf16[4,1024,256]{2,1,0:T(8,128)(2,1)} async-done(((bf16[4,1024,256]{2,1,0:T(8,128)(2,1)}), bf16[4,1024,256]{2,1,0:T(8,128)(2,1)}, u32[]{:S(2)}, u32[]{:S(2)}) %all-to-all-start.6) | async-done | bytes 2097184 | tf_op jit(solution)/shard_map/all_to_all | solution.py:221
  223.6 12.0 %copy.112 = bf16[4096,1024]{1,0:T(8,128)(2,1)} copy(bf16[4096,1024]{0,1:T(8,128)(2,1)} %bitcast.91) | data formatting | bytes 16777216 | tf_op jit(solution)/shard_map/dot_general | solution.py:233
  239.6 6.0 %fusion.14 = f32[256,2,2,1024]{3,0,2,1:T(8,128)S(1)} fusion(bf16[256,1024,1,1]{0,1,3,2:T(8,128)(2,1)} %bitcast.114, bf16[2,2,1024,1024]{3,2,1,0:T(8,128)(2,1)} %bitcast.92), kind=kOutput, calls=%fused_computation.62 | convolution fusion | flops 2147483648 | bytes 13107200 | tf_op jit(solution)/shard_map/dot_general | solution.py:233
  251.6 6.1 %query_weight_terms.1 = bf16[1024,1024]{1,0:T(8,128)(2,1)} custom-call(bf16[1024,1024]{1,0:T(8,128)(2,1)} %maximum_select_fusion.2.x_ref, bf16[4,1024,256]{2,1,0:T(8,128)(2,1)} %all-to-all-done.6.dq_ref), custom_call_target="tpu_custom_call" | custom-call | flops 2147483648 | bytes 6291456 | tf_op jit(solution)/shard_map/query_weight_terms/pallas_call | solution.py:138
  257.7 5.6 %all-to-all-start.7 = ((bf16[8,128,1024]{2,1,0:T(8,128)(2,1)}), bf16[8,128,1024]{2,1,0:T(8,128)(2,1)}, u32[]{:S(2)}, u32[]{:S(2)}) async-start(bf16[8,128,1024]{2,1,0:T(8,128)(2,1)} %bitcast.109), calls=%async_computation.7 | async-start | bytes 4194304 | tf_op jit(solution)/shard_map/all_to_all | solution.py:226
  269.3 30.8 %collective-permute-done.5 = bf16[256,1024]{1,0:T(8,128)(2,1)S(1)} collective-permute-done((bf16[256,1024]{1,0:T(8,128)(2,1)S(1)}, bf16[256,1024]{1,0:T(8,128)(2,1)S(1)}, u32[]{:S(2)}, u32[]{:S(2)}) %collective-permute-start.5) | collective-permute-done | bytes 524320 | tf_op jit(solution)/shard_map/ppermute | solution.py:240
  (85 shorter events, 71.2 us)
Async XLA Ops:
  0.6 17.6 %copy-start.7 = (bf16[256,1024]{1,0:T(8,128)(2,1)S(1)}, bf16[256,1024]{1,0:T(8,128)(2,1)}, u32[]{:S(2)}) copy-start(bf16[256,1024]{1,0:T(8,128)(2,1)} %param.8) | copy-start | bytes 1572868
  0.6 21.2 %copy-start.8 = (bf16[8,4096]{1,0:T(8,128)(2,1)S(1)}, bf16[8,4096]{1,0:T(8,128)(2,1)}, u32[]{:S(2)}) copy-start(bf16[8,4096]{1,0:T(8,128)(2,1)} %param.12) | copy-start | bytes 196612
  0.7 21.1 %copy-start.9 = (bf16[8,4096]{1,0:T(8,128)(2,1)S(1)}, bf16[8,4096]{1,0:T(8,128)(2,1)}, u32[]{:S(2)}) copy-start(bf16[8,4096]{1,0:T(8,128)(2,1)} %param.11) | copy-start | bytes 196612
  2.0 15.1 %collective-permute-start.2 = (bf16[256,1024]{0,1:T(8,128)(2,1)S(1)}, bf16[256,1024]{0,1:T(8,128)(2,1)S(1)}, u32[]{:S(2)}, u32[]{:S(2)}) collective-permute-start(bf16[256,1024]{0,1:T(8,128)(2,1)S(1)} %copy.95), channel_id=1, source_target_pairs={{0,64},{64,0},{1,65},{65,1},{2,66},{66,2},{3,67},{67,3},{4,68},{68... | collective-permute-start | bytes 1572872 | tf_op jit(solution)/shard_map/ppermute | solution.py:179
  18.3 28.1 %collective-permute-start.3 = (bf16[256,2,1024]{0,2,1:T(8,128)(2,1)}, bf16[256,2,1024]{0,2,1:T(8,128)(2,1)}, u32[]{:S(2)}, u32[]{:S(2)}) collective-permute-start(bf16[256,2,1024]{0,2,1:T(8,128)(2,1)} %maximum_select_fusion.6), channel_id=1, source_target_pairs={{0,32},{32,0},{1,33},{33,1},{2,34},{34,2},{3,35},{35,3},{4,36},{36... | collective-permute-start | bytes 3145736 | tf_op jit(solution)/shard_map/ppermute | solution.py:180
  18.5 27.3 %collective-permute-start = (bf16[256,1024]{0,1:T(8,128)(2,1)S(1)}, bf16[256,1024]{0,1:T(8,128)(2,1)S(1)}, u32[]{:S(2)}, u32[]{:S(2)}) collective-permute-start(bf16[256,1024]{0,1:T(8,128)(2,1)S(1)} %copy.89), channel_id=1, source_target_pairs={{0,64},{64,0},{1,65},{65,1},{2,66},{66,2},{3,67},{67,3},{4,68},{68... | collective-permute-start | bytes 1572872 | tf_op jit(solution)/shard_map/ppermute | solution.py:179
  22.5 16.8 %all-to-all-start.2 = ((bf16[16,2,8,256]{3,2,1,0:T(8,128)(2,1)}), bf16[16,2,8,256]{3,2,1,0:T(8,128)(2,1)S(1)}, u32[]{:S(2)}, u32[]{:S(2)}) async-start(bf16[16,2,8,256]{3,2,1,0:T(8,128)(2,1)} %maximum_bitcast_fusion), calls=%async_computation.2 | async-start | bytes 262144 | tf_op jit(solution)/shard_map/all_to_all | solution.py:185
  40.3 21.4 %all-to-all-start.3 = ((bf16[8,2,128,256]{3,2,1,0:T(8,128)(2,1)}), bf16[8,2,128,256]{3,2,1,0:T(8,128)(2,1)S(1)}, u32[]{:S(2)}, u32[]{:S(2)}) async-start(bf16[8,2,128,256]{3,2,1,0:T(8,128)(2,1)} %broadcast_in_dim.91), calls=%async_computation.3 | async-start | bytes 2097152 | tf_op jit(solution)/shard_map/all_to_all | solution.py:187
  45.9 9.9 %collective-permute-start.1 = (bf16[256,2,1024]{0,2,1:T(8,128)(2,1)S(1)}, bf16[256,2,1024]{0,2,1:T(8,128)(2,1)S(1)}, u32[]{:S(2)}, u32[]{:S(2)}) collective-permute-start(bf16[256,2,1024]{0,2,1:T(8,128)(2,1)S(1)} %maximum_select_fusion.4), channel_id=1, source_target_pairs={{0,32},{32,0},{1,33},{33,1},{2,34},{34,2},{3,35},{35,3},{4,36},{36... | collective-permute-start | bytes 3145736 | tf_op jit(solution)/shard_map/ppermute | solution.py:180
  61.8 9.9 %copy-start.4 = (bf16[8,2,128,256]{3,2,1,0:T(8,128)(2,1)}, bf16[8,2,128,256]{3,2,1,0:T(8,128)(2,1)S(1)}, u32[]{:S(2)}) copy-start(bf16[8,2,128,256]{3,2,1,0:T(8,128)(2,1)S(1)} %all-to-all-done.3) | copy-start | bytes 3145732
  61.8 13.1 %all-to-all-start.1 = ((bf16[4,256,256]{2,1,0:T(8,128)(2,1)}), bf16[4,256,256]{2,1,0:T(8,128)(2,1)}, u32[]{:S(2)}, u32[]{:S(2)}) async-start(bf16[4,256,256]{2,1,0:T(8,128)(2,1)} %bitcast.110), calls=%async_computation.1 | async-start | bytes 1048576 | tf_op jit(solution)/shard_map/all_to_all | solution.py:201
  71.7 7.3 %copy-start.10 = (s32[4]{0:T(128)S(1)}, s32[4]{0:T(128)}, u32[]{:S(2)}) copy-start(s32[4]{0:T(128)} %param.13) | copy-start | bytes 52
  74.8 12.3 %all-to-all-start = ((bf16[4,256,256]{2,1,0:T(8,128)(2,1)}), bf16[4,256,256]{2,1,0:T(8,128)(2,1)}, u32[]{:S(2)}, u32[]{:S(2)}) async-start(bf16[4,256,256]{2,1,0:T(8,128)(2,1)} %bitcast.87), calls=%async_computation | async-start | bytes 1048576 | tf_op jit(solution)/shard_map/all_to_all | solution.py:201
  87.1 21.7 %all-to-all-start.8 = ((bf16[4,256,512]{2,1,0:T(8,128)(2,1)}), bf16[4,256,512]{2,1,0:T(8,128)(2,1)S(1)}, u32[]{:S(2)}, u32[]{:S(2)}) async-start(bf16[4,256,512]{2,1,0:T(8,128)(2,1)} %bitcast.103), calls=%async_computation.8 | async-start | bytes 2097152 | tf_op jit(solution)/shard_map/all_to_all | solution.py:208
  108.9 18.8 %all-to-all-start.10 = ((bf16[8,2,128,256]{3,2,1,0:T(8,128)(2,1)}), bf16[8,2,128,256]{3,2,1,0:T(8,128)(2,1)}, u32[]{:S(2)}, u32[]{:S(2)}) async-start(bf16[8,2,128,256]{3,2,1,0:T(8,128)(2,1)} %pad_maximum_fusion), calls=%async_computation.10 | async-start | bytes 2097152 | tf_op jit(solution)/shard_map/all_to_all | solution.py:226
  127.6 16.2 %all-to-all-start.5 = ((bf16[4,256,512]{2,1,0:T(8,128)(2,1)}), bf16[4,256,512]{2,1,0:T(8,128)(2,1)S(1)}, u32[]{:S(2)}, u32[]{:S(2)}) async-start(bf16[4,256,512]{2,1,0:T(8,128)(2,1)} %bitcast.36), calls=%async_computation.5 | async-start | bytes 2097152 | tf_op jit(solution)/shard_map/all_to_all | solution.py:208
  157.5 30.3 %copy-start.6 = (bf16[1024,256]{1,0:T(8,128)(2,1)S(1)}, bf16[1024,256]{1,0:T(8,128)(2,1)}, u32[]{:S(2)}) copy-start(bf16[1024,256]{1,0:T(8,128)(2,1)} %get-tuple-element.10) | copy-start | bytes 1572868
  189.3 30.7 %all-to-all-start.6 = ((bf16[4,1024,256]{2,1,0:T(8,128)(2,1)}), bf16[4,1024,256]{2,1,0:T(8,128)(2,1)}, u32[]{:S(2)}, u32[]{:S(2)}) async-start(bf16[4,1024,256]{2,1,0:T(8,128)(2,1)} %broadcast_in_dim.93), calls=%async_computation.6 | async-start | bytes 4194304 | tf_op jit(solution)/shard_map/all_to_all | solution.py:221
  194.0 2.7 collective-permute-start.7
  220.0 37.7 %all-to-all-start.9 = ((bf16[8,1024,128]{2,1,0:T(8,128)(2,1)}), bf16[8,1024,128]{2,1,0:T(8,128)(2,1)S(1)}, u32[]{:S(2)}, u32[]{:S(2)}) async-start(bf16[8,1024,128]{2,1,0:T(8,128)(2,1)} %output_weight_terms.1), calls=%async_computation.9 | async-start | bytes 4194304 | tf_op jit(solution)/shard_map/all_to_all | solution.py:226
  235.7 11.7 %collective-permute-start.6 = (bf16[1024,512]{1,0:T(8,128)(2,1)S(1)}, bf16[1024,512]{1,0:T(8,128)(2,1)}, u32[]{:S(2)}, u32[]{:S(2)}) collective-permute-start(bf16[1024,512]{1,0:T(8,128)(2,1)S(1)} %bitcast.99), channel_id=1, source_target_pairs={{0,32},{32,0},{1,33},{33,1},{2,34},{34,2},{3,35},{35,3},{4,36},{36... | collective-permute-start | bytes 3145736 | tf_op jit(solution)/shard_map/ppermute | solution.py:210
  246.8 16.5 %collective-permute-start.4 = (bf16[256,2,1024]{2,0,1:T(8,128)(2,1)}, bf16[256,2,1024]{2,0,1:T(8,128)(2,1)}, u32[]{:S(2)}, u32[]{:S(2)}) collective-permute-start(bf16[256,2,1024]{2,0,1:T(8,128)(2,1)} %fusion), channel_id=1, source_target_pairs={{0,32},{32,0},{1,33},{33,1},{2,34},{34,2},{3,35},{35,3},{4,36},{36... | collective-permute-start | bytes 3145736 | tf_op jit(solution)/shard_map/ppermute | solution.py:237
  257.7 45.6 %all-to-all-start.7 = ((bf16[8,128,1024]{2,1,0:T(8,128)(2,1)}), bf16[8,128,1024]{2,1,0:T(8,128)(2,1)}, u32[]{:S(2)}, u32[]{:S(2)}) async-start(bf16[8,128,1024]{2,1,0:T(8,128)(2,1)} %bitcast.109), calls=%async_computation.7 | async-start | bytes 4194304 | tf_op jit(solution)/shard_map/all_to_all | solution.py:226
  267.0 33.1 %collective-permute-start.5 = (bf16[256,1024]{1,0:T(8,128)(2,1)S(1)}, bf16[256,1024]{1,0:T(8,128)(2,1)S(1)}, u32[]{:S(2)}, u32[]{:S(2)}) collective-permute-start(bf16[256,1024]{1,0:T(8,128)(2,1)S(1)} %fusion.2), channel_id=1, source_target_pairs={{0,64},{64,0},{1,65},{65,1},{2,66},{66,2},{3,67},{67,3},{4,68},{68... | collective-permute-start | bytes 1572872 | tf_op jit(solution)/shard_map/ppermute | solution.py:240
  (6 other events, 28.0 us)

commit v2 on v0

v2 whole, which is shorter than its diff:
```python
import math

import jax
import jax.numpy as jnp
from jax import lax
from jax.experimental import pallas as pl
from jax.experimental.pallas import tpu as pltpu
from jax.sharding import Mesh
from jax.sharding import PartitionSpec as P

HEAD = 128
SCALE = 1.0 / math.sqrt(HEAD)
F32 = jnp.float32
BF16 = jnp.bfloat16
AXES = (("xh", 2), ("core", 2), ("z", 4), ("y", 4), ("xl", 2))
HEADS = ("xh", "core")
SEQ = ("z", "y", "xl")
XH, CORE, Z, Y, XL = range(5)
SWAP = [(0, 1), (1, 0)]
VMEM = 56 * 1024 * 1024
TOK = 256
PIECE = 256
GROUP = 4 * TOK
BLOCK = 1024
PLANES = 8


def dot(a, b, contract=((1,), (0,))):
    return lax.dot_general(a, b, (contract, ((), ())), preferred_element_type=F32)


def shifted(index, by, size=4):
    return lax.rem(index + by + size, size)


def head_block(step, pos):
    return lax.rem(pos[XH] + step // 2, 2) * 2 + lax.rem(pos[CORE] + step % 2, 2)


def plane_at(r, pos):
    return shifted(pos[Y], r // 2) * 2 + lax.rem(pos[XL] + r % 2, 2)


def struct(shape, dtype=BF16):
    return jax.ShapeDtypeStruct(shape, dtype)


def whole(shape):
    return pl.BlockSpec(shape, lambda *_: (0,) * len(shape))


def call(kernel, name, grid, in_specs, out_specs, out_shape, scratch, flops, moved, pos, *args):
    return pl.pallas_call(
        kernel,
        grid_spec=pltpu.PrefetchScalarGridSpec(
            num_scalar_prefetch=1,
            grid=grid,
            in_specs=in_specs,
            out_specs=out_specs,
            scratch_shapes=scratch,
        ),
        out_shape=out_shape,
        compiler_params=pltpu.CompilerParams(vmem_limit_bytes=VMEM),
        cost_estimate=pl.CostEstimate(flops=flops, bytes_accessed=moved, transcendentals=0),
        name=name,
    )(pos, *args)


def project_kernel(transposed, pos, x0, x1, x2, x3, w_ref, *rest):
    rows, parts, (total, held) = rest[:4], rest[4:8], rest[8:]
    step = pl.program_id(0)
    contract = ((1,), (1,)) if transposed else ((1,), (0,))
    for i, x in enumerate((x0, x1, x2, x3)):

        @pl.when(step == i)
        def _(i=i, x=x):
            product = dot(x[...], w_ref[...], contract)
            total[...] = product if i == 0 else total[...] + product
            held[head_block(i, pos)] = x[...]

    @pl.when(step == 3)
    def _():
        half = pl.multiple_of(pos[CORE] * (BLOCK // 2), BLOCK // 2)
        for d in range(4):
            layer = shifted(pos[Z], d)
            start = pl.multiple_of(layer * PIECE, PIECE)
            rows[d][...] = total[:, pl.ds(start, PIECE)].astype(BF16)
            parts[d][...] = held[layer, :, pl.ds(half, BLOCK // 2)]


def project(name, pos, blocks, weight, transposed):
    where = (lambda i, pos: (0, head_block(i, pos))) if transposed else (lambda i, pos: (head_block(i, pos), 0))
    outs = call(
        lambda *refs: project_kernel(transposed, *refs),
        name,
        (4,),
        [whole((TOK, BLOCK))] * 4 + [pl.BlockSpec((BLOCK, BLOCK), where)],
        [whole((TOK, PIECE))] * 4 + [whole((TOK, BLOCK // 2))] * 4,
        [struct((TOK, PIECE))] * 4 + [struct((TOK, BLOCK // 2))] * 4,
        [pltpu.VMEM((TOK, BLOCK), F32), pltpu.VMEM((4, TOK, BLOCK), BF16)],
        2 * TOK * 4 * BLOCK * BLOCK,
        2 * 4 * BLOCK * BLOCK,
        pos,
        *blocks,
        weight,
    )
    return outs[:4], outs[4:]


def assemble_kernel(transposed, pos, *refs):
    out = refs[8]
    for d in range(4):
        token = pl.multiple_of(shifted(pos[Z], -d) * TOK, TOK)
        for side in range(2):
            half = pl.multiple_of(lax.rem(pos[CORE] + side, 2) * (BLOCK // 2), BLOCK // 2)
            part = refs[4 * side + d][...]
            if transposed:
                out[pl.ds(half, BLOCK // 2), pl.ds(token, TOK)] = part.T
            else:
                out[pl.ds(token, TOK), pl.ds(half, BLOCK // 2)] = part


def assemble(name, pos, mine, other, transposed):
    return call(
        lambda *refs: assemble_kernel(transposed, *refs),
        name,
        (1,),
        [whole((TOK, BLOCK // 2))] * 8,
        whole((BLOCK, GROUP)),
        struct((BLOCK, GROUP)),
        [],
        0,
        4 * BLOCK * GROUP,
        pos,
        *mine,
        *other,
    )


def attention_kernel(pos, bias, *refs):
    q_refs, g_refs, kv_refs = refs[:4], refs[4:8], refs[8:16]
    out_ref, dq_ref, grad_refs = refs[16], refs[17], refs[18:26]
    dk_sum, dv_sum = refs[26:]
    k = jnp.concatenate([ref[0] for ref in kv_refs], axis=0)
    v = jnp.concatenate([ref[1] for ref in kv_refs], axis=0)
    for d in range(4):
        q, g = q_refs[d][...], g_refs[d][...]
        scores = dot(q, k, ((1,), (1,))) + bias[...]
        top = jnp.max(scores, axis=1, keepdims=True)
        weights = jnp.exp((scores - top) * SCALE)
        probs = weights * (1.0 / jnp.sum(weights, axis=1, keepdims=True))
        probs_low = probs.astype(BF16)
        heads_out = dot(probs_low, v).astype(BF16)
        value_dots = dot(g, v, ((1,), (1,)))
        delta = jnp.sum(g.astype(F32) * heads_out.astype(F32), axis=1, keepdims=True)
        score_grad = (probs * (value_dots - delta) * SCALE).astype(BF16)
        token = pl.multiple_of(shifted(pos[Z], -d) * TOK, TOK)
        out_ref[:, pl.ds(token, TOK)] = heads_out.T
        dq_ref[pl.ds(token, TOK), :] = dot(score_grad, k).astype(BF16)
        dk_term, dv_term = dot(q, score_grad, ((0,), (0,))), dot(g, probs_low, ((0,), (0,)))
        dk_sum[...] = dk_term if d == 0 else dk_sum[...] + dk_term
        dv_sum[...] = dv_term if d == 0 else dv_sum[...] + dv_term
    dk, dv = dk_sum[...].T.astype(BF16), dv_sum[...].T.astype(BF16)
    for r in range(PLANES):
        grad_refs[r][0] = dk[r * 128 : (r + 1) * 128]
        grad_refs[r][1] = dv[r * 128 : (r + 1) * 128]


def attention(pos, bias, queries, grads, context):
    rows = pl.BlockSpec((TOK, HEAD), lambda h, pos: (0, h))
    pair = pl.BlockSpec((2, 128, HEAD), lambda h, pos: (0, 0, h))
    tokens = PLANES * 128
    outs = call(
        attention_kernel,
        "attention",
        (PIECE // HEAD,),
        [whole((1, tokens))] + [rows] * 8 + [pair] * 8,
        [
            pl.BlockSpec((HEAD, GROUP), lambda h, pos: (h, 0)),
            pl.BlockSpec((GROUP, HEAD), lambda h, pos: (0, h)),
        ]
        + [pair] * 8,
        [struct((PIECE, GROUP)), struct((GROUP, PIECE))] + [struct((2, 128, PIECE))] * 8,
        [pltpu.VMEM((HEAD, tokens), F32)] * 2,
        30 * GROUP * PIECE * tokens,
        2 * (4 * GROUP * PIECE + 4 * tokens * PIECE),
        pos,
        bias,
        *queries,
        *grads,
        *context,
    )
    return outs[0], outs[1], outs[2:]


def output_grad_kernel(pos, *refs):
    left, right, outs, held = refs[:4], refs[4], refs[5:13], refs[13]
    for e in range(4):
        row = pl.multiple_of(shifted(pos[Z], -e) * PIECE, PIECE)
        product = dot(left[e][...], right[...]).astype(BF16)
        for p in range(PLANES):
            held[p, pl.ds(row, PIECE), :] = product[:, p * 128 : (p + 1) * 128]
    for r in range(PLANES):
        outs[r][...] = held[plane_at(r, pos)]


def query_grad_kernel(pos, *refs):
    left, right, outs, held = refs[0], refs[1:5], refs[5:13], refs[13]
    for e in range(4):
        col = pl.multiple_of(shifted(pos[Z], -e) * PIECE, PIECE)
        held[:, pl.ds(col, PIECE)] = dot(left[...], right[e][...]).astype(BF16)
    for r in range(PLANES):
        outs[r][...] = held[pl.ds(pl.multiple_of(plane_at(r, pos) * 128, 128), 128), :]


def weight_terms(name, kernel, pos, args, out, held):
    return call(
        kernel,
        name,
        (1,),
        [whole(a.shape) for a in args],
        [whole(out)] * PLANES,
        [struct(out)] * PLANES,
        [pltpu.VMEM(held, BF16)],
        2 * GROUP * BLOCK * BLOCK,
        6 * BLOCK * BLOCK,
        pos,
        *args,
    )


def output_kernel(pos, *refs):
    rows, w_ref, give, keep = refs[:4], refs[4], refs[5], refs[6]
    step = pl.program_id(0)
    product = jnp.zeros((TOK, BLOCK), F32)
    for e in range(4):
        row = pl.multiple_of(shifted(pos[Z], -e) * PIECE, PIECE)
        product = product + dot(rows[e][...], w_ref[pl.ds(row, PIECE), :], ((0,), (0,)))

    @pl.when(step < 2)
    def _():
        give[0] = product.astype(BF16)

    @pl.when(step >= 2)
    def _():
        keep[0] = product


def output_terms(pos, every_out, weight):
    return call(
        output_kernel,
        "output_terms",
        (4,),
        [pl.BlockSpec((PIECE, TOK), lambda n, pos: (0, pos[Z]))] * 4
        + [pl.BlockSpec((BLOCK, BLOCK), lambda n, pos: (0, head_block((n % 2) * 2 + 1 - n // 2, pos)))],
        [
            pl.BlockSpec((1, TOK, BLOCK), lambda n, pos: (jnp.minimum(n, 1), 0, 0)),
            pl.BlockSpec((1, TOK, BLOCK), lambda n, pos: (jnp.maximum(n - 2, 0), 0, 0)),
        ],
        [struct((2, TOK, BLOCK)), struct((2, TOK, BLOCK), F32)],
        [],
        2 * TOK * 4 * BLOCK * BLOCK,
        2 * 4 * BLOCK * BLOCK,
        pos,
        *every_out,
        weight,
    )


def context_bias(pos, lengths, slot_passage):
    slot_lengths = jnp.sum(
        jnp.where(slot_passage[:, None] == jnp.arange(4)[None, :], lengths[None, :], 0), axis=1
    )
    token = jnp.arange(PLANES * 128, dtype=jnp.int32)
    r, slot, layer, row = token // 128, (token // 32) % 4, (token // 8) % 4, token % 8
    plane = ((pos[Y] - r // 2 + 4) % 4) * 2 + (pos[XL] + r % 2) % 2
    position = (layer * PLANES + plane) * 8 + row
    limit = jnp.sum(jnp.where(slot[:, None] == jnp.arange(4)[None, :], slot_lengths[None, :], 0), axis=1)
    return jnp.where(position < limit, 0.0, -jnp.inf).astype(F32)[None, :]


def on_device(
    decoder_states,
    query_weight,
    output_weight,
    context_keys,
    context_values,
    lengths,
    slot_passage,
    output_cotangent,
):
    pos = jnp.stack([lax.axis_index(name) for name, _ in AXES]).astype(jnp.int32)

    def to_layer(x, d):
        return lax.ppermute(x, "z", [(i, (i + d) % 4) for i in range(4)]) if d else x

    def to_plane(x, r):
        pairs = [
            (y * 2 + xl, ((y + r // 2) % 4) * 2 + (xl + r % 2) % 2) for y in range(4) for xl in range(2)
        ]
        return lax.ppermute(x, ("y", "xl"), pairs) if r else x

    def back(r):
        return ((4 - r // 2) % 4) * 2 + r % 2

    def swap(x, axis):
        return lax.ppermute(x, axis, SWAP)

    def head_blocks(local):
        over_x = swap(local, "xh")
        return local, swap(local, "core"), over_x, swap(over_x, "core")

    states = head_blocks(decoder_states)
    cotangent = head_blocks(output_cotangent)

    own = jnp.stack([context_keys, context_values]).reshape(2, 8, 16, PIECE).transpose(2, 0, 1, 3)
    parts = lax.all_to_all(own, HEADS + ("z",), 0, 0, tiled=True)
    parts = parts.transpose(1, 0, 2, 3).reshape(2, 128, PIECE)
    context = [to_plane(parts, r) for r in range(PLANES)]
    bias = context_bias(pos, lengths, slot_passage)

    queries, state_parts = project("queries", pos, states, query_weight, False)
    heads_grad, cotangent_parts = project("heads_grad", pos, cotangent, output_weight, True)
    queries = [to_layer(x, d) for d, x in enumerate(queries)]
    heads_grad = [to_layer(x, d) for d, x in enumerate(heads_grad)]
    cotangent_parts = [to_layer(x, d) for d, x in enumerate(cotangent_parts)]
    state_parts = [to_layer(x, d) for d, x in enumerate(state_parts)]

    out_local, query_grad_local, context_grads = attention(pos, bias, queries, heads_grad, context)
    every_out = [to_layer(out_local, e) for e in range(4)]
    every_query_grad = [to_layer(query_grad_local, e) for e in range(4)]

    group_cotangent = assemble(
        "group_cotangent", pos, cotangent_parts, [swap(x, "core") for x in cotangent_parts], False
    )
    group_states = assemble("group_states", pos, state_parts, [swap(x, "core") for x in state_parts], True)

    def plane_sum(terms, reverse):
        moved = [to_plane(x, back(r) if reverse else r).astype(F32) for r, x in enumerate(terms)]
        total = moved[0]
        for term in moved[1:]:
            total = total + term
        return total

    terms = weight_terms(
        "output_weight_terms",
        output_grad_kernel,
        pos,
        (*every_out, group_cotangent),
        (BLOCK, 128),
        (PLANES, BLOCK, 128),
    )
    output_weight_grad = plane_sum(terms, False)

    give, keep = output_terms(pos, every_out, output_weight)
    pair = keep + swap(give, "core").astype(F32)
    attended = (pair[0] + swap(pair[1].astype(BF16), "xh").astype(F32)).astype(BF16)

    terms = weight_terms(
        "query_weight_terms",
        query_grad_kernel,
        pos,
        (group_states, *every_query_grad),
        (128, BLOCK),
        (BLOCK, BLOCK),
    )
    query_weight_grad = plane_sum(terms, False)

    sums = plane_sum(context_grads, True).astype(BF16)
    owned = lax.all_to_all(
        sums.reshape(2, 16, 8, PIECE).transpose(1, 0, 2, 3), HEADS + ("z",), 0, 0, tiled=True
    )
    owned = owned.transpose(1, 2, 0, 3).reshape(2, 8, 16 * PIECE).astype(F32)
    return attended, query_weight_grad, output_weight_grad, owned[0], owned[1]


def solution(mesh):
    devices = mesh.devices.reshape([size for _, size in AXES])
    split = Mesh(devices, [name for name, _ in AXES])
    return jax.shard_map(
        on_device,
        mesh=split,
        in_specs=(
            P(SEQ, HEADS),
            P(None, HEADS),
            P(HEADS, None),
            P(HEADS + SEQ, None),
            P(HEADS + SEQ, None),
            P(),
            P(),
            P(SEQ, HEADS),
        ),
        out_specs=(
            P(SEQ, HEADS),
            P(SEQ, HEADS),
            P(HEADS, SEQ),
            P(HEADS + SEQ, None),
            P(HEADS + SEQ, None),
        ),
        check_vma=False,
    )
```

time: 898 us -> 284 us (0.32)
  waiting for transfers between devices: 719 us -> 103 us
  starting transfers between devices: 18.4 us -> 107 us
  matrix products: 59.7 us -> 0 us
  local copies, waits for them, and re-layouts: 62 us -> 3.75 us
  Pallas kernels: 0 us -> 57.5 us
  between operations: 14.3 us -> 1.38 us
  blocking collectives: 10.1 us -> 0 us
    all_gather x4 -> x0, waiting for transfers between devices: 324 us -> none  [the longest x1 150 us: on_device(): lax.all_gather(block_keys, 'seq', axis=0, tiled=True)]
    unnamed x9 -> x0, waiting for transfers between devices: 301 us -> none
    ppermute x0 -> x62, waiting for transfers between devices: none -> 95.7 us  [the longest x18 44.2 us: to_layer(): lax.ppermute(x, 'z', [(i, (i + d) % 4) for i in range(4)])]
    ppermute x0 -> x62, starting transfers between devices: none -> 93 us  [the longest x28 46.9 us: to_plane(): return lax.ppermute(x, ('y', 'xl'), pairs) if r else x]
    all_to_all x3 -> x2, waiting for transfers between devices: 92.8 us -> 7.23 us  [the longest x1 4.04 us: on_device(): parts = lax.all_to_all(own, HEADS + ('z',), 0, 0, tiled=True)]
    pallas_call x0 -> x8, Pallas kernels: none -> 57.5 us  [call(): pl.pallas_call(kernel, grid_spec=pltpu.PrefetchScalarGridSpec(num_scalar_...]
    dot_general x10 -> x0, matrix products: 54.6 us -> none  [the longest x1 7.7 us: on_device(): jnp.dot(heads_out, output_weight, preferred_element_type=jnp.float32)]
    unnamed x16 -> x114, local copies, waits for them, and re-layouts: 31.4 us -> 2.33 us
  transfers between devices with their start and end apart: 10 -> 64, of which waited for: 9 -> 20; matrix products, arithmetic and copies ran while one was open for 13% -> 3% of each run, Pallas kernels for 0% -> 16%
where the time goes in v2:
time: 284 us; the launch traced here: 280 us
  starting transfers between devices  107 us (38%)
  waiting for transfers between devices  103 us (36%)
  Pallas kernels  57.5 us (20%)
  other arithmetic  7.42 us (3%)
  local copies, waits for them, and re-layouts  3.75 us (1%)
    pallas_call x8, Pallas kernels, call(): pl.pallas_call(kernel, grid_spec=pltpu.PrefetchScalarGridSpec(num_scalar_...  57.5 us
    ppermute x28, starting transfers between devices, to_plane(): return lax.ppermute(x, ('y', 'xl'), pairs) if r else x  46.9 us
    ppermute x18, waiting for transfers between devices, to_layer(): lax.ppermute(x, 'z', [(i, (i + d) % 4) for i in range(4)])  44.2 us
    ppermute x28, waiting for transfers between devices, to_plane(): return lax.ppermute(x, ('y', 'xl'), pairs) if r else x  31.7 us
    ppermute x18, starting transfers between devices, to_layer(): lax.ppermute(x, 'z', [(i, (i + d) % 4) for i in range(4)])  28.1 us
    ppermute x16, waiting for transfers between devices, swap(): return lax.ppermute(x, axis, SWAP)  19.8 us
    ppermute x16, starting transfers between devices, swap(): return lax.ppermute(x, axis, SWAP)  17.9 us
    all_to_all x1, starting transfers between devices, on_device(): parts = lax.all_to_all(own, HEADS + ('z',), 0, 0, tiled=True)  7.96 us
  transfers between devices with their start and end apart: 64, of which 20 were waited for; matrix products, arithmetic and copies ran while one was open for 3% of the time, Pallas kernels for 16%

profile of v2, /device:TPU:0, one launch (start us, length us, event | category | flops | bytes accessed | tf_op | source)
XLA Modules:
  0.0 279.6 jit_solution(7205166625387614465)
XLA Ops:
  6.3 8.0 %all-to-all-start = ((bf16[16,2,8,256]{3,2,1,0:T(8,128)(2,1)}), bf16[16,2,8,256]{3,2,1,0:T(8,128)(2,1)S(1)}, u32[]{:S(2)}, u32[]{:S(2)}) async-start(bf16[16,2,8,256]{3,2,1,0:T(8,128)(2,1)} %maximum_bitcast_fusion), calls=%async_computation | async-start | bytes 262144 | tf_op jit(solution)/shard_map/all_to_all | solution.py:317
  18.8 9.1 %collective-permute-done.7.refs_3_ = bf16[256,1024]{1,0:T(8,128)(2,1)S(1)} collective-permute-done((bf16[256,1024]{1,0:T(8,128)(2,1)}, bf16[256,1024]{1,0:T(8,128)(2,1)S(1)}, u32[]{:S(2)}, u32[]{:S(2)}) %collective-permute-start.7) | collective-permute-done | bytes 524320 | tf_op jit(solution)/shard_map/ppermute | solution.py:307
  28.0 4.0 %all-to-all-done = bf16[16,2,8,256]{3,2,1,0:T(8,128)(2,1)S(1)} async-done(((bf16[16,2,8,256]{3,2,1,0:T(8,128)(2,1)}), bf16[16,2,8,256]{3,2,1,0:T(8,128)(2,1)S(1)}, u32[]{:S(2)}, u32[]{:S(2)}) %all-to-all-start) | async-done | bytes 131104 | tf_op jit(solution)/shard_map/all_to_all | solution.py:317
  32.0 4.0 %collective-permute-start.18 = (bf16[2,128,256]{2,1,0:T(8,128)(2,1)S(1)}, bf16[2,128,256]{2,1,0:T(8,128)(2,1)S(1)}, u32[]{:S(2)}, u32[]{:S(2)}) collective-permute-start(bf16[2,128,256]{2,1,0:T(8,128)(2,1)S(1)} %copy_bitcast_fusion.1.refs_8_), channel_id=1, source_target_pairs={{0,7},{1,6},{2,1},{3,0},{4,3},{5,2},{6,5},{7,4},{8,15},{9,14},{10,... | collective-permute-start | bytes 393224 | tf_op jit(solution)/shard_map/ppermute | solution.py:301
  37.6 8.2 %queries.1 = (bf16[256,256]{1,0:T(8,128)(2,1)}, bf16[256,256]{1,0:T(8,128)(2,1)}, bf16[256,256]{1,0:T(8,128)(2,1)}, bf16[256,256]{1,0:T(8,128)(2,1)}, bf16[256,5...) custom-call(s32[5]{0:T(128)} %stack.32.refs_0_.pos, ...), custom_call_target="tpu_custom_call" | custom-call | flops 2147483648 | bytes 8388608 | tf_op jit(solution)/shard_map/queries/pallas_call | solution.py:53
  52.3 8.4 %heads_grad.1 = (bf16[256,256]{1,0:T(8,128)(2,1)}, bf16[256,256]{1,0:T(8,128)(2,1)}, bf16[256,256]{1,0:T(8,128)(2,1)}, bf16[256,256]{1,0:T(8,128)(2,1)}, bf16[25...) custom-call(s32[5]{0:T(128)} %stack.32.refs_0_.pos, ...), custom_call_target="tpu_custom_call" | custom-call | flops 2147483648 | bytes 8388608 | tf_op jit(solution)/shard_map/heads_grad/pallas_call | solution.py:53
  74.9 12.0 %attention.1 = (bf16[256,1024]{1,0:T(8,128)(2,1)}, bf16[1024,256]{1,0:T(8,128)(2,1)}, bf16[2,128,256]{2,1,0:T(8,128)(2,1)}, bf16[2,128,256]{2,1,0:T(8,128)(2,1)}...) custom-call(s32[5]{0:T(128)} %stack.32.refs_0_.pos, ...), custom_call_target="tpu_custom_call" | custom-call | flops 8053063680 | bytes 4194304 | tf_op jit(solution)/shard_map/attention/pallas_call | solution.py:53
  92.5 4.2 %collective-permute-start.59 = (bf16[2,128,256]{2,1,0:T(8,128)(2,1)}, bf16[2,128,256]{2,1,0:T(8,128)(2,1)S(1)}, u32[]{:S(2)}, u32[]{:S(2)}) collective-permute-start(bf16[2,128,256]{2,1,0:T(8,128)(2,1)} %get-tuple-element.90), channel_id=1, source_target_pairs={{0,5},{1,4},{2,7},{3,6},{4,1},{5,0},{6,3},{7,2},{8,13},{9,12},{10,... | collective-permute-start | bytes 393224 | tf_op jit(solution)/shard_map/ppermute | solution.py:301
  111.8 5.3 %collective-permute-done.25.refs_3_ = bf16[256,512]{1,0:T(8,128)(2,1)} collective-permute-done((bf16[256,512]{1,0:T(8,128)(2,1)S(1)}, bf16[256,512]{1,0:T(8,128)(2,1)}, u32[]{:S(2)}, u32[]{:S(2)}) %collective-permute-start.25) | collective-permute-done | bytes 262176 | tf_op jit(solution)/shard_map/ppermute | solution.py:295
  117.0 20.4 %collective-permute-done.26.refs_4_ = bf16[256,512]{1,0:T(8,128)(2,1)} collective-permute-done((bf16[256,512]{1,0:T(8,128)(2,1)S(1)}, bf16[256,512]{1,0:T(8,128)(2,1)}, u32[]{:S(2)}, u32[]{:S(2)}) %collective-permute-start.26) | collective-permute-done | bytes 262176 | tf_op jit(solution)/shard_map/ppermute | solution.py:295
  144.0 7.9 %output_terms.1 = (bf16[2,256,1024]{2,1,0:T(8,128)(2,1)}, f32[2,256,1024]{2,1,0:T(8,128)}) custom-call(s32[5]{0:T(128)} %stack.32.refs_0_.pos, bf16[256,1024]{1,0:T(8,128)(2,1)} %get-tuple-element.57.refs_0_, bf16[256,1024]{1,0:T(8,128)(2,1)} %copy-done.3, bf16[256,1024]{1,0:T(8,128)(2,1)} %copy-done.2, bf16[256,1024]{1,0:T(8,128)(2,1)} %copy-done.1, ...), custom_call_target="tpu_custom_call" | custom-call | flops 2147483648 | bytes 8388608 | tf_op jit(solution)/shard_map/output_terms/pallas_call | solution.py:53
  152.3 9.6 %collective-permute-start.30 = (bf16[256,512]{1,0:T(8,128)(2,1)}, bf16[256,512]{1,0:T(8,128)(2,1)S(1)}, u32[]{:S(2)}, u32[]{:S(2)}) collective-permute-start(bf16[256,512]{1,0:T(8,128)(2,1)} %collective-permute-done.26.refs_4_), channel_id=1, source_target_pairs={{0,32},{32,0},{1,33},{33,1},{2,34},{34,2},{3,35},{35,3},{4,36},{36... | collective-permute-start | bytes 786440 | tf_op jit(solution)/shard_map/ppermute | solution.py:307
  163.3 5.6 %all-to-all-start.1 = ((bf16[16,2,8,256]{3,2,1,0:T(8,128)(2,1)}), bf16[16,2,8,256]{3,2,1,0:T(8,128)(2,1)S(1)}, u32[]{:S(2)}, u32[]{:S(2)}) async-start(bf16[16,2,8,256]{3,2,1,0:T(8,128)(2,1)} %copy_bitcast_fusion), calls=%async_computation.1 | async-start | bytes 262144 | tf_op jit(solution)/shard_map/all_to_all | solution.py:370
  177.9 4.1 %group_states.1.refs_0_ = bf16[1024,1024]{1,0:T(8,128)(2,1)} custom-call(s32[5]{0:T(128)} %stack.32.refs_0_.pos, bf16[256,512]{1,0:T(8,128)(2,1)} %get-tuple-element.60.refs_1_, bf16[256,512]{1,0:T(8,128)(2,1)} %copy-done.12, bf16[256,512]{1,0:T(8,128)(2,1)} %collective-permute-done.25.refs_3_, bf16[256,512]{1,0:T(8,128)(2,1)} %collective-permute-done.26.refs_4_, ...), custom_call_target="tpu_custom_call" | custom-call | bytes 4194304 | tf_op jit(solution)/shard_map/group_states/pallas_call | solution.py:53
  182.1 3.7 %group_cotangent.1.refs_4_ = bf16[1024,1024]{1,0:T(8,128)(2,1)} custom-call(s32[5]{0:T(128)} %stack.32.refs_0_.pos, bf16[256,512]{1,0:T(8,128)(2,1)} %get-tuple-element.73.refs_1_, bf16[256,512]{1,0:T(8,128)(2,1)} %collective-permute-done.41.refs_2_, bf16[256,512]{1,0:T(8,128)(2,1)} %copy-done.14, bf16[256,512]{1,0:T(8,128)(2,1)} %copy-done.17, ...), custom_call_target="tpu_custom_call" | custom-call | bytes 4194304 | tf_op jit(solution)/shard_map/group_cotangent/pallas_call | solution.py:53
  185.7 10.2 %collective-permute-done.33.refs_4_ = bf16[1024,256]{1,0:T(8,128)(2,1)} collective-permute-done((bf16[1024,256]{1,0:T(8,128)(2,1)}, bf16[1024,256]{1,0:T(8,128)(2,1)}, u32[]{:S(2)}, u32[]{:S(2)}) %collective-permute-start.33) | collective-permute-done | bytes 524320 | tf_op jit(solution)/shard_map/ppermute | solution.py:295
  196.0 3.5 %collective-permute-done.31.refs_2_ = bf16[1024,256]{1,0:T(8,128)(2,1)} collective-permute-done((bf16[1024,256]{1,0:T(8,128)(2,1)}, bf16[1024,256]{1,0:T(8,128)(2,1)}, u32[]{:S(2)}, u32[]{:S(2)}) %collective-permute-start.31) | collective-permute-done | bytes 524320 | tf_op jit(solution)/shard_map/ppermute | solution.py:295
  199.5 6.6 %query_weight_terms.1 = (bf16[128,1024]{1,0:T(8,128)(2,1)}, bf16[128,1024]{1,0:T(8,128)(2,1)}, bf16[128,1024]{1,0:T(8,128)(2,1)}, bf16[128,1024]{1,0:T(8,128)(2,...) custom-call(s32[5]{0:T(128)} %stack.32.refs_0_.pos, ...), custom_call_target="tpu_custom_call" | custom-call | flops 2147483648 | bytes 6291456 | tf_op jit(solution)/shard_map/query_weight_terms/pallas_call | solution.py:53
  212.4 6.6 %output_weight_terms.1 = (bf16[1024,128]{1,0:T(8,128)(2,1)}, bf16[1024,128]{1,0:T(8,128)(2,1)}, bf16[1024,128]{1,0:T(8,128)(2,1)}, bf16[1024,128]{1,0:T(8,128)(2...) custom-call(s32[5]{0:T(128)} %stack.32.refs_0_.pos, ...), custom_call_target="tpu_custom_call" | custom-call | flops 2147483648 | bytes 6291456 | tf_op jit(solution)/shard_map/output_weight_terms/pallas_call | solution.py:53
  224.6 7.0 %collective-permute-start.40 = (bf16[128,1024]{1,0:T(8,128)(2,1)S(1)}, bf16[128,1024]{1,0:T(8,128)(2,1)S(1)}, u32[]{:S(2)}, u32[]{:S(2)}) collective-permute-start(bf16[128,1024]{1,0:T(8,128)(2,1)S(1)} %copy-done.36), channel_id=1, source_target_pairs={{0,7},{1,6},{2,1},{3,0},{4,3},{5,2},{6,5},{7,4},{8,15},{9,14},{10,... | collective-permute-start | bytes 786440 | tf_op jit(solution)/shard_map/ppermute | solution.py:301
  235.7 3.8 %collective-permute-done.39 = bf16[128,1024]{1,0:T(8,128)(2,1)S(1)} collective-permute-done((bf16[128,1024]{1,0:T(8,128)(2,1)S(1)}, bf16[128,1024]{1,0:T(8,128)(2,1)S(1)}, u32[]{:S(2)}, u32[]{:S(2)}) %collective-permute-start.39) | collective-permute-done | bytes 262176 | tf_op jit(solution)/shard_map/ppermute | solution.py:301
  245.7 13.9 %collective-permute-done.49 = bf16[1024,128]{1,0:T(8,128)(2,1)S(1)} collective-permute-done((bf16[1024,128]{1,0:T(8,128)(2,1)S(1)}, bf16[1024,128]{1,0:T(8,128)(2,1)S(1)}, u32[]{:S(2)}, u32[]{:S(2)}) %collective-permute-start.49) | collective-permute-done | bytes 262176 | tf_op jit(solution)/shard_map/ppermute | solution.py:301
  263.6 6.1 %collective-permute-done.54 = bf16[1024,128]{1,0:T(8,128)(2,1)S(1)} collective-permute-done((bf16[1024,128]{1,0:T(8,128)(2,1)S(1)}, bf16[1024,128]{1,0:T(8,128)(2,1)S(1)}, u32[]{:S(2)}, u32[]{:S(2)}) %collective-permute-start.54) | collective-permute-done | bytes 262176 | tf_op jit(solution)/shard_map/ppermute | solution.py:301
  270.8 7.7 %collective-permute-done.23 = bf16[256,1024]{1,0:T(8,128)(2,1)S(1)} collective-permute-done((bf16[256,1024]{1,0:T(8,128)(2,1)S(1)}, bf16[256,1024]{1,0:T(8,128)(2,1)S(1)}, u32[]{:S(2)}, u32[]{:S(2)}) %collective-permute-start.23) | collective-permute-done | bytes 524320 | tf_op jit(solution)/shard_map/ppermute | solution.py:307
  (241 shorter events, 98.3 us)
Async XLA Ops:
  3.8 24.1 %collective-permute-start.7 = (bf16[256,1024]{1,0:T(8,128)(2,1)}, bf16[256,1024]{1,0:T(8,128)(2,1)S(1)}, u32[]{:S(2)}, u32[]{:S(2)}) collective-permute-start(bf16[256,1024]{1,0:T(8,128)(2,1)} %refs_1_.3), channel_id=1, source_target_pairs={{0,64},{64,0},{1,65},{65,1},{2,66},{66,2},{3,67},{67,3},{4,68},{68... | collective-permute-start | bytes 1572872 | tf_op jit(solution)/shard_map/ppermute | solution.py:307
  4.2 31.8 %collective-permute-start = (bf16[256,1024]{1,0:T(8,128)(2,1)}, bf16[256,1024]{1,0:T(8,128)(2,1)S(1)}, u32[]{:S(2)}, u32[]{:S(2)}) collective-permute-start(bf16[256,1024]{1,0:T(8,128)(2,1)} %refs_1_.2), channel_id=1, source_target_pairs={{0,32},{32,0},{1,33},{33,1},{2,34},{34,2},{3,35},{35,3},{4,36},{36... | collective-permute-start | bytes 1572872 | tf_op jit(solution)/shard_map/ppermute | solution.py:307
  4.2 46.7 %collective-permute-start.6 = (bf16[256,1024]{1,0:T(8,128)(2,1)}, bf16[256,1024]{1,0:T(8,128)(2,1)S(1)}, u32[]{:S(2)}, u32[]{:S(2)}) collective-permute-start(bf16[256,1024]{1,0:T(8,128)(2,1)} %refs_1_.3), channel_id=1, source_target_pairs={{0,32},{32,0},{1,33},{33,1},{2,34},{34,2},{3,35},{35,3},{4,36},{36... | collective-permute-start | bytes 1572872 | tf_op jit(solution)/shard_map/ppermute | solution.py:307
  6.3 25.7 %all-to-all-start = ((bf16[16,2,8,256]{3,2,1,0:T(8,128)(2,1)}), bf16[16,2,8,256]{3,2,1,0:T(8,128)(2,1)S(1)}, u32[]{:S(2)}, u32[]{:S(2)}) async-start(bf16[16,2,8,256]{3,2,1,0:T(8,128)(2,1)} %maximum_bitcast_fusion), calls=%async_computation | async-start | bytes 262144 | tf_op jit(solution)/shard_map/all_to_all | solution.py:317
  17.3 19.6 %collective-permute-start.2 = (bf16[256,1024]{1,0:T(8,128)(2,1)S(1)}, bf16[256,1024]{1,0:T(8,128)(2,1)S(1)}, u32[]{:S(2)}, u32[]{:S(2)}) collective-permute-start(bf16[256,1024]{1,0:T(8,128)(2,1)S(1)} %collective-permute-done.1.refs_3_), channel_id=1, source_target_pairs={{0,32},{32,0},{1,33},{33,1},{2,34},{34,2},{3,35},{35,3},{4,36},{36... | collective-permute-start | bytes 1572872 | tf_op jit(solution)/shard_map/ppermute | solution.py:307
  27.9 23.7 %collective-permute-start.8 = (bf16[256,1024]{1,0:T(8,128)(2,1)S(1)}, bf16[256,1024]{1,0:T(8,128)(2,1)S(1)}, u32[]{:S(2)}, u32[]{:S(2)}) collective-permute-start(bf16[256,1024]{1,0:T(8,128)(2,1)S(1)} %collective-permute-done.7.refs_3_), channel_id=1, source_target_pairs={{0,32},{32,0},{1,33},{33,1},{2,34},{34,2},{3,35},{35,3},{4,36},{36... | collective-permute-start | bytes 1572872 | tf_op jit(solution)/shard_map/ppermute | solution.py:307
  105.1 37.7 %collective-permute-start.21 = (bf16[256,1024]{1,0:T(8,128)(2,1)}, bf16[256,1024]{1,0:T(8,128)(2,1)S(1)}, u32[]{:S(2)}, u32[]{:S(2)}) collective-permute-start(bf16[256,1024]{1,0:T(8,128)(2,1)} %get-tuple-element.57.refs_0_), channel_id=1, source_target_pairs={{0,24},{8,0},{16,8},{24,16},{1,25},{9,1},{17,9},{25,17},{2,26},{10... | collective-permute-start | bytes 1572872 | tf_op jit(solution)/shard_map/ppermute | solution.py:295
  106.6 36.3 %collective-permute-start.20 = (bf16[256,1024]{1,0:T(8,128)(2,1)}, bf16[256,1024]{1,0:T(8,128)(2,1)S(1)}, u32[]{:S(2)}, u32[]{:S(2)}) collective-permute-start(bf16[256,1024]{1,0:T(8,128)(2,1)} %get-tuple-element.57.refs_0_), channel_id=1, source_target_pairs={{0,16},{8,24},{16,0},{24,8},{1,17},{9,25},{17,1},{25,9},{2,18},{10... | collective-permute-start | bytes 1572872 | tf_op jit(solution)/shard_map/ppermute | solution.py:295
  108.2 34.8 %collective-permute-start.19 = (bf16[256,1024]{1,0:T(8,128)(2,1)}, bf16[256,1024]{1,0:T(8,128)(2,1)S(1)}, u32[]{:S(2)}, u32[]{:S(2)}) collective-permute-start(bf16[256,1024]{1,0:T(8,128)(2,1)} %get-tuple-element.57.refs_0_), channel_id=1, source_target_pairs={{0,8},{8,16},{16,24},{24,0},{1,9},{9,17},{17,25},{25,1},{2,10},{10... | collective-permute-start | bytes 1572872 | tf_op jit(solution)/shard_map/ppermute | solution.py:295
  109.7 27.8 %collective-permute-start.26 = (bf16[256,512]{1,0:T(8,128)(2,1)S(1)}, bf16[256,512]{1,0:T(8,128)(2,1)}, u32[]{:S(2)}, u32[]{:S(2)}) collective-permute-start(bf16[256,512]{1,0:T(8,128)(2,1)S(1)} %copy-done.28), channel_id=1, source_target_pairs={{0,24},{8,0},{16,8},{24,16},{1,25},{9,1},{17,9},{25,17},{2,26},{10... | collective-permute-start | bytes 786440 | tf_op jit(solution)/shard_map/ppermute | solution.py:295
  117.0 22.8 %collective-permute-start.27 = (bf16[256,512]{1,0:T(8,128)(2,1)S(1)}, bf16[256,512]{1,0:T(8,128)(2,1)S(1)}, u32[]{:S(2)}, u32[]{:S(2)}) collective-permute-start(bf16[256,512]{1,0:T(8,128)(2,1)S(1)} %copy-done.10), channel_id=1, source_target_pairs={{0,32},{32,0},{1,33},{33,1},{2,34},{34,2},{3,35},{35,3},{4,36},{36... | collective-permute-start | bytes 786440 | tf_op jit(solution)/shard_map/ppermute | solution.py:307
  143.1 19.3 %collective-permute-start.28 = (bf16[256,512]{1,0:T(8,128)(2,1)S(1)}, bf16[256,512]{1,0:T(8,128)(2,1)S(1)}, u32[]{:S(2)}, u32[]{:S(2)}) collective-permute-start(bf16[256,512]{1,0:T(8,128)(2,1)S(1)} %collective-permute-done.24.refs_2_), channel_id=1, source_target_pairs={{0,32},{32,0},{1,33},{33,1},{2,34},{34,2},{3,35},{35,3},{4,36},{36... | collective-permute-start | bytes 786440 | tf_op jit(solution)/shard_map/ppermute | solution.py:307
  152.3 19.9 %collective-permute-start.30 = (bf16[256,512]{1,0:T(8,128)(2,1)}, bf16[256,512]{1,0:T(8,128)(2,1)S(1)}, u32[]{:S(2)}, u32[]{:S(2)}) collective-permute-start(bf16[256,512]{1,0:T(8,128)(2,1)} %collective-permute-done.26.refs_4_), channel_id=1, source_target_pairs={{0,32},{32,0},{1,33},{33,1},{2,34},{34,2},{3,35},{35,3},{4,36},{36... | collective-permute-start | bytes 786440 | tf_op jit(solution)/shard_map/ppermute | solution.py:307
  162.4 56.6 %collective-permute-start.22 = (bf16[2,256,1024]{2,1,0:T(8,128)(2,1)}, bf16[2,256,1024]{2,1,0:T(8,128)(2,1)S(1)}, u32[]{:S(2)}, u32[]{:S(2)}) collective-permute-start(bf16[2,256,1024]{2,1,0:T(8,128)(2,1)} %get-tuple-element.59), channel_id=1, source_target_pairs={{0,32},{32,0},{1,33},{33,1},{2,34},{34,2},{3,35},{35,3},{4,36},{36... | collective-permute-start | bytes 3145736 | tf_op jit(solution)/shard_map/ppermute | solution.py:307
  169.0 27.0 %collective-permute-start.33 = (bf16[1024,256]{1,0:T(8,128)(2,1)}, bf16[1024,256]{1,0:T(8,128)(2,1)}, u32[]{:S(2)}, u32[]{:S(2)}) collective-permute-start(bf16[1024,256]{1,0:T(8,128)(2,1)} %get-tuple-element.64.refs_1_), channel_id=1, source_target_pairs={{0,24},{8,0},{16,8},{24,16},{1,25},{9,1},{17,9},{25,17},{2,26},{10... | collective-permute-start | bytes 1572872 | tf_op jit(solution)/shard_map/ppermute | solution.py:295
  172.2 23.8 %collective-permute-start.32 = (bf16[1024,256]{1,0:T(8,128)(2,1)}, bf16[1024,256]{1,0:T(8,128)(2,1)}, u32[]{:S(2)}, u32[]{:S(2)}) collective-permute-start(bf16[1024,256]{1,0:T(8,128)(2,1)} %get-tuple-element.64.refs_1_), channel_id=1, source_target_pairs={{0,16},{8,24},{16,0},{24,8},{1,17},{9,25},{17,1},{25,9},{2,18},{10... | collective-permute-start | bytes 1572872 | tf_op jit(solution)/shard_map/ppermute | solution.py:295
  173.1 26.4 %collective-permute-start.31 = (bf16[1024,256]{1,0:T(8,128)(2,1)}, bf16[1024,256]{1,0:T(8,128)(2,1)}, u32[]{:S(2)}, u32[]{:S(2)}) collective-permute-start(bf16[1024,256]{1,0:T(8,128)(2,1)} %get-tuple-element.64.refs_1_), channel_id=1, source_target_pairs={{0,8},{8,16},{16,24},{24,0},{1,9},{9,17},{17,25},{25,1},{2,10},{10... | collective-permute-start | bytes 1572872 | tf_op jit(solution)/shard_map/ppermute | solution.py:295
  208.4 23.2 %collective-permute-start.36 = (bf16[128,1024]{1,0:T(8,128)(2,1)}, bf16[128,1024]{1,0:T(8,128)(2,1)S(1)}, u32[]{:S(2)}, u32[]{:S(2)}) collective-permute-start(bf16[128,1024]{1,0:T(8,128)(2,1)} %get-tuple-element.68), channel_id=1, source_target_pairs={{0,3},{1,2},{2,5},{3,4},{4,7},{5,6},{6,1},{7,0},{8,11},{9,10},{10,... | collective-permute-start | bytes 786440 | tf_op jit(solution)/shard_map/ppermute | solution.py:301
  210.3 23.9 %collective-permute-start.37 = (bf16[128,1024]{1,0:T(8,128)(2,1)}, bf16[128,1024]{1,0:T(8,128)(2,1)S(1)}, u32[]{:S(2)}, u32[]{:S(2)}) collective-permute-start(bf16[128,1024]{1,0:T(8,128)(2,1)} %get-tuple-element.69), channel_id=1, source_target_pairs={{0,4},{1,5},{2,6},{3,7},{4,0},{5,1},{6,2},{7,3},{8,12},{9,13},{10,... | collective-permute-start | bytes 786440 | tf_op jit(solution)/shard_map/ppermute | solution.py:301
  234.2 25.4 %collective-permute-start.49 = (bf16[1024,128]{1,0:T(8,128)(2,1)S(1)}, bf16[1024,128]{1,0:T(8,128)(2,1)S(1)}, u32[]{:S(2)}, u32[]{:S(2)}) collective-permute-start(bf16[1024,128]{1,0:T(8,128)(2,1)S(1)} %copy-done.39), channel_id=1, source_target_pairs={{0,2},{1,3},{2,4},{3,5},{4,6},{5,7},{6,0},{7,1},{8,10},{9,11},{10,... | collective-permute-start | bytes 786440 | tf_op jit(solution)/shard_map/ppermute | solution.py:301
  234.2 25.8 %collective-permute-start.50 = (bf16[1024,128]{1,0:T(8,128)(2,1)S(1)}, bf16[1024,128]{1,0:T(8,128)(2,1)S(1)}, u32[]{:S(2)}, u32[]{:S(2)}) collective-permute-start(bf16[1024,128]{1,0:T(8,128)(2,1)S(1)} %copy-done.37), channel_id=1, source_target_pairs={{0,3},{1,2},{2,5},{3,4},{4,7},{5,6},{6,1},{7,0},{8,11},{9,10},{10,... | collective-permute-start | bytes 786440 | tf_op jit(solution)/shard_map/ppermute | solution.py:301
  239.5 24.1 %collective-permute-start.51 = (bf16[1024,128]{1,0:T(8,128)(2,1)S(1)}, bf16[1024,128]{1,0:T(8,128)(2,1)S(1)}, u32[]{:S(2)}, u32[]{:S(2)}) collective-permute-start(bf16[1024,128]{1,0:T(8,128)(2,1)S(1)} %copy-done.35), channel_id=1, source_target_pairs={{0,4},{1,5},{2,6},{3,7},{4,0},{5,1},{6,2},{7,3},{8,12},{9,13},{10,... | collective-permute-start | bytes 786440 | tf_op jit(solution)/shard_map/ppermute | solution.py:301
  241.4 22.3 %collective-permute-start.52 = (bf16[1024,128]{1,0:T(8,128)(2,1)S(1)}, bf16[1024,128]{1,0:T(8,128)(2,1)S(1)}, u32[]{:S(2)}, u32[]{:S(2)}) collective-permute-start(bf16[1024,128]{1,0:T(8,128)(2,1)S(1)} %copy-done.34), channel_id=1, source_target_pairs={{0,5},{1,4},{2,7},{3,6},{4,1},{5,0},{6,3},{7,2},{8,13},{9,12},{10,... | collective-permute-start | bytes 786440 | tf_op jit(solution)/shard_map/ppermute | solution.py:301
  243.0 20.6 %collective-permute-start.53 = (bf16[1024,128]{1,0:T(8,128)(2,1)S(1)}, bf16[1024,128]{1,0:T(8,128)(2,1)S(1)}, u32[]{:S(2)}, u32[]{:S(2)}) collective-permute-start(bf16[1024,128]{1,0:T(8,128)(2,1)S(1)} %copy-done.33), channel_id=1, source_target_pairs={{0,6},{1,7},{2,0},{3,1},{4,2},{5,3},{6,4},{7,5},{8,14},{9,15},{10,... | collective-permute-start | bytes 786440 | tf_op jit(solution)/shard_map/ppermute | solution.py:301
  (97 other events, 1607.8 us)

commit v3 on v2

v3 whole, which is shorter than its diff:
```python
import math

import jax
import jax.numpy as jnp
from jax import lax
from jax.experimental import pallas as pl
from jax.experimental.pallas import tpu as pltpu
from jax.sharding import Mesh
from jax.sharding import PartitionSpec as P

HEAD = 128
SCALE = 1.0 / math.sqrt(HEAD)
F32 = jnp.float32
BF16 = jnp.bfloat16
AXES = (("xh", 2), ("core", 2), ("z", 4), ("y", 4), ("xl", 2))
HEADS = ("xh", "core")
SEQ = ("z", "y", "xl")
XH, CORE, Z = range(3)
SWAP = [(0, 1), (1, 0)]
VMEM = 56 * 1024 * 1024
TOK = 256
PIECE = 256
GROUP = 4 * TOK
BLOCK = 1024
PLANES = 8


def dot(a, b, contract=((1,), (0,))):
    return lax.dot_general(a, b, (contract, ((), ())), preferred_element_type=F32)


def shifted(index, by, size=4):
    return lax.rem(index + by + size, size)


def head_block(step, pos):
    return lax.rem(pos[XH] + step // 2, 2) * 2 + lax.rem(pos[CORE] + step % 2, 2)


def struct(shape, dtype=BF16):
    return jax.ShapeDtypeStruct(shape, dtype)


def whole(shape):
    return pl.BlockSpec(shape, lambda *_: (0,) * len(shape))


def call(kernel, name, grid, in_specs, out_specs, out_shape, scratch, flops, moved, pos, *args):
    return pl.pallas_call(
        kernel,
        grid_spec=pltpu.PrefetchScalarGridSpec(
            num_scalar_prefetch=1,
            grid=grid,
            in_specs=in_specs,
            out_specs=out_specs,
            scratch_shapes=scratch,
        ),
        out_shape=out_shape,
        compiler_params=pltpu.CompilerParams(vmem_limit_bytes=VMEM),
        cost_estimate=pl.CostEstimate(flops=flops, bytes_accessed=moved, transcendentals=0),
        name=name,
    )(pos, *args)


def project_kernel(transposed, final, pos, *refs):
    blocks, w_ref, refs = refs[:4], refs[4], refs[5:]
    before, refs = (refs[0], refs[1:]) if final else (None, refs)
    step = pl.program_id(0)
    contract = ((1,), (1,)) if transposed else ((1,), (0,))
    total = refs[5] if final else refs[0]

    @pl.when(step == 0)
    def _():
        product = dot(blocks[2 if final else 0][...], w_ref[...], contract)
        total[...] = product + before[...] if final else product

    @pl.when(step == 1)
    def _():
        product = total[...] + dot(blocks[3 if final else 1][...], w_ref[...], contract)
        total[...] = product
        if final:
            rows, parts, held = refs[:4], refs[4], refs[6]
            half = pl.multiple_of(pos[CORE] * (BLOCK // 2), BLOCK // 2)
            for d in range(4):
                start = pl.multiple_of(shifted(pos[Z], d) * PIECE, PIECE)
                rows[d][...] = total[:, pl.ds(start, PIECE)].astype(BF16)
                held[...] = blocks[d][...]
                parts[head_block(d, pos)] = held[:, pl.ds(half, BLOCK // 2)]


def project(name, pos, blocks, weight, transposed, before=None):
    final = before is not None
    first = 2 if final else 0

    def where(i, pos):
        block = head_block(i + first, pos)
        return (0, block) if transposed else (block, 0)

    return call(
        lambda *refs: project_kernel(transposed, final, *refs),
        name,
        (2,),
        [whole((TOK, BLOCK))] * 4
        + [pl.BlockSpec((BLOCK, BLOCK), where)]
        + ([whole((TOK, BLOCK))] if final else []),
        [whole((TOK, PIECE))] * 4 + [whole((4, TOK, BLOCK // 2))] if final else whole((TOK, BLOCK)),
        [struct((TOK, PIECE))] * 4 + [struct((4, TOK, BLOCK // 2))] if final else struct((TOK, BLOCK), F32),
        [pltpu.VMEM((TOK, BLOCK), F32), pltpu.VMEM((TOK, BLOCK), BF16)] if final else [],
        4 * TOK * BLOCK * BLOCK,
        4 * BLOCK * BLOCK,
        pos,
        *(blocks if final else blocks[:2] + blocks[:2]),
        weight,
        *([before] if final else []),
    )


def assemble_kernel(transposed, pos, mine, other, out):
    for side, ref in enumerate((mine, other)):
        half = pl.multiple_of(lax.rem(pos[CORE] + side, 2) * (BLOCK // 2), BLOCK // 2)
        if transposed:
            out[pl.ds(half, BLOCK // 2), :] = ref[...].T
        else:
            out[:, pl.ds(half, BLOCK // 2)] = ref[...]


def assemble(name, pos, mine, other, transposed):
    return call(
        lambda *refs: assemble_kernel(transposed, *refs),
        name,
        (1,),
        [whole((GROUP, BLOCK // 2))] * 2,
        whole((BLOCK, GROUP)),
        struct((BLOCK, GROUP)),
        [],
        0,
        4 * BLOCK * GROUP,
        pos,
        mine,
        other,
    )


def forward_kernel(pos, bias, *refs):
    q_refs, (k_ref, v_ref, out_ref, turned_ref, probs_ref) = refs[:4], refs[4:]
    k, v = k_ref[...], v_ref[...]
    for d in range(4):
        scores = dot(q_refs[d][...], k, ((1,), (1,))) + bias[...]
        top = jnp.max(scores, axis=1, keepdims=True)
        weights = jnp.exp((scores - top) * SCALE)
        probs = (weights * (1.0 / jnp.sum(weights, axis=1, keepdims=True))).astype(BF16)
        heads_out = dot(probs, v).astype(BF16)
        probs_ref[0, d * TOK : (d + 1) * TOK, :] = probs
        out_ref[d * TOK : (d + 1) * TOK, :] = heads_out
        token = pl.multiple_of(shifted(pos[Z], -d) * TOK, TOK)
        turned_ref[:, pl.ds(token, TOK)] = heads_out.T


def forward(pos, bias, queries, keys, values):
    rows = pl.BlockSpec((TOK, HEAD), lambda h, pos: (0, h))
    column = pl.BlockSpec((GROUP, HEAD), lambda h, pos: (0, h))
    context = keys.shape[0]
    return call(
        forward_kernel,
        "attention_forward",
        (PIECE // HEAD,),
        [whole((1, context))] + [rows] * 4 + [column] * 2,
        [
            column,
            pl.BlockSpec((HEAD, GROUP), lambda h, pos: (h, 0)),
            pl.BlockSpec((1, GROUP, context), lambda h, pos: (h, 0, 0)),
        ],
        [struct((GROUP, PIECE)), struct((PIECE, GROUP)), struct((PIECE // HEAD, GROUP, context))],
        [],
        12 * GROUP * PIECE * context,
        2 * (4 * GROUP * PIECE + 2 * GROUP * context),
        pos,
        bias,
        *queries,
        keys,
        values,
    )


def backward_kernel(pos, *refs):
    q_refs, g_refs, (k_ref, v_ref, out_ref, probs_ref) = refs[:4], refs[4:8], refs[8:12]
    dq_ref, dk_ref, dv_ref, dk_sum, dv_sum = refs[12:]
    k, v = k_ref[...], v_ref[...]
    for d in range(4):
        q, g = q_refs[d][...], g_refs[d][...]
        probs = probs_ref[0, d * TOK : (d + 1) * TOK, :]
        value_dots = dot(g, v, ((1,), (1,)))
        heads_out = out_ref[d * TOK : (d + 1) * TOK, :]
        delta = jnp.sum(g.astype(F32) * heads_out.astype(F32), axis=1, keepdims=True)
        score_grad = (probs.astype(F32) * ((value_dots - delta) * SCALE)).astype(BF16)
        token = pl.multiple_of(shifted(pos[Z], -d) * TOK, TOK)
        dq_ref[pl.ds(token, TOK), :] = dot(score_grad, k).astype(BF16)
        dk_term, dv_term = dot(q, score_grad, ((0,), (0,))), dot(g, probs, ((0,), (0,)))
        dk_sum[...] = dk_term if d == 0 else dk_sum[...] + dk_term
        dv_sum[...] = dv_term if d == 0 else dv_sum[...] + dv_term
    dk_ref[...] = dk_sum[...].T.astype(BF16)
    dv_ref[...] = dv_sum[...].T.astype(BF16)


def backward(pos, queries, grads, keys, values, heads_out, probs):
    rows = pl.BlockSpec((TOK, HEAD), lambda h, pos: (0, h))
    column = pl.BlockSpec((GROUP, HEAD), lambda h, pos: (0, h))
    context = keys.shape[0]
    return call(
        backward_kernel,
        "attention_backward",
        (PIECE // HEAD,),
        [rows] * 8 + [column] * 3 + [pl.BlockSpec((1, GROUP, context), lambda h, pos: (h, 0, 0))],
        [column] * 3,
        [struct((GROUP, PIECE))] * 3,
        [pltpu.VMEM((HEAD, context), F32)] * 2,
        16 * GROUP * PIECE * context,
        2 * (6 * GROUP * PIECE + 2 * GROUP * context),
        pos,
        *queries,
        *grads,
        keys,
        values,
        heads_out,
        probs,
    )


GATHERED = ((0, 0), (1, 0), (3, 0), (2, 0), (2, 1))


def output_grad_kernel(pos, *refs):
    left, right, out = refs[:5], refs[5], refs[6]
    for ref, (e, part) in zip(left, GATHERED):
        rows = ref.shape[0]
        row = pl.multiple_of(shifted(pos[Z], -e) * PIECE + part * rows, rows)
        product = dot(ref[...], right[...]).astype(BF16)
        for p in range(PLANES):
            out[p, pl.ds(row, rows), :] = product[:, p * 128 : (p + 1) * 128]


def query_grad_kernel(pos, *refs):
    left, right, out = refs[0], refs[1:6], refs[6]
    for e, ref in enumerate(right[:3]):
        col = pl.multiple_of(shifted(pos[Z], -GATHERED[e][0]) * PIECE, PIECE)
        out[:, pl.ds(col, PIECE)] = dot(left[...], ref[...]).astype(BF16)
    col = pl.multiple_of(shifted(pos[Z], -2) * PIECE, PIECE)
    far = jnp.concatenate([right[3][...], right[4][...]], axis=0)
    out[:, pl.ds(col, PIECE)] = dot(left[...], far).astype(BF16)


def weight_terms(name, kernel, pos, args, out):
    return call(
        kernel,
        name,
        (1,),
        [whole(a.shape) for a in args],
        whole(out),
        struct(out),
        [],
        2 * GROUP * BLOCK * BLOCK,
        6 * BLOCK * BLOCK,
        pos,
        *args,
    )


def output_kernel(pos, *refs):
    rows, w_ref, give, keep = refs[:5], refs[5], refs[6], refs[7]
    step = pl.program_id(0)
    product = jnp.zeros((TOK, BLOCK), F32)
    for ref, (e, part) in zip(rows, GATHERED):
        size = ref.shape[0]
        row = pl.multiple_of(shifted(pos[Z], -e) * PIECE + part * size, size)
        product = product + dot(ref[...], w_ref[pl.ds(row, size), :], ((0,), (0,)))

    @pl.when(step < 2)
    def _():
        give[0] = product.astype(BF16)

    @pl.when(step >= 2)
    def _():
        keep[0] = product


def output_terms(pos, every_out, weight):
    return call(
        output_kernel,
        "output_terms",
        (4,),
        [pl.BlockSpec((a.shape[0], TOK), lambda n, pos: (0, pos[Z])) for a in every_out]
        + [pl.BlockSpec((BLOCK, BLOCK), lambda n, pos: (0, head_block((n % 2) * 2 + 1 - n // 2, pos)))],
        [
            pl.BlockSpec((1, TOK, BLOCK), lambda n, pos: (jnp.minimum(n, 1), 0, 0)),
            pl.BlockSpec((1, TOK, BLOCK), lambda n, pos: (jnp.maximum(n - 2, 0), 0, 0)),
        ],
        [struct((2, TOK, BLOCK)), struct((2, TOK, BLOCK), F32)],
        [],
        2 * TOK * 4 * BLOCK * BLOCK,
        2 * 4 * BLOCK * BLOCK,
        pos,
        *every_out,
        weight,
    )


def context_bias(lengths, slot_passage):
    slot_lengths = jnp.sum(
        jnp.where(slot_passage[:, None] == jnp.arange(4)[None, :], lengths[None, :], 0), axis=1
    )
    position = jnp.arange(TOK, dtype=jnp.int32)
    valid = position[None, :] < slot_lengths[:, None]
    return jnp.where(valid, 0.0, -jnp.inf).astype(F32).reshape(1, 4 * TOK)


def on_device(
    decoder_states,
    query_weight,
    output_weight,
    context_keys,
    context_values,
    lengths,
    slot_passage,
    output_cotangent,
):
    pos = jnp.stack([lax.axis_index(name) for name, _ in AXES]).astype(jnp.int32)

    def to_layer(x, d):
        return lax.ppermute(x, "z", [(i, (i + d) % 4) for i in range(4)]) if d else x

    def swap(x, axis):
        return lax.ppermute(x, axis, SWAP)

    own = jnp.stack([context_keys, context_values]).reshape(2, 8, 16, PIECE).transpose(2, 0, 1, 3)
    own = jnp.broadcast_to(own[:, None], (16, PLANES, 2, 8, PIECE)).reshape(128, 2, 8, PIECE)
    context = lax.all_to_all(own, HEADS + SEQ, 0, 0, tiled=True)
    keys = context[:, 0].reshape(4 * TOK, PIECE)
    values = context[:, 1].reshape(4 * TOK, PIECE)
    bias = context_bias(lengths, slot_passage)

    def projected(name, local, weight, transposed):
        over_x = swap(local, "xh")
        near = (local, swap(local, "core"))
        first = project(name + "_near", pos, near, weight, transposed)
        blocks = near + (over_x, swap(over_x, "core"))
        outs = project(name, pos, blocks, weight, transposed, first)
        return [to_layer(x, d) for d, x in enumerate(outs[:4])], outs[4]

    queries, state_parts = projected("queries", decoder_states, query_weight, False)
    heads_grad, cotangent_parts = projected("heads_grad", output_cotangent, output_weight, True)

    def column_block(name, parts, transposed):
        mine = lax.all_to_all(parts, "z", 0, 0, tiled=True).reshape(GROUP, BLOCK // 2)
        return assemble(name, pos, mine, swap(mine, "core"), transposed)

    def along_z(x):
        half = x.shape[0] // 2
        left, right = to_layer(x, 1), to_layer(x, 3)
        return x, left, right, to_layer(left[:half], 1), to_layer(right[half:], 3)

    heads_out, turned_out, probs = forward(pos, bias, queries, keys, values)
    every_out = along_z(turned_out)
    query_grad, key_terms, value_terms = backward(
        pos, queries, heads_grad, keys, values, heads_out, probs
    )
    every_query_grad = along_z(query_grad)

    group_states = column_block("group_states", state_parts, True)
    group_cotangent = column_block("group_cotangent", cotangent_parts, False)

    give, keep = output_terms(pos, every_out, output_weight)
    pair = keep + swap(give, "core").astype(F32)
    attended = (pair[0] + swap(pair[1].astype(BF16), "xh").astype(F32)).astype(BF16)

    def plane_sum(terms):
        return jnp.sum(lax.all_to_all(terms, ("y", "xl"), 0, 0, tiled=True).astype(F32), axis=0)

    terms = weight_terms(
        "output_weight_terms", output_grad_kernel, pos, (*every_out, group_cotangent), (PLANES, BLOCK, 128)
    )
    output_weight_grad = plane_sum(terms)

    terms = jnp.stack([key_terms.reshape(128, 8, PIECE), value_terms.reshape(128, 8, PIECE)], 1)
    moved = lax.all_to_all(terms, HEADS + SEQ, 0, 0, tiled=True)
    owned = jnp.sum(moved.reshape(16, PLANES, 2, 8, PIECE).astype(F32), axis=1)
    owned = owned.transpose(1, 2, 0, 3).reshape(2, 8, 16 * PIECE)

    terms = weight_terms(
        "query_weight_terms", query_grad_kernel, pos, (group_states, *every_query_grad), (BLOCK, BLOCK)
    )
    query_weight_grad = plane_sum(terms.reshape(PLANES, 128, BLOCK))
    return attended, query_weight_grad, output_weight_grad, owned[0], owned[1]


def solution(mesh):
    devices = mesh.devices.reshape([size for _, size in AXES])
    split = Mesh(devices, [name for name, _ in AXES])
    return jax.shard_map(
        on_device,
        mesh=split,
        in_specs=(
            P(SEQ, HEADS),
            P(None, HEADS),
            P(HEADS, None),
            P(HEADS + SEQ, None),
            P(HEADS + SEQ, None),
            P(),
            P(),
            P(SEQ, HEADS),
        ),
        out_specs=(
            P(SEQ, HEADS),
            P(SEQ, HEADS),
            P(HEADS, SEQ),
            P(HEADS + SEQ, None),
            P(HEADS + SEQ, None),
        ),
        check_vma=False,
    )
```

time: 284 us -> 248 us (0.87); the launches traced: 280 us -> 248 us
  starting transfers between devices: 107 us -> 70.6 us
  waiting for transfers between devices: 103 us -> 81.2 us
  Pallas kernels: 57.5 us -> 70.2 us
  local copies, waits for them, and re-layouts: 3.75 us -> 13.8 us
  other arithmetic: 7.42 us -> 10.7 us
    ppermute x28 -> x0, starting transfers between devices: 46.9 us -> none  [to_plane(): return lax.ppermute(x, ('y', 'xl'), pairs) if r else x]
    ppermute x16 -> x10, waiting for transfers between devices: 19.8 us -> 51.7 us  [swap(): return lax.ppermute(x, axis, SWAP)]
    ppermute x28 -> x0, waiting for transfers between devices: 31.7 us -> none  [to_plane(): return lax.ppermute(x, ('y', 'xl'), pairs) if r else x]
    all_to_all x2 -> x6, starting transfers between devices: 13.6 us -> 38.2 us  [the longest x2 10.6 us: plane_sum(): lax.all_to_all(terms, ('y', 'xl'), 0, 0, tiled=True).astype(F32)]
    ppermute x18 -> x14, waiting for transfers between devices: 44.2 us -> 29.5 us  [to_layer(): lax.ppermute(x, 'z', [(i, (i + d) % 4) for i in range(4)])]
    pallas_call x8 -> x11, Pallas kernels: 57.5 us -> 70.2 us  [call(): pl.pallas_call(kernel, grid_spec=pltpu.PrefetchScalarGridSpec(num_scalar_...]
    ppermute x16 -> x10, starting transfers between devices: 17.9 us -> 9.25 us  [swap(): return lax.ppermute(x, axis, SWAP)]
    unnamed x114 -> x59, local copies, waits for them, and re-layouts: 2.33 us -> 10.3 us
  transfers between devices with their start and end apart: 64 -> 30, of which waited for: 20 -> 6; matrix products, arithmetic and copies ran while one was open for 3% -> 5% of each run, Pallas kernels for 16% -> 28%
where the time goes in v3:
time: 248 us
  waiting for transfers between devices  81.2 us (33%)
  starting transfers between devices  70.6 us (28%)
  Pallas kernels  70.2 us (28%)
  local copies, waits for them, and re-layouts  13.8 us (6%)
  other arithmetic  10.7 us (4%)
    pallas_call x11, Pallas kernels, call(): pl.pallas_call(kernel, grid_spec=pltpu.PrefetchScalarGridSpec(num_scalar_...  70.2 us
    ppermute x10, waiting for transfers between devices, swap(): return lax.ppermute(x, axis, SWAP)  51.7 us
    ppermute x14, waiting for transfers between devices, to_layer(): lax.ppermute(x, 'z', [(i, (i + d) % 4) for i in range(4)])  29.5 us
    ppermute x14, starting transfers between devices, to_layer(): lax.ppermute(x, 'z', [(i, (i + d) % 4) for i in range(4)])  23.1 us
    all_to_all x2, starting transfers between devices, plane_sum(): lax.all_to_all(terms, ('y', 'xl'), 0, 0, tiled=True).astype(F32)  10.6 us
    unnamed x59, local copies, waits for them, and re-layouts  10.3 us
    all_to_all x1, starting transfers between devices, on_device(): moved = lax.all_to_all(terms, HEADS + SEQ, 0, 0, tiled=True)  9.67 us
    ppermute x10, starting transfers between devices, swap(): return lax.ppermute(x, axis, SWAP)  9.25 us
  transfers between devices with their start and end apart: 30, of which 6 were waited for; matrix products, arithmetic and copies ran while one was open for 5% of the time, Pallas kernels for 28%

profile of v3, /device:TPU:0, one launch (start us, length us, event | category | flops | bytes accessed | tf_op | source)
XLA Modules:
  0.0 247.5 jit_solution(2983994547425205286)
XLA Ops:
  5.8 9.2 %all-to-all-start = ((bf16[128,2,8,256]{3,2,1,0:T(8,128)(2,1)}), bf16[128,2,8,256]{3,2,1,0:T(8,128)(2,1)S(1)}, u32[]{:S(2)}, u32[]{:S(2)}) async-start(bf16[128,2,8,256]{3,2,1,0:T(8,128)(2,1)} %bitcast.8), calls=%async_computation | async-start | bytes 2097152 | tf_op jit(solution)/shard_map/all_to_all | solution.py:336
  18.7 21.6 %collective-permute-done.1.refs_3_ = bf16[256,1024]{1,0:T(8,128)(2,1)} collective-permute-done((bf16[256,1024]{1,0:T(8,128)(2,1)S(1)}, bf16[256,1024]{1,0:T(8,128)(2,1)}, u32[]{:S(2)}, u32[]{:S(2)}) %collective-permute-start.1) | collective-permute-done | bytes 524320 | tf_op jit(solution)/shard_map/ppermute | solution.py:332
  41.2 5.9 %heads_grad_near.1.refs_6_ = f32[256,1024]{1,0:T(8,128)} custom-call(s32[5]{0:T(128)} %stack.35.refs_0_.pos, bf16[256,1024]{1,0:T(8,128)(2,1)} %refs_1_.7, bf16[256,1024]{1,0:T(8,128)(2,1)} %copy-done.3, bf16[256,1024]{1,0:T(8,128)(2,1)} %refs_1_.7, bf16[256,1024]{1,0:T(8,128)(2,1)} %copy-done.3, bf16[1024,4096]{1,0:T(8,128)(2,1)} %refs_5_.9), custom_call_target="tpu_custom_call" | custom-call | flops 1073741824 | bytes 4194304 | tf_op jit(solution)/shard_map/heads_grad_near/pallas_call | solution.py:49
  47.0 6.3 %heads_grad.1 = (bf16[256,256]{1,0:T(8,128)(2,1)}, bf16[256,256]{1,0:T(8,128)(2,1)}, bf16[256,256]{1,0:T(8,128)(2,1)}, bf16[256,256]{1,0:T(8,128)(2,1)}, bf16[4,256,512]{2,1,0:T(8,128)(2,1)}) custom-call(s32[5]{0:T(128)} %stack.35.refs_0_.pos, bf16[256,1024]{1,0:T(8,128)(2,1)} %refs_1_.7, bf16[256,1024]{1,0:T(8,128)(2,1)} %copy-done.3, ...), custom_call_target="tpu_custom_call" | custom-call | flops 1073741824 | bytes 4194304 | tf_op jit(solution)/shard_map/heads_grad/pallas_call | solution.py:49
  54.3 4.7 %all-to-all-start.3 = ((bf16[4,256,512]{2,1,0:T(8,128)(2,1)}), bf16[4,256,512]{2,1,0:T(8,128)(2,1)S(1)}, u32[]{:S(2)}, u32[]{:S(2)}) async-start(bf16[4,256,512]{2,1,0:T(8,128)(2,1)} %get-tuple-element.38), calls=%async_computation.3 | async-start | bytes 2097152 | tf_op jit(solution)/shard_map/all_to_all | solution.py:353
  60.6 5.9 %queries_near.1.refs_6_ = f32[256,1024]{1,0:T(8,128)} custom-call(s32[5]{0:T(128)} %stack.35.refs_0_.pos, bf16[256,1024]{1,0:T(8,128)(2,1)} %refs_1_.5, bf16[256,1024]{1,0:T(8,128)(2,1)} %copy-done.2, bf16[256,1024]{1,0:T(8,128)(2,1)} %refs_1_.5, bf16[256,1024]{1,0:T(8,128)(2,1)} %copy-done.2, bf16[4096,1024]{1,0:T(8,128)(2,1)} %refs_5_.6), custom_call_target="tpu_custom_call" | custom-call | flops 1073741824 | bytes 4194304 | tf_op jit(solution)/shard_map/queries_near/pallas_call | solution.py:49
  66.5 6.3 %queries.1 = (bf16[256,256]{1,0:T(8,128)(2,1)}, bf16[256,256]{1,0:T(8,128)(2,1)}, bf16[256,256]{1,0:T(8,128)(2,1)}, bf16[256,256]{1,0:T(8,128)(2,1)}, bf16[4,256,512]{2,1,0:T(8,128)(2,1)}) custom-call(s32[5]{0:T(128)} %stack.35.refs_0_.pos, bf16[256,1024]{1,0:T(8,128)(2,1)} %refs_1_.5, bf16[256,1024]{1,0:T(8,128)(2,1)} %copy-done.2, ...), custom_call_target="tpu_custom_call" | custom-call | flops 1073741824 | bytes 4194304 | tf_op jit(solution)/shard_map/queries/pallas_call | solution.py:49
  84.5 4.1 %all-to-all-start.1 = ((bf16[4,256,512]{2,1,0:T(8,128)(2,1)}), bf16[4,256,512]{2,1,0:T(8,128)(2,1)S(1)}, u32[]{:S(2)}, u32[]{:S(2)}) async-start(bf16[4,256,512]{2,1,0:T(8,128)(2,1)} %get-tuple-element.30), calls=%async_computation.1 | async-start | bytes 2097152 | tf_op jit(solution)/shard_map/all_to_all | solution.py:353
  89.4 9.1 %attention_forward.1 = (bf16[1024,256]{1,0:T(8,128)(2,1)}, bf16[256,1024]{1,0:T(8,128)(2,1)}, bf16[2,1024,1024]{2,1,0:T(8,128)(2,1)}) custom-call(s32[5]{0:T(128)} %stack.35.refs_0_.pos, f32[1,1024]{1,0:T(1,128)} %bitcast.53, bf16[256,256]{1,0:T(8,128)(2,1)} %get-tuple-element.23.refs_0_, bf16[256,256]{1,0:T(8,128)(2,1)} %copy-done.23, ...), custom_call_target="tpu_custom_call" | custom-call | flops 3221225472 | bytes 6291456 | tf_op jit(solution)/shard_map/attention_forward/pallas_call | solution.py:49
  99.2 7.4 %attention_backward.1 = (bf16[1024,256]{1,0:T(8,128)(2,1)}, bf16[1024,256]{1,0:T(8,128)(2,1)}, bf16[1024,256]{1,0:T(8,128)(2,1)}) custom-call(s32[5]{0:T(128)} %stack.35.refs_0_.pos, bf16[256,256]{1,0:T(8,128)(2,1)} %get-tuple-element.23.refs_0_, bf16[256,256]{1,0:T(8,128)(2,1)} %copy-done.23, bf16[256,256]{1,0:T(8,128)(2,1)} %copy-done.24, ...), custom_call_target="tpu_custom_call" | custom-call | flops 4294967296 | bytes 7340032 | tf_op jit(solution)/shard_map/attention_backward/pallas_call | solution.py:49
  109.0 9.7 %all-to-all-start.5 = ((bf16[128,2,8,256]{3,2,1,0:T(8,128)(2,1)}), bf16[128,2,8,256]{3,2,1,0:T(8,128)(2,1)S(1)}, u32[]{:S(2)}, u32[]{:S(2)}) async-start(bf16[128,2,8,256]{3,2,1,0:T(8,128)(2,1)} %pad_maximum_fusion), calls=%async_computation.5 | async-start | bytes 2097152 | tf_op jit(solution)/shard_map/all_to_all | solution.py:384
  122.0 22.9 %collective-permute-done.6.refs_1_ = bf16[256,1024]{1,0:T(8,128)(2,1)S(1)} collective-permute-done((bf16[256,1024]{1,0:T(8,128)(2,1)}, bf16[256,1024]{1,0:T(8,128)(2,1)S(1)}, u32[]{:S(2)}, u32[]{:S(2)}) %collective-permute-start.6) | collective-permute-done | bytes 524320 | tf_op jit(solution)/shard_map/ppermute | solution.py:329
  145.0 3.3 %collective-permute-start.9 = (bf16[128,1024]{1,0:T(8,128)(2,1)S(1)}, bf16[128,1024]{1,0:T(8,128)(2,1)S(1)}, u32[]{:S(2)}, u32[]{:S(2)}) collective-permute-start(bf16[128,1024]{1,0:T(8,128)(2,1)S(1)} %slice.46), channel_id=1, source_target_pairs={{0,24},{8,0},{16,8},{24,16},{1,25},{9,1},{17,9},{25,17},{2,26},{10... | collective-permute-start | bytes 786440 | tf_op jit(solution)/shard_map/ppermute | solution.py:329
  148.3 3.7 %group_cotangent.1.refs_5_ = bf16[1024,1024]{1,0:T(8,128)(2,1)} custom-call(s32[5]{0:T(128)} %stack.35.refs_0_.pos, bf16[1024,512]{1,0:T(8,128)(2,1)} %bitcast.43, bf16[1024,512]{1,0:T(8,128)(2,1)} %collective-permute-done.23.refs_2_), custom_call_target="tpu_custom_call" | custom-call | bytes 4194304 | tf_op jit(solution)/shard_map/group_cotangent/pallas_call | solution.py:49
  155.6 6.6 %output_weight_terms.1 = bf16[8,1024,128]{2,1,0:T(8,128)(2,1)} custom-call(s32[5]{0:T(128)} %stack.35.refs_0_.pos, bf16[256,1024]{1,0:T(8,128)(2,1)} %get-tuple-element.27.refs_0_, bf16[256,1024]{1,0:T(8,128)(2,1)} %copy-done.11, bf16[256,1024]{1,0:T(8,128)(2,1)} %copy-done.12, bf16[128,1024]{1,0:T(8,128)(2,1)} %copy-done.14, bf16[128,1024]{1,0:T(8,128)(2,1)} %copy-done.15, ...), custom_call_target="tpu_custom_call" | custom-call | flops 2147483648 | bytes 6291456 | tf_op jit(solution)/shard_map/output_weight_terms/pallas_call | solution.py:49
  163.1 5.0 %all-to-all-start.4 = ((bf16[8,1024,128]{2,1,0:T(8,128)(2,1)}), bf16[8,1024,128]{2,1,0:T(8,128)(2,1)S(1)}, u32[]{:S(2)}, u32[]{:S(2)}) async-start(bf16[8,1024,128]{2,1,0:T(8,128)(2,1)} %output_weight_terms.1), calls=%async_computation.4 | async-start | bytes 4194304 | tf_op jit(solution)/shard_map/all_to_all | solution.py:376
  168.3 3.2 %collective-permute-start.20 = (bf16[1024,256]{1,0:T(8,128)(2,1)}, bf16[1024,256]{1,0:T(8,128)(2,1)S(1)}, u32[]{:S(2)}, u32[]{:S(2)}) collective-permute-start(bf16[1024,256]{1,0:T(8,128)(2,1)} %get-tuple-element.37.refs_1_), channel_id=1, source_target_pairs={{0,24},{8,0},{16,8},{24,16},{1,25},{9,1},{17,9},{25,17},{2,26},{10... | collective-permute-start | bytes 1572872 | tf_op jit(solution)/shard_map/ppermute | solution.py:329
  171.5 8.3 %output_terms.1 = (bf16[2,256,1024]{2,1,0:T(8,128)(2,1)}, f32[2,256,1024]{2,1,0:T(8,128)}) custom-call(s32[5]{0:T(128)} %stack.35.refs_0_.pos, bf16[256,1024]{1,0:T(8,128)(2,1)} %get-tuple-element.27.refs_0_, bf16[256,1024]{1,0:T(8,128)(2,1)} %copy-done.11, bf16[256,1024]{1,0:T(8,128)(2,1)} %copy-done.12, bf16[128,1024]{1,0:T(8,128)(2,1)} %copy-done.14, ...), custom_call_target="tpu_custom_call" | custom-call | flops 2147483648 | bytes 8388608 | tf_op jit(solution)/shard_map/output_terms/pallas_call | solution.py:49
  179.8 4.2 %collective-permute-done.19.refs_2_ = bf16[1024,256]{1,0:T(8,128)(2,1)S(1)} collective-permute-done((bf16[1024,256]{1,0:T(8,128)(2,1)}, bf16[1024,256]{1,0:T(8,128)(2,1)S(1)}, u32[]{:S(2)}, u32[]{:S(2)}) %collective-permute-start.19) | collective-permute-done | bytes 524320 | tf_op jit(solution)/shard_map/ppermute | solution.py:329
  184.1 3.5 %collective-permute-start.22 = (bf16[512,256]{1,0:T(8,128)(2,1)S(1)}, bf16[512,256]{1,0:T(8,128)(2,1)S(1)}, u32[]{:S(2)}, u32[]{:S(2)}) collective-permute-start(bf16[512,256]{1,0:T(8,128)(2,1)S(1)} %slice.50), channel_id=1, source_target_pairs={{0,24},{8,0},{16,8},{24,16},{1,25},{9,1},{17,9},{25,17},{2,26},{10... | collective-permute-start | bytes 786440 | tf_op jit(solution)/shard_map/ppermute | solution.py:329
  188.6 4.2 %group_states.1.refs_0_ = bf16[1024,1024]{1,0:T(8,128)(2,1)} custom-call(s32[5]{0:T(128)} %stack.35.refs_0_.pos, bf16[1024,512]{1,0:T(8,128)(2,1)} %bitcast.42, bf16[1024,512]{1,0:T(8,128)(2,1)} %copy-done.13), custom_call_target="tpu_custom_call" | custom-call | bytes 4194304 | tf_op jit(solution)/shard_map/group_states/pallas_call | solution.py:49
  194.6 6.5 %query_weight_terms.1 = bf16[1024,1024]{1,0:T(8,128)(2,1)} custom-call(s32[5]{0:T(128)} %stack.35.refs_0_.pos, bf16[1024,1024]{1,0:T(8,128)(2,1)} %group_states.1.refs_0_, bf16[1024,256]{1,0:T(8,128)(2,1)} %get-tuple-element.37.refs_1_, bf16[1024,256]{1,0:T(8,128)(2,1)} %copy-done.16, bf16[1024,256]{1,0:T(8,128)(2,1)} %copy-done.17, ...), custom_call_target="tpu_custom_call" | custom-call | flops 2147483648 | bytes 6291456 | tf_op jit(solution)/shard_map/query_weight_terms/pallas_call | solution.py:49
  201.0 5.6 %all-to-all-start.2 = ((bf16[8,128,1024]{2,1,0:T(8,128)(2,1)}), bf16[8,128,1024]{2,1,0:T(8,128)(2,1)}, u32[]{:S(2)}, u32[]{:S(2)}) async-start(bf16[8,128,1024]{2,1,0:T(8,128)(2,1)} %bitcast.45), calls=%async_computation.2 | async-start | bytes 4194304 | tf_op jit(solution)/shard_map/all_to_all | solution.py:376
  212.6 30.1 %collective-permute-done.11 = bf16[256,1024]{1,0:T(8,128)(2,1)S(1)} collective-permute-done((bf16[256,1024]{1,0:T(8,128)(2,1)S(1)}, bf16[256,1024]{1,0:T(8,128)(2,1)S(1)}, u32[]{:S(2)}, u32[]{:S(2)}) %collective-permute-start.11) | collective-permute-done | bytes 524320 | tf_op jit(solution)/shard_map/ppermute | solution.py:332
  (125 shorter events, 49.5 us)
Async XLA Ops:
  0.7 16.9 %collective-permute-start.14 = (bf16[256,1024]{1,0:T(8,128)(2,1)}, bf16[256,1024]{1,0:T(8,128)(2,1)}, u32[]{:S(2)}, u32[]{:S(2)}) collective-permute-start(bf16[256,1024]{1,0:T(8,128)(2,1)} %refs_1_.7), channel_id=1, source_target_pairs={{0,64},{64,0},{1,65},{65,1},{2,66},{66,2},{3,67},{67,3},{4,68},{68... | collective-permute-start | bytes 1572872 | tf_op jit(solution)/shard_map/ppermute | solution.py:332
  5.8 47.5 %all-to-all-start = ((bf16[128,2,8,256]{3,2,1,0:T(8,128)(2,1)}), bf16[128,2,8,256]{3,2,1,0:T(8,128)(2,1)S(1)}, u32[]{:S(2)}, u32[]{:S(2)}) async-start(bf16[128,2,8,256]{3,2,1,0:T(8,128)(2,1)} %bitcast.8), calls=%async_computation | async-start | bytes 2097152 | tf_op jit(solution)/shard_map/all_to_all | solution.py:336
  15.0 25.4 %collective-permute-start.1 = (bf16[256,1024]{1,0:T(8,128)(2,1)S(1)}, bf16[256,1024]{1,0:T(8,128)(2,1)}, u32[]{:S(2)}, u32[]{:S(2)}) collective-permute-start(bf16[256,1024]{1,0:T(8,128)(2,1)S(1)} %copy-done.1), channel_id=1, source_target_pairs={{0,64},{64,0},{1,65},{65,1},{2,66},{66,2},{3,67},{67,3},{4,68},{68... | collective-permute-start | bytes 1572872 | tf_op jit(solution)/shard_map/ppermute | solution.py:332
  17.5 22.8 %collective-permute-start.13 = (bf16[256,1024]{1,0:T(8,128)(2,1)S(1)}, bf16[256,1024]{1,0:T(8,128)(2,1)S(1)}, u32[]{:S(2)}, u32[]{:S(2)}) collective-permute-start(bf16[256,1024]{1,0:T(8,128)(2,1)S(1)} %copy-done), channel_id=1, source_target_pairs={{0,32},{32,0},{1,33},{33,1},{2,34},{34,2},{3,35},{35,3},{4,36},{36... | collective-permute-start | bytes 1572872 | tf_op jit(solution)/shard_map/ppermute | solution.py:332
  17.6 29.5 %collective-permute-start.15 = (bf16[256,1024]{1,0:T(8,128)(2,1)}, bf16[256,1024]{1,0:T(8,128)(2,1)}, u32[]{:S(2)}, u32[]{:S(2)}) collective-permute-start(bf16[256,1024]{1,0:T(8,128)(2,1)} %collective-permute-done.14.refs_3_), channel_id=1, source_target_pairs={{0,32},{32,0},{1,33},{33,1},{2,34},{34,2},{3,35},{35,3},{4,36},{36... | collective-permute-start | bytes 1572872 | tf_op jit(solution)/shard_map/ppermute | solution.py:332
  18.1 41.8 %collective-permute-start = (bf16[256,1024]{1,0:T(8,128)(2,1)S(1)}, bf16[256,1024]{1,0:T(8,128)(2,1)S(1)}, u32[]{:S(2)}, u32[]{:S(2)}) collective-permute-start(bf16[256,1024]{1,0:T(8,128)(2,1)S(1)} %copy-done.1), channel_id=1, source_target_pairs={{0,32},{32,0},{1,33},{33,1},{2,34},{34,2},{3,35},{35,3},{4,36},{36... | collective-permute-start | bytes 1572872 | tf_op jit(solution)/shard_map/ppermute | solution.py:332
  40.4 26.1 %collective-permute-start.2 = (bf16[256,1024]{1,0:T(8,128)(2,1)}, bf16[256,1024]{1,0:T(8,128)(2,1)}, u32[]{:S(2)}, u32[]{:S(2)}) collective-permute-start(bf16[256,1024]{1,0:T(8,128)(2,1)} %collective-permute-done.1.refs_3_), channel_id=1, source_target_pairs={{0,32},{32,0},{1,33},{33,1},{2,34},{34,2},{3,35},{35,3},{4,36},{36... | collective-permute-start | bytes 1572872 | tf_op jit(solution)/shard_map/ppermute | solution.py:332
  54.3 29.2 %all-to-all-start.3 = ((bf16[4,256,512]{2,1,0:T(8,128)(2,1)}), bf16[4,256,512]{2,1,0:T(8,128)(2,1)S(1)}, u32[]{:S(2)}, u32[]{:S(2)}) async-start(bf16[4,256,512]{2,1,0:T(8,128)(2,1)} %get-tuple-element.38), calls=%async_computation.3 | async-start | bytes 2097152 | tf_op jit(solution)/shard_map/all_to_all | solution.py:353
  74.9 13.7 %collective-permute-start.4 = (bf16[256,256]{1,0:T(8,128)(2,1)}, bf16[256,256]{1,0:T(8,128)(2,1)S(1)}, u32[]{:S(2)}, u32[]{:S(2)}) collective-permute-start(bf16[256,256]{1,0:T(8,128)(2,1)} %get-tuple-element.25), channel_id=1, source_target_pairs={{0,16},{8,24},{16,0},{24,8},{1,17},{9,25},{17,1},{25,9},{2,18},{10... | collective-permute-start | bytes 393224 | tf_op jit(solution)/shard_map/ppermute | solution.py:329
  80.1 18.5 %collective-permute-start.16 = (bf16[256,256]{1,0:T(8,128)(2,1)S(1)}, bf16[256,256]{1,0:T(8,128)(2,1)S(1)}, u32[]{:S(2)}, u32[]{:S(2)}) collective-permute-start(bf16[256,256]{1,0:T(8,128)(2,1)S(1)} %copy-done.22), channel_id=1, source_target_pairs={{0,8},{8,16},{16,24},{24,0},{1,9},{9,17},{17,25},{25,1},{2,10},{10... | collective-permute-start | bytes 393224 | tf_op jit(solution)/shard_map/ppermute | solution.py:329
  80.7 17.9 %collective-permute-start.17 = (bf16[256,256]{1,0:T(8,128)(2,1)S(1)}, bf16[256,256]{1,0:T(8,128)(2,1)}, u32[]{:S(2)}, u32[]{:S(2)}) collective-permute-start(bf16[256,256]{1,0:T(8,128)(2,1)S(1)} %copy-done.21), channel_id=1, source_target_pairs={{0,16},{8,24},{16,0},{24,8},{1,17},{9,25},{17,1},{25,9},{2,18},{10... | collective-permute-start | bytes 393224 | tf_op jit(solution)/shard_map/ppermute | solution.py:329
  81.6 17.0 %collective-permute-start.18 = (bf16[256,256]{1,0:T(8,128)(2,1)S(1)}, bf16[256,256]{1,0:T(8,128)(2,1)}, u32[]{:S(2)}, u32[]{:S(2)}) collective-permute-start(bf16[256,256]{1,0:T(8,128)(2,1)S(1)} %copy-done.20), channel_id=1, source_target_pairs={{0,24},{8,0},{16,8},{24,16},{1,25},{9,1},{17,9},{25,17},{2,26},{10... | collective-permute-start | bytes 393224 | tf_op jit(solution)/shard_map/ppermute | solution.py:329
  84.5 24.5 %all-to-all-start.1 = ((bf16[4,256,512]{2,1,0:T(8,128)(2,1)}), bf16[4,256,512]{2,1,0:T(8,128)(2,1)S(1)}, u32[]{:S(2)}, u32[]{:S(2)}) async-start(bf16[4,256,512]{2,1,0:T(8,128)(2,1)} %get-tuple-element.30), calls=%async_computation.1 | async-start | bytes 2097152 | tf_op jit(solution)/shard_map/all_to_all | solution.py:353
  98.5 49.8 %collective-permute-start.23 = (bf16[1024,512]{1,0:T(8,128)(2,1)S(1)}, bf16[1024,512]{1,0:T(8,128)(2,1)}, u32[]{:S(2)}, u32[]{:S(2)}) collective-permute-start(bf16[1024,512]{1,0:T(8,128)(2,1)S(1)} %bitcast.44), channel_id=1, source_target_pairs={{0,32},{32,0},{1,33},{33,1},{2,34},{34,2},{3,35},{35,3},{4,36},{36... | collective-permute-start | bytes 3145736 | tf_op jit(solution)/shard_map/ppermute | solution.py:332
  109.0 53.2 %all-to-all-start.5 = ((bf16[128,2,8,256]{3,2,1,0:T(8,128)(2,1)}), bf16[128,2,8,256]{3,2,1,0:T(8,128)(2,1)S(1)}, u32[]{:S(2)}, u32[]{:S(2)}) async-start(bf16[128,2,8,256]{3,2,1,0:T(8,128)(2,1)} %pad_maximum_fusion), calls=%async_computation.5 | async-start | bytes 2097152 | tf_op jit(solution)/shard_map/all_to_all | solution.py:384
  118.7 26.2 %collective-permute-start.6 = (bf16[256,1024]{1,0:T(8,128)(2,1)}, bf16[256,1024]{1,0:T(8,128)(2,1)S(1)}, u32[]{:S(2)}, u32[]{:S(2)}) collective-permute-start(bf16[256,1024]{1,0:T(8,128)(2,1)} %get-tuple-element.27.refs_0_), channel_id=1, source_target_pairs={{0,8},{8,16},{16,24},{24,0},{1,9},{9,17},{17,25},{25,1},{2,10},{10... | collective-permute-start | bytes 1572872 | tf_op jit(solution)/shard_map/ppermute | solution.py:329
  119.8 25.2 %collective-permute-start.7 = (bf16[256,1024]{1,0:T(8,128)(2,1)}, bf16[256,1024]{1,0:T(8,128)(2,1)S(1)}, u32[]{:S(2)}, u32[]{:S(2)}) collective-permute-start(bf16[256,1024]{1,0:T(8,128)(2,1)} %get-tuple-element.27.refs_0_), channel_id=1, source_target_pairs={{0,24},{8,0},{16,8},{24,16},{1,25},{9,1},{17,9},{25,17},{2,26},{10... | collective-permute-start | bytes 1572872 | tf_op jit(solution)/shard_map/ppermute | solution.py:329
  163.1 37.9 %all-to-all-start.4 = ((bf16[8,1024,128]{2,1,0:T(8,128)(2,1)}), bf16[8,1024,128]{2,1,0:T(8,128)(2,1)S(1)}, u32[]{:S(2)}, u32[]{:S(2)}) async-start(bf16[8,1024,128]{2,1,0:T(8,128)(2,1)} %output_weight_terms.1), calls=%async_computation.4 | async-start | bytes 4194304 | tf_op jit(solution)/shard_map/all_to_all | solution.py:376
  168.1 19.5 %collective-permute-start.12 = (bf16[1024,512]{1,0:T(8,128)(2,1)S(1)}, bf16[1024,512]{1,0:T(8,128)(2,1)S(1)}, u32[]{:S(2)}, u32[]{:S(2)}) collective-permute-start(bf16[1024,512]{1,0:T(8,128)(2,1)S(1)} %bitcast.41), channel_id=1, source_target_pairs={{0,32},{32,0},{1,33},{33,1},{2,34},{34,2},{3,35},{35,3},{4,36},{36... | collective-permute-start | bytes 3145736 | tf_op jit(solution)/shard_map/ppermute | solution.py:332
  168.2 15.8 %collective-permute-start.19 = (bf16[1024,256]{1,0:T(8,128)(2,1)}, bf16[1024,256]{1,0:T(8,128)(2,1)S(1)}, u32[]{:S(2)}, u32[]{:S(2)}) collective-permute-start(bf16[1024,256]{1,0:T(8,128)(2,1)} %get-tuple-element.37.refs_1_), channel_id=1, source_target_pairs={{0,8},{8,16},{16,24},{24,0},{1,9},{9,17},{17,25},{25,1},{2,10},{10... | collective-permute-start | bytes 1572872 | tf_op jit(solution)/shard_map/ppermute | solution.py:329
  168.3 15.8 %collective-permute-start.20 = (bf16[1024,256]{1,0:T(8,128)(2,1)}, bf16[1024,256]{1,0:T(8,128)(2,1)S(1)}, u32[]{:S(2)}, u32[]{:S(2)}) collective-permute-start(bf16[1024,256]{1,0:T(8,128)(2,1)} %get-tuple-element.37.refs_1_), channel_id=1, source_target_pairs={{0,24},{8,0},{16,8},{24,16},{1,25},{9,1},{17,9},{25,17},{2,26},{10... | collective-permute-start | bytes 1572872 | tf_op jit(solution)/shard_map/ppermute | solution.py:329
  179.8 26.8 %collective-permute-start.10 = (bf16[2,256,1024]{2,1,0:T(8,128)(2,1)}, bf16[2,256,1024]{2,1,0:T(8,128)(2,1)}, u32[]{:S(2)}, u32[]{:S(2)}) collective-permute-start(bf16[2,256,1024]{2,1,0:T(8,128)(2,1)} %get-tuple-element.29), channel_id=1, source_target_pairs={{0,32},{32,0},{1,33},{33,1},{2,34},{34,2},{3,35},{35,3},{4,36},{36... | collective-permute-start | bytes 3145736 | tf_op jit(solution)/shard_map/ppermute | solution.py:332
  201.0 43.7 %all-to-all-start.2 = ((bf16[8,128,1024]{2,1,0:T(8,128)(2,1)}), bf16[8,128,1024]{2,1,0:T(8,128)(2,1)}, u32[]{:S(2)}, u32[]{:S(2)}) async-start(bf16[8,128,1024]{2,1,0:T(8,128)(2,1)} %bitcast.45), calls=%async_computation.2 | async-start | bytes 4194304 | tf_op jit(solution)/shard_map/all_to_all | solution.py:376
  209.0 33.7 %collective-permute-start.11 = (bf16[256,1024]{1,0:T(8,128)(2,1)S(1)}, bf16[256,1024]{1,0:T(8,128)(2,1)S(1)}, u32[]{:S(2)}, u32[]{:S(2)}) collective-permute-start(bf16[256,1024]{1,0:T(8,128)(2,1)S(1)} %fusion.2), channel_id=1, source_target_pairs={{0,64},{64,0},{1,65},{65,1},{2,66},{66,2},{3,67},{67,3},{4,68},{68... | collective-permute-start | bytes 1572872 | tf_op jit(solution)/shard_map/ppermute | solution.py:332
  (35 other events, 257.9 us)

commit v4 on v3

--- a/solution.py
+++ b/solution.py
@@ -10,6 +10,7 @@
 
 HEAD = 128
 SCALE = 1.0 / math.sqrt(HEAD)
+LOG2E = math.log2(math.e)
 F32 = jnp.float32
 BF16 = jnp.bfloat16
 AXES = (("xh", 2), ("core", 2), ("z", 4), ("y", 4), ("xl", 2))
@@ -17,7 +18,7 @@
 SEQ = ("z", "y", "xl")
 XH, CORE, Z = range(3)
 SWAP = [(0, 1), (1, 0)]
-VMEM = 56 * 1024 * 1024
+WORK = 8 * 1024 * 1024
 TOK = 256
 PIECE = 256
 GROUP = 4 * TOK
@@ -46,6 +47,10 @@
 
 
 def call(kernel, name, grid, in_specs, out_specs, out_shape, scratch, flops, moved, pos, *args):
+    outs = zip(jax.tree.leaves(out_specs), jax.tree.leaves(out_shape))
+    blocks = [(s.block_shape, a.dtype) for s, a in [*zip(in_specs, args), *outs]]
+    room = sum(2 * math.prod(shape) * dtype.itemsize for shape, dtype in blocks)
+    room += sum(math.prod(s.shape) * jnp.dtype(s.dtype).itemsize for s in scratch)
     return pl.pallas_call(
         kernel,
         grid_spec=pltpu.PrefetchScalarGridSpec(
@@ -56,7 +61,7 @@
             scratch_shapes=scratch,
         ),
         out_shape=out_shape,
-        compiler_params=pltpu.CompilerParams(vmem_limit_bytes=VMEM),
+        compiler_params=pltpu.CompilerParams(vmem_limit_bytes=room + WORK),
         cost_estimate=pl.CostEstimate(flops=flops, bytes_accessed=moved, transcendentals=0),
         name=name,
     )(pos, *args)
@@ -142,16 +147,19 @@
 
 
 def forward_kernel(pos, bias, *refs):
-    q_refs, (k_ref, v_ref, out_ref, turned_ref, probs_ref) = refs[:4], refs[4:]
+    q_refs, (k_ref, v_ref, out_ref, turned_ref, weights_ref, share_ref) = refs[:4], refs[4:]
     k, v = k_ref[...], v_ref[...]
     for d in range(4):
+        here = slice(d * TOK, (d + 1) * TOK)
         scores = dot(q_refs[d][...], k, ((1,), (1,))) + bias[...]
         top = jnp.max(scores, axis=1, keepdims=True)
-        weights = jnp.exp((scores - top) * SCALE)
-        probs = (weights * (1.0 / jnp.sum(weights, axis=1, keepdims=True))).astype(BF16)
-        heads_out = dot(probs, v).astype(BF16)
-        probs_ref[0, d * TOK : (d + 1) * TOK, :] = probs
-        out_ref[d * TOK : (d + 1) * TOK, :] = heads_out
+        weights = jnp.exp2((scores - top) * (SCALE * LOG2E))
+        share = 1.0 / jnp.sum(weights, axis=1, keepdims=True)
+        weights = weights.astype(BF16)
+        heads_out = (dot(weights, v) * share).astype(BF16)
+        weights_ref[0, here, :] = weights
+        out_ref[here, :] = heads_out
+        share_ref[here, :] = jnp.broadcast_to(share, (TOK, HEAD))
         token = pl.multiple_of(shifted(pos[Z], -d) * TOK, TOK)
         turned_ref[:, pl.ds(token, TOK)] = heads_out.T
 
@@ -169,8 +177,14 @@
             column,
             pl.BlockSpec((HEAD, GROUP), lambda h, pos: (h, 0)),
             pl.BlockSpec((1, GROUP, context), lambda h, pos: (h, 0, 0)),
+            column,
         ],
-        [struct((GROUP, PIECE)), struct((PIECE, GROUP)), struct((PIECE // HEAD, GROUP, context))],
+        [
+            struct((GROUP, PIECE)),
+            struct((PIECE, GROUP)),
+            struct((PIECE // HEAD, GROUP, context)),
+            struct((GROUP, PIECE), F32),
+        ],
         [],
         12 * GROUP * PIECE * context,
         2 * (4 * GROUP * PIECE + 2 * GROUP * context),
@@ -183,26 +197,25 @@
 
 
 def backward_kernel(pos, *refs):
-    q_refs, g_refs, (k_ref, v_ref, out_ref, probs_ref) = refs[:4], refs[4:8], refs[8:12]
-    dq_ref, dk_ref, dv_ref, dk_sum, dv_sum = refs[12:]
+    q_refs, g_refs, (k_ref, v_ref, out_ref, weights_ref, share_ref) = refs[:4], refs[4:8], refs[8:13]
+    dq_ref, dk_ref, dv_ref, dk_sum, dv_sum = refs[13:]
     k, v = k_ref[...], v_ref[...]
     for d in range(4):
-        q, g = q_refs[d][...], g_refs[d][...]
-        probs = probs_ref[0, d * TOK : (d + 1) * TOK, :]
-        value_dots = dot(g, v, ((1,), (1,)))
-        heads_out = out_ref[d * TOK : (d + 1) * TOK, :]
-        delta = jnp.sum(g.astype(F32) * heads_out.astype(F32), axis=1, keepdims=True)
-        score_grad = (probs.astype(F32) * ((value_dots - delta) * SCALE)).astype(BF16)
+        here = slice(d * TOK, (d + 1) * TOK)
+        g = (g_refs[d][...].astype(F32) * (share_ref[here, :] * SCALE)).astype(BF16)
+        q, weights = q_refs[d][...], weights_ref[0, here, :]
+        delta = jnp.sum(g.astype(F32) * out_ref[here, :].astype(F32), axis=1, keepdims=True)
+        score_grad = (weights.astype(F32) * (dot(g, v, ((1,), (1,))) - delta)).astype(BF16)
         token = pl.multiple_of(shifted(pos[Z], -d) * TOK, TOK)
         dq_ref[pl.ds(token, TOK), :] = dot(score_grad, k).astype(BF16)
-        dk_term, dv_term = dot(q, score_grad, ((0,), (0,))), dot(g, probs, ((0,), (0,)))
+        dk_term, dv_term = dot(q, score_grad, ((0,), (0,))), dot(g, weights, ((0,), (0,)))
         dk_sum[...] = dk_term if d == 0 else dk_sum[...] + dk_term
         dv_sum[...] = dv_term if d == 0 else dv_sum[...] + dv_term
     dk_ref[...] = dk_sum[...].T.astype(BF16)
-    dv_ref[...] = dv_sum[...].T.astype(BF16)
-
-
-def backward(pos, queries, grads, keys, values, heads_out, probs):
+    dv_ref[...] = (dv_sum[...] * (1.0 / SCALE)).T.astype(BF16)
+
+
+def backward(pos, queries, grads, keys, values, heads_out, weights, share):
     rows = pl.BlockSpec((TOK, HEAD), lambda h, pos: (0, h))
     column = pl.BlockSpec((GROUP, HEAD), lambda h, pos: (0, h))
     context = keys.shape[0]
@@ -210,7 +223,9 @@
         backward_kernel,
         "attention_backward",
         (PIECE // HEAD,),
-        [rows] * 8 + [column] * 3 + [pl.BlockSpec((1, GROUP, context), lambda h, pos: (h, 0, 0))],
+        [rows] * 8
+        + [column] * 3
+        + [pl.BlockSpec((1, GROUP, context), lambda h, pos: (h, 0, 0)), column],
         [column] * 3,
         [struct((GROUP, PIECE))] * 3,
         [pltpu.VMEM((HEAD, context), F32)] * 2,
@@ -222,7 +237,8 @@
         keys,
         values,
         heads_out,
-        probs,
+        weights,
+        share,
     )
 
 
@@ -331,42 +347,57 @@
     def swap(x, axis):
         return lax.ppermute(x, axis, SWAP)
 
+    def after(x, *others):
+        return lax.optimization_barrier((x, *others))[0]
+
+    def near(name, local, weight, transposed):
+        blocks = (local, swap(local, "core"))
+        return blocks, project(name, pos, blocks, weight, transposed)
+
+    def far(name, blocks, over_x, weight, transposed, first):
+        blocks = blocks + (over_x, swap(over_x, "core"))
+        outs = project(name, pos, blocks, weight, transposed, first)
+        return [to_layer(x, d) for d, x in enumerate(outs[:4])], outs[4]
+
+    states_x = swap(decoder_states, "xh")
+    states, first_queries = near("queries_near", decoder_states, query_weight, False)
+    cotangent, first_grad = near("heads_grad_near", output_cotangent, output_weight, True)
+    states_x = after(states_x, first_queries, first_grad)
+    cotangent_x = swap(after(output_cotangent, states_x), "xh")
+
     own = jnp.stack([context_keys, context_values]).reshape(2, 8, 16, PIECE).transpose(2, 0, 1, 3)
     own = jnp.broadcast_to(own[:, None], (16, PLANES, 2, 8, PIECE)).reshape(128, 2, 8, PIECE)
-    context = lax.all_to_all(own, HEADS + SEQ, 0, 0, tiled=True)
+    context = lax.all_to_all(after(own, first_queries, first_grad), HEADS + SEQ, 0, 0, tiled=True)
     keys = context[:, 0].reshape(4 * TOK, PIECE)
     values = context[:, 1].reshape(4 * TOK, PIECE)
     bias = context_bias(lengths, slot_passage)
 
-    def projected(name, local, weight, transposed):
-        over_x = swap(local, "xh")
-        near = (local, swap(local, "core"))
-        first = project(name + "_near", pos, near, weight, transposed)
-        blocks = near + (over_x, swap(over_x, "core"))
-        outs = project(name, pos, blocks, weight, transposed, first)
-        return [to_layer(x, d) for d, x in enumerate(outs[:4])], outs[4]
-
-    queries, state_parts = projected("queries", decoder_states, query_weight, False)
-    heads_grad, cotangent_parts = projected("heads_grad", output_cotangent, output_weight, True)
-
     def column_block(name, parts, transposed):
         mine = lax.all_to_all(parts, "z", 0, 0, tiled=True).reshape(GROUP, BLOCK // 2)
         return assemble(name, pos, mine, swap(mine, "core"), transposed)
 
-    def along_z(x):
+    def ring_ends(x):
+        return to_layer(x, 1), to_layer(x, 3)
+
+    def ring(x, left, right):
         half = x.shape[0] // 2
-        left, right = to_layer(x, 1), to_layer(x, 3)
         return x, left, right, to_layer(left[:half], 1), to_layer(right[half:], 3)
 
-    heads_out, turned_out, probs = forward(pos, bias, queries, keys, values)
-    every_out = along_z(turned_out)
+    queries, state_parts = far("queries", states, states_x, query_weight, False, first_queries)
+    group_states = column_block("group_states", state_parts, True)
+    heads_out, turned_out, weights, share = forward(pos, bias, queries, keys, values)
+    left, right = ring_ends(turned_out)
+    every_out = ring(turned_out, left, right)
+
+    heads_grad, cotangent_parts = far(
+        "heads_grad", cotangent, cotangent_x, output_weight, True, first_grad
+    )
+    group_cotangent = column_block("group_cotangent", cotangent_parts, False)
     query_grad, key_terms, value_terms = backward(
-        pos, queries, heads_grad, keys, values, heads_out, probs
-    )
-    every_query_grad = along_z(query_grad)
-
-    group_states = column_block("group_states", state_parts, True)
-    group_cotangent = column_block("group_cotangent", cotangent_parts, False)
+        pos, queries, heads_grad, keys, values, after(heads_out, left, right), weights, share
+    )
+    left, right = ring_ends(query_grad)
+    every_query_grad = ring(query_grad, left, right)
 
     give, keep = output_terms(pos, every_out, output_weight)
     pair = keep + swap(give, "core").astype(F32)
@@ -378,10 +409,13 @@
     terms = weight_terms(
         "output_weight_terms", output_grad_kernel, pos, (*every_out, group_cotangent), (PLANES, BLOCK, 128)
     )
-    output_weight_grad = plane_sum(terms)
+    pair = lax.psum_scatter(terms, "y", scatter_dimension=0, tiled=True)
+    xl = lax.axis_index("xl")
+    kept, given = (lax.dynamic_index_in_dim(pair, i, 0, False) for i in (xl, 1 - xl))
+    output_weight_grad = kept.astype(F32) + swap(given, "xl").astype(F32)
 
     terms = jnp.stack([key_terms.reshape(128, 8, PIECE), value_terms.reshape(128, 8, PIECE)], 1)
-    moved = lax.all_to_all(terms, HEADS + SEQ, 0, 0, tiled=True)
+    moved = lax.all_to_all(after(terms, left, right), HEADS + SEQ, 0, 0, tiled=True)
     owned = jnp.sum(moved.reshape(16, PLANES, 2, 8, PIECE).astype(F32), axis=1)
     owned = owned.transpose(1, 2, 0, 3).reshape(2, 8, 16 * PIECE)
 

time: 248 us -> 255 us (1.028)
  local copies, waits for them, and re-layouts: 13.8 us -> 47.6 us
  Pallas kernels: 70.2 us -> 43.7 us
  between operations: 0.95 us -> 14.4 us
  waiting for transfers between devices: 81.2 us -> 70.7 us
  starting transfers between devices: 70.6 us -> 65.7 us
    unnamed x59 -> x113, local copies, waits for them, and re-layouts: 10.3 us -> 43.3 us
    pallas_call x11, Pallas kernels: 70.2 us -> 43.7 us  [call(): pl.pallas_call(kernel, grid_spec=pltpu.PrefetchScalarGridSpec(num_scalar_...]
    ppermute x10 -> x11, waiting for transfers between devices: 51.7 us -> 32.7 us  [swap(): return lax.ppermute(x, axis, SWAP)]
    all_to_all x2 -> x1, starting transfers between devices: 10.6 us -> 4.72 us  [plane_sum(): lax.all_to_all(terms, ('y', 'xl'), 0, 0, tiled=True).astype(F32)]
    all_to_all x2, waiting for transfers between devices: 0.01 us -> 4.41 us  [the longest x1 4.41 us: on_device(): lax.all_to_all(after(own, first_queries, first_grad), HEADS + SEQ, 0, 0,...]
    ppermute x14, waiting for transfers between devices: 29.5 us -> 32.3 us  [to_layer(): lax.ppermute(x, 'z', [(i, (i + d) % 4) for i in range(4)])]
    ppermute x10 -> x11, starting transfers between devices: 9.25 us -> 11.6 us  [swap(): return lax.ppermute(x, axis, SWAP)]
  transfers between devices with their start and end apart: 30 -> 31, of which waited for: 6 -> 15; matrix products, arithmetic and copies ran while one was open for 5% -> 5% of each run, Pallas kernels for 28% -> 16%
where the time goes in v4:
time: 255 us; the launch traced here: 253 us
  waiting for transfers between devices  70.7 us (28%)
  starting transfers between devices  65.7 us (26%)
  local copies, waits for them, and re-layouts  47.6 us (19%)
  Pallas kernels  43.7 us (17%)
  between operations  14.4 us (6%)
  other arithmetic  10.9 us (4%)
    pallas_call x11, Pallas kernels, call(): pl.pallas_call(kernel, grid_spec=pltpu.PrefetchScalarGridSpec(num_scalar_...  43.7 us
    unnamed x113, local copies, waits for them, and re-layouts  43.3 us
    ppermute x11, waiting for transfers between devices, swap(): return lax.ppermute(x, axis, SWAP)  32.7 us
    ppermute x14, waiting for transfers between devices, to_layer(): lax.ppermute(x, 'z', [(i, (i + d) % 4) for i in range(4)])  32.3 us
    ppermute x14, starting transfers between devices, to_layer(): lax.ppermute(x, 'z', [(i, (i + d) % 4) for i in range(4)])  21 us
    ppermute x11, starting transfers between devices, swap(): return lax.ppermute(x, axis, SWAP)  11.6 us
    all_to_all x1, starting transfers between devices, on_device(): lax.all_to_all(after(terms, left, right), HEADS + SEQ, 0, 0, tiled=True)  10.3 us
    all_to_all x1, starting transfers between devices, on_device(): lax.all_to_all(after(own, first_queries, first_grad), HEADS + SEQ, 0, 0,...  9.71 us
  transfers between devices with their start and end apart: 31, of which 15 were waited for; matrix products, arithmetic and copies ran while one was open for 5% of the time, Pallas kernels for 16%

profile of v4, /device:TPU:0, one launch (start us, length us, event | category | flops | bytes accessed | tf_op | source)
XLA Modules:
  0.0 253.1 jit_solution(8600968661530321073)
XLA Ops:
  7.8 3.1 %collective-permute-start.1 = (bf16[256,1024]{1,0:T(8,128)(2,1)}, bf16[256,1024]{1,0:T(8,128)(2,1)S(1)}, u32[]{:S(2)}, u32[]{:S(2)}) collective-permute-start(bf16[256,1024]{1,0:T(8,128)(2,1)} %refs_1_.6), channel_id=1, source_target_pairs={{0,64},{64,0},{1,65},{65,1},{2,66},{66,2},{3,67},{67,3},{4,68},{68... | collective-permute-start | bytes 1572872 | tf_op jit(solution)/shard_map/ppermute | solution.py:348
  11.0 3.4 %copy-done.3 = bf16[4096,1024]{1,0:T(8,128)(2,1)S(1)} copy-done((bf16[4096,1024]{1,0:T(8,128)(2,1)S(1)}, bf16[4096,1024]{1,0:T(8,128)(2,1)}, u32[]{:S(2)}) %copy-start.3) | copy-done | bytes 8388632
  23.4 3.1 %collective-permute-start.14 = (bf16[256,1024]{1,0:T(8,128)(2,1)S(1)}, bf16[256,1024]{1,0:T(8,128)(2,1)}, u32[]{:S(2)}, u32[]{:S(2)}) collective-permute-start(bf16[256,1024]{1,0:T(8,128)(2,1)S(1)} %copy-done.5), channel_id=1, source_target_pairs={{0,64},{64,0},{1,65},{65,1},{2,66},{66,2},{3,67},{67,3},{4,68},{68... | collective-permute-start | bytes 1572872 | tf_op jit(solution)/shard_map/ppermute | solution.py:348
  27.6 9.7 %all-to-all-start = ((bf16[128,2,8,256]{3,2,1,0:T(8,128)(2,1)}), bf16[128,2,8,256]{3,2,1,0:T(8,128)(2,1)}, u32[]{:S(2)}, u32[]{:S(2)}) async-start(bf16[128,2,8,256]{3,2,1,0:T(8,128)(2,1)} %bitcast.51), calls=%async_computation | async-start | bytes 2097152 | tf_op jit(solution)/shard_map/all_to_all | solution.py:370
  41.0 3.4 %copy-done.1 = bf16[1024,4096]{1,0:T(8,128)(2,1)S(1)} copy-done((bf16[1024,4096]{1,0:T(8,128)(2,1)S(1)}, bf16[1024,4096]{1,0:T(8,128)(2,1)}, u32[]{:S(2)}) %copy-start.1) | copy-done | bytes 8388632
  45.6 3.7 %heads_grad.1 = (bf16[256,256]{1,0:T(8,128)(2,1)S(1)}, bf16[256,256]{1,0:T(8,128)(2,1)S(1)}, bf16[256,256]{1,0:T(8,128)(2,1)S(1)}, bf16[256,256]{1,0:T(8,128)(2,1)S(1)}, bf16[4,256,512]{2,1,0:T(8,128)(2,1)S(1)}) custom-call(s32[5]{0:T(128)S(1)} %stack.35.refs_0_.pos, bf16[256,1024]{1,0:T(8,128)(2,1)S(1)} %copy-done.5, ...), custom_call_target="tpu_custom_call" | custom-call | flops 1073741824 | bytes 4194304 | tf_op jit(solution)/shard_map/heads_grad/pallas_call | solution.py:54
  51.7 4.4 %all-to-all-done = bf16[128,2,8,256]{3,2,1,0:T(8,128)(2,1)} async-done(((bf16[128,2,8,256]{3,2,1,0:T(8,128)(2,1)}), bf16[128,2,8,256]{3,2,1,0:T(8,128)(2,1)}, u32[]{:S(2)}, u32[]{:S(2)}) %all-to-all-start) | async-done | bytes 1048608 | tf_op jit(solution)/shard_map/all_to_all | solution.py:370
  56.1 4.2 %all-to-all-start.3 = ((bf16[4,256,512]{2,1,0:T(8,128)(2,1)}), bf16[4,256,512]{2,1,0:T(8,128)(2,1)}, u32[]{:S(2)}, u32[]{:S(2)}) async-start(bf16[4,256,512]{2,1,0:T(8,128)(2,1)} %copy-done.14), calls=%async_computation.3 | async-start | bytes 2097152 | tf_op jit(solution)/shard_map/all_to_all | solution.py:376
  60.7 3.4 %copy-done.4 = bf16[4096,1024]{1,0:T(8,128)(2,1)S(1)} copy-done((bf16[4096,1024]{1,0:T(8,128)(2,1)S(1)}, bf16[4096,1024]{1,0:T(8,128)(2,1)}, u32[]{:S(2)}) %copy-start.4) | copy-done | bytes 8388632
  64.1 4.4 %queries.1 = (bf16[256,256]{1,0:T(8,128)(2,1)S(1)}, bf16[256,256]{1,0:T(8,128)(2,1)S(1)}, bf16[256,256]{1,0:T(8,128)(2,1)S(1)}, bf16[256,256]{1,0:T(8,128)(2,1)S(1)}, bf16[4,256,512]{2,1,0:T(8,128)(2,1)}) custom-call(s32[5]{0:T(128)S(1)} %stack.35.refs_0_.pos, bf16[256,1024]{1,0:T(8,128)(2,1)S(1)} %copy-done.7, ...), custom_call_target="tpu_custom_call" | custom-call | flops 1073741824 | bytes 4194304 | tf_op jit(solution)/shard_map/queries/pallas_call | solution.py:54
  81.0 5.8 %attention_forward.1 = (bf16[1024,256]{1,0:T(8,128)(2,1)S(1)}, bf16[256,1024]{1,0:T(8,128)(2,1)S(1)}, bf16[2,1024,1024]{2,1,0:T(8,128)(2,1)S(1)}, f32[1024,256]{1,0:T(8,128)S(1)}) custom-call(s32[5]{0:T(128)S(1)} %stack.35.refs_0_.pos, f32[1,1024]{1,0:T(1,128)S(1)} %bitcast.50, bf16[256,256]{1,0:T(8,128)(2,1)S(1)} %get-tuple-element.30.refs_0_, ...), custom_call_target="tpu_custom_call" | custom-call | flops 3221225472 | bytes 6291456 | tf_op jit(solution)/shard_map/attention_forward/pallas_call | solution.py:54
  90.9 10.6 %collective-permute-done.8.refs_2_ = bf16[256,1024]{1,0:T(8,128)(2,1)S(1)} collective-permute-done((bf16[256,1024]{1,0:T(8,128)(2,1)S(1)}, bf16[256,1024]{1,0:T(8,128)(2,1)S(1)}, u32[]{:S(2)}, u32[]{:S(2)}) %collective-permute-start.8) | collective-permute-done | bytes 524320 | tf_op jit(solution)/shard_map/ppermute | solution.py:345
  108.9 3.2 %collective-permute-done.9.refs_3_ = bf16[128,1024]{1,0:T(8,128)(2,1)S(1)} collective-permute-done((bf16[128,1024]{1,0:T(8,128)(2,1)S(1)}, bf16[128,1024]{1,0:T(8,128)(2,1)S(1)}, u32[]{:S(2)}, u32[]{:S(2)}) %collective-permute-start.9) | collective-permute-done | bytes 262176 | tf_op jit(solution)/shard_map/ppermute | solution.py:345
  112.1 4.2 %output_weight_terms.1 = bf16[8,1024,128]{2,1,0:T(8,128)(2,1)} custom-call(s32[5]{0:T(128)S(1)} %stack.35.refs_0_.pos, bf16[256,1024]{1,0:T(8,128)(2,1)S(1)} %get-tuple-element.35.refs_0_, bf16[256,1024]{1,0:T(8,128)(2,1)S(1)} %collective-permute-done.7.refs_1_, bf16[256,1024]{1,0:T(8,128)(2,1)S(1)} %collective-permute-done.8.refs_2_, ...), custom_call_target="tpu_custom_call" | custom-call | flops 2147483648 | bytes 6291456 | tf_op jit(solution)/shard_map/output_weight_terms/pallas_call | solution.py:54
  121.2 4.1 %all-to-all-start.1 = ((bf16[4,256,512]{2,1,0:T(8,128)(2,1)}), bf16[4,256,512]{2,1,0:T(8,128)(2,1)S(1)}, u32[]{:S(2)}, u32[]{:S(2)}) async-start(bf16[4,256,512]{2,1,0:T(8,128)(2,1)} %get-tuple-element.38), calls=%async_computation.1 | async-start | bytes 2097152 | tf_op jit(solution)/shard_map/all_to_all | solution.py:376
  139.8 5.6 %attention_backward.1 = (bf16[1024,256]{1,0:T(8,128)(2,1)}, bf16[1024,256]{1,0:T(8,128)(2,1)S(1)}, bf16[1024,256]{1,0:T(8,128)(2,1)S(1)}) custom-call(s32[5]{0:T(128)S(1)} %stack.35.refs_0_.pos, bf16[256,256]{1,0:T(8,128)(2,1)S(1)} %copy-done.30, bf16[256,256]{1,0:T(8,128)(2,1)S(1)} %copy-done.32, bf16[256,256]{1,0:T(8,128)(2,1)S(1)} %copy-done.34, ...), custom_call_target="tpu_custom_call" | custom-call | flops 4294967296 | bytes 7340032 | tf_op jit(solution)/shard_map/attention_backward/pallas_call | solution.py:54
  149.8 6.2 %collective-permute-done.19.refs_2_ = bf16[1024,256]{1,0:T(8,128)(2,1)S(1)} collective-permute-done((bf16[1024,256]{1,0:T(8,128)(2,1)}, bf16[1024,256]{1,0:T(8,128)(2,1)S(1)}, u32[]{:S(2)}, u32[]{:S(2)}) %collective-permute-start.19) | collective-permute-done | bytes 524320 | tf_op jit(solution)/shard_map/ppermute | solution.py:345
  157.0 10.3 %all-to-all-start.4 = ((bf16[128,2,8,256]{3,2,1,0:T(8,128)(2,1)}), bf16[128,2,8,256]{3,2,1,0:T(8,128)(2,1)}, u32[]{:S(2)}, u32[]{:S(2)}) async-start(bf16[128,2,8,256]{3,2,1,0:T(8,128)(2,1)} %pad_maximum_fusion), calls=%async_computation.5 | async-start | bytes 2097152 | tf_op jit(solution)/shard_map/all_to_all | solution.py:418
  167.3 3.4 %copy-done.2 = bf16[1024,4096]{1,0:T(8,128)(2,1)S(1)} copy-done((bf16[1024,4096]{1,0:T(8,128)(2,1)S(1)}, bf16[1024,4096]{1,0:T(8,128)(2,1)}, u32[]{:S(2)}) %copy-start.2) | copy-done | bytes 8388632
  174.7 6.1 %output_terms.1 = (bf16[2,256,1024]{2,1,0:T(8,128)(2,1)}, f32[2,256,1024]{2,1,0:T(8,128)S(1)}) custom-call(s32[5]{0:T(128)S(1)} %stack.35.refs_0_.pos, bf16[256,1024]{1,0:T(8,128)(2,1)S(1)} %copy-done.16, bf16[256,1024]{1,0:T(8,128)(2,1)S(1)} %copy-done.13, bf16[256,1024]{1,0:T(8,128)(2,1)S(1)} %copy-done.11, bf16[128,1024]{1,0:T(8,128)(2,1)S(1)} %copy-done.18, ...), custom_call_target="tpu_custom_call" | custom-call | flops 2147483648 | bytes 8388608 | tf_op jit(solution)/shard_map/output_terms/pallas_call | solution.py:54
  186.7 4.4 %collective-permute-done.21.refs_4_ = bf16[512,256]{1,0:T(8,128)(2,1)S(1)} collective-permute-done((bf16[512,256]{1,0:T(8,128)(2,1)S(1)}, bf16[512,256]{1,0:T(8,128)(2,1)S(1)}, u32[]{:S(2)}, u32[]{:S(2)}) %collective-permute-start.21) | collective-permute-done | bytes 262176 | tf_op jit(solution)/shard_map/ppermute | solution.py:345
  191.0 5.3 %query_weight_terms.1 = bf16[1024,1024]{1,0:T(8,128)(2,1)} custom-call(s32[5]{0:T(128)S(1)} %stack.35.refs_0_.pos, bf16[1024,1024]{1,0:T(8,128)(2,1)S(1)} %group_states.1.refs_0_, bf16[1024,256]{1,0:T(8,128)(2,1)} %get-tuple-element.48.refs_1_, bf16[1024,256]{1,0:T(8,128)(2,1)S(1)} %copy-done.20, bf16[1024,256]{1,0:T(8,128)(2,1)S(1)} %copy-done.22, ...), custom_call_target="tpu_custom_call" | custom-call | flops 2147483648 | bytes 6291456 | tf_op jit(solution)/shard_map/query_weight_terms/pallas_call | solution.py:54
  196.3 4.7 %all-to-all-start.2 = ((bf16[8,128,1024]{2,1,0:T(8,128)(2,1)}), bf16[8,128,1024]{2,1,0:T(8,128)(2,1)}, u32[]{:S(2)}, u32[]{:S(2)}) async-start(bf16[8,128,1024]{2,1,0:T(8,128)(2,1)} %bitcast.14), calls=%async_computation.2 | async-start | bytes 4194304 | tf_op jit(solution)/shard_map/all_to_all | solution.py:407
  211.3 28.3 %collective-permute-done.12 = bf16[256,1024]{1,0:T(8,128)(2,1)} collective-permute-done((bf16[256,1024]{1,0:T(8,128)(2,1)S(1)}, bf16[256,1024]{1,0:T(8,128)(2,1)}, u32[]{:S(2)}, u32[]{:S(2)}) %collective-permute-start.12) | collective-permute-done | bytes 524320 | tf_op jit(solution)/shard_map/ppermute | solution.py:348
  (183 shorter events, 93.9 us)
Async XLA Ops:
  7.3 10.2 %collective-permute-start.2 = (bf16[256,1024]{1,0:T(8,128)(2,1)}, bf16[256,1024]{1,0:T(8,128)(2,1)S(1)}, u32[]{:S(2)}, u32[]{:S(2)}) collective-permute-start(bf16[256,1024]{1,0:T(8,128)(2,1)} %refs_1_.7), channel_id=1, source_target_pairs={{0,32},{32,0},{1,33},{33,1},{2,34},{34,2},{3,35},{35,3},{4,36},{36... | collective-permute-start | bytes 1572872 | tf_op jit(solution)/shard_map/ppermute | solution.py:348
  7.8 15.6 %collective-permute-start.1 = (bf16[256,1024]{1,0:T(8,128)(2,1)}, bf16[256,1024]{1,0:T(8,128)(2,1)S(1)}, u32[]{:S(2)}, u32[]{:S(2)}) collective-permute-start(bf16[256,1024]{1,0:T(8,128)(2,1)} %refs_1_.6), channel_id=1, source_target_pairs={{0,64},{64,0},{1,65},{65,1},{2,66},{66,2},{3,67},{67,3},{4,68},{68... | collective-permute-start | bytes 1572872 | tf_op jit(solution)/shard_map/ppermute | solution.py:348
  23.4 14.8 %collective-permute-start.14 = (bf16[256,1024]{1,0:T(8,128)(2,1)S(1)}, bf16[256,1024]{1,0:T(8,128)(2,1)}, u32[]{:S(2)}, u32[]{:S(2)}) collective-permute-start(bf16[256,1024]{1,0:T(8,128)(2,1)S(1)} %copy-done.5), channel_id=1, source_target_pairs={{0,64},{64,0},{1,65},{65,1},{2,66},{66,2},{3,67},{67,3},{4,68},{68... | collective-permute-start | bytes 1572872 | tf_op jit(solution)/shard_map/ppermute | solution.py:348
  27.6 28.5 %all-to-all-start = ((bf16[128,2,8,256]{3,2,1,0:T(8,128)(2,1)}), bf16[128,2,8,256]{3,2,1,0:T(8,128)(2,1)}, u32[]{:S(2)}, u32[]{:S(2)}) async-start(bf16[128,2,8,256]{3,2,1,0:T(8,128)(2,1)} %bitcast.51), calls=%async_computation | async-start | bytes 2097152 | tf_op jit(solution)/shard_map/all_to_all | solution.py:370
  38.2 22.5 %collective-permute-start.3 = (bf16[256,1024]{1,0:T(8,128)(2,1)S(1)}, bf16[256,1024]{1,0:T(8,128)(2,1)}, u32[]{:S(2)}, u32[]{:S(2)}) collective-permute-start(bf16[256,1024]{1,0:T(8,128)(2,1)S(1)} %collective-permute-done.1.refs_3_), channel_id=1, source_target_pairs={{0,32},{32,0},{1,33},{33,1},{2,34},{34,2},{3,35},{35,3},{4,36},{36... | collective-permute-start | bytes 1572872 | tf_op jit(solution)/shard_map/ppermute | solution.py:348
  56.1 21.0 %all-to-all-start.3 = ((bf16[4,256,512]{2,1,0:T(8,128)(2,1)}), bf16[4,256,512]{2,1,0:T(8,128)(2,1)}, u32[]{:S(2)}, u32[]{:S(2)}) async-start(bf16[4,256,512]{2,1,0:T(8,128)(2,1)} %copy-done.14), calls=%async_computation.3 | async-start | bytes 2097152 | tf_op jit(solution)/shard_map/all_to_all | solution.py:376
  60.4 148.5 %reduce-scatter.2.cloned.1.call-start = ((), (), s32[]{:S(2)}) async-start(), calls=%async_computation.6 | async-start | bytes 2621440 | tf_op jit(solution)/shard_map/reduce_scatter | solution.py:412
  68.5 11.1 %collective-permute-start.4 = (bf16[256,256]{1,0:T(8,128)(2,1)S(1)}, bf16[256,256]{1,0:T(8,128)(2,1)S(1)}, u32[]{:S(2)}, u32[]{:S(2)}) collective-permute-start(bf16[256,256]{1,0:T(8,128)(2,1)S(1)} %get-tuple-element.31), channel_id=1, source_target_pairs={{0,8},{8,16},{16,24},{24,0},{1,9},{9,17},{17,25},{25,1},{2,10},{10... | collective-permute-start | bytes 393224 | tf_op jit(solution)/shard_map/ppermute | solution.py:345
  70.4 10.6 %collective-permute-start.5 = (bf16[256,256]{1,0:T(8,128)(2,1)S(1)}, bf16[256,256]{1,0:T(8,128)(2,1)S(1)}, u32[]{:S(2)}, u32[]{:S(2)}) collective-permute-start(bf16[256,256]{1,0:T(8,128)(2,1)S(1)} %get-tuple-element.32), channel_id=1, source_target_pairs={{0,16},{8,24},{16,0},{24,8},{1,17},{9,25},{17,1},{25,9},{2,18},{10... | collective-permute-start | bytes 393224 | tf_op jit(solution)/shard_map/ppermute | solution.py:345
  77.1 27.5 %collective-permute-start.23 = (bf16[1024,512]{1,0:T(8,128)(2,1)}, bf16[1024,512]{1,0:T(8,128)(2,1)S(1)}, u32[]{:S(2)}, u32[]{:S(2)}) collective-permute-start(bf16[1024,512]{1,0:T(8,128)(2,1)} %bitcast.15.refs_1_), channel_id=1, source_target_pairs={{0,32},{32,0},{1,33},{33,1},{2,34},{34,2},{3,35},{35,3},{4,36},{36... | collective-permute-start | bytes 3145736 | tf_op jit(solution)/shard_map/ppermute | solution.py:348
  88.8 12.6 %collective-permute-start.8 = (bf16[256,1024]{1,0:T(8,128)(2,1)S(1)}, bf16[256,1024]{1,0:T(8,128)(2,1)S(1)}, u32[]{:S(2)}, u32[]{:S(2)}) collective-permute-start(bf16[256,1024]{1,0:T(8,128)(2,1)S(1)} %get-tuple-element.35.refs_0_), channel_id=1, source_target_pairs={{0,24},{8,0},{16,8},{24,16},{1,25},{9,1},{17,9},{25,17},{2,26},{10... | collective-permute-start | bytes 1572872 | tf_op jit(solution)/shard_map/ppermute | solution.py:345
  90.0 14.5 %collective-permute-start.7 = (bf16[256,1024]{1,0:T(8,128)(2,1)S(1)}, bf16[256,1024]{1,0:T(8,128)(2,1)S(1)}, u32[]{:S(2)}, u32[]{:S(2)}) collective-permute-start(bf16[256,1024]{1,0:T(8,128)(2,1)S(1)} %get-tuple-element.35.refs_0_), channel_id=1, source_target_pairs={{0,8},{8,16},{16,24},{24,0},{1,9},{9,17},{17,25},{25,1},{2,10},{10... | collective-permute-start | bytes 1572872 | tf_op jit(solution)/shard_map/ppermute | solution.py:345
  119.5 8.8 %collective-permute-start.18 = (bf16[256,256]{1,0:T(8,128)(2,1)S(1)}, bf16[256,256]{1,0:T(8,128)(2,1)S(1)}, u32[]{:S(2)}, u32[]{:S(2)}) collective-permute-start(bf16[256,256]{1,0:T(8,128)(2,1)S(1)} %copy-done.24), channel_id=1, source_target_pairs={{0,24},{8,0},{16,8},{24,16},{1,25},{9,1},{17,9},{25,17},{2,26},{10... | collective-permute-start | bytes 393224 | tf_op jit(solution)/shard_map/ppermute | solution.py:345
  121.2 27.4 %all-to-all-start.1 = ((bf16[4,256,512]{2,1,0:T(8,128)(2,1)}), bf16[4,256,512]{2,1,0:T(8,128)(2,1)S(1)}, u32[]{:S(2)}, u32[]{:S(2)}) async-start(bf16[4,256,512]{2,1,0:T(8,128)(2,1)} %get-tuple-element.38), calls=%async_computation.1 | async-start | bytes 2097152 | tf_op jit(solution)/shard_map/all_to_all | solution.py:376
  145.4 10.6 %collective-permute-start.19 = (bf16[1024,256]{1,0:T(8,128)(2,1)}, bf16[1024,256]{1,0:T(8,128)(2,1)S(1)}, u32[]{:S(2)}, u32[]{:S(2)}) collective-permute-start(bf16[1024,256]{1,0:T(8,128)(2,1)} %get-tuple-element.48.refs_1_), channel_id=1, source_target_pairs={{0,8},{8,16},{16,24},{24,0},{1,9},{9,17},{17,25},{25,1},{2,10},{10... | collective-permute-start | bytes 1572872 | tf_op jit(solution)/shard_map/ppermute | solution.py:345
  145.8 10.2 %collective-permute-start.20 = (bf16[1024,256]{1,0:T(8,128)(2,1)}, bf16[1024,256]{1,0:T(8,128)(2,1)S(1)}, u32[]{:S(2)}, u32[]{:S(2)}) collective-permute-start(bf16[1024,256]{1,0:T(8,128)(2,1)} %get-tuple-element.48.refs_1_), channel_id=1, source_target_pairs={{0,24},{8,0},{16,8},{24,16},{1,25},{9,1},{17,9},{25,17},{2,26},{10... | collective-permute-start | bytes 1572872 | tf_op jit(solution)/shard_map/ppermute | solution.py:345
  148.6 35.6 %collective-permute-start.13 = (bf16[1024,512]{1,0:T(8,128)(2,1)S(1)}, bf16[1024,512]{1,0:T(8,128)(2,1)}, u32[]{:S(2)}, u32[]{:S(2)}) collective-permute-start(bf16[1024,512]{1,0:T(8,128)(2,1)S(1)} %bitcast.46), channel_id=1, source_target_pairs={{0,32},{32,0},{1,33},{33,1},{2,34},{34,2},{3,35},{35,3},{4,36},{36... | collective-permute-start | bytes 3145736 | tf_op jit(solution)/shard_map/ppermute | solution.py:348
  157.0 39.3 %all-to-all-start.4 = ((bf16[128,2,8,256]{3,2,1,0:T(8,128)(2,1)}), bf16[128,2,8,256]{3,2,1,0:T(8,128)(2,1)}, u32[]{:S(2)}, u32[]{:S(2)}) async-start(bf16[128,2,8,256]{3,2,1,0:T(8,128)(2,1)} %pad_maximum_fusion), calls=%async_computation.5 | async-start | bytes 2097152 | tf_op jit(solution)/shard_map/all_to_all | solution.py:418
  180.8 20.2 %collective-permute-start.11 = (bf16[2,256,1024]{2,1,0:T(8,128)(2,1)}, bf16[2,256,1024]{2,1,0:T(8,128)(2,1)}, u32[]{:S(2)}, u32[]{:S(2)}) collective-permute-start(bf16[2,256,1024]{2,1,0:T(8,128)(2,1)} %get-tuple-element.37), channel_id=1, source_target_pairs={{0,32},{32,0},{1,33},{33,1},{2,34},{34,2},{3,35},{35,3},{4,36},{36... | collective-permute-start | bytes 3145736 | tf_op jit(solution)/shard_map/ppermute | solution.py:348
  180.8 10.2 %collective-permute-start.21 = (bf16[512,256]{1,0:T(8,128)(2,1)S(1)}, bf16[512,256]{1,0:T(8,128)(2,1)S(1)}, u32[]{:S(2)}, u32[]{:S(2)}) collective-permute-start(bf16[512,256]{1,0:T(8,128)(2,1)S(1)} %slice.49), channel_id=1, source_target_pairs={{0,8},{8,16},{16,24},{24,0},{1,9},{9,17},{17,25},{25,1},{2,10},{10... | collective-permute-start | bytes 786440 | tf_op jit(solution)/shard_map/ppermute | solution.py:345
  181.9 9.1 %collective-permute-start.22 = (bf16[512,256]{1,0:T(8,128)(2,1)S(1)}, bf16[512,256]{1,0:T(8,128)(2,1)S(1)}, u32[]{:S(2)}, u32[]{:S(2)}) collective-permute-start(bf16[512,256]{1,0:T(8,128)(2,1)S(1)} %slice.50), channel_id=1, source_target_pairs={{0,24},{8,0},{16,8},{24,16},{1,25},{9,1},{17,9},{25,17},{2,26},{10... | collective-permute-start | bytes 786440 | tf_op jit(solution)/shard_map/ppermute | solution.py:345
  196.3 45.3 %all-to-all-start.2 = ((bf16[8,128,1024]{2,1,0:T(8,128)(2,1)}), bf16[8,128,1024]{2,1,0:T(8,128)(2,1)}, u32[]{:S(2)}, u32[]{:S(2)}) async-start(bf16[8,128,1024]{2,1,0:T(8,128)(2,1)} %bitcast.14), calls=%async_computation.2 | async-start | bytes 4194304 | tf_op jit(solution)/shard_map/all_to_all | solution.py:407
  204.0 35.7 %collective-permute-start.12 = (bf16[256,1024]{1,0:T(8,128)(2,1)S(1)}, bf16[256,1024]{1,0:T(8,128)(2,1)}, u32[]{:S(2)}, u32[]{:S(2)}) collective-permute-start(bf16[256,1024]{1,0:T(8,128)(2,1)S(1)} %fusion.2), channel_id=1, source_target_pairs={{0,64},{64,0},{1,65},{65,1},{2,66},{66,2},{3,67},{67,3},{4,68},{68... | collective-permute-start | bytes 1572872 | tf_op jit(solution)/shard_map/ppermute | solution.py:348
  209.9 34.6 %collective-permute-start.24 = (bf16[1024,128]{1,0:T(8,128)(2,1)S(1)}, bf16[1024,128]{1,0:T(8,128)(2,1)}, u32[]{:S(2)}, u32[]{:S(2)}) collective-permute-start(bf16[1024,128]{1,0:T(8,128)(2,1)S(1)} %dynamic-slice_bitcast_fusion), channel_id=1, source_target_pairs={{0,1},{1,0},{2,3},{3,2},{4,5},{5,4},{6,7},{7,6},{8,9},{9,8},{10,11... | collective-permute-start | bytes 786440 | tf_op jit(solution)/shard_map/ppermute | solution.py:348
  (63 other events, 349.7 us)
Sparse Core Ops, SparseCore 0:
  117.2 28.1 reduce-scatter.1

commit v5 on v4

--- a/solution.py
+++ b/solution.py
@@ -48,9 +48,10 @@
 
 def call(kernel, name, grid, in_specs, out_specs, out_shape, scratch, flops, moved, pos, *args):
     outs = zip(jax.tree.leaves(out_specs), jax.tree.leaves(out_shape))
-    blocks = [(s.block_shape, a.dtype) for s, a in [*zip(in_specs, args), *outs]]
+    blocks = [(s.block_shape, a.dtype) for s, a in [*zip(in_specs, args), *outs] if s is not HBM]
     room = sum(2 * math.prod(shape) * dtype.itemsize for shape, dtype in blocks)
-    room += sum(math.prod(s.shape) * jnp.dtype(s.dtype).itemsize for s in scratch)
+    held = [s for s in scratch if s.memory_space == pltpu.VMEM]
+    room += sum(math.prod(s.shape) * jnp.dtype(s.dtype).itemsize for s in held)
     return pl.pallas_call(
         kernel,
         grid_spec=pltpu.PrefetchScalarGridSpec(
@@ -67,81 +68,128 @@
     )(pos, *args)
 
 
-def project_kernel(transposed, final, pos, *refs):
-    blocks, w_ref, refs = refs[:4], refs[4], refs[5:]
-    before, refs = (refs[0], refs[1:]) if final else (None, refs)
-    step = pl.program_id(0)
+def weight_copies(pos, w_ref, held, sems, blocks, by_columns):
+    copies = []
+    for i, block in enumerate(blocks):
+        part = pl.ds(pl.multiple_of(head_block(block, pos) * BLOCK, BLOCK), BLOCK)
+        source = w_ref.at[:, part] if by_columns else w_ref.at[part, :]
+        copies.append(pltpu.make_async_copy(source, held.at[i], sems.at[i]))
+        copies[i].start()
+    return copies
+
+
+def near_kernel(transposed, pos, x0, x1, w_ref, out, weights, sems):
     contract = ((1,), (1,)) if transposed else ((1,), (0,))
-    total = refs[5] if final else refs[0]
-
-    @pl.when(step == 0)
-    def _():
-        product = dot(blocks[2 if final else 0][...], w_ref[...], contract)
-        total[...] = product + before[...] if final else product
-
-    @pl.when(step == 1)
-    def _():
-        product = total[...] + dot(blocks[3 if final else 1][...], w_ref[...], contract)
-        total[...] = product
-        if final:
-            rows, parts, held = refs[:4], refs[4], refs[6]
-            half = pl.multiple_of(pos[CORE] * (BLOCK // 2), BLOCK // 2)
-            for d in range(4):
-                start = pl.multiple_of(shifted(pos[Z], d) * PIECE, PIECE)
-                rows[d][...] = total[:, pl.ds(start, PIECE)].astype(BF16)
-                held[...] = blocks[d][...]
-                parts[head_block(d, pos)] = held[:, pl.ds(half, BLOCK // 2)]
-
-
-def project(name, pos, blocks, weight, transposed, before=None):
-    final = before is not None
-    first = 2 if final else 0
-
-    def where(i, pos):
-        block = head_block(i + first, pos)
-        return (0, block) if transposed else (block, 0)
-
-    return call(
-        lambda *refs: project_kernel(transposed, final, *refs),
+    copies = weight_copies(pos, w_ref, weights, sems, (0, 1), transposed)
+    for i, x in enumerate((x0, x1)):
+        copies[i].wait()
+        product = dot(x[...], weights[i], contract)
+        out[...] = product if i == 0 else out[...] + product
+
+
+def far_kernel(transposed, pos, x0, x1, x2, x3, before, w_ref, *refs):
+    rows, parts, (total, weights, sems) = refs[:4], refs[4], refs[5:]
+    contract = ((1,), (1,)) if transposed else ((1,), (0,))
+    copies = weight_copies(pos, w_ref, weights, sems, (2, 3), transposed)
+    half = pl.multiple_of(pos[CORE] * (BLOCK // 2), BLOCK // 2)
+    for i, x in enumerate((x0, x1, x2, x3)):
+        parts[head_block(i, pos)] = x[:, pl.ds(half, BLOCK // 2)]
+    for i, (x, known) in enumerate(((x2, before), (x3, total))):
+        copies[i].wait()
+        total[...] = known[...] + dot(x[...], weights[i], contract)
+    for d in range(4):
+        start = pl.multiple_of(shifted(pos[Z], d) * PIECE, PIECE)
+        rows[d][...] = total[:, pl.ds(start, PIECE)].astype(BF16)
+
+
+HBM = pl.BlockSpec(memory_space=pltpu.HBM)
+
+
+def near_project(name, pos, blocks, weight, transposed):
+    return call(
+        lambda *refs: near_kernel(transposed, *refs),
         name,
-        (2,),
-        [whole((TOK, BLOCK))] * 4
-        + [pl.BlockSpec((BLOCK, BLOCK), where)]
-        + ([whole((TOK, BLOCK))] if final else []),
-        [whole((TOK, PIECE))] * 4 + [whole((4, TOK, BLOCK // 2))] if final else whole((TOK, BLOCK)),
-        [struct((TOK, PIECE))] * 4 + [struct((4, TOK, BLOCK // 2))] if final else struct((TOK, BLOCK), F32),
-        [pltpu.VMEM((TOK, BLOCK), F32), pltpu.VMEM((TOK, BLOCK), BF16)] if final else [],
+        (1,),
+        [whole((TOK, BLOCK))] * 2 + [HBM],
+        whole((TOK, BLOCK)),
+        struct((TOK, BLOCK), F32),
+        [pltpu.VMEM((2, BLOCK, BLOCK), BF16), pltpu.SemaphoreType.DMA((2,))],
         4 * TOK * BLOCK * BLOCK,
         4 * BLOCK * BLOCK,
         pos,
-        *(blocks if final else blocks[:2] + blocks[:2]),
+        *blocks,
         weight,
-        *([before] if final else []),
-    )
-
-
-def assemble_kernel(transposed, pos, mine, other, out):
+    )
+
+
+def far_project(name, pos, blocks, weight, transposed, before):
+    outs = call(
+        lambda *refs: far_kernel(transposed, *refs),
+        name,
+        (1,),
+        [whole((TOK, BLOCK))] * 5 + [HBM],
+        [whole((TOK, PIECE))] * 4 + [whole((4, TOK, BLOCK // 2))],
+        [struct((TOK, PIECE))] * 4 + [struct((4, TOK, BLOCK // 2))],
+        [
+            pltpu.VMEM((TOK, BLOCK), F32),
+            pltpu.VMEM((2, BLOCK, BLOCK), BF16),
+            pltpu.SemaphoreType.DMA((2,)),
+        ],
+        4 * TOK * BLOCK * BLOCK,
+        4 * BLOCK * BLOCK,
+        pos,
+        *blocks,
+        before,
+        weight,
+    )
+    return outs[:4], outs[4]
+
+
+def assemble_kernel(pos, mine, other, out):
     for side, ref in enumerate((mine, other)):
         half = pl.multiple_of(lax.rem(pos[CORE] + side, 2) * (BLOCK // 2), BLOCK // 2)
-        if transposed:
-            out[pl.ds(half, BLOCK // 2), :] = ref[...].T
-        else:
-            out[:, pl.ds(half, BLOCK // 2)] = ref[...]
-
-
-def assemble(name, pos, mine, other, transposed):
-    return call(
-        lambda *refs: assemble_kernel(transposed, *refs),
+        out[:, pl.ds(half, BLOCK // 2)] = ref[...]
+
+
+def assemble(name, pos, mine, other):
+    return call(
+        assemble_kernel,
         name,
         (1,),
         [whole((GROUP, BLOCK // 2))] * 2,
+        whole((GROUP, BLOCK)),
+        struct((GROUP, BLOCK)),
+        [],
+        0,
+        4 * BLOCK * GROUP,
+        pos,
+        mine,
+        other,
+    )
+
+
+def assemble_turned_kernel(pos, m0, m1, m2, m3, other, out):
+    for d, mine in enumerate((m0, m1, m2, m3)):
+        token = pl.multiple_of(shifted(pos[Z], -d) * TOK, TOK)
+        for side in range(2):
+            half = pl.multiple_of(lax.rem(pos[CORE] + side, 2) * (BLOCK // 2), BLOCK // 2)
+            part = other[d] if side else mine[...]
+            out[pl.ds(half, BLOCK // 2), pl.ds(token, TOK)] = part.T
+
+
+def assemble_turned(name, pos, mine, other):
+    return call(
+        assemble_turned_kernel,
+        name,
+        (1,),
+        [whole((TOK, BLOCK // 2))] * 4 + [whole((4, TOK, BLOCK // 2))],
         whole((BLOCK, GROUP)),
         struct((BLOCK, GROUP)),
         [],
         0,
         4 * BLOCK * GROUP,
         pos,
-        mine,
+        *mine,
         other,
     )
 
@@ -282,36 +330,30 @@
 
 
 def output_kernel(pos, *refs):
-    rows, w_ref, give, keep = refs[:5], refs[5], refs[6], refs[7]
-    step = pl.program_id(0)
-    product = jnp.zeros((TOK, BLOCK), F32)
-    for ref, (e, part) in zip(rows, GATHERED):
-        size = ref.shape[0]
-        row = pl.multiple_of(shifted(pos[Z], -e) * PIECE + part * size, size)
-        product = product + dot(ref[...], w_ref[pl.ds(row, size), :], ((0,), (0,)))
-
-    @pl.when(step < 2)
-    def _():
-        give[0] = product.astype(BF16)
-
-    @pl.when(step >= 2)
-    def _():
-        keep[0] = product
+    rows, w_ref, give, keep, weights, sems = refs[:5], *refs[5:]
+    copies = weight_copies(pos, w_ref, weights, sems, (1, 3, 0, 2), True)
+    for n in range(4):
+        copies[n].wait()
+        product = jnp.zeros((TOK, BLOCK), F32)
+        for ref, (e, part) in zip(rows, GATHERED):
+            size = ref.shape[0]
+            row = pl.multiple_of(shifted(pos[Z], -e) * PIECE + part * size, size)
+            product = product + dot(ref[...], weights[n, pl.ds(row, size), :], ((0,), (0,)))
+        if n < 2:
+            give[n] = product.astype(BF16)
+        else:
+            keep[n - 2] = product
 
 
 def output_terms(pos, every_out, weight):
     return call(
         output_kernel,
         "output_terms",
-        (4,),
-        [pl.BlockSpec((a.shape[0], TOK), lambda n, pos: (0, pos[Z])) for a in every_out]
-        + [pl.BlockSpec((BLOCK, BLOCK), lambda n, pos: (0, head_block((n % 2) * 2 + 1 - n // 2, pos)))],
-        [
-            pl.BlockSpec((1, TOK, BLOCK), lambda n, pos: (jnp.minimum(n, 1), 0, 0)),
-            pl.BlockSpec((1, TOK, BLOCK), lambda n, pos: (jnp.maximum(n - 2, 0), 0, 0)),
-        ],
+        (1,),
+        [pl.BlockSpec((a.shape[0], TOK), lambda n, pos: (0, pos[Z])) for a in every_out] + [HBM],
+        [whole((2, TOK, BLOCK))] * 2,
         [struct((2, TOK, BLOCK)), struct((2, TOK, BLOCK), F32)],
-        [],
+        [pltpu.VMEM((4, BLOCK, BLOCK), BF16), pltpu.SemaphoreType.DMA((4,))],
         2 * TOK * 4 * BLOCK * BLOCK,
         2 * 4 * BLOCK * BLOCK,
         pos,
@@ -352,12 +394,19 @@
 
     def near(name, local, weight, transposed):
         blocks = (local, swap(local, "core"))
-        return blocks, project(name, pos, blocks, weight, transposed)
+        return blocks, near_project(name, pos, blocks, weight, transposed)
 
     def far(name, blocks, over_x, weight, transposed, first):
         blocks = blocks + (over_x, swap(over_x, "core"))
-        outs = project(name, pos, blocks, weight, transposed, first)
-        return [to_layer(x, d) for d, x in enumerate(outs[:4])], outs[4]
+        rows, parts = far_project(name, pos, blocks, weight, transposed, first)
+        return [to_layer(x, d) for d, x in enumerate(rows)], parts
+
+    own = jnp.stack([context_keys, context_values]).reshape(2, 8, 16, PIECE).transpose(2, 0, 1, 3)
+    own = jnp.broadcast_to(own[:, None], (16, PLANES, 2, 8, PIECE)).reshape(128, 2, 8, PIECE)
+    context = lax.all_to_all(own, HEADS + SEQ, 0, 0, tiled=True)
+    keys = context[:, 0].reshape(4 * TOK, PIECE)
+    values = context[:, 1].reshape(4 * TOK, PIECE)
+    bias = context_bias(lengths, slot_passage)
 
     states_x = swap(decoder_states, "xh")
     states, first_queries = near("queries_near", decoder_states, query_weight, False)
@@ -365,17 +414,6 @@
     states_x = after(states_x, first_queries, first_grad)
     cotangent_x = swap(after(output_cotangent, states_x), "xh")
 
-    own = jnp.stack([context_keys, context_values]).reshape(2, 8, 16, PIECE).transpose(2, 0, 1, 3)
-    own = jnp.broadcast_to(own[:, None], (16, PLANES, 2, 8, PIECE)).reshape(128, 2, 8, PIECE)
-    context = lax.all_to_all(after(own, first_queries, first_grad), HEADS + SEQ, 0, 0, tiled=True)
-    keys = context[:, 0].reshape(4 * TOK, PIECE)
-    values = context[:, 1].reshape(4 * TOK, PIECE)
-    bias = context_bias(lengths, slot_passage)
-
-    def column_block(name, parts, transposed):
-        mine = lax.all_to_all(parts, "z", 0, 0, tiled=True).reshape(GROUP, BLOCK // 2)
-        return assemble(name, pos, mine, swap(mine, "core"), transposed)
-
     def ring_ends(x):
         return to_layer(x, 1), to_layer(x, 3)
 
@@ -384,45 +422,56 @@
         return x, left, right, to_layer(left[:half], 1), to_layer(right[half:], 3)
 
     queries, state_parts = far("queries", states, states_x, query_weight, False, first_queries)
-    group_states = column_block("group_states", state_parts, True)
-    heads_out, turned_out, weights, share = forward(pos, bias, queries, keys, values)
+    mine = []
+    for d in range(4):
+        part = lax.dynamic_index_in_dim(state_parts, shifted(pos[Z], d), 0, False)
+        mine.append(to_layer(after(part, *queries) if d else part, d))
+    heads_out, turned_out, weights, share = forward(pos, bias, after(queries, *mine[1:]), keys, values)
     left, right = ring_ends(turned_out)
     every_out = ring(turned_out, left, right)
 
     heads_grad, cotangent_parts = far(
-        "heads_grad", cotangent, cotangent_x, output_weight, True, first_grad
-    )
-    group_cotangent = column_block("group_cotangent", cotangent_parts, False)
+        "heads_grad", cotangent, cotangent_x, output_weight, True, after(first_grad, turned_out)
+    )
     query_grad, key_terms, value_terms = backward(
         pos, queries, heads_grad, keys, values, after(heads_out, left, right), weights, share
     )
     left, right = ring_ends(query_grad)
     every_query_grad = ring(query_grad, left, right)
 
-    give, keep = output_terms(pos, every_out, output_weight)
-    pair = keep + swap(give, "core").astype(F32)
-    attended = (pair[0] + swap(pair[1].astype(BF16), "xh").astype(F32)).astype(BF16)
-
-    def plane_sum(terms):
-        return jnp.sum(lax.all_to_all(terms, ("y", "xl"), 0, 0, tiled=True).astype(F32), axis=0)
+    block = lax.all_to_all(after(cotangent_parts, *heads_grad), "z", 0, 0, tiled=True)
+    block = block.reshape(GROUP, BLOCK // 2)
+    group_cotangent = assemble("group_cotangent", pos, block, swap(block, "core"))
+    other = swap(jnp.stack(after(mine, block)), "core")
+    group_states = assemble_turned("group_states", pos, mine, other)
 
     terms = weight_terms(
-        "output_weight_terms", output_grad_kernel, pos, (*every_out, group_cotangent), (PLANES, BLOCK, 128)
+        "output_weight_terms",
+        output_grad_kernel,
+        pos,
+        (*after(every_out, left, right), group_cotangent),
+        (PLANES, BLOCK, 128),
     )
     pair = lax.psum_scatter(terms, "y", scatter_dimension=0, tiled=True)
     xl = lax.axis_index("xl")
     kept, given = (lax.dynamic_index_in_dim(pair, i, 0, False) for i in (xl, 1 - xl))
     output_weight_grad = kept.astype(F32) + swap(given, "xl").astype(F32)
+    every_out = after(every_out, terms)
+
+    give, keep = output_terms(pos, every_out, output_weight)
+    pair = keep + swap(give, "core").astype(F32)
+    attended = (pair[0] + swap(pair[1].astype(BF16), "xh").astype(F32)).astype(BF16)
 
     terms = jnp.stack([key_terms.reshape(128, 8, PIECE), value_terms.reshape(128, 8, PIECE)], 1)
-    moved = lax.all_to_all(after(terms, left, right), HEADS + SEQ, 0, 0, tiled=True)
+    moved = lax.all_to_all(after(terms, left, right, block), HEADS + SEQ, 0, 0, tiled=True)
     owned = jnp.sum(moved.reshape(16, PLANES, 2, 8, PIECE).astype(F32), axis=1)
     owned = owned.transpose(1, 2, 0, 3).reshape(2, 8, 16 * PIECE)
 
     terms = weight_terms(
         "query_weight_terms", query_grad_kernel, pos, (group_states, *every_query_grad), (BLOCK, BLOCK)
     )
-    query_weight_grad = plane_sum(terms.reshape(PLANES, 128, BLOCK))
+    terms = lax.all_to_all(terms.reshape(PLANES, 128, BLOCK), ("y", "xl"), 0, 0, tiled=True)
+    query_weight_grad = jnp.sum(terms.astype(F32), axis=0)
     return attended, query_weight_grad, output_weight_grad, owned[0], owned[1]
 
 

time: 255 us -> 269 us (1.055)
  waiting for transfers between devices: 70.7 us -> 90.8 us
  local copies, waits for them, and re-layouts: 47.6 us -> 41.9 us
  starting transfers between devices: 65.7 us -> 63 us
    ppermute x14 -> x17, waiting for transfers between devices: 32.3 us -> 49.5 us  [to_layer(): lax.ppermute(x, 'z', [(i, (i + d) % 4) for i in range(4)])]
    all_to_all x5 -> x4, starting transfers between devices: 33.1 us -> 25.5 us  [the longest x1 9.71 us: on_device(): context = lax.all_to_all(own, HEADS + SEQ, 0, 0, tiled=True)]
    all_to_all x5 -> x4, waiting for transfers between devices: 5.7 us -> 13.3 us  [the longest x1 13.3 us: on_device(): lax.all_to_all(after(cotangent_parts, *heads_grad), 'z', 0, 0, tiled=True)]
    unnamed x113 -> x125, local copies, waits for them, and re-layouts: 43.3 us -> 36.8 us
    ppermute x14 -> x17, starting transfers between devices: 21 us -> 26.8 us  [to_layer(): lax.ppermute(x, 'z', [(i, (i + d) % 4) for i in range(4)])]
    ppermute x11, waiting for transfers between devices: 32.7 us -> 28.1 us  [swap(): return lax.ppermute(x, axis, SWAP)]
  transfers between devices with their start and end apart: 31 -> 33, of which waited for: 15 -> 14; matrix products, arithmetic and copies ran while one was open for 5% -> 6% of each run, Pallas kernels for 16% -> 13%
where the time goes in v5:
time: 269 us; the launch traced here: 267 us
  waiting for transfers between devices  90.8 us (34%)
  starting transfers between devices  63 us (23%)
  Pallas kernels  44.1 us (16%)
  local copies, waits for them, and re-layouts  41.9 us (16%)
  between operations  14.6 us (5%)
  other arithmetic  12.9 us (5%)
    ppermute x17, waiting for transfers between devices, to_layer(): lax.ppermute(x, 'z', [(i, (i + d) % 4) for i in range(4)])  49.5 us
    pallas_call x11, Pallas kernels, call(): pl.pallas_call(kernel, grid_spec=pltpu.PrefetchScalarGridSpec(num_scalar_...  44.1 us
    unnamed x125, local copies, waits for them, and re-layouts  36.8 us
    ppermute x11, waiting for transfers between devices, swap(): return lax.ppermute(x, axis, SWAP)  28.1 us
    ppermute x17, starting transfers between devices, to_layer(): lax.ppermute(x, 'z', [(i, (i + d) % 4) for i in range(4)])  26.8 us
    all_to_all x1, waiting for transfers between devices, on_device(): lax.all_to_all(after(cotangent_parts, *heads_grad), 'z', 0, 0, tiled=True)  13.3 us
    ppermute x11, starting transfers between devices, swap(): return lax.ppermute(x, axis, SWAP)  10.6 us
    all_to_all x1, starting transfers between devices, on_device(): context = lax.all_to_all(own, HEADS + SEQ, 0, 0, tiled=True)  9.71 us
  transfers between devices with their start and end apart: 33, of which 14 were waited for; matrix products, arithmetic and copies ran while one was open for 6% of the time, Pallas kernels for 13%

profile of v5, /device:TPU:0, one launch (start us, length us, event | category | flops | bytes accessed | tf_op | source)
XLA Modules:
  0.0 267.3 jit_solution(626820024158271687)
XLA Ops:
  12.8 9.7 %all-to-all-start = ((bf16[128,2,8,256]{3,2,1,0:T(8,128)(2,1)}), bf16[128,2,8,256]{3,2,1,0:T(8,128)(2,1)}, u32[]{:S(2)}, u32[]{:S(2)}) async-start(bf16[128,2,8,256]{3,2,1,0:T(8,128)(2,1)} %bitcast.11), calls=%async_computation | async-start | bytes 2097152 | tf_op jit(solution)/shard_map/all_to_all | solution.py:406
  22.7 3.4 %copy-done = bf16[1024,4096]{1,0:T(8,128)(2,1)S(1)} copy-done((bf16[1024,4096]{1,0:T(8,128)(2,1)S(1)}, bf16[1024,4096]{1,0:T(8,128)(2,1)}, u32[]{:S(2)}) %copy-start) | copy-done | bytes 8388632
  40.2 3.6 %queries.1 = (bf16[256,256]{1,0:T(8,128)(2,1)S(1)}, bf16[256,256]{1,0:T(8,128)(2,1)S(1)}, bf16[256,256]{1,0:T(8,128)(2,1)S(1)}, bf16[256,256]{1,0:T(8,128)(2,1)S(1)}, bf16[4,256,512]{2,1,0:T(8,128)(2,1)S(1)}) custom-call(s32[5]{0:T(128)S(1)} %stack.50.refs_0_.pos, bf16[256,1024]{1,0:T(8,128)(2,1)S(1)} %copy-done.5, bf16[256,1024]{1,0:T(8,128)(2,1)S(1)} %copy-done.11, ...), custom_call_target="tpu_custom_call" | custom-call | flops 1073741824 | bytes 4194304 | tf_op jit(solution)/shard_map/queries/pallas_call | solution.py:55
  51.0 4.0 %collective-permute-done.5.refs_2_ = bf16[256,256]{1,0:T(8,128)(2,1)S(1)} collective-permute-done((bf16[256,256]{1,0:T(8,128)(2,1)S(1)}, bf16[256,256]{1,0:T(8,128)(2,1)S(1)}, u32[]{:S(2)}, u32[]{:S(2)}) %collective-permute-start.5) | collective-permute-done | bytes 131104 | tf_op jit(solution)/shard_map/ppermute | solution.py:387
  62.1 3.4 %collective-permute-done.7.m1 = bf16[256,512]{1,0:T(8,128)(2,1)S(1)} collective-permute-done((bf16[256,512]{1,0:T(8,128)(2,1)}, bf16[256,512]{1,0:T(8,128)(2,1)S(1)}, u32[]{:S(2)}, u32[]{:S(2)}) %collective-permute-start.7) | collective-permute-done | bytes 262176 | tf_op jit(solution)/shard_map/ppermute | solution.py:387
  65.5 5.3 %collective-permute-done.8.m2 = bf16[256,512]{1,0:T(8,128)(2,1)S(1)} collective-permute-done((bf16[256,512]{1,0:T(8,128)(2,1)}, bf16[256,512]{1,0:T(8,128)(2,1)S(1)}, u32[]{:S(2)}, u32[]{:S(2)}) %collective-permute-start.8) | collective-permute-done | bytes 262176 | tf_op jit(solution)/shard_map/ppermute | solution.py:387
  70.8 6.5 %attention_forward.1 = (bf16[1024,256]{1,0:T(8,128)(2,1)S(1)}, bf16[256,1024]{1,0:T(8,128)(2,1)}, bf16[2,1024,1024]{2,1,0:T(8,128)(2,1)S(1)}, f32[1024,256]{1,0:T(8,128)S(1)}) custom-call(s32[5]{0:T(128)S(1)} %stack.50.refs_0_.pos, f32[1,1024]{1,0:T(1,128)S(1)} %bitcast.65, bf16[256,256]{1,0:T(8,128)(2,1)S(1)} %get-tuple-element.60.refs_0_, ...), custom_call_target="tpu_custom_call" | custom-call | flops 3221225472 | bytes 6291456 | tf_op jit(solution)/shard_map/attention_forward/pallas_call | solution.py:55
  81.1 3.4 %copy-done.1 = bf16[1024,4096]{1,0:T(8,128)(2,1)S(1)} copy-done((bf16[1024,4096]{1,0:T(8,128)(2,1)S(1)}, bf16[1024,4096]{1,0:T(8,128)(2,1)}, u32[]{:S(2)}) %copy-start.1) | copy-done | bytes 8388632
  84.5 4.5 %heads_grad.1 = (bf16[256,256]{1,0:T(8,128)(2,1)S(1)}, bf16[256,256]{1,0:T(8,128)(2,1)S(1)}, bf16[256,256]{1,0:T(8,128)(2,1)S(1)}, bf16[256,256]{1,0:T(8,128)(2,1)S(1)}, bf16[4,256,512]{2,1,0:T(8,128)(2,1)}) custom-call(s32[5]{0:T(128)S(1)} %stack.50.refs_0_.pos, bf16[256,1024]{1,0:T(8,128)(2,1)S(1)} %copy-done.6, bf16[256,1024]{1,0:T(8,128)(2,1)S(1)} %copy-done.8, ...), custom_call_target="tpu_custom_call" | custom-call | flops 1073741824 | bytes 4194304 | tf_op jit(solution)/shard_map/heads_grad/pallas_call | solution.py:55
  95.9 4.0 %collective-permute-done.17.refs_6_ = bf16[256,256]{1,0:T(8,128)(2,1)S(1)} collective-permute-done((bf16[256,256]{1,0:T(8,128)(2,1)S(1)}, bf16[256,256]{1,0:T(8,128)(2,1)S(1)}, u32[]{:S(2)}, u32[]{:S(2)}) %collective-permute-start.17) | collective-permute-done | bytes 131104 | tf_op jit(solution)/shard_map/ppermute | solution.py:387
  99.9 3.5 %all-to-all-start.1 = ((bf16[4,256,512]{2,1,0:T(8,128)(2,1)}), bf16[4,256,512]{2,1,0:T(8,128)(2,1)S(1)}, u32[]{:S(2)}, u32[]{:S(2)}) async-start(bf16[4,256,512]{2,1,0:T(8,128)(2,1)} %get-tuple-element.82), calls=%async_computation.1 | async-start | bytes 2097152 | tf_op jit(solution)/shard_map/all_to_all | solution.py:442
  106.8 13.3 %all-to-all-done.1 = bf16[4,256,512]{2,1,0:T(8,128)(2,1)S(1)} async-done(((bf16[4,256,512]{2,1,0:T(8,128)(2,1)}), bf16[4,256,512]{2,1,0:T(8,128)(2,1)S(1)}, u32[]{:S(2)}, u32[]{:S(2)}) %all-to-all-start.1) | async-done | bytes 1048608 | tf_op jit(solution)/shard_map/all_to_all | solution.py:442
  120.0 7.9 %collective-permute-done.11.refs_2_ = bf16[256,1024]{1,0:T(8,128)(2,1)S(1)} collective-permute-done((bf16[256,1024]{1,0:T(8,128)(2,1)}, bf16[256,1024]{1,0:T(8,128)(2,1)S(1)}, u32[]{:S(2)}, u32[]{:S(2)}) %collective-permute-start.11) | collective-permute-done | bytes 524320 | tf_op jit(solution)/shard_map/ppermute | solution.py:387
  140.3 5.2 %attention_backward.1 = (bf16[1024,256]{1,0:T(8,128)(2,1)S(1)}, bf16[1024,256]{1,0:T(8,128)(2,1)S(1)}, bf16[1024,256]{1,0:T(8,128)(2,1)S(1)}) custom-call(s32[5]{0:T(128)S(1)} %stack.50.refs_0_.pos, bf16[256,256]{1,0:T(8,128)(2,1)S(1)} %get-tuple-element.60.refs_0_, bf16[256,256]{1,0:T(8,128)(2,1)S(1)} %collective-permute-done.4.refs_1_, ...), custom_call_target="tpu_custom_call" | custom-call | flops 4294967296 | bytes 7340032 | tf_op jit(solution)/shard_map/attention_backward/pallas_call | solution.py:55
  150.2 13.1 %collective-permute-done.13.refs_4_ = bf16[128,1024]{1,0:T(8,128)(2,1)S(1)} collective-permute-done((bf16[128,1024]{1,0:T(8,128)(2,1)S(1)}, bf16[128,1024]{1,0:T(8,128)(2,1)S(1)}, u32[]{:S(2)}, u32[]{:S(2)}) %collective-permute-start.13) | collective-permute-done | bytes 262176 | tf_op jit(solution)/shard_map/ppermute | solution.py:387
  166.3 5.2 %output_weight_terms.1 = bf16[8,1024,128]{2,1,0:T(8,128)(2,1)} custom-call(s32[5]{0:T(128)S(1)} %stack.50.refs_0_.pos, bf16[256,1024]{1,0:T(8,128)(2,1)} %get-tuple-element.83.refs_0_, bf16[256,1024]{1,0:T(8,128)(2,1)S(1)} %collective-permute-done.10.refs_1_, bf16[256,1024]{1,0:T(8,128)(2,1)S(1)} %collective-permute-done.11.refs_2_, ...), custom_call_target="tpu_custom_call" | custom-call | flops 2147483648 | bytes 6291456 | tf_op jit(solution)/shard_map/output_weight_terms/pallas_call | solution.py:55
  174.0 7.0 %all-to-all-start.3 = ((bf16[128,2,8,256]{3,2,1,0:T(8,128)(2,1)}), bf16[128,2,8,256]{3,2,1,0:T(8,128)(2,1)}, u32[]{:S(2)}, u32[]{:S(2)}) async-start(bf16[128,2,8,256]{3,2,1,0:T(8,128)(2,1)} %pad_maximum_fusion.1), calls=%async_computation.4 | async-start | bytes 2097152 | tf_op jit(solution)/shard_map/all_to_all | solution.py:466
  181.1 3.4 %copy-done.2 = bf16[1024,4096]{1,0:T(8,128)(2,1)S(1)} copy-done((bf16[1024,4096]{1,0:T(8,128)(2,1)S(1)}, bf16[1024,4096]{1,0:T(8,128)(2,1)}, u32[]{:S(2)}) %copy-start.2) | copy-done | bytes 8388632
  186.4 6.8 %output_terms.1 = (bf16[2,256,1024]{2,1,0:T(8,128)(2,1)}, f32[2,256,1024]{2,1,0:T(8,128)S(1)}) custom-call(s32[5]{0:T(128)S(1)} %stack.50.refs_0_.pos, bf16[256,1024]{1,0:T(8,128)(2,1)} %get-tuple-element.83.refs_0_, bf16[256,1024]{1,0:T(8,128)(2,1)S(1)} %copy-done.15, bf16[256,1024]{1,0:T(8,128)(2,1)S(1)} %copy-done.13, bf16[128,1024]{1,0:T(8,128)(2,1)S(1)} %copy-done.33, ...), custom_call_target="tpu_custom_call" | custom-call | flops 2147483648 | bytes 8388608 | tf_op jit(solution)/shard_map/output_terms/pallas_call | solution.py:55
  198.9 3.7 %collective-permute-done.26.refs_5_ = bf16[512,256]{1,0:T(8,128)(2,1)S(1)} collective-permute-done((bf16[512,256]{1,0:T(8,128)(2,1)S(1)}, bf16[512,256]{1,0:T(8,128)(2,1)S(1)}, u32[]{:S(2)}, u32[]{:S(2)}) %collective-permute-start.26) | collective-permute-done | bytes 262176 | tf_op jit(solution)/shard_map/ppermute | solution.py:387
  202.6 3.4 %collective-permute-done.25.refs_4_ = bf16[512,256]{1,0:T(8,128)(2,1)S(1)} collective-permute-done((bf16[512,256]{1,0:T(8,128)(2,1)S(1)}, bf16[512,256]{1,0:T(8,128)(2,1)S(1)}, u32[]{:S(2)}, u32[]{:S(2)}) %collective-permute-start.25) | collective-permute-done | bytes 262176 | tf_op jit(solution)/shard_map/ppermute | solution.py:387
  205.9 4.2 %query_weight_terms.1 = bf16[1024,1024]{1,0:T(8,128)(2,1)} custom-call(s32[5]{0:T(128)S(1)} %stack.50.refs_0_.pos, bf16[1024,1024]{1,0:T(8,128)(2,1)S(1)} %group_states.1.refs_0_, bf16[1024,256]{1,0:T(8,128)(2,1)S(1)} %copy-done.39, bf16[1024,256]{1,0:T(8,128)(2,1)S(1)} %copy-done.37, bf16[1024,256]{1,0:T(8,128)(2,1)S(1)} %copy-done.35, ...), custom_call_target="tpu_custom_call" | custom-call | flops 2147483648 | bytes 6291456 | tf_op jit(solution)/shard_map/query_weight_terms/pallas_call | solution.py:55
  210.2 5.3 %all-to-all-start.2 = ((bf16[8,128,1024]{2,1,0:T(8,128)(2,1)}), bf16[8,128,1024]{2,1,0:T(8,128)(2,1)}, u32[]{:S(2)}, u32[]{:S(2)}) async-start(bf16[8,128,1024]{2,1,0:T(8,128)(2,1)} %bitcast.22), calls=%async_computation.2 | async-start | bytes 4194304 | tf_op jit(solution)/shard_map/all_to_all | solution.py:473
  225.8 28.0 %collective-permute-done.23 = bf16[256,1024]{1,0:T(8,128)(2,1)} collective-permute-done((bf16[256,1024]{1,0:T(8,128)(2,1)S(1)}, bf16[256,1024]{1,0:T(8,128)(2,1)}, u32[]{:S(2)}, u32[]{:S(2)}) %collective-permute-start.23) | collective-permute-done | bytes 524320 | tf_op jit(solution)/shard_map/ppermute | solution.py:390
  (201 shorter events, 94.9 us)
Async XLA Ops:
  7.2 15.5 %collective-permute-start.2 = (bf16[256,1024]{1,0:T(8,128)(2,1)}, bf16[256,1024]{1,0:T(8,128)(2,1)S(1)}, u32[]{:S(2)}, u32[]{:S(2)}) collective-permute-start(bf16[256,1024]{1,0:T(8,128)(2,1)} %refs_1_.7), channel_id=1, source_target_pairs={{0,32},{32,0},{1,33},{33,1},{2,34},{34,2},{3,35},{35,3},{4,36},{36... | collective-permute-start | bytes 1572872 | tf_op jit(solution)/shard_map/ppermute | solution.py:390
  7.3 21.5 %collective-permute-start = (bf16[256,1024]{1,0:T(8,128)(2,1)}, bf16[256,1024]{1,0:T(8,128)(2,1)S(1)}, u32[]{:S(2)}, u32[]{:S(2)}) collective-permute-start(bf16[256,1024]{1,0:T(8,128)(2,1)} %refs_1_.6), channel_id=1, source_target_pairs={{0,32},{32,0},{1,33},{33,1},{2,34},{34,2},{3,35},{35,3},{4,36},{36... | collective-permute-start | bytes 1572872 | tf_op jit(solution)/shard_map/ppermute | solution.py:390
  7.8 25.1 %collective-permute-start.1 = (bf16[256,1024]{1,0:T(8,128)(2,1)}, bf16[256,1024]{1,0:T(8,128)(2,1)}, u32[]{:S(2)}, u32[]{:S(2)}) collective-permute-start(bf16[256,1024]{1,0:T(8,128)(2,1)} %refs_1_.6), channel_id=1, source_target_pairs={{0,64},{64,0},{1,65},{65,1},{2,66},{66,2},{3,67},{67,3},{4,68},{68... | collective-permute-start | bytes 1572872 | tf_op jit(solution)/shard_map/ppermute | solution.py:390
  12.8 47.9 %all-to-all-start = ((bf16[128,2,8,256]{3,2,1,0:T(8,128)(2,1)}), bf16[128,2,8,256]{3,2,1,0:T(8,128)(2,1)}, u32[]{:S(2)}, u32[]{:S(2)}) async-start(bf16[128,2,8,256]{3,2,1,0:T(8,128)(2,1)} %bitcast.11), calls=%async_computation | async-start | bytes 2097152 | tf_op jit(solution)/shard_map/all_to_all | solution.py:406
  33.0 17.0 %collective-permute-start.14 = (bf16[256,1024]{1,0:T(8,128)(2,1)S(1)}, bf16[256,1024]{1,0:T(8,128)(2,1)}, u32[]{:S(2)}, u32[]{:S(2)}) collective-permute-start(bf16[256,1024]{1,0:T(8,128)(2,1)S(1)} %copy-done.6), channel_id=1, source_target_pairs={{0,64},{64,0},{1,65},{65,1},{2,66},{66,2},{3,67},{67,3},{4,68},{68... | collective-permute-start | bytes 1572872 | tf_op jit(solution)/shard_map/ppermute | solution.py:390
  50.0 31.2 %collective-permute-start.15 = (bf16[256,1024]{1,0:T(8,128)(2,1)}, bf16[256,1024]{1,0:T(8,128)(2,1)S(1)}, u32[]{:S(2)}, u32[]{:S(2)}) collective-permute-start(bf16[256,1024]{1,0:T(8,128)(2,1)} %collective-permute-done.14.refs_3_), channel_id=1, source_target_pairs={{0,32},{32,0},{1,33},{33,1},{2,34},{34,2},{3,35},{35,3},{4,36},{36... | collective-permute-start | bytes 1572872 | tf_op jit(solution)/shard_map/ppermute | solution.py:390
  55.7 9.8 %collective-permute-start.7 = (bf16[256,512]{1,0:T(8,128)(2,1)}, bf16[256,512]{1,0:T(8,128)(2,1)S(1)}, u32[]{:S(2)}, u32[]{:S(2)}) collective-permute-start(bf16[256,512]{1,0:T(8,128)(2,1)} %get-tuple-element.57), channel_id=1, source_target_pairs={{0,8},{8,16},{16,24},{24,0},{1,9},{9,17},{17,25},{25,1},{2,10},{10... | collective-permute-start | bytes 786440 | tf_op jit(solution)/shard_map/ppermute | solution.py:387
  56.9 13.9 %collective-permute-start.8 = (bf16[256,512]{1,0:T(8,128)(2,1)}, bf16[256,512]{1,0:T(8,128)(2,1)S(1)}, u32[]{:S(2)}, u32[]{:S(2)}) collective-permute-start(bf16[256,512]{1,0:T(8,128)(2,1)} %get-tuple-element.58), channel_id=1, source_target_pairs={{0,16},{8,24},{16,0},{24,8},{1,17},{9,25},{17,1},{25,9},{2,18},{10... | collective-permute-start | bytes 786440 | tf_op jit(solution)/shard_map/ppermute | solution.py:387
  59.3 11.5 %collective-permute-start.9 = (bf16[256,512]{1,0:T(8,128)(2,1)}, bf16[256,512]{1,0:T(8,128)(2,1)S(1)}, u32[]{:S(2)}, u32[]{:S(2)}) collective-permute-start(bf16[256,512]{1,0:T(8,128)(2,1)} %get-tuple-element.59), channel_id=1, source_target_pairs={{0,24},{8,0},{16,8},{24,16},{1,25},{9,1},{17,9},{25,17},{2,26},{10... | collective-permute-start | bytes 786440 | tf_op jit(solution)/shard_map/ppermute | solution.py:387
  99.9 20.1 %all-to-all-start.1 = ((bf16[4,256,512]{2,1,0:T(8,128)(2,1)}), bf16[4,256,512]{2,1,0:T(8,128)(2,1)S(1)}, u32[]{:S(2)}, u32[]{:S(2)}) async-start(bf16[4,256,512]{2,1,0:T(8,128)(2,1)} %get-tuple-element.82), calls=%async_computation.1 | async-start | bytes 2097152 | tf_op jit(solution)/shard_map/all_to_all | solution.py:442
  103.5 119.9 %reduce-scatter.2.cloned.1.call-start = ((), (), s32[]{:S(2)}) async-start(), calls=%async_computation.5 | async-start | bytes 2621440 | tf_op jit(solution)/shard_map/reduce_scatter | solution.py:455
  103.5 24.4 %collective-permute-start.11 = (bf16[256,1024]{1,0:T(8,128)(2,1)}, bf16[256,1024]{1,0:T(8,128)(2,1)S(1)}, u32[]{:S(2)}, u32[]{:S(2)}) collective-permute-start(bf16[256,1024]{1,0:T(8,128)(2,1)} %get-tuple-element.83.refs_0_), channel_id=1, source_target_pairs={{0,24},{8,0},{16,8},{24,16},{1,25},{9,1},{17,9},{25,17},{2,26},{10... | collective-permute-start | bytes 1572872 | tf_op jit(solution)/shard_map/ppermute | solution.py:387
  106.8 22.3 %collective-permute-start.10 = (bf16[256,1024]{1,0:T(8,128)(2,1)}, bf16[256,1024]{1,0:T(8,128)(2,1)S(1)}, u32[]{:S(2)}, u32[]{:S(2)}) collective-permute-start(bf16[256,1024]{1,0:T(8,128)(2,1)} %get-tuple-element.83.refs_0_), channel_id=1, source_target_pairs={{0,8},{8,16},{16,24},{24,0},{1,9},{9,17},{17,25},{25,1},{2,10},{10... | collective-permute-start | bytes 1572872 | tf_op jit(solution)/shard_map/ppermute | solution.py:387
  120.0 45.2 %collective-permute-start.21 = (bf16[1024,512]{1,0:T(8,128)(2,1)S(1)}, bf16[1024,512]{1,0:T(8,128)(2,1)S(1)}, u32[]{:S(2)}, u32[]{:S(2)}) collective-permute-start(bf16[1024,512]{1,0:T(8,128)(2,1)S(1)} %bitcast.57), channel_id=1, source_target_pairs={{0,32},{32,0},{1,33},{33,1},{2,34},{34,2},{3,35},{35,3},{4,36},{36... | collective-permute-start | bytes 3145736 | tf_op jit(solution)/shard_map/ppermute | solution.py:390
  145.6 19.6 %collective-permute-start.20 = (bf16[1024,256]{1,0:T(8,128)(2,1)S(1)}, bf16[1024,256]{1,0:T(8,128)(2,1)S(1)}, u32[]{:S(2)}, u32[]{:S(2)}) collective-permute-start(bf16[1024,256]{1,0:T(8,128)(2,1)S(1)} %get-tuple-element.75.refs_1_), channel_id=1, source_target_pairs={{0,24},{8,0},{16,8},{24,16},{1,25},{9,1},{17,9},{25,17},{2,26},{10... | collective-permute-start | bytes 1572872 | tf_op jit(solution)/shard_map/ppermute | solution.py:387
  146.6 18.6 %collective-permute-start.19 = (bf16[1024,256]{1,0:T(8,128)(2,1)S(1)}, bf16[1024,256]{1,0:T(8,128)(2,1)S(1)}, u32[]{:S(2)}, u32[]{:S(2)}) collective-permute-start(bf16[1024,256]{1,0:T(8,128)(2,1)S(1)} %get-tuple-element.75.refs_1_), channel_id=1, source_target_pairs={{0,8},{8,16},{16,24},{24,0},{1,9},{9,17},{17,25},{25,1},{2,10},{10... | collective-permute-start | bytes 1572872 | tf_op jit(solution)/shard_map/ppermute | solution.py:387
  147.7 15.6 %collective-permute-start.13 = (bf16[128,1024]{1,0:T(8,128)(2,1)S(1)}, bf16[128,1024]{1,0:T(8,128)(2,1)S(1)}, u32[]{:S(2)}, u32[]{:S(2)}) collective-permute-start(bf16[128,1024]{1,0:T(8,128)(2,1)S(1)} %slice.46), channel_id=1, source_target_pairs={{0,24},{8,0},{16,8},{24,16},{1,25},{9,1},{17,9},{25,17},{2,26},{10... | collective-permute-start | bytes 786440 | tf_op jit(solution)/shard_map/ppermute | solution.py:387
  149.9 15.3 %collective-permute-start.12 = (bf16[128,1024]{1,0:T(8,128)(2,1)S(1)}, bf16[128,1024]{1,0:T(8,128)(2,1)S(1)}, u32[]{:S(2)}, u32[]{:S(2)}) collective-permute-start(bf16[128,1024]{1,0:T(8,128)(2,1)S(1)} %slice.45), channel_id=1, source_target_pairs={{0,8},{8,16},{16,24},{24,0},{1,9},{9,17},{17,25},{25,1},{2,10},{10... | collective-permute-start | bytes 786440 | tf_op jit(solution)/shard_map/ppermute | solution.py:387
  172.7 23.7 %collective-permute-start.24 = (bf16[4,256,512]{2,1,0:T(8,128)(2,1)}, bf16[4,256,512]{2,1,0:T(8,128)(2,1)}, u32[]{:S(2)}, u32[]{:S(2)}) collective-permute-start(bf16[4,256,512]{2,1,0:T(8,128)(2,1)} %pad_maximum_fusion), channel_id=1, source_target_pairs={{0,32},{32,0},{1,33},{33,1},{2,34},{34,2},{3,35},{35,3},{4,36},{36... | collective-permute-start | bytes 3145736 | tf_op jit(solution)/shard_map/ppermute | solution.py:390
  174.0 36.1 %all-to-all-start.3 = ((bf16[128,2,8,256]{3,2,1,0:T(8,128)(2,1)}), bf16[128,2,8,256]{3,2,1,0:T(8,128)(2,1)}, u32[]{:S(2)}, u32[]{:S(2)}) async-start(bf16[128,2,8,256]{3,2,1,0:T(8,128)(2,1)} %pad_maximum_fusion.1), calls=%async_computation.4 | async-start | bytes 2097152 | tf_op jit(solution)/shard_map/all_to_all | solution.py:466
  193.2 22.3 %collective-permute-start.22 = (bf16[2,256,1024]{2,1,0:T(8,128)(2,1)}, bf16[2,256,1024]{2,1,0:T(8,128)(2,1)}, u32[]{:S(2)}, u32[]{:S(2)}) collective-permute-start(bf16[2,256,1024]{2,1,0:T(8,128)(2,1)} %get-tuple-element.89), channel_id=1, source_target_pairs={{0,32},{32,0},{1,33},{33,1},{2,34},{34,2},{3,35},{35,3},{4,36},{36... | collective-permute-start | bytes 3145736 | tf_op jit(solution)/shard_map/ppermute | solution.py:390
  210.2 45.7 %all-to-all-start.2 = ((bf16[8,128,1024]{2,1,0:T(8,128)(2,1)}), bf16[8,128,1024]{2,1,0:T(8,128)(2,1)}, u32[]{:S(2)}, u32[]{:S(2)}) async-start(bf16[8,128,1024]{2,1,0:T(8,128)(2,1)} %bitcast.22), calls=%async_computation.2 | async-start | bytes 4194304 | tf_op jit(solution)/shard_map/all_to_all | solution.py:473
  218.5 35.4 %collective-permute-start.23 = (bf16[256,1024]{1,0:T(8,128)(2,1)S(1)}, bf16[256,1024]{1,0:T(8,128)(2,1)}, u32[]{:S(2)}, u32[]{:S(2)}) collective-permute-start(bf16[256,1024]{1,0:T(8,128)(2,1)S(1)} %fusion.2), channel_id=1, source_target_pairs={{0,64},{64,0},{1,65},{65,1},{2,66},{66,2},{3,67},{67,3},{4,68},{68... | collective-permute-start | bytes 1572872 | tf_op jit(solution)/shard_map/ppermute | solution.py:390
  224.3 34.3 %collective-permute-start.27 = (bf16[1024,128]{1,0:T(8,128)(2,1)S(1)}, bf16[1024,128]{1,0:T(8,128)(2,1)}, u32[]{:S(2)}, u32[]{:S(2)}) collective-permute-start(bf16[1024,128]{1,0:T(8,128)(2,1)S(1)} %dynamic-slice_bitcast_fusion), channel_id=1, source_target_pairs={{0,1},{1,0},{2,3},{3,2},{4,5},{5,4},{6,7},{7,6},{8,9},{9,8},{10,11... | collective-permute-start | bytes 786440 | tf_op jit(solution)/shard_map/ppermute | solution.py:390
  (71 other events, 796.8 us)
Sparse Core Ops, SparseCore 0:
  171.6 38.6 reduce-scatter.1

commit v6 on v5

--- a/solution.py
+++ b/solution.py
@@ -18,7 +18,7 @@
 SEQ = ("z", "y", "xl")
 XH, CORE, Z = range(3)
 SWAP = [(0, 1), (1, 0)]
-WORK = 8 * 1024 * 1024
+VMEM = 56 * 1024 * 1024
 TOK = 256
 PIECE = 256
 GROUP = 4 * TOK
@@ -47,11 +47,6 @@
 
 
 def call(kernel, name, grid, in_specs, out_specs, out_shape, scratch, flops, moved, pos, *args):
-    outs = zip(jax.tree.leaves(out_specs), jax.tree.leaves(out_shape))
-    blocks = [(s.block_shape, a.dtype) for s, a in [*zip(in_specs, args), *outs] if s is not HBM]
-    room = sum(2 * math.prod(shape) * dtype.itemsize for shape, dtype in blocks)
-    held = [s for s in scratch if s.memory_space == pltpu.VMEM]
-    room += sum(math.prod(s.shape) * jnp.dtype(s.dtype).itemsize for s in held)
     return pl.pallas_call(
         kernel,
         grid_spec=pltpu.PrefetchScalarGridSpec(
@@ -62,7 +57,7 @@
             scratch_shapes=scratch,
         ),
         out_shape=out_shape,
-        compiler_params=pltpu.CompilerParams(vmem_limit_bytes=room + WORK),
+        compiler_params=pltpu.CompilerParams(vmem_limit_bytes=VMEM),
         cost_estimate=pl.CostEstimate(flops=flops, bytes_accessed=moved, transcendentals=0),
         name=name,
     )(pos, *args)
@@ -87,19 +82,27 @@
         out[...] = product if i == 0 else out[...] + product
 
 
-def far_kernel(transposed, pos, x0, x1, x2, x3, before, w_ref, *refs):
-    rows, parts, (total, weights, sems) = refs[:4], refs[4], refs[5:]
+def far_kernel(transposed, joined, pos, x0, x1, x2, x3, before, w_ref, *refs):
+    rows, (total, weights, sems) = refs[:4], refs[-3:]
     contract = ((1,), (1,)) if transposed else ((1,), (0,))
     copies = weight_copies(pos, w_ref, weights, sems, (2, 3), transposed)
     half = pl.multiple_of(pos[CORE] * (BLOCK // 2), BLOCK // 2)
     for i, x in enumerate((x0, x1, x2, x3)):
-        parts[head_block(i, pos)] = x[:, pl.ds(half, BLOCK // 2)]
+        part = x[:, pl.ds(half, BLOCK // 2)]
+        if joined:
+            for d in range(4):
+
+                @pl.when(shifted(pos[Z], d) == head_block(i, pos))
+                def _(d=d, part=part):
+                    rows[d][:, PIECE:] = part
+        else:
+            refs[4][head_block(i, pos)] = part
     for i, (x, known) in enumerate(((x2, before), (x3, total))):
         copies[i].wait()
         total[...] = known[...] + dot(x[...], weights[i], contract)
     for d in range(4):
         start = pl.multiple_of(shifted(pos[Z], d) * PIECE, PIECE)
-        rows[d][...] = total[:, pl.ds(start, PIECE)].astype(BF16)
+        rows[d][:, :PIECE] = total[:, pl.ds(start, PIECE)].astype(BF16)
 
 
 HBM = pl.BlockSpec(memory_space=pltpu.HBM)
@@ -122,14 +125,16 @@
     )
 
 
-def far_project(name, pos, blocks, weight, transposed, before):
+def far_project(name, pos, blocks, weight, transposed, joined, before):
+    wide = PIECE + BLOCK // 2 if joined else PIECE
+    shapes = [(TOK, wide)] * 4 + ([] if joined else [(4, TOK, BLOCK // 2)])
     outs = call(
-        lambda *refs: far_kernel(transposed, *refs),
+        lambda *refs: far_kernel(transposed, joined, *refs),
         name,
         (1,),
         [whole((TOK, BLOCK))] * 5 + [HBM],
-        [whole((TOK, PIECE))] * 4 + [whole((4, TOK, BLOCK // 2))],
-        [struct((TOK, PIECE))] * 4 + [struct((4, TOK, BLOCK // 2))],
+        [whole(shape) for shape in shapes],
+        [struct(shape) for shape in shapes],
         [
             pltpu.VMEM((TOK, BLOCK), F32),
             pltpu.VMEM((2, BLOCK, BLOCK), BF16),
@@ -142,7 +147,7 @@
         before,
         weight,
     )
-    return outs[:4], outs[4]
+    return outs[:4], outs[4:]
 
 
 def assemble_kernel(pos, mine, other, out):
@@ -168,13 +173,12 @@
     )
 
 
-def assemble_turned_kernel(pos, m0, m1, m2, m3, other, out):
-    for d, mine in enumerate((m0, m1, m2, m3)):
+def assemble_turned_kernel(pos, mine, other, out):
+    for d in range(4):
         token = pl.multiple_of(shifted(pos[Z], -d) * TOK, TOK)
-        for side in range(2):
+        for side, ref in enumerate((mine, other)):
             half = pl.multiple_of(lax.rem(pos[CORE] + side, 2) * (BLOCK // 2), BLOCK // 2)
-            part = other[d] if side else mine[...]
-            out[pl.ds(half, BLOCK // 2), pl.ds(token, TOK)] = part.T
+            out[pl.ds(half, BLOCK // 2), pl.ds(token, TOK)] = ref[d].T
 
 
 def assemble_turned(name, pos, mine, other):
@@ -182,111 +186,63 @@
         assemble_turned_kernel,
         name,
         (1,),
-        [whole((TOK, BLOCK // 2))] * 4 + [whole((4, TOK, BLOCK // 2))],
+        [whole((4, TOK, BLOCK // 2))] * 2,
         whole((BLOCK, GROUP)),
         struct((BLOCK, GROUP)),
         [],
         0,
         4 * BLOCK * GROUP,
         pos,
-        *mine,
+        mine,
         other,
     )
 
 
-def forward_kernel(pos, bias, *refs):
-    q_refs, (k_ref, v_ref, out_ref, turned_ref, weights_ref, share_ref) = refs[:4], refs[4:]
+def attention_kernel(pos, bias, *refs):
+    q_refs, g_refs, (k_ref, v_ref), refs = refs[:4], refs[4:8], refs[8:10], refs[10:]
+    turned_ref, dq_ref, dk_ref, dv_ref, dk_sum, dv_sum = refs
     k, v = k_ref[...], v_ref[...]
     for d in range(4):
-        here = slice(d * TOK, (d + 1) * TOK)
-        scores = dot(q_refs[d][...], k, ((1,), (1,))) + bias[...]
+        q = q_refs[d][...]
+        scores = dot(q, k, ((1,), (1,))) + bias[...]
         top = jnp.max(scores, axis=1, keepdims=True)
         weights = jnp.exp2((scores - top) * (SCALE * LOG2E))
         share = 1.0 / jnp.sum(weights, axis=1, keepdims=True)
-        weights = weights.astype(BF16)
-        heads_out = (dot(weights, v) * share).astype(BF16)
-        weights_ref[0, here, :] = weights
-        out_ref[here, :] = heads_out
-        share_ref[here, :] = jnp.broadcast_to(share, (TOK, HEAD))
+        low = weights.astype(BF16)
+        heads_out = (dot(low, v) * share).astype(BF16)
         token = pl.multiple_of(shifted(pos[Z], -d) * TOK, TOK)
         turned_ref[:, pl.ds(token, TOK)] = heads_out.T
-
-
-def forward(pos, bias, queries, keys, values):
-    rows = pl.BlockSpec((TOK, HEAD), lambda h, pos: (0, h))
-    column = pl.BlockSpec((GROUP, HEAD), lambda h, pos: (0, h))
-    context = keys.shape[0]
-    return call(
-        forward_kernel,
-        "attention_forward",
-        (PIECE // HEAD,),
-        [whole((1, context))] + [rows] * 4 + [column] * 2,
-        [
-            column,
-            pl.BlockSpec((HEAD, GROUP), lambda h, pos: (h, 0)),
-            pl.BlockSpec((1, GROUP, context), lambda h, pos: (h, 0, 0)),
-            column,
-        ],
-        [
-            struct((GROUP, PIECE)),
-            struct((PIECE, GROUP)),
-            struct((PIECE // HEAD, GROUP, context)),
-            struct((GROUP, PIECE), F32),
-        ],
-        [],
-        12 * GROUP * PIECE * context,
-        2 * (4 * GROUP * PIECE + 2 * GROUP * context),
-        pos,
-        bias,
-        *queries,
-        keys,
-        values,
-    )
-
-
-def backward_kernel(pos, *refs):
-    q_refs, g_refs, (k_ref, v_ref, out_ref, weights_ref, share_ref) = refs[:4], refs[4:8], refs[8:13]
-    dq_ref, dk_ref, dv_ref, dk_sum, dv_sum = refs[13:]
-    k, v = k_ref[...], v_ref[...]
-    for d in range(4):
-        here = slice(d * TOK, (d + 1) * TOK)
-        g = (g_refs[d][...].astype(F32) * (share_ref[here, :] * SCALE)).astype(BF16)
-        q, weights = q_refs[d][...], weights_ref[0, here, :]
-        delta = jnp.sum(g.astype(F32) * out_ref[here, :].astype(F32), axis=1, keepdims=True)
-        score_grad = (weights.astype(F32) * (dot(g, v, ((1,), (1,))) - delta)).astype(BF16)
-        token = pl.multiple_of(shifted(pos[Z], -d) * TOK, TOK)
+        g = (g_refs[d][...].astype(F32) * (share * SCALE)).astype(BF16)
+        delta = jnp.sum(g.astype(F32) * heads_out.astype(F32), axis=1, keepdims=True)
+        score_grad = (low.astype(F32) * (dot(g, v, ((1,), (1,))) - delta)).astype(BF16)
         dq_ref[pl.ds(token, TOK), :] = dot(score_grad, k).astype(BF16)
-        dk_term, dv_term = dot(q, score_grad, ((0,), (0,))), dot(g, weights, ((0,), (0,)))
+        dk_term, dv_term = dot(q, score_grad, ((0,), (0,))), dot(g, low, ((0,), (0,)))
         dk_sum[...] = dk_term if d == 0 else dk_sum[...] + dk_term
         dv_sum[...] = dv_term if d == 0 else dv_sum[...] + dv_term
     dk_ref[...] = dk_sum[...].T.astype(BF16)
     dv_ref[...] = (dv_sum[...] * (1.0 / SCALE)).T.astype(BF16)
 
 
-def backward(pos, queries, grads, keys, values, heads_out, weights, share):
+def attention(pos, bias, queries, grads, keys, values):
     rows = pl.BlockSpec((TOK, HEAD), lambda h, pos: (0, h))
     column = pl.BlockSpec((GROUP, HEAD), lambda h, pos: (0, h))
     context = keys.shape[0]
     return call(
-        backward_kernel,
-        "attention_backward",
+        attention_kernel,
+        "attention",
         (PIECE // HEAD,),
-        [rows] * 8
-        + [column] * 3
-        + [pl.BlockSpec((1, GROUP, context), lambda h, pos: (h, 0, 0)), column],
-        [column] * 3,
-        [struct((GROUP, PIECE))] * 3,
+        [whole((1, context))] + [rows] * 8 + [column] * 2,
+        [pl.BlockSpec((HEAD, GROUP), lambda h, pos: (h, 0))] + [column] * 3,
+        [struct((PIECE, GROUP))] + [struct((GROUP, PIECE))] * 3,
         [pltpu.VMEM((HEAD, context), F32)] * 2,
-        16 * GROUP * PIECE * context,
-        2 * (6 * GROUP * PIECE + 2 * GROUP * context),
-        pos,
+        30 * GROUP * PIECE * context,
+        16 * GROUP * PIECE,
+        pos,
+        bias,
         *queries,
         *grads,
         keys,
         values,
-        heads_out,
-        weights,
-        share,
     )
 
 
@@ -396,9 +352,9 @@
         blocks = (local, swap(local, "core"))
         return blocks, near_project(name, pos, blocks, weight, transposed)
 
-    def far(name, blocks, over_x, weight, transposed, first):
+    def far(name, blocks, over_x, weight, transposed, joined, first):
         blocks = blocks + (over_x, swap(over_x, "core"))
-        rows, parts = far_project(name, pos, blocks, weight, transposed, first)
+        rows, parts = far_project(name, pos, blocks, weight, transposed, joined, first)
         return [to_layer(x, d) for d, x in enumerate(rows)], parts
 
     own = jnp.stack([context_keys, context_values]).reshape(2, 8, 16, PIECE).transpose(2, 0, 1, 3)
@@ -421,35 +377,32 @@
         half = x.shape[0] // 2
         return x, left, right, to_layer(left[:half], 1), to_layer(right[half:], 3)
 
-    queries, state_parts = far("queries", states, states_x, query_weight, False, first_queries)
-    mine = []
-    for d in range(4):
-        part = lax.dynamic_index_in_dim(state_parts, shifted(pos[Z], d), 0, False)
-        mine.append(to_layer(after(part, *queries) if d else part, d))
-    heads_out, turned_out, weights, share = forward(pos, bias, after(queries, *mine[1:]), keys, values)
+    queries, _ = far("queries", states, states_x, query_weight, False, True, first_queries)
+    heads_grad, parts = far(
+        "heads_grad", cotangent, cotangent_x, output_weight, True, False, after(first_grad, first_queries)
+    )
+    cotangent_block = lax.all_to_all(after(parts[0], *heads_grad), "z", 0, 0, tiled=True)
+    cotangent_block = cotangent_block.reshape(GROUP, BLOCK // 2)
+
+    turned_out, query_grad, key_terms, value_terms = attention(
+        pos, bias, queries, heads_grad, keys, values
+    )
     left, right = ring_ends(turned_out)
     every_out = ring(turned_out, left, right)
-
-    heads_grad, cotangent_parts = far(
-        "heads_grad", cotangent, cotangent_x, output_weight, True, after(first_grad, turned_out)
-    )
-    query_grad, key_terms, value_terms = backward(
-        pos, queries, heads_grad, keys, values, after(heads_out, left, right), weights, share
-    )
+    query_grad = after(query_grad, left, right)
     left, right = ring_ends(query_grad)
     every_query_grad = ring(query_grad, left, right)
 
-    block = lax.all_to_all(after(cotangent_parts, *heads_grad), "z", 0, 0, tiled=True)
-    block = block.reshape(GROUP, BLOCK // 2)
-    group_cotangent = assemble("group_cotangent", pos, block, swap(block, "core"))
-    other = swap(jnp.stack(after(mine, block)), "core")
-    group_states = assemble_turned("group_states", pos, mine, other)
+    cotangent_block = after(cotangent_block, turned_out)
+    group_cotangent = assemble("group_cotangent", pos, cotangent_block, swap(cotangent_block, "core"))
+    state_block = jnp.stack([x[:, PIECE:] for x in after(queries, turned_out)])
+    group_states = assemble_turned("group_states", pos, state_block, swap(state_block, "core"))
 
     terms = weight_terms(
         "output_weight_terms",
         output_grad_kernel,
         pos,
-        (*after(every_out, left, right), group_cotangent),
+        (*every_out, group_cotangent),
         (PLANES, BLOCK, 128),
     )
     pair = lax.psum_scatter(terms, "y", scatter_dimension=0, tiled=True)
@@ -463,7 +416,7 @@
     attended = (pair[0] + swap(pair[1].astype(BF16), "xh").astype(F32)).astype(BF16)
 
     terms = jnp.stack([key_terms.reshape(128, 8, PIECE), value_terms.reshape(128, 8, PIECE)], 1)
-    moved = lax.all_to_all(after(terms, left, right, block), HEADS + SEQ, 0, 0, tiled=True)
+    moved = lax.all_to_all(after(terms, left, right), HEADS + SEQ, 0, 0, tiled=True)
     owned = jnp.sum(moved.reshape(16, PLANES, 2, 8, PIECE).astype(F32), axis=1)
     owned = owned.transpose(1, 2, 0, 3).reshape(2, 8, 16 * PIECE)
 

time: 269 us -> 257 us (0.955)
  local copies, waits for them, and re-layouts: 41.9 us -> 16.8 us
  Pallas kernels: 44.1 us -> 65.1 us
  starting transfers between devices: 63 us -> 52.5 us
  waiting for transfers between devices: 90.8 us -> 98.7 us
  other arithmetic: 12.9 us -> 8.04 us
    unnamed x125 -> x75, local copies, waits for them, and re-layouts: 36.8 us -> 10.1 us
    all_to_all x1, waiting for transfers between devices: 0.01 us -> 22.9 us  [on_device(): lax.all_to_all(terms.reshape(PLANES, 128, BLOCK), ('y', 'xl'), 0, 0, tile...]
    pallas_call x11 -> x10, Pallas kernels: 44.1 us -> 65.1 us  [call(): pl.pallas_call(kernel, grid_spec=pltpu.PrefetchScalarGridSpec(num_scalar_...]
    all_to_all x2, waiting for transfers between devices: 13.3 us -> 2 us  [the longest x1 2 us: on_device(): lax.all_to_all(after(parts[0], *heads_grad), 'z', 0, 0, tiled=True)]
    ppermute x17 -> x14, starting transfers between devices: 26.8 us -> 19.6 us  [to_layer(): lax.ppermute(x, 'z', [(i, (i + d) % 4) for i in range(4)])]
    ppermute x11, waiting for transfers between devices: 28.1 us -> 23.8 us  [swap(): return lax.ppermute(x, axis, SWAP)]
    ppermute x17 -> x14, waiting for transfers between devices: 49.5 us -> 50 us  [to_layer(): lax.ppermute(x, 'z', [(i, (i + d) % 4) for i in range(4)])]
  transfers between devices with their start and end apart: 33 -> 30, of which waited for: 14 -> 14; matrix products, arithmetic and copies ran while one was open for 6% -> 6% of each run, Pallas kernels for 13% -> 23%
where the time goes in v6:
time: 257 us; the launch traced here: 256 us
  waiting for transfers between devices  98.7 us (38%)
  Pallas kernels  65.1 us (25%)
  starting transfers between devices  52.5 us (20%)
  local copies, waits for them, and re-layouts  16.8 us (7%)
  between operations  14.5 us (6%)
  other arithmetic  8.04 us (3%)
    pallas_call x10, Pallas kernels, call(): pl.pallas_call(kernel, grid_spec=pltpu.PrefetchScalarGridSpec(num_scalar_...  65.1 us
    ppermute x14, waiting for transfers between devices, to_layer(): lax.ppermute(x, 'z', [(i, (i + d) % 4) for i in range(4)])  50 us
    ppermute x11, waiting for transfers between devices, swap(): return lax.ppermute(x, axis, SWAP)  23.8 us
    all_to_all x1, waiting for transfers between devices, on_device(): lax.all_to_all(terms.reshape(PLANES, 128, BLOCK), ('y', 'xl'), 0, 0, tile...  22.9 us
    ppermute x14, starting transfers between devices, to_layer(): lax.ppermute(x, 'z', [(i, (i + d) % 4) for i in range(4)])  19.6 us
    unnamed x75, local copies, waits for them, and re-layouts  10.1 us
    all_to_all x1, starting transfers between devices, on_device(): context = lax.all_to_all(own, HEADS + SEQ, 0, 0, tiled=True)  9.36 us
    ppermute x11, starting transfers between devices, swap(): return lax.ppermute(x, axis, SWAP)  7.99 us
  transfers between devices with their start and end apart: 30, of which 14 were waited for; matrix products, arithmetic and copies ran while one was open for 6% of the time, Pallas kernels for 23%

profile of v6, /device:TPU:0, one launch (start us, length us, event | category | flops | bytes accessed | tf_op | source)
XLA Modules:
  0.0 255.7 jit_solution(5004332606345070778)
XLA Ops:
  7.8 3.1 %collective-permute-start.1 = (bf16[256,1024]{1,0:T(8,128)(2,1)}, bf16[256,1024]{1,0:T(8,128)(2,1)S(1)}, u32[]{:S(2)}, u32[]{:S(2)}) collective-permute-start(bf16[256,1024]{1,0:T(8,128)(2,1)} %refs_1_.6), channel_id=1, source_target_pairs={{0,64},{64,0},{1,65},{65,1},{2,66},{66,2},{3,67},{67,3},{4,68},{68... | collective-permute-start | bytes 1572872 | tf_op jit(solution)/shard_map/ppermute | solution.py:346
  12.3 5.8 %queries_near.1.refs_5_ = f32[256,1024]{1,0:T(8,128)} custom-call(s32[5]{0:T(128)} %stack.50.refs_0_.pos, bf16[256,1024]{1,0:T(8,128)(2,1)} %refs_1_.6, bf16[256,1024]{1,0:T(8,128)(2,1)} %copy-done.4, bf16[4096,1024]{1,0:T(8,128)(2,1)} %refs_6_.2), custom_call_target="tpu_custom_call" | custom-call | flops 1073741824 | bytes 4194304 | tf_op jit(solution)/shard_map/queries_near/pallas_call | solution.py:50
  18.9 5.8 %heads_grad_near.1.refs_5_ = f32[256,1024]{1,0:T(8,128)} custom-call(s32[5]{0:T(128)} %stack.50.refs_0_.pos, bf16[256,1024]{1,0:T(8,128)(2,1)} %refs_1_.7, bf16[256,1024]{1,0:T(8,128)(2,1)} %copy-done.5, bf16[1024,4096]{1,0:T(8,128)(2,1)} %refs_5_.1), custom_call_target="tpu_custom_call" | custom-call | flops 1073741824 | bytes 4194304 | tf_op jit(solution)/shard_map/heads_grad_near/pallas_call | solution.py:50
  26.5 13.5 %collective-permute-done.7.refs_3_ = bf16[256,1024]{1,0:T(8,128)(2,1)S(1)} collective-permute-done((bf16[256,1024]{1,0:T(8,128)(2,1)S(1)}, bf16[256,1024]{1,0:T(8,128)(2,1)S(1)}, u32[]{:S(2)}, u32[]{:S(2)}) %collective-permute-start.7) | collective-permute-done | bytes 524320 | tf_op jit(solution)/shard_map/ppermute | solution.py:346
  41.2 9.4 %all-to-all-start = ((bf16[128,2,8,256]{3,2,1,0:T(8,128)(2,1)}), bf16[128,2,8,256]{3,2,1,0:T(8,128)(2,1)S(1)}, u32[]{:S(2)}, u32[]{:S(2)}) async-start(bf16[128,2,8,256]{3,2,1,0:T(8,128)(2,1)} %bitcast.8), calls=%async_computation | async-start | bytes 2097152 | tf_op jit(solution)/shard_map/all_to_all | solution.py:362
  51.5 6.9 %heads_grad.1 = (bf16[256,256]{1,0:T(8,128)(2,1)}, bf16[256,256]{1,0:T(8,128)(2,1)}, bf16[256,256]{1,0:T(8,128)(2,1)}, bf16[256,256]{1,0:T(8,128)(2,1)}, bf16[4,256,512]{2,1,0:T(8,128)(2,1)}) custom-call(s32[5]{0:T(128)} %stack.50.refs_0_.pos, bf16[256,1024]{1,0:T(8,128)(2,1)} %refs_1_.7, bf16[256,1024]{1,0:T(8,128)(2,1)} %copy-done.5, ...), custom_call_target="tpu_custom_call" | custom-call | flops 1073741824 | bytes 4194304 | tf_op jit(solution)/shard_map/heads_grad/pallas_call | solution.py:50
  60.7 6.8 %queries.1 = (bf16[256,768]{1,0:T(8,128)(2,1)}, bf16[256,768]{1,0:T(8,128)(2,1)}, bf16[256,768]{1,0:T(8,128)(2,1)}, bf16[256,768]{1,0:T(8,128)(2,1)}) custom-call(s32[5]{0:T(128)} %stack.50.refs_0_.pos, bf16[256,1024]{1,0:T(8,128)(2,1)} %refs_1_.6, bf16[256,1024]{1,0:T(8,128)(2,1)} %copy-done.4, bf16[256,1024]{1,0:T(8,128)(2,1)} %copy-done.10, ...), custom_call_target="tpu_custom_call" | custom-call | flops 1073741824 | bytes 4194304 | tf_op jit(solution)/shard_map/queries/pallas_call | solution.py:50
  76.6 15.2 %collective-permute-done.10.refs_6_ = bf16[256,256]{1,0:T(8,128)(2,1)S(1)} collective-permute-done((bf16[256,256]{1,0:T(8,128)(2,1)S(1)}, bf16[256,256]{1,0:T(8,128)(2,1)S(1)}, u32[]{:S(2)}, u32[]{:S(2)}) %collective-permute-start.10) | collective-permute-done | bytes 131104 | tf_op jit(solution)/shard_map/ppermute | solution.py:343
  91.8 3.0 %collective-permute-done.11.refs_7_ = bf16[256,256]{1,0:T(8,128)(2,1)S(1)} collective-permute-done((bf16[256,256]{1,0:T(8,128)(2,1)S(1)}, bf16[256,256]{1,0:T(8,128)(2,1)S(1)}, u32[]{:S(2)}, u32[]{:S(2)}) %collective-permute-start.11) | collective-permute-done | bytes 131104 | tf_op jit(solution)/shard_map/ppermute | solution.py:343
  95.5 4.5 %all-to-all-start.1 = ((bf16[4,256,512]{2,1,0:T(8,128)(2,1)}), bf16[4,256,512]{2,1,0:T(8,128)(2,1)S(1)}, u32[]{:S(2)}, u32[]{:S(2)}) async-start(bf16[4,256,512]{2,1,0:T(8,128)(2,1)} %get-tuple-element.49), calls=%async_computation.1 | async-start | bytes 2097152 | tf_op jit(solution)/shard_map/all_to_all | solution.py:384
  102.0 10.6 %attention.1 = (bf16[256,1024]{1,0:T(8,128)(2,1)}, bf16[1024,256]{1,0:T(8,128)(2,1)}, bf16[1024,256]{1,0:T(8,128)(2,1)}, bf16[1024,256]{1,0:T(8,128)(2,1)}) custom-call(s32[5]{0:T(128)} %stack.50.refs_0_.pos, f32[1,1024]{1,0:T(1,128)} %bitcast.63, bf16[256,768]{1,0:T(8,128)(2,1)} %get-tuple-element.58.refs_0_, bf16[256,768]{1,0:T(8,128)(2,1)} %copy-done.20, ...), custom_call_target="tpu_custom_call" | custom-call | flops 8053063680 | bytes 4194304 | tf_op jit(solution)/shard_map/attention/pallas_call | solution.py:50
  116.7 12.5 %collective-permute-done.13.refs_2_ = bf16[256,1024]{1,0:T(8,128)(2,1)S(1)} collective-permute-done((bf16[256,1024]{1,0:T(8,128)(2,1)}, bf16[256,1024]{1,0:T(8,128)(2,1)S(1)}, u32[]{:S(2)}, u32[]{:S(2)}) %collective-permute-start.13) | collective-permute-done | bytes 524320 | tf_op jit(solution)/shard_map/ppermute | solution.py:343
  133.0 3.7 %group_cotangent.1.refs_5_ = bf16[1024,1024]{1,0:T(8,128)(2,1)} custom-call(s32[5]{0:T(128)} %stack.50.refs_0_.pos, bf16[1024,512]{1,0:T(8,128)(2,1)} %bitcast.54, bf16[1024,512]{1,0:T(8,128)(2,1)} %copy-done.9), custom_call_target="tpu_custom_call" | custom-call | bytes 4194304 | tf_op jit(solution)/shard_map/group_cotangent/pallas_call | solution.py:50
  137.2 3.5 %collective-permute-done.14.refs_3_ = bf16[128,1024]{1,0:T(8,128)(2,1)S(1)} collective-permute-done((bf16[128,1024]{1,0:T(8,128)(2,1)S(1)}, bf16[128,1024]{1,0:T(8,128)(2,1)S(1)}, u32[]{:S(2)}, u32[]{:S(2)}) %collective-permute-start.14) | collective-permute-done | bytes 262176 | tf_op jit(solution)/shard_map/ppermute | solution.py:343
  141.4 6.6 %output_weight_terms.1 = bf16[8,1024,128]{2,1,0:T(8,128)(2,1)} custom-call(s32[5]{0:T(128)} %stack.50.refs_0_.pos, bf16[256,1024]{1,0:T(8,128)(2,1)} %get-tuple-element.51.refs_0_, bf16[256,1024]{1,0:T(8,128)(2,1)} %copy-done.7, bf16[256,1024]{1,0:T(8,128)(2,1)} %copy-done.6, bf16[128,1024]{1,0:T(8,128)(2,1)} %copy-done.18, bf16[128,1024]{1,0:T(8,128)(2,1)} %copy-done.17, ...), custom_call_target="tpu_custom_call" | custom-call | flops 2147483648 | bytes 6291456 | tf_op jit(solution)/shard_map/output_weight_terms/pallas_call | solution.py:50
  153.0 9.1 %collective-permute-done.21.refs_3_ = bf16[1024,256]{1,0:T(8,128)(2,1)} collective-permute-done((bf16[1024,256]{1,0:T(8,128)(2,1)}, bf16[1024,256]{1,0:T(8,128)(2,1)}, u32[]{:S(2)}, u32[]{:S(2)}) %collective-permute-start.21) | collective-permute-done | bytes 524320 | tf_op jit(solution)/shard_map/ppermute | solution.py:343
  164.2 7.5 %all-to-all-start.3 = ((bf16[128,2,8,256]{3,2,1,0:T(8,128)(2,1)}), bf16[128,2,8,256]{3,2,1,0:T(8,128)(2,1)S(1)}, u32[]{:S(2)}, u32[]{:S(2)}) async-start(bf16[128,2,8,256]{3,2,1,0:T(8,128)(2,1)} %pad_maximum_fusion.1), calls=%async_computation.4 | async-start | bytes 2097152 | tf_op jit(solution)/shard_map/all_to_all | solution.py:419
  177.8 4.2 %group_states.1.refs_0_ = bf16[1024,1024]{1,0:T(8,128)(2,1)} custom-call(s32[5]{0:T(128)} %stack.50.refs_0_.pos, bf16[4,256,512]{2,1,0:T(8,128)(2,1)} %copy-done.2, bf16[4,256,512]{2,1,0:T(8,128)(2,1)} %copy-done.8), custom_call_target="tpu_custom_call" | custom-call | bytes 4194304 | tf_op jit(solution)/shard_map/group_states/pallas_call | solution.py:50
  182.0 8.2 %output_terms.1 = (bf16[2,256,1024]{2,1,0:T(8,128)(2,1)}, f32[2,256,1024]{2,1,0:T(8,128)}) custom-call(s32[5]{0:T(128)} %stack.50.refs_0_.pos, bf16[256,1024]{1,0:T(8,128)(2,1)} %get-tuple-element.51.refs_0_, bf16[256,1024]{1,0:T(8,128)(2,1)} %copy-done.7, bf16[256,1024]{1,0:T(8,128)(2,1)} %copy-done.6, bf16[128,1024]{1,0:T(8,128)(2,1)} %copy-done.18, ...), custom_call_target="tpu_custom_call" | custom-call | flops 2147483648 | bytes 8388608 | tf_op jit(solution)/shard_map/output_terms/pallas_call | solution.py:50
  190.8 3.4 %collective-permute-done.22.refs_4_ = bf16[512,256]{1,0:T(8,128)(2,1)S(1)} collective-permute-done((bf16[512,256]{1,0:T(8,128)(2,1)S(1)}, bf16[512,256]{1,0:T(8,128)(2,1)S(1)}, u32[]{:S(2)}, u32[]{:S(2)}) %collective-permute-start.22) | collective-permute-done | bytes 262176 | tf_op jit(solution)/shard_map/ppermute | solution.py:343
  194.9 6.5 %query_weight_terms.1 = bf16[1024,1024]{1,0:T(8,128)(2,1)} custom-call(s32[5]{0:T(128)} %stack.50.refs_0_.pos, bf16[1024,1024]{1,0:T(8,128)(2,1)} %group_states.1.refs_0_, bf16[1024,256]{1,0:T(8,128)(2,1)} %get-tuple-element.63.refs_1_, bf16[1024,256]{1,0:T(8,128)(2,1)} %collective-permute-done.20.refs_2_, ...), custom_call_target="tpu_custom_call" | custom-call | flops 2147483648 | bytes 6291456 | tf_op jit(solution)/shard_map/query_weight_terms/pallas_call | solution.py:50
  201.4 3.6 %all-to-all-start.2 = ((bf16[8,128,1024]{2,1,0:T(8,128)(2,1)}), bf16[8,128,1024]{2,1,0:T(8,128)(2,1)S(1)}, u32[]{:S(2)}, u32[]{:S(2)}) async-start(bf16[8,128,1024]{2,1,0:T(8,128)(2,1)} %bitcast.55), calls=%async_computation.2 | async-start | bytes 4194304 | tf_op jit(solution)/shard_map/all_to_all | solution.py:426
  210.4 22.9 %all-to-all-done.2 = bf16[8,128,1024]{2,1,0:T(8,128)(2,1)S(1)} async-done(((bf16[8,128,1024]{2,1,0:T(8,128)(2,1)}), bf16[8,128,1024]{2,1,0:T(8,128)(2,1)S(1)}, u32[]{:S(2)}, u32[]{:S(2)}) %all-to-all-start.2) | async-done | bytes 2097184 | tf_op jit(solution)/shard_map/all_to_all | solution.py:426
  235.6 7.3 %collective-permute-done.18 = bf16[256,1024]{1,0:T(8,128)(2,1)S(1)} collective-permute-done((bf16[256,1024]{1,0:T(8,128)(2,1)S(1)}, bf16[256,1024]{1,0:T(8,128)(2,1)S(1)}, u32[]{:S(2)}, u32[]{:S(2)}) %collective-permute-start.18) | collective-permute-done | bytes 524320 | tf_op jit(solution)/shard_map/ppermute | solution.py:346
  (145 shorter events, 57.5 us)
Async XLA Ops:
  7.8 17.0 %collective-permute-start.1 = (bf16[256,1024]{1,0:T(8,128)(2,1)}, bf16[256,1024]{1,0:T(8,128)(2,1)S(1)}, u32[]{:S(2)}, u32[]{:S(2)}) collective-permute-start(bf16[256,1024]{1,0:T(8,128)(2,1)} %refs_1_.6), channel_id=1, source_target_pairs={{0,64},{64,0},{1,65},{65,1},{2,66},{66,2},{3,67},{67,3},{4,68},{68... | collective-permute-start | bytes 1572872 | tf_op jit(solution)/shard_map/ppermute | solution.py:346
  24.8 15.2 %collective-permute-start.7 = (bf16[256,1024]{1,0:T(8,128)(2,1)S(1)}, bf16[256,1024]{1,0:T(8,128)(2,1)S(1)}, u32[]{:S(2)}, u32[]{:S(2)}) collective-permute-start(bf16[256,1024]{1,0:T(8,128)(2,1)S(1)} %copy-done.3), channel_id=1, source_target_pairs={{0,64},{64,0},{1,65},{65,1},{2,66},{66,2},{3,67},{67,3},{4,68},{68... | collective-permute-start | bytes 1572872 | tf_op jit(solution)/shard_map/ppermute | solution.py:346
  41.2 53.6 %all-to-all-start = ((bf16[128,2,8,256]{3,2,1,0:T(8,128)(2,1)}), bf16[128,2,8,256]{3,2,1,0:T(8,128)(2,1)S(1)}, u32[]{:S(2)}, u32[]{:S(2)}) async-start(bf16[128,2,8,256]{3,2,1,0:T(8,128)(2,1)} %bitcast.8), calls=%async_computation | async-start | bytes 2097152 | tf_op jit(solution)/shard_map/all_to_all | solution.py:362
  58.5 15.3 %collective-permute-start.9 = (bf16[256,256]{1,0:T(8,128)(2,1)}, bf16[256,256]{1,0:T(8,128)(2,1)S(1)}, u32[]{:S(2)}, u32[]{:S(2)}) collective-permute-start(bf16[256,256]{1,0:T(8,128)(2,1)} %get-tuple-element.44), channel_id=1, source_target_pairs={{0,8},{8,16},{16,24},{24,0},{1,9},{9,17},{17,25},{25,1},{2,10},{10... | collective-permute-start | bytes 393224 | tf_op jit(solution)/shard_map/ppermute | solution.py:343
  67.6 33.4 %collective-permute-start.4 = (bf16[256,768]{1,0:T(8,128)(2,1)}, bf16[256,768]{1,0:T(8,128)(2,1)S(1)}, u32[]{:S(2)}, u32[]{:S(2)}) collective-permute-start(bf16[256,768]{1,0:T(8,128)(2,1)} %get-tuple-element.38), channel_id=1, source_target_pairs={{0,8},{8,16},{16,24},{24,0},{1,9},{9,17},{17,25},{25,1},{2,10},{10... | collective-permute-start | bytes 1179656 | tf_op jit(solution)/shard_map/ppermute | solution.py:343
  69.4 31.6 %collective-permute-start.5 = (bf16[256,768]{1,0:T(8,128)(2,1)}, bf16[256,768]{1,0:T(8,128)(2,1)S(1)}, u32[]{:S(2)}, u32[]{:S(2)}) collective-permute-start(bf16[256,768]{1,0:T(8,128)(2,1)} %get-tuple-element.39), channel_id=1, source_target_pairs={{0,16},{8,24},{16,0},{24,8},{1,17},{9,25},{17,1},{25,9},{2,18},{10... | collective-permute-start | bytes 1179656 | tf_op jit(solution)/shard_map/ppermute | solution.py:343
  71.1 29.9 %collective-permute-start.6 = (bf16[256,768]{1,0:T(8,128)(2,1)}, bf16[256,768]{1,0:T(8,128)(2,1)S(1)}, u32[]{:S(2)}, u32[]{:S(2)}) collective-permute-start(bf16[256,768]{1,0:T(8,128)(2,1)} %get-tuple-element.40), channel_id=1, source_target_pairs={{0,24},{8,0},{16,8},{24,16},{1,25},{9,1},{17,9},{25,17},{2,26},{10... | collective-permute-start | bytes 1179656 | tf_op jit(solution)/shard_map/ppermute | solution.py:343
  73.5 18.3 %collective-permute-start.10 = (bf16[256,256]{1,0:T(8,128)(2,1)S(1)}, bf16[256,256]{1,0:T(8,128)(2,1)S(1)}, u32[]{:S(2)}, u32[]{:S(2)}) collective-permute-start(bf16[256,256]{1,0:T(8,128)(2,1)S(1)} %copy-done.33), channel_id=1, source_target_pairs={{0,16},{8,24},{16,0},{24,8},{1,17},{9,25},{17,1},{25,9},{2,18},{10... | collective-permute-start | bytes 393224 | tf_op jit(solution)/shard_map/ppermute | solution.py:343
  73.8 21.0 %collective-permute-start.11 = (bf16[256,256]{1,0:T(8,128)(2,1)S(1)}, bf16[256,256]{1,0:T(8,128)(2,1)S(1)}, u32[]{:S(2)}, u32[]{:S(2)}) collective-permute-start(bf16[256,256]{1,0:T(8,128)(2,1)S(1)} %copy-done.32), channel_id=1, source_target_pairs={{0,24},{8,0},{16,8},{24,16},{1,25},{9,1},{17,9},{25,17},{2,26},{10... | collective-permute-start | bytes 393224 | tf_op jit(solution)/shard_map/ppermute | solution.py:343
  95.5 19.2 %all-to-all-start.1 = ((bf16[4,256,512]{2,1,0:T(8,128)(2,1)}), bf16[4,256,512]{2,1,0:T(8,128)(2,1)S(1)}, u32[]{:S(2)}, u32[]{:S(2)}) async-start(bf16[4,256,512]{2,1,0:T(8,128)(2,1)} %get-tuple-element.49), calls=%async_computation.1 | async-start | bytes 2097152 | tf_op jit(solution)/shard_map/all_to_all | solution.py:384
  99.9 134.6 %reduce-scatter.2.cloned.1.call-start = ((), (), s32[]{:S(2)}) async-start(), calls=%async_computation.5 | async-start | bytes 2621440 | tf_op jit(solution)/shard_map/reduce_scatter | solution.py:408
  114.6 17.3 %collective-permute-start.16 = (bf16[1024,512]{1,0:T(8,128)(2,1)S(1)}, bf16[1024,512]{1,0:T(8,128)(2,1)S(1)}, u32[]{:S(2)}, u32[]{:S(2)}) collective-permute-start(bf16[1024,512]{1,0:T(8,128)(2,1)S(1)} %bitcast.53), channel_id=1, source_target_pairs={{0,32},{32,0},{1,33},{33,1},{2,34},{34,2},{3,35},{35,3},{4,36},{36... | collective-permute-start | bytes 3145736 | tf_op jit(solution)/shard_map/ppermute | solution.py:346
  114.6 14.5 %collective-permute-start.13 = (bf16[256,1024]{1,0:T(8,128)(2,1)}, bf16[256,1024]{1,0:T(8,128)(2,1)S(1)}, u32[]{:S(2)}, u32[]{:S(2)}) collective-permute-start(bf16[256,1024]{1,0:T(8,128)(2,1)} %get-tuple-element.51.refs_0_), channel_id=1, source_target_pairs={{0,24},{8,0},{16,8},{24,16},{1,25},{9,1},{17,9},{25,17},{2,26},{10... | collective-permute-start | bytes 1572872 | tf_op jit(solution)/shard_map/ppermute | solution.py:343
  116.1 15.8 %collective-permute-start.12 = (bf16[256,1024]{1,0:T(8,128)(2,1)}, bf16[256,1024]{1,0:T(8,128)(2,1)S(1)}, u32[]{:S(2)}, u32[]{:S(2)}) collective-permute-start(bf16[256,1024]{1,0:T(8,128)(2,1)} %get-tuple-element.51.refs_0_), channel_id=1, source_target_pairs={{0,8},{8,16},{16,24},{24,0},{1,9},{9,17},{17,25},{25,1},{2,10},{10... | collective-permute-start | bytes 1572872 | tf_op jit(solution)/shard_map/ppermute | solution.py:343
  149.4 12.7 %collective-permute-start.21 = (bf16[1024,256]{1,0:T(8,128)(2,1)}, bf16[1024,256]{1,0:T(8,128)(2,1)}, u32[]{:S(2)}, u32[]{:S(2)}) collective-permute-start(bf16[1024,256]{1,0:T(8,128)(2,1)} %get-tuple-element.63.refs_1_), channel_id=1, source_target_pairs={{0,24},{8,0},{16,8},{24,16},{1,25},{9,1},{17,9},{25,17},{2,26},{10... | collective-permute-start | bytes 1572872 | tf_op jit(solution)/shard_map/ppermute | solution.py:343
  150.3 13.8 %collective-permute-start.20 = (bf16[1024,256]{1,0:T(8,128)(2,1)}, bf16[1024,256]{1,0:T(8,128)(2,1)}, u32[]{:S(2)}, u32[]{:S(2)}) collective-permute-start(bf16[1024,256]{1,0:T(8,128)(2,1)} %get-tuple-element.63.refs_1_), channel_id=1, source_target_pairs={{0,8},{8,16},{16,24},{24,0},{1,9},{9,17},{17,25},{25,1},{2,10},{10... | collective-permute-start | bytes 1572872 | tf_op jit(solution)/shard_map/ppermute | solution.py:343
  151.6 25.2 %collective-permute-start.19 = (bf16[4,256,512]{2,1,0:T(8,128)(2,1)S(1)}, bf16[4,256,512]{2,1,0:T(8,128)(2,1)S(1)}, u32[]{:S(2)}, u32[]{:S(2)}) collective-permute-start(bf16[4,256,512]{2,1,0:T(8,128)(2,1)S(1)} %pad_maximum_fusion.mine), channel_id=1, source_target_pairs={{0,32},{32,0},{1,33},{33,1},{2,34},{34,2},{3,35},{35,3},{4,36},{36... | collective-permute-start | bytes 3145736 | tf_op jit(solution)/shard_map/ppermute | solution.py:346
  164.2 37.3 %all-to-all-start.3 = ((bf16[128,2,8,256]{3,2,1,0:T(8,128)(2,1)}), bf16[128,2,8,256]{3,2,1,0:T(8,128)(2,1)S(1)}, u32[]{:S(2)}, u32[]{:S(2)}) async-start(bf16[128,2,8,256]{3,2,1,0:T(8,128)(2,1)} %pad_maximum_fusion.1), calls=%async_computation.4 | async-start | bytes 2097152 | tf_op jit(solution)/shard_map/all_to_all | solution.py:419
  172.6 18.2 %collective-permute-start.23 = (bf16[512,256]{1,0:T(8,128)(2,1)S(1)}, bf16[512,256]{1,0:T(8,128)(2,1)S(1)}, u32[]{:S(2)}, u32[]{:S(2)}) collective-permute-start(bf16[512,256]{1,0:T(8,128)(2,1)S(1)} %slice.66), channel_id=1, source_target_pairs={{0,24},{8,0},{16,8},{24,16},{1,25},{9,1},{17,9},{25,17},{2,26},{10... | collective-permute-start | bytes 786440 | tf_op jit(solution)/shard_map/ppermute | solution.py:343
  176.5 17.7 %collective-permute-start.22 = (bf16[512,256]{1,0:T(8,128)(2,1)S(1)}, bf16[512,256]{1,0:T(8,128)(2,1)S(1)}, u32[]{:S(2)}, u32[]{:S(2)}) collective-permute-start(bf16[512,256]{1,0:T(8,128)(2,1)S(1)} %slice.65), channel_id=1, source_target_pairs={{0,8},{8,16},{16,24},{24,0},{1,9},{9,17},{17,25},{25,1},{2,10},{10... | collective-permute-start | bytes 786440 | tf_op jit(solution)/shard_map/ppermute | solution.py:343
  190.2 15.0 %collective-permute-start.17 = (bf16[2,256,1024]{2,1,0:T(8,128)(2,1)}, bf16[2,256,1024]{2,1,0:T(8,128)(2,1)}, u32[]{:S(2)}, u32[]{:S(2)}) collective-permute-start(bf16[2,256,1024]{2,1,0:T(8,128)(2,1)} %get-tuple-element.57), channel_id=1, source_target_pairs={{0,32},{32,0},{1,33},{33,1},{2,34},{34,2},{3,35},{35,3},{4,36},{36... | collective-permute-start | bytes 3145736 | tf_op jit(solution)/shard_map/ppermute | solution.py:346
  201.4 31.9 %all-to-all-start.2 = ((bf16[8,128,1024]{2,1,0:T(8,128)(2,1)}), bf16[8,128,1024]{2,1,0:T(8,128)(2,1)S(1)}, u32[]{:S(2)}, u32[]{:S(2)}) async-start(bf16[8,128,1024]{2,1,0:T(8,128)(2,1)} %bitcast.55), calls=%async_computation.2 | async-start | bytes 4194304 | tf_op jit(solution)/shard_map/all_to_all | solution.py:426
  207.5 35.5 %collective-permute-start.18 = (bf16[256,1024]{1,0:T(8,128)(2,1)S(1)}, bf16[256,1024]{1,0:T(8,128)(2,1)S(1)}, u32[]{:S(2)}, u32[]{:S(2)}) collective-permute-start(bf16[256,1024]{1,0:T(8,128)(2,1)S(1)} %fusion.2), channel_id=1, source_target_pairs={{0,64},{64,0},{1,65},{65,1},{2,66},{66,2},{3,67},{67,3},{4,68},{68... | collective-permute-start | bytes 1572872 | tf_op jit(solution)/shard_map/ppermute | solution.py:346
  235.6 12.5 %collective-permute-start.24 = (bf16[1024,128]{1,0:T(8,128)(2,1)S(1)}, bf16[1024,128]{1,0:T(8,128)(2,1)S(1)}, u32[]{:S(2)}, u32[]{:S(2)}) collective-permute-start(bf16[1024,128]{1,0:T(8,128)(2,1)S(1)} %dynamic-slice_bitcast_fusion), channel_id=1, source_target_pairs={{0,1},{1,0},{2,3},{3,2},{4,5},{5,4},{6,7},{7,6},{8,9},{9,8},{10,11... | collective-permute-start | bytes 786440 | tf_op jit(solution)/shard_map/ppermute | solution.py:346
  (43 other events, 307.7 us)
Sparse Core Ops, SparseCore 0:
  148.2 37.9 reduce-scatter.1

commit v7 on v6

--- a/solution.py
+++ b/solution.py
@@ -16,7 +16,7 @@
 AXES = (("xh", 2), ("core", 2), ("z", 4), ("y", 4), ("xl", 2))
 HEADS = ("xh", "core")
 SEQ = ("z", "y", "xl")
-XH, CORE, Z = range(3)
+XH, CORE, Z, Y, XL = range(5)
 SWAP = [(0, 1), (1, 0)]
 VMEM = 56 * 1024 * 1024
 TOK = 256
@@ -82,27 +82,33 @@
         out[...] = product if i == 0 else out[...] + product
 
 
-def far_kernel(transposed, joined, pos, x0, x1, x2, x3, before, w_ref, *refs):
-    rows, (total, weights, sems) = refs[:4], refs[-3:]
+def far_kernel(transposed, pos, x0, x1, x2, x3, before, w_ref, *refs):
+    states, refs = (None, refs) if len(refs) == 11 else (refs[0], refs[1:])
+    rows, parts, (blocks, known, total, weights, weight_sems, sems) = refs[:4], refs[4], refs[5:]
     contract = ((1,), (1,)) if transposed else ((1,), (0,))
-    copies = weight_copies(pos, w_ref, weights, sems, (2, 3), transposed)
+    weight_moves = weight_copies(pos, w_ref, weights, weight_sems, (2, 3), transposed)
+    moves = [pltpu.make_async_copy(before, known, sems.at[4])]
+    moves[0].start()
+    for i, x in ((2, x2), (3, x3), (0, x0), (1, x1)):
+        moves.append(pltpu.make_async_copy(x, blocks.at[i], sems.at[i]))
+        moves[-1].start()
     half = pl.multiple_of(pos[CORE] * (BLOCK // 2), BLOCK // 2)
-    for i, x in enumerate((x0, x1, x2, x3)):
-        part = x[:, pl.ds(half, BLOCK // 2)]
-        if joined:
-            for d in range(4):
-
-                @pl.when(shifted(pos[Z], d) == head_block(i, pos))
-                def _(d=d, part=part):
-                    rows[d][:, PIECE:] = part
+    if states is not None:
+        parts[:, 0] = states[...]
+    for move in moves:
+        move.wait()
+    for i in range(4):
+        part = blocks[i, :, pl.ds(half, BLOCK // 2)]
+        if states is None:
+            parts[head_block(i, pos)] = part
         else:
-            refs[4][head_block(i, pos)] = part
-    for i, (x, known) in enumerate(((x2, before), (x3, total))):
-        copies[i].wait()
-        total[...] = known[...] + dot(x[...], weights[i], contract)
+            parts[head_block(i, pos), 1] = part
+    for i, start in ((2, known), (3, total)):
+        weight_moves[i - 2].wait()
+        total[...] = start[...] + dot(blocks[i], weights[i - 2], contract)
     for d in range(4):
         start = pl.multiple_of(shifted(pos[Z], d) * PIECE, PIECE)
-        rows[d][:, :PIECE] = total[:, pl.ds(start, PIECE)].astype(BF16)
+        rows[d][...] = total[:, pl.ds(start, PIECE)].astype(BF16)
 
 
 HBM = pl.BlockSpec(memory_space=pltpu.HBM)
@@ -125,20 +131,23 @@
     )
 
 
-def far_project(name, pos, blocks, weight, transposed, joined, before):
-    wide = PIECE + BLOCK // 2 if joined else PIECE
-    shapes = [(TOK, wide)] * 4 + ([] if joined else [(4, TOK, BLOCK // 2)])
+def far_project(name, pos, blocks, weight, transposed, before, states=None):
+    part = (4, TOK, BLOCK // 2) if states is None else (4, 2, TOK, BLOCK // 2)
+    extra = () if states is None else (states,)
     outs = call(
-        lambda *refs: far_kernel(transposed, joined, *refs),
+        lambda *refs: far_kernel(transposed, *refs),
         name,
         (1,),
-        [whole((TOK, BLOCK))] * 5 + [HBM],
-        [whole(shape) for shape in shapes],
-        [struct(shape) for shape in shapes],
+        [HBM] * 6 + [whole(a.shape) for a in extra],
+        [whole((TOK, PIECE))] * 4 + [whole(part)],
+        [struct((TOK, PIECE))] * 4 + [struct(part)],
         [
+            pltpu.VMEM((4, TOK, BLOCK), BF16),
+            pltpu.VMEM((TOK, BLOCK), F32),
             pltpu.VMEM((TOK, BLOCK), F32),
             pltpu.VMEM((2, BLOCK, BLOCK), BF16),
             pltpu.SemaphoreType.DMA((2,)),
+            pltpu.SemaphoreType.DMA((5,)),
         ],
         4 * TOK * BLOCK * BLOCK,
         4 * BLOCK * BLOCK,
@@ -146,49 +155,31 @@
         *blocks,
         before,
         weight,
-    )
-    return outs[:4], outs[4:]
-
-
-def assemble_kernel(pos, mine, other, out):
+        *extra,
+    )
+    return outs[:4], outs[4]
+
+
+def assemble_kernel(turned, pos, mine, other, out):
     for side, ref in enumerate((mine, other)):
         half = pl.multiple_of(lax.rem(pos[CORE] + side, 2) * (BLOCK // 2), BLOCK // 2)
-        out[:, pl.ds(half, BLOCK // 2)] = ref[...]
-
-
-def assemble(name, pos, mine, other):
+        for layer in range(4):
+            token = slice(layer * TOK, (layer + 1) * TOK)
+            if turned:
+                out[pl.ds(half, BLOCK // 2), token] = ref[layer, 0].T
+            else:
+                out[token, pl.ds(half, BLOCK // 2)] = ref[layer, 0]
+
+
+def assemble(name, pos, mine, other, which, turned):
+    half = pl.BlockSpec((4, 1, TOK, BLOCK // 2), lambda i, pos: (0, which, 0, 0))
     return call(
-        assemble_kernel,
+        lambda *refs: assemble_kernel(turned, *refs),
         name,
         (1,),
-        [whole((GROUP, BLOCK // 2))] * 2,
+        [half] * 2,
         whole((GROUP, BLOCK)),
         struct((GROUP, BLOCK)),
-        [],
-        0,
-        4 * BLOCK * GROUP,
-        pos,
-        mine,
-        other,
-    )
-
-
-def assemble_turned_kernel(pos, mine, other, out):
-    for d in range(4):
-        token = pl.multiple_of(shifted(pos[Z], -d) * TOK, TOK)
-        for side, ref in enumerate((mine, other)):
-            half = pl.multiple_of(lax.rem(pos[CORE] + side, 2) * (BLOCK // 2), BLOCK // 2)
-            out[pl.ds(half, BLOCK // 2), pl.ds(token, TOK)] = ref[d].T
-
-
-def assemble_turned(name, pos, mine, other):
-    return call(
-        assemble_turned_kernel,
-        name,
-        (1,),
-        [whole((4, TOK, BLOCK // 2))] * 2,
-        whole((BLOCK, GROUP)),
-        struct((BLOCK, GROUP)),
         [],
         0,
         4 * BLOCK * GROUP,
@@ -250,13 +241,15 @@
 
 
 def output_grad_kernel(pos, *refs):
-    left, right, out = refs[:5], refs[5], refs[6]
+    left, right, outs, held = refs[:5], refs[5], refs[6:10], refs[10]
     for ref, (e, part) in zip(left, GATHERED):
         rows = ref.shape[0]
         row = pl.multiple_of(shifted(pos[Z], -e) * PIECE + part * rows, rows)
         product = dot(ref[...], right[...]).astype(BF16)
         for p in range(PLANES):
-            out[p, pl.ds(row, rows), :] = product[:, p * 128 : (p + 1) * 128]
+            held[p, pl.ds(row, rows), :] = product[:, p * 128 : (p + 1) * 128]
+    for d in range(4):
+        outs[d][...] = held[pl.ds(shifted(pos[Y], d) * 2, 2)]
 
 
 def query_grad_kernel(pos, *refs):
@@ -269,15 +262,15 @@
     out[:, pl.ds(col, PIECE)] = dot(left[...], far).astype(BF16)
 
 
-def weight_terms(name, kernel, pos, args, out):
+def weight_terms(name, kernel, pos, args, out, count, scratch):
     return call(
         kernel,
         name,
         (1,),
         [whole(a.shape) for a in args],
-        whole(out),
-        struct(out),
-        [],
+        [whole(out)] * count,
+        [struct(out)] * count,
+        scratch,
         2 * GROUP * BLOCK * BLOCK,
         6 * BLOCK * BLOCK,
         pos,
@@ -348,13 +341,13 @@
     def after(x, *others):
         return lax.optimization_barrier((x, *others))[0]
 
-    def near(name, local, weight, transposed):
+    def near(name, local, weight, transposed, *others):
         blocks = (local, swap(local, "core"))
-        return blocks, near_project(name, pos, blocks, weight, transposed)
-
-    def far(name, blocks, over_x, weight, transposed, joined, first):
+        return blocks, near_project(name, pos, after(blocks, *others), weight, transposed)
+
+    def far(name, blocks, over_x, weight, transposed, first, *extra):
         blocks = blocks + (over_x, swap(over_x, "core"))
-        rows, parts = far_project(name, pos, blocks, weight, transposed, joined, first)
+        rows, parts = far_project(name, pos, blocks, weight, transposed, first, *extra)
         return [to_layer(x, d) for d, x in enumerate(rows)], parts
 
     own = jnp.stack([context_keys, context_values]).reshape(2, 8, 16, PIECE).transpose(2, 0, 1, 3)
@@ -364,11 +357,10 @@
     values = context[:, 1].reshape(4 * TOK, PIECE)
     bias = context_bias(lengths, slot_passage)
 
-    states_x = swap(decoder_states, "xh")
+    states_x, cotangent_x = swap(decoder_states, "xh"), swap(output_cotangent, "xh")
     states, first_queries = near("queries_near", decoder_states, query_weight, False)
-    cotangent, first_grad = near("heads_grad_near", output_cotangent, output_weight, True)
-    states_x = after(states_x, first_queries, first_grad)
-    cotangent_x = swap(after(output_cotangent, states_x), "xh")
+    cotangent, first_grad = near("heads_grad_near", output_cotangent, output_weight, True, keys)
+    states_x, cotangent_x = after((states_x, cotangent_x), first_queries, first_grad)
 
     def ring_ends(x):
         return to_layer(x, 1), to_layer(x, 3)
@@ -377,52 +369,59 @@
         half = x.shape[0] // 2
         return x, left, right, to_layer(left[:half], 1), to_layer(right[half:], 3)
 
-    queries, _ = far("queries", states, states_x, query_weight, False, True, first_queries)
+    queries, state_parts = far(
+        "queries", states, states_x, query_weight, False, after(first_queries, keys)
+    )
     heads_grad, parts = far(
-        "heads_grad", cotangent, cotangent_x, output_weight, True, False, after(first_grad, first_queries)
-    )
-    cotangent_block = lax.all_to_all(after(parts[0], *heads_grad), "z", 0, 0, tiled=True)
-    cotangent_block = cotangent_block.reshape(GROUP, BLOCK // 2)
+        "heads_grad", cotangent, cotangent_x, output_weight, True, first_grad, state_parts
+    )
+    column_parts = lax.all_to_all(after(parts, *heads_grad), "z", 0, 0, tiled=True)
 
     turned_out, query_grad, key_terms, value_terms = attention(
         pos, bias, queries, heads_grad, keys, values
     )
     left, right = ring_ends(turned_out)
     every_out = ring(turned_out, left, right)
-    query_grad = after(query_grad, left, right)
+    query_grad, key_terms, value_terms = after((query_grad, key_terms, value_terms), left, right)
     left, right = ring_ends(query_grad)
     every_query_grad = ring(query_grad, left, right)
 
-    cotangent_block = after(cotangent_block, turned_out)
-    group_cotangent = assemble("group_cotangent", pos, cotangent_block, swap(cotangent_block, "core"))
-    state_block = jnp.stack([x[:, PIECE:] for x in after(queries, turned_out)])
-    group_states = assemble_turned("group_states", pos, state_block, swap(state_block, "core"))
+    column_parts = after(column_parts, turned_out)
+    other_parts = swap(column_parts, "core")
+    group_cotangent = assemble("group_cotangent", pos, column_parts, other_parts, 1, False)
+    group_states = assemble("group_states", pos, column_parts, other_parts, 0, True)
+
+    def along_y(x, d):
+        return lax.ppermute(x, "y", [(i, (i + d) % 4) for i in range(4)]) if d else x
 
     terms = weight_terms(
         "output_weight_terms",
         output_grad_kernel,
         pos,
-        (*every_out, group_cotangent),
-        (PLANES, BLOCK, 128),
-    )
-    pair = lax.psum_scatter(terms, "y", scatter_dimension=0, tiled=True)
-    xl = lax.axis_index("xl")
-    kept, given = (lax.dynamic_index_in_dim(pair, i, 0, False) for i in (xl, 1 - xl))
-    output_weight_grad = kept.astype(F32) + swap(given, "xl").astype(F32)
+        (*after(every_out, left, right), group_cotangent),
+        (2, BLOCK, 128),
+        4,
+        [pltpu.VMEM((PLANES, BLOCK, 128), BF16)],
+    )
     every_out = after(every_out, terms)
+    terms = after(terms, every_query_grad)
+    total = sum(along_y(x, d).astype(F32) for d, x in enumerate(terms))
+    kept, given = (lax.dynamic_index_in_dim(total, i, 0, False) for i in (pos[XL], 1 - pos[XL]))
+    output_weight_grad = kept + swap(given.astype(BF16), "xl").astype(F32)
 
     give, keep = output_terms(pos, every_out, output_weight)
     pair = keep + swap(give, "core").astype(F32)
     attended = (pair[0] + swap(pair[1].astype(BF16), "xh").astype(F32)).astype(BF16)
 
     terms = jnp.stack([key_terms.reshape(128, 8, PIECE), value_terms.reshape(128, 8, PIECE)], 1)
-    moved = lax.all_to_all(after(terms, left, right), HEADS + SEQ, 0, 0, tiled=True)
+    moved = lax.all_to_all(terms, HEADS + SEQ, 0, 0, tiled=True)
     owned = jnp.sum(moved.reshape(16, PLANES, 2, 8, PIECE).astype(F32), axis=1)
     owned = owned.transpose(1, 2, 0, 3).reshape(2, 8, 16 * PIECE)
 
-    terms = weight_terms(
-        "query_weight_terms", query_grad_kernel, pos, (group_states, *every_query_grad), (BLOCK, BLOCK)
-    )
+    (terms,) = weight_terms(
+        "query_weight_terms", query_grad_kernel, pos, (group_states, *after(every_query_grad, moved)), (BLOCK, BLOCK), 1, []
+    )
+    terms = after(terms, pair)
     terms = lax.all_to_all(terms.reshape(PLANES, 128, BLOCK), ("y", "xl"), 0, 0, tiled=True)
     query_weight_grad = jnp.sum(terms.astype(F32), axis=0)
     return attended, query_weight_grad, output_weight_grad, owned[0], owned[1]

time: 257 us -> 281 us (1.093)
  starting transfers between devices: 52.5 us -> 93.2 us
  between operations: 14.5 us -> 1.01 us
  local copies, waits for them, and re-layouts: 16.8 us -> 11.4 us
    all_to_all x1, waiting for transfers between devices: 22.9 us -> 0.01 us  [on_device(): lax.all_to_all(terms.reshape(PLANES, 128, BLOCK), ('y', 'xl'), 0, 0, tile...]
    ppermute x11 -> x10, starting transfers between devices: 7.99 us -> 30.6 us  [swap(): return lax.ppermute(x, axis, SWAP)]
    all_to_all x1, waiting for transfers between devices: 0.01 us -> 8.3 us  [on_device(): context = lax.all_to_all(own, HEADS + SEQ, 0, 0, tiled=True)]
    all_to_all x2, starting transfers between devices: 12 us -> 20.2 us  [the longest x1 16.6 us: on_device(): moved = lax.all_to_all(terms, HEADS + SEQ, 0, 0, tiled=True)]
    ppermute x0 -> x3, waiting for transfers between devices: none -> 7.92 us  [along_y(): lax.ppermute(x, 'y', [(i, (i + d) % 4) for i in range(4)])]
    ppermute x0 -> x3, starting transfers between devices: none -> 5.74 us  [along_y(): lax.ppermute(x, 'y', [(i, (i + d) % 4) for i in range(4)])]
    ppermute x11 -> x10, waiting for transfers between devices: 23.8 us -> 28.7 us  [swap(): return lax.ppermute(x, axis, SWAP)]
    unnamed x75 -> x49, local copies, waits for them, and re-layouts: 10.1 us -> 5.18 us
  transfers between devices with their start and end apart: 30 -> 31, of which waited for: 14 -> 14; matrix products, arithmetic and copies ran while one was open for 6% -> 5% of each run, Pallas kernels for 23% -> 21%
where the time goes in v7:
time: 281 us; the launch traced here: 280 us
  waiting for transfers between devices  98 us (35%)
  starting transfers between devices  93.2 us (33%)
  Pallas kernels  66.5 us (24%)
  local copies, waits for them, and re-layouts  11.4 us (4%)
  other arithmetic  10.1 us (4%)
    pallas_call x10, Pallas kernels, call(): pl.pallas_call(kernel, grid_spec=pltpu.PrefetchScalarGridSpec(num_scalar_...  66.5 us
    ppermute x14, waiting for transfers between devices, to_layer(): lax.ppermute(x, 'z', [(i, (i + d) % 4) for i in range(4)])  53.1 us
    ppermute x10, starting transfers between devices, swap(): return lax.ppermute(x, axis, SWAP)  30.6 us
    ppermute x10, waiting for transfers between devices, swap(): return lax.ppermute(x, axis, SWAP)  28.7 us
    ppermute x14, starting transfers between devices, to_layer(): lax.ppermute(x, 'z', [(i, (i + d) % 4) for i in range(4)])  21.9 us
    all_to_all x1, starting transfers between devices, on_device(): moved = lax.all_to_all(terms, HEADS + SEQ, 0, 0, tiled=True)  16.6 us
    all_to_all x1, starting transfers between devices, on_device(): context = lax.all_to_all(own, HEADS + SEQ, 0, 0, tiled=True)  11.1 us
    all_to_all x1, waiting for transfers between devices, on_device(): context = lax.all_to_all(own, HEADS + SEQ, 0, 0, tiled=True)  8.3 us
  transfers between devices with their start and end apart: 31, of which 14 were waited for; matrix products, arithmetic and copies ran while one was open for 5% of the time, Pallas kernels for 21%

profile of v7, /device:TPU:0, one launch (start us, length us, event | category | flops | bytes accessed | tf_op | source)
XLA Modules:
  0.0 280.2 jit_solution(15730911276279840286)
XLA Ops:
  2.7 11.1 %all-to-all-start = ((bf16[128,2,8,256]{3,2,1,0:T(8,128)(2,1)}), bf16[128,2,8,256]{3,2,1,0:T(8,128)(2,1)S(1)}, u32[]{:S(2)}, u32[]{:S(2)}) async-start(bf16[128,2,8,256]{3,2,1,0:T(8,128)(2,1)} %bitcast.8), calls=%async_computation | async-start | bytes 2097152 | tf_op jit(solution)/shard_map/all_to_all | solution.py:355
  19.4 5.8 %queries_near.1.refs_5_ = f32[256,1024]{1,0:T(8,128)} custom-call(s32[5]{0:T(128)} %stack.35.refs_0_.pos, bf16[256,1024]{1,0:T(8,128)(2,1)} %refs_1_.4, bf16[256,1024]{1,0:T(8,128)(2,1)} %copy-done.6, bf16[4096,1024]{1,0:T(8,128)(2,1)} %refs_6_.2), custom_call_target="tpu_custom_call" | custom-call | flops 1073741824 | bytes 4194304 | tf_op jit(solution)/shard_map/queries_near/pallas_call | solution.py:50
  25.2 8.3 %all-to-all-done = bf16[128,2,8,256]{3,2,1,0:T(8,128)(2,1)S(1)} async-done(((bf16[128,2,8,256]{3,2,1,0:T(8,128)(2,1)}), bf16[128,2,8,256]{3,2,1,0:T(8,128)(2,1)S(1)}, u32[]{:S(2)}, u32[]{:S(2)}) %all-to-all-start) | async-done | bytes 1048608 | tf_op jit(solution)/shard_map/all_to_all | solution.py:355
  35.4 5.8 %heads_grad_near.1.refs_5_ = f32[256,1024]{1,0:T(8,128)} custom-call(s32[5]{0:T(128)} %stack.35.refs_0_.pos, bf16[256,1024]{1,0:T(8,128)(2,1)} %refs_1_.5, bf16[256,1024]{1,0:T(8,128)(2,1)} %copy-done.5, bf16[1024,4096]{1,0:T(8,128)(2,1)} %refs_5_.1), custom_call_target="tpu_custom_call" | custom-call | flops 1073741824 | bytes 4194304 | tf_op jit(solution)/shard_map/heads_grad_near/pallas_call | solution.py:50
  41.2 9.3 %collective-permute-done.2.refs_3_ = bf16[256,1024]{1,0:T(8,128)(2,1)} collective-permute-done((bf16[256,1024]{1,0:T(8,128)(2,1)S(1)}, bf16[256,1024]{1,0:T(8,128)(2,1)}, u32[]{:S(2)}, u32[]{:S(2)}) %collective-permute-start.2) | collective-permute-done | bytes 524320 | tf_op jit(solution)/shard_map/ppermute | solution.py:339
  53.4 6.5 %queries.1 = (bf16[256,256]{1,0:T(8,128)(2,1)}, bf16[256,256]{1,0:T(8,128)(2,1)}, bf16[256,256]{1,0:T(8,128)(2,1)}, bf16[256,256]{1,0:T(8,128)(2,1)}, bf16[4,256,512]{2,1,0:T(8,128)(2,1)}) custom-call(s32[5]{0:T(128)} %stack.35.refs_0_.pos, bf16[256,1024]{1,0:T(8,128)(2,1)} %refs_1_.4, bf16[256,1024]{1,0:T(8,128)(2,1)} %copy-done.6, ...), custom_call_target="tpu_custom_call" | custom-call | flops 1073741824 | bytes 4194304 | tf_op jit(solution)/shard_map/queries/pallas_call | solution.py:50
  60.7 8.2 %heads_grad.1 = (bf16[256,256]{1,0:T(8,128)(2,1)}, bf16[256,256]{1,0:T(8,128)(2,1)}, bf16[256,256]{1,0:T(8,128)(2,1)}, bf16[256,256]{1,0:T(8,128)(2,1)}, bf16[4,2,256,512]{3,2,1,0:T(8,128)(2,1)}) custom-call(s32[5]{0:T(128)} %stack.35.refs_0_.pos, bf16[256,1024]{1,0:T(8,128)(2,1)} %refs_1_.5, bf16[256,1024]{1,0:T(8,128)(2,1)} %copy-done.5, ...), custom_call_target="tpu_custom_call" | custom-call | flops 1073741824 | bytes 4194304 | tf_op jit(solution)/shard_map/heads_grad/pallas_call | solution.py:50
  76.4 4.0 %collective-permute-done.10.refs_6_ = bf16[256,256]{1,0:T(8,128)(2,1)S(1)} collective-permute-done((bf16[256,256]{1,0:T(8,128)(2,1)}, bf16[256,256]{1,0:T(8,128)(2,1)S(1)}, u32[]{:S(2)}, u32[]{:S(2)}) %collective-permute-start.10) | collective-permute-done | bytes 131104 | tf_op jit(solution)/shard_map/ppermute | solution.py:336
  81.0 3.6 %all-to-all-start.1 = ((bf16[4,2,256,512]{3,2,1,0:T(8,128)(2,1)}), bf16[4,2,256,512]{3,2,1,0:T(8,128)(2,1)S(1)}, u32[]{:S(2)}, u32[]{:S(2)}) async-start(bf16[4,2,256,512]{3,2,1,0:T(8,128)(2,1)} %get-tuple-element.84), calls=%async_computation.1 | async-start | bytes 4194304 | tf_op jit(solution)/shard_map/all_to_all | solution.py:378
  91.8 22.9 %collective-permute-done.5.refs_1_ = bf16[256,256]{1,0:T(8,128)(2,1)S(1)} collective-permute-done((bf16[256,256]{1,0:T(8,128)(2,1)S(1)}, bf16[256,256]{1,0:T(8,128)(2,1)S(1)}, u32[]{:S(2)}, u32[]{:S(2)}) %collective-permute-start.5) | collective-permute-done | bytes 131104 | tf_op jit(solution)/shard_map/ppermute | solution.py:336
  117.1 10.7 %attention.1 = (bf16[256,1024]{1,0:T(8,128)(2,1)}, bf16[1024,256]{1,0:T(8,128)(2,1)}, bf16[1024,256]{1,0:T(8,128)(2,1)}, bf16[1024,256]{1,0:T(8,128)(2,1)}) custom-call(s32[5]{0:T(128)} %stack.35.refs_0_.pos, f32[1,1024]{1,0:T(1,128)} %bitcast.51, bf16[256,256]{1,0:T(8,128)(2,1)} %get-tuple-element.63.refs_0_, bf16[256,256]{1,0:T(8,128)(2,1)} %copy-done.19, ...), custom_call_target="tpu_custom_call" | custom-call | flops 8053063680 | bytes 4194304 | tf_op jit(solution)/shard_map/attention/pallas_call | solution.py:50
  130.0 12.5 %collective-permute-done.13.refs_2_ = bf16[256,1024]{1,0:T(8,128)(2,1)S(1)} collective-permute-done((bf16[256,1024]{1,0:T(8,128)(2,1)}, bf16[256,1024]{1,0:T(8,128)(2,1)S(1)}, u32[]{:S(2)}, u32[]{:S(2)}) %collective-permute-start.13) | collective-permute-done | bytes 524320 | tf_op jit(solution)/shard_map/ppermute | solution.py:336
  150.8 16.6 %all-to-all-start.2 = ((bf16[128,2,8,256]{3,2,1,0:T(8,128)(2,1)}), bf16[128,2,8,256]{3,2,1,0:T(8,128)(2,1)S(1)}, u32[]{:S(2)}, u32[]{:S(2)}) async-start(bf16[128,2,8,256]{3,2,1,0:T(8,128)(2,1)} %pad_maximum_fusion), calls=%async_computation.2 | async-start | bytes 2097152 | tf_op jit(solution)/shard_map/all_to_all | solution.py:417
  167.4 3.7 %group_cotangent.1.refs_5_ = bf16[1024,1024]{1,0:T(8,128)(2,1)} custom-call(s32[5]{0:T(128)} %stack.35.refs_0_.pos, bf16[4,2,256,512]{3,2,1,0:T(8,128)(2,1)} %copy-done, bf16[4,2,256,512]{3,2,1,0:T(8,128)(2,1)} %collective-permute-done.18.refs_2_), custom_call_target="tpu_custom_call" | custom-call | bytes 4194304 | tf_op jit(solution)/shard_map/group_cotangent/pallas_call | solution.py:50
  171.1 6.8 %output_weight_terms.1 = (bf16[2,1024,128]{2,1,0:T(8,128)(2,1)}, bf16[2,1024,128]{2,1,0:T(8,128)(2,1)}, bf16[2,1024,128]{2,1,0:T(8,128)(2,1)}, bf16[2,1024,128]{2,1,0:T(8,128)(2,1)}) custom-call(s32[5]{0:T(128)} %stack.35.refs_0_.pos, bf16[256,1024]{1,0:T(8,128)(2,1)} %get-tuple-element.90.refs_0_, bf16[256,1024]{1,0:T(8,128)(2,1)} %copy-done.8, ...), custom_call_target="tpu_custom_call" | custom-call | flops 2147483648 | bytes 6291456 | tf_op jit(solution)/shard_map/output_weight_terms/pallas_call | solution.py:50
  177.9 8.2 %output_terms.1 = (bf16[2,256,1024]{2,1,0:T(8,128)(2,1)}, f32[2,256,1024]{2,1,0:T(8,128)}) custom-call(s32[5]{0:T(128)} %stack.35.refs_0_.pos, bf16[256,1024]{1,0:T(8,128)(2,1)} %get-tuple-element.90.refs_0_, bf16[256,1024]{1,0:T(8,128)(2,1)} %copy-done.8, bf16[256,1024]{1,0:T(8,128)(2,1)} %copy-done.7, bf16[128,1024]{1,0:T(8,128)(2,1)} %collective-permute-done.14.refs_3_, ...), custom_call_target="tpu_custom_call" | custom-call | flops 2147483648 | bytes 8388608 | tf_op jit(solution)/shard_map/output_terms/pallas_call | solution.py:50
  191.5 5.0 %collective-permute-done.22.refs_5_ = bf16[512,256]{1,0:T(8,128)(2,1)S(1)} collective-permute-done((bf16[512,256]{1,0:T(8,128)(2,1)S(1)}, bf16[512,256]{1,0:T(8,128)(2,1)S(1)}, u32[]{:S(2)}, u32[]{:S(2)}) %collective-permute-start.22) | collective-permute-done | bytes 262176 | tf_op jit(solution)/shard_map/ppermute | solution.py:336
  196.5 4.4 %collective-permute-done.21.refs_4_ = bf16[512,256]{1,0:T(8,128)(2,1)S(1)} collective-permute-done((bf16[512,256]{1,0:T(8,128)(2,1)S(1)}, bf16[512,256]{1,0:T(8,128)(2,1)S(1)}, u32[]{:S(2)}, u32[]{:S(2)}) %collective-permute-start.21) | collective-permute-done | bytes 262176 | tf_op jit(solution)/shard_map/ppermute | solution.py:336
  206.7 4.2 %group_states.1.refs_0_ = bf16[1024,1024]{1,0:T(8,128)(2,1)} custom-call(s32[5]{0:T(128)} %stack.35.refs_0_.pos, bf16[4,2,256,512]{3,2,1,0:T(8,128)(2,1)} %copy-done, bf16[4,2,256,512]{3,2,1,0:T(8,128)(2,1)} %collective-permute-done.18.refs_2_), custom_call_target="tpu_custom_call" | custom-call | bytes 4194304 | tf_op jit(solution)/shard_map/group_states/pallas_call | solution.py:50
  210.9 6.6 %query_weight_terms.1 = bf16[1024,1024]{1,0:T(8,128)(2,1)} custom-call(s32[5]{0:T(128)} %stack.35.refs_0_.pos, bf16[1024,1024]{1,0:T(8,128)(2,1)} %group_states.1.refs_0_, bf16[1024,256]{1,0:T(8,128)(2,1)} %get-tuple-element.99.refs_1_, bf16[1024,256]{1,0:T(8,128)(2,1)} %collective-permute-done.16.refs_2_, ...), custom_call_target="tpu_custom_call" | custom-call | flops 2147483648 | bytes 6291456 | tf_op jit(solution)/shard_map/query_weight_terms/pallas_call | solution.py:50
  223.0 6.8 %collective-permute-done.24 = bf16[2,1024,128]{2,1,0:T(8,128)(2,1)} collective-permute-done((bf16[2,1024,128]{2,1,0:T(8,128)(2,1)}, bf16[2,1024,128]{2,1,0:T(8,128)(2,1)}, u32[]{:S(2)}, u32[]{:S(2)}) %collective-permute-start.24) | collective-permute-done | bytes 524320 | tf_op jit(solution)/shard_map/ppermute | solution.py:395
  232.7 8.0 %collective-permute-start.26 = (bf16[1024,128]{1,0:T(8,128)(2,1)S(1)}, bf16[1024,128]{1,0:T(8,128)(2,1)S(1)}, u32[]{:S(2)}, u32[]{:S(2)}) collective-permute-start(bf16[1024,128]{1,0:T(8,128)(2,1)S(1)} %fusion.3), channel_id=1, source_target_pairs={{0,1},{1,0},{2,3},{3,2},{4,5},{5,4},{6,7},{7,6},{8,9},{9,8},{10,11... | collective-permute-start | bytes 786440 | tf_op jit(solution)/shard_map/ppermute | solution.py:339
  240.8 17.8 %collective-permute-start.20 = (bf16[256,1024]{1,0:T(8,128)(2,1)S(1)}, bf16[256,1024]{1,0:T(8,128)(2,1)S(1)}, u32[]{:S(2)}, u32[]{:S(2)}) collective-permute-start(bf16[256,1024]{1,0:T(8,128)(2,1)S(1)} %fusion.2), channel_id=1, source_target_pairs={{0,64},{64,0},{1,65},{65,1},{2,66},{66,2},{3,67},{67,3},{4,68},{68... | collective-permute-start | bytes 1572872 | tf_op jit(solution)/shard_map/ppermute | solution.py:339
  260.3 17.8 %collective-permute-done.20 = bf16[256,1024]{1,0:T(8,128)(2,1)S(1)} collective-permute-done((bf16[256,1024]{1,0:T(8,128)(2,1)S(1)}, bf16[256,1024]{1,0:T(8,128)(2,1)S(1)}, u32[]{:S(2)}, u32[]{:S(2)}) %collective-permute-start.20) | collective-permute-done | bytes 524320 | tf_op jit(solution)/shard_map/ppermute | solution.py:339
  (118 shorter events, 64.6 us)
Async XLA Ops:
  2.7 30.8 %all-to-all-start = ((bf16[128,2,8,256]{3,2,1,0:T(8,128)(2,1)}), bf16[128,2,8,256]{3,2,1,0:T(8,128)(2,1)S(1)}, u32[]{:S(2)}, u32[]{:S(2)}) async-start(bf16[128,2,8,256]{3,2,1,0:T(8,128)(2,1)} %bitcast.8), calls=%async_computation | async-start | bytes 2097152 | tf_op jit(solution)/shard_map/all_to_all | solution.py:355
  14.0 20.6 %collective-permute-start.3 = (bf16[256,1024]{1,0:T(8,128)(2,1)S(1)}, bf16[256,1024]{1,0:T(8,128)(2,1)S(1)}, u32[]{:S(2)}, u32[]{:S(2)}) collective-permute-start(bf16[256,1024]{1,0:T(8,128)(2,1)S(1)} %copy-done.4), channel_id=1, source_target_pairs={{0,32},{32,0},{1,33},{33,1},{2,34},{34,2},{3,35},{35,3},{4,36},{36... | collective-permute-start | bytes 1572872 | tf_op jit(solution)/shard_map/ppermute | solution.py:339
  14.5 26.7 %collective-permute-start.1 = (bf16[256,1024]{1,0:T(8,128)(2,1)S(1)}, bf16[256,1024]{1,0:T(8,128)(2,1)}, u32[]{:S(2)}, u32[]{:S(2)}) collective-permute-start(bf16[256,1024]{1,0:T(8,128)(2,1)S(1)} %copy-done.3), channel_id=1, source_target_pairs={{0,64},{64,0},{1,65},{65,1},{2,66},{66,2},{3,67},{67,3},{4,68},{68... | collective-permute-start | bytes 1572872 | tf_op jit(solution)/shard_map/ppermute | solution.py:339
  16.9 33.5 %collective-permute-start.2 = (bf16[256,1024]{1,0:T(8,128)(2,1)S(1)}, bf16[256,1024]{1,0:T(8,128)(2,1)}, u32[]{:S(2)}, u32[]{:S(2)}) collective-permute-start(bf16[256,1024]{1,0:T(8,128)(2,1)S(1)} %copy-done.4), channel_id=1, source_target_pairs={{0,64},{64,0},{1,65},{65,1},{2,66},{66,2},{3,67},{67,3},{4,68},{68... | collective-permute-start | bytes 1572872 | tf_op jit(solution)/shard_map/ppermute | solution.py:339
  70.6 9.7 %collective-permute-start.10 = (bf16[256,256]{1,0:T(8,128)(2,1)}, bf16[256,256]{1,0:T(8,128)(2,1)S(1)}, u32[]{:S(2)}, u32[]{:S(2)}) collective-permute-start(bf16[256,256]{1,0:T(8,128)(2,1)} %get-tuple-element.71), channel_id=1, source_target_pairs={{0,16},{8,24},{16,0},{24,8},{1,17},{9,25},{17,1},{25,9},{2,18},{10... | collective-permute-start | bytes 393224 | tf_op jit(solution)/shard_map/ppermute | solution.py:336
  81.0 46.7 %all-to-all-start.1 = ((bf16[4,2,256,512]{3,2,1,0:T(8,128)(2,1)}), bf16[4,2,256,512]{3,2,1,0:T(8,128)(2,1)S(1)}, u32[]{:S(2)}, u32[]{:S(2)}) async-start(bf16[4,2,256,512]{3,2,1,0:T(8,128)(2,1)} %get-tuple-element.84), calls=%async_computation.1 | async-start | bytes 4194304 | tf_op jit(solution)/shard_map/all_to_all | solution.py:378
  84.9 29.8 %collective-permute-start.5 = (bf16[256,256]{1,0:T(8,128)(2,1)S(1)}, bf16[256,256]{1,0:T(8,128)(2,1)S(1)}, u32[]{:S(2)}, u32[]{:S(2)}) collective-permute-start(bf16[256,256]{1,0:T(8,128)(2,1)S(1)} %copy-done.15), channel_id=1, source_target_pairs={{0,8},{8,16},{16,24},{24,0},{1,9},{9,17},{17,25},{25,1},{2,10},{10... | collective-permute-start | bytes 393224 | tf_op jit(solution)/shard_map/ppermute | solution.py:336
  87.0 29.4 %collective-permute-start.6 = (bf16[256,256]{1,0:T(8,128)(2,1)S(1)}, bf16[256,256]{1,0:T(8,128)(2,1)S(1)}, u32[]{:S(2)}, u32[]{:S(2)}) collective-permute-start(bf16[256,256]{1,0:T(8,128)(2,1)S(1)} %copy-done.14), channel_id=1, source_target_pairs={{0,16},{8,24},{16,0},{24,8},{1,17},{9,25},{17,1},{25,9},{2,18},{10... | collective-permute-start | bytes 393224 | tf_op jit(solution)/shard_map/ppermute | solution.py:336
  89.6 26.7 %collective-permute-start.7 = (bf16[256,256]{1,0:T(8,128)(2,1)S(1)}, bf16[256,256]{1,0:T(8,128)(2,1)S(1)}, u32[]{:S(2)}, u32[]{:S(2)}) collective-permute-start(bf16[256,256]{1,0:T(8,128)(2,1)S(1)} %copy-done.13), channel_id=1, source_target_pairs={{0,24},{8,0},{16,8},{24,16},{1,25},{9,1},{17,9},{25,17},{2,26},{10... | collective-permute-start | bytes 393224 | tf_op jit(solution)/shard_map/ppermute | solution.py:336
  127.8 39.6 %collective-permute-start.18 = (bf16[4,2,256,512]{3,2,1,0:T(8,128)(2,1)S(1)}, bf16[4,2,256,512]{3,2,1,0:T(8,128)(2,1)}, u32[]{:S(2)}, u32[]{:S(2)}) collective-permute-start(bf16[4,2,256,512]{3,2,1,0:T(8,128)(2,1)S(1)} %all-to-all-done.1.refs_1_), channel_id=1, source_target_pairs={{0,32},{32,0},{1,33},{33,1},{2,34},{34,2},{3,35},{35,3},{4,36},{36... | collective-permute-start | bytes 6291464 | tf_op jit(solution)/shard_map/ppermute | solution.py:339
  127.9 14.5 %collective-permute-start.13 = (bf16[256,1024]{1,0:T(8,128)(2,1)}, bf16[256,1024]{1,0:T(8,128)(2,1)S(1)}, u32[]{:S(2)}, u32[]{:S(2)}) collective-permute-start(bf16[256,1024]{1,0:T(8,128)(2,1)} %get-tuple-element.90.refs_0_), channel_id=1, source_target_pairs={{0,24},{8,0},{16,8},{24,16},{1,25},{9,1},{17,9},{25,17},{2,26},{10... | collective-permute-start | bytes 1572872 | tf_op jit(solution)/shard_map/ppermute | solution.py:336
  127.9 15.7 %collective-permute-start.12 = (bf16[256,1024]{1,0:T(8,128)(2,1)}, bf16[256,1024]{1,0:T(8,128)(2,1)S(1)}, u32[]{:S(2)}, u32[]{:S(2)}) collective-permute-start(bf16[256,1024]{1,0:T(8,128)(2,1)} %get-tuple-element.90.refs_0_), channel_id=1, source_target_pairs={{0,8},{8,16},{16,24},{24,0},{1,9},{9,17},{17,25},{25,1},{2,10},{10... | collective-permute-start | bytes 1572872 | tf_op jit(solution)/shard_map/ppermute | solution.py:336
  143.6 23.8 %collective-permute-start.17 = (bf16[1024,256]{1,0:T(8,128)(2,1)}, bf16[1024,256]{1,0:T(8,128)(2,1)}, u32[]{:S(2)}, u32[]{:S(2)}) collective-permute-start(bf16[1024,256]{1,0:T(8,128)(2,1)} %get-tuple-element.99.refs_1_), channel_id=1, source_target_pairs={{0,24},{8,0},{16,8},{24,16},{1,25},{9,1},{17,9},{25,17},{2,26},{10... | collective-permute-start | bytes 1572872 | tf_op jit(solution)/shard_map/ppermute | solution.py:336
  144.0 23.4 %collective-permute-start.16 = (bf16[1024,256]{1,0:T(8,128)(2,1)}, bf16[1024,256]{1,0:T(8,128)(2,1)}, u32[]{:S(2)}, u32[]{:S(2)}) collective-permute-start(bf16[1024,256]{1,0:T(8,128)(2,1)} %get-tuple-element.99.refs_1_), channel_id=1, source_target_pairs={{0,8},{8,16},{16,24},{24,0},{1,9},{9,17},{17,25},{25,1},{2,10},{10... | collective-permute-start | bytes 1572872 | tf_op jit(solution)/shard_map/ppermute | solution.py:336
  145.7 21.7 %collective-permute-start.15 = (bf16[128,1024]{1,0:T(8,128)(2,1)S(1)}, bf16[128,1024]{1,0:T(8,128)(2,1)}, u32[]{:S(2)}, u32[]{:S(2)}) collective-permute-start(bf16[128,1024]{1,0:T(8,128)(2,1)S(1)} %slice.46), channel_id=1, source_target_pairs={{0,24},{8,0},{16,8},{24,16},{1,25},{9,1},{17,9},{25,17},{2,26},{10... | collective-permute-start | bytes 786440 | tf_op jit(solution)/shard_map/ppermute | solution.py:336
  148.0 19.3 %collective-permute-start.14 = (bf16[128,1024]{1,0:T(8,128)(2,1)}, bf16[128,1024]{1,0:T(8,128)(2,1)}, u32[]{:S(2)}, u32[]{:S(2)}) collective-permute-start(bf16[128,1024]{1,0:T(8,128)(2,1)} %slice.45), channel_id=1, source_target_pairs={{0,8},{8,16},{16,24},{24,0},{1,9},{9,17},{17,25},{25,1},{2,10},{10... | collective-permute-start | bytes 786440 | tf_op jit(solution)/shard_map/ppermute | solution.py:336
  150.8 50.2 %all-to-all-start.2 = ((bf16[128,2,8,256]{3,2,1,0:T(8,128)(2,1)}), bf16[128,2,8,256]{3,2,1,0:T(8,128)(2,1)S(1)}, u32[]{:S(2)}, u32[]{:S(2)}) async-start(bf16[128,2,8,256]{3,2,1,0:T(8,128)(2,1)} %pad_maximum_fusion), calls=%async_computation.2 | async-start | bytes 2097152 | tf_op jit(solution)/shard_map/all_to_all | solution.py:417
  186.1 31.4 %collective-permute-start.19 = (bf16[2,256,1024]{2,1,0:T(8,128)(2,1)}, bf16[2,256,1024]{2,1,0:T(8,128)(2,1)S(1)}, u32[]{:S(2)}, u32[]{:S(2)}) collective-permute-start(bf16[2,256,1024]{2,1,0:T(8,128)(2,1)} %get-tuple-element.96), channel_id=1, source_target_pairs={{0,32},{32,0},{1,33},{33,1},{2,34},{34,2},{3,35},{35,3},{4,36},{36... | collective-permute-start | bytes 3145736 | tf_op jit(solution)/shard_map/ppermute | solution.py:339
  201.0 22.0 %collective-permute-start.23 = (bf16[2,1024,128]{2,1,0:T(8,128)(2,1)}, bf16[2,1024,128]{2,1,0:T(8,128)(2,1)}, u32[]{:S(2)}, u32[]{:S(2)}) collective-permute-start(bf16[2,1024,128]{2,1,0:T(8,128)(2,1)} %get-tuple-element.106), channel_id=1, source_target_pairs={{0,2},{2,4},{4,6},{6,0},{1,3},{3,5},{5,7},{7,1},{8,10},{10,12},{12... | collective-permute-start | bytes 1572872 | tf_op jit(solution)/shard_map/ppermute | solution.py:395
  202.5 27.3 %collective-permute-start.24 = (bf16[2,1024,128]{2,1,0:T(8,128)(2,1)}, bf16[2,1024,128]{2,1,0:T(8,128)(2,1)}, u32[]{:S(2)}, u32[]{:S(2)}) collective-permute-start(bf16[2,1024,128]{2,1,0:T(8,128)(2,1)} %get-tuple-element.107), channel_id=1, source_target_pairs={{0,4},{2,6},{4,0},{6,2},{1,5},{3,7},{5,1},{7,3},{8,12},{10,14},{12... | collective-permute-start | bytes 1572872 | tf_op jit(solution)/shard_map/ppermute | solution.py:395
  205.3 25.6 %collective-permute-start.25 = (bf16[2,1024,128]{2,1,0:T(8,128)(2,1)}, bf16[2,1024,128]{2,1,0:T(8,128)(2,1)}, u32[]{:S(2)}, u32[]{:S(2)}) collective-permute-start(bf16[2,1024,128]{2,1,0:T(8,128)(2,1)} %get-tuple-element.108), channel_id=1, source_target_pairs={{0,6},{2,0},{4,2},{6,4},{1,7},{3,1},{5,3},{7,5},{8,14},{10,8},{12,... | collective-permute-start | bytes 1572872 | tf_op jit(solution)/shard_map/ppermute | solution.py:395
  219.4 59.7 %all-to-all-start.3 = ((bf16[8,128,1024]{2,1,0:T(8,128)(2,1)}), bf16[8,128,1024]{2,1,0:T(8,128)(2,1)S(1)}, u32[]{:S(2)}, u32[]{:S(2)}) async-start(bf16[8,128,1024]{2,1,0:T(8,128)(2,1)} %bitcast.43), calls=%async_computation.3 | async-start | bytes 4194304 | tf_op jit(solution)/shard_map/all_to_all | solution.py:425
  232.7 26.8 %collective-permute-start.26 = (bf16[1024,128]{1,0:T(8,128)(2,1)S(1)}, bf16[1024,128]{1,0:T(8,128)(2,1)S(1)}, u32[]{:S(2)}, u32[]{:S(2)}) collective-permute-start(bf16[1024,128]{1,0:T(8,128)(2,1)S(1)} %fusion.3), channel_id=1, source_target_pairs={{0,1},{1,0},{2,3},{3,2},{4,5},{5,4},{6,7},{7,6},{8,9},{9,8},{10,11... | collective-permute-start | bytes 786440 | tf_op jit(solution)/shard_map/ppermute | solution.py:339
  240.8 37.3 %collective-permute-start.20 = (bf16[256,1024]{1,0:T(8,128)(2,1)S(1)}, bf16[256,1024]{1,0:T(8,128)(2,1)S(1)}, u32[]{:S(2)}, u32[]{:S(2)}) collective-permute-start(bf16[256,1024]{1,0:T(8,128)(2,1)S(1)} %fusion.2), channel_id=1, source_target_pairs={{0,64},{64,0},{1,65},{65,1},{2,66},{66,2},{3,67},{67,3},{4,68},{68... | collective-permute-start | bytes 1572872 | tf_op jit(solution)/shard_map/ppermute | solution.py:339
  (31 other events, 195.1 us)

commit v8 on v7

v8 whole, which is shorter than its diff:
```python
import math

import jax
import jax.numpy as jnp
from jax import lax
from jax.experimental import pallas as pl
from jax.experimental.pallas import tpu as pltpu
from jax.sharding import Mesh
from jax.sharding import PartitionSpec as P

HEAD = 128
SCALE = 1.0 / math.sqrt(HEAD)
LOG2E = math.log2(math.e)
F32 = jnp.float32
BF16 = jnp.bfloat16
AXES = (("xh", 2), ("core", 2), ("z", 4), ("y", 4), ("xl", 2))
HEADS = ("xh", "core")
SEQ = ("z", "y", "xl")
XH, CORE, Z, Y, XL = range(5)
SWAP = [(0, 1), (1, 0)]
VMEM = 56 * 1024 * 1024
TOK = 256
PIECE = 256
GROUP = 4 * TOK
BLOCK = 1024
PLANES = 8


def dot(a, b, contract=((1,), (0,))):
    return lax.dot_general(a, b, (contract, ((), ())), preferred_element_type=F32)


def shifted(index, by, size=4):
    return lax.rem(index + by + size, size)


def head_block(step, pos):
    return lax.rem(pos[XH] + step // 2, 2) * 2 + lax.rem(pos[CORE] + step % 2, 2)


def struct(shape, dtype=BF16):
    return jax.ShapeDtypeStruct(shape, dtype)


def whole(shape):
    return pl.BlockSpec(shape, lambda *_: (0,) * len(shape))


def call(kernel, name, grid, in_specs, out_specs, out_shape, scratch, flops, moved, pos, *args):
    return pl.pallas_call(
        kernel,
        grid_spec=pltpu.PrefetchScalarGridSpec(
            num_scalar_prefetch=1,
            grid=grid,
            in_specs=in_specs,
            out_specs=out_specs,
            scratch_shapes=scratch,
        ),
        out_shape=out_shape,
        compiler_params=pltpu.CompilerParams(vmem_limit_bytes=VMEM),
        cost_estimate=pl.CostEstimate(flops=flops, bytes_accessed=moved, transcendentals=0),
        name=name,
    )(pos, *args)


HBM = pl.BlockSpec(memory_space=pltpu.HBM)


def moved_in(pairs, sems):
    copies = [pltpu.make_async_copy(source, target, sems.at[i]) for i, (source, target) in enumerate(pairs)]
    for copy in copies:
        copy.start()
    return copies


def weight_block(w_ref, step, pos, by_columns):
    part = pl.ds(pl.multiple_of(head_block(step, pos) * BLOCK, BLOCK), BLOCK)
    return w_ref.at[:, part] if by_columns else w_ref.at[part, :]


def project_kernel(first, pos, *refs):
    before, refs = (None, refs) if first == 0 else (refs[0], refs[1:])
    sources, (wq, wo, out, blocks, weights, known, block_sems, weight_sems, known_sems) = refs[:4], refs[4:]
    pairs = [
        (weight_block(w, first + i, pos, w is wo), weights.at[2 * n + i])
        for n, w in enumerate((wq, wo))
        for i in range(2)
    ]
    moves = moved_in([(x, blocks.at[i]) for i, x in enumerate(sources)], block_sems)
    weight_moves = moved_in(pairs, weight_sems)
    if before is not None:
        moves += moved_in([(before, known)], known_sems)
    for move in moves:
        move.wait()
    for n in range(2):
        contract = ((1,), (1,)) if n else ((1,), (0,))
        weight_moves[2 * n].wait()
        total = dot(blocks[2 * n], weights[2 * n], contract)
        if before is not None:
            total = total + known[n]
        weight_moves[2 * n + 1].wait()
        total = total + dot(blocks[2 * n + 1], weights[2 * n + 1], contract)
        if before is None:
            out[n] = total
        else:
            for layer in range(4):
                out[layer, n] = total[:, layer * PIECE : (layer + 1) * PIECE].astype(BF16)


def project(name, pos, blocks, query_weight, output_weight, before=None):
    shape, dtype = ((2, TOK, BLOCK), F32) if before is None else ((4, 2, TOK, PIECE), BF16)
    args = (*(() if before is None else (before,)), *blocks, query_weight, output_weight)
    return call(
        lambda *refs: project_kernel(0 if before is None else 2, *refs),
        name,
        (1,),
        [HBM] * len(args),
        whole(shape),
        struct(shape, dtype),
        [
            pltpu.VMEM((4, TOK, BLOCK), BF16),
            pltpu.VMEM((4, BLOCK, BLOCK), BF16),
            pltpu.VMEM((2, TOK, BLOCK), F32),
            pltpu.SemaphoreType.DMA((4,)),
            pltpu.SemaphoreType.DMA((4,)),
            pltpu.SemaphoreType.DMA((1,)),
        ],
        8 * TOK * BLOCK * BLOCK,
        8 * BLOCK * BLOCK,
        pos,
        *args,
    )


def assemble_kernel(pos, p0, p1, p2, p3, turned, straight):
    for i, piece in enumerate((p0, p1, p2, p3)):
        token = pl.multiple_of(head_block(i, pos) * TOK, TOK)
        turned[:, pl.ds(token, TOK)] = piece[0].T
        straight[pl.ds(token, TOK), :] = piece[1]


def assemble(pos, pieces):
    return call(
        assemble_kernel,
        "column_blocks",
        (1,),
        [whole((2, TOK, BLOCK))] * 4,
        [whole((BLOCK, GROUP)), whole((GROUP, BLOCK))],
        [struct((BLOCK, GROUP)), struct((GROUP, BLOCK))],
        [],
        0,
        8 * BLOCK * GROUP,
        pos,
        *pieces,
    )


def attention_kernel(pos, bias, rows, k_ref, v_ref, out, dk_ref, dv_ref, dk_sum, dv_sum):
    k, v = k_ref[...], v_ref[...]
    for layer in range(4):
        q = rows[layer, 0]
        scores = dot(q, k, ((1,), (1,))) + bias[...]
        top = jnp.max(scores, axis=1, keepdims=True)
        weights = jnp.exp2((scores - top) * (SCALE * LOG2E))
        share = 1.0 / jnp.sum(weights, axis=1, keepdims=True)
        low = weights.astype(BF16)
        heads_out = (dot(low, v) * share).astype(BF16)
        token = slice(layer * TOK, (layer + 1) * TOK)
        out[0, :, token] = heads_out.T
        g = (rows[layer, 1].astype(F32) * (share * SCALE)).astype(BF16)
        delta = jnp.sum(g.astype(F32) * heads_out.astype(F32), axis=1, keepdims=True)
        score_grad = (low.astype(F32) * (dot(g, v, ((1,), (1,))) - delta)).astype(BF16)
        out[1, :, token] = dot(score_grad, k).astype(BF16).T
        dk_term, dv_term = dot(q, score_grad, ((0,), (0,))), dot(g, low, ((0,), (0,)))
        dk_sum[...] = dk_term if layer == 0 else dk_sum[...] + dk_term
        dv_sum[...] = dv_term if layer == 0 else dv_sum[...] + dv_term
    dk_ref[...] = dk_sum[...].T.astype(BF16)
    dv_ref[...] = (dv_sum[...] * (1.0 / SCALE)).T.astype(BF16)


def attention(pos, bias, rows, keys, values):
    column = pl.BlockSpec((GROUP, HEAD), lambda h, pos: (0, h))
    context = keys.shape[0]
    return call(
        attention_kernel,
        "attention",
        (PIECE // HEAD,),
        [whole((1, context)), pl.BlockSpec((4, 2, TOK, HEAD), lambda h, pos: (0, 0, 0, h))] + [column] * 2,
        [pl.BlockSpec((2, HEAD, GROUP), lambda h, pos: (0, h, 0))] + [column] * 2,
        [struct((2, PIECE, GROUP))] + [struct((GROUP, PIECE))] * 2,
        [pltpu.VMEM((HEAD, context), F32)] * 2,
        30 * GROUP * PIECE * context,
        16 * GROUP * PIECE,
        pos,
        bias,
        rows,
        keys,
        values,
    )


GATHERED = ((0, 0), (1, 0), (3, 0), (2, 0), (2, 1))


def output_grad_kernel(pos, *refs):
    left, right, outs, held = refs[:5], refs[5], refs[6:10], refs[10]
    for ref, (e, part) in zip(left, GATHERED):
        rows = ref.shape[1]
        row = pl.multiple_of(shifted(pos[Z], -e) * PIECE + part * rows, rows)
        product = dot(ref[0], right[...]).astype(BF16)
        for p in range(PLANES):
            held[p, pl.ds(row, rows), :] = product[:, p * 128 : (p + 1) * 128]
    for d in range(4):
        outs[d][...] = held[pl.ds(shifted(pos[Y], d) * 2, 2)]


def query_grad_kernel(pos, *refs):
    right, left, out = refs[:5], refs[5], refs[6]
    for ref, (e, part) in zip(right, GATHERED):
        cols = ref.shape[1]
        col = pl.multiple_of(shifted(pos[Z], -e) * PIECE + part * cols, cols)
        out[:, pl.ds(col, cols)] = dot(left[...], ref[0], ((1,), (1,))).astype(BF16)


def weight_terms(name, kernel, pos, which, gathered, block, out, count, scratch):
    return call(
        kernel,
        name,
        (1,),
        [pl.BlockSpec((1, *a.shape[1:]), lambda i, pos: (which, 0, 0)) for a in gathered] + [whole(block.shape)],
        [whole(out)] * count,
        [struct(out)] * count,
        scratch,
        2 * GROUP * BLOCK * BLOCK,
        6 * BLOCK * BLOCK,
        pos,
        *gathered,
        block,
    )


def output_kernel(pos, *refs):
    rows, w_ref, give, keep, weights, sems = refs[:5], *refs[5:]
    order = (1, 3, 0, 2)
    moves = moved_in([(weight_block(w_ref, i, pos, True), weights.at[n]) for n, i in enumerate(order)], sems)
    for n in range(4):
        moves[n].wait()
        product = jnp.zeros((TOK, BLOCK), F32)
        for ref, (e, part) in zip(rows, GATHERED):
            size = ref.shape[1]
            row = pl.multiple_of(shifted(pos[Z], -e) * PIECE + part * size, size)
            product = product + dot(ref[0], weights[n, pl.ds(row, size), :], ((0,), (0,)))
        if n < 2:
            give[n] = product.astype(BF16)
        else:
            keep[n - 2] = product


def output_terms(pos, gathered, weight):
    return call(
        output_kernel,
        "output_terms",
        (1,),
        [pl.BlockSpec((1, a.shape[1], TOK), lambda n, pos: (0, 0, pos[Z])) for a in gathered] + [HBM],
        [whole((2, TOK, BLOCK))] * 2,
        [struct((2, TOK, BLOCK)), struct((2, TOK, BLOCK), F32)],
        [pltpu.VMEM((4, BLOCK, BLOCK), BF16), pltpu.SemaphoreType.DMA((4,))],
        2 * TOK * 4 * BLOCK * BLOCK,
        2 * 4 * BLOCK * BLOCK,
        pos,
        *gathered,
        weight,
    )


def context_bias(lengths, slot_passage):
    slot_lengths = jnp.sum(
        jnp.where(slot_passage[:, None] == jnp.arange(4)[None, :], lengths[None, :], 0), axis=1
    )
    position = jnp.arange(TOK, dtype=jnp.int32)
    valid = position[None, :] < slot_lengths[:, None]
    return jnp.where(valid, 0.0, -jnp.inf).astype(F32).reshape(1, 4 * TOK)


def on_device(
    decoder_states,
    query_weight,
    output_weight,
    context_keys,
    context_values,
    lengths,
    slot_passage,
    output_cotangent,
):
    pos = jnp.stack([lax.axis_index(name) for name, _ in AXES]).astype(jnp.int32)

    def shift(x, axis, d):
        return lax.ppermute(x, axis, [(i, (i + d) % 4) for i in range(4)])

    def swap(x, axis):
        return lax.ppermute(x, axis, SWAP)

    def after(x, *others):
        return lax.optimization_barrier((x, *others))[0]

    far_states, far_cotangent = swap(decoder_states, "xh"), swap(output_cotangent, "xh")
    near = (decoder_states, swap(decoder_states, "core"), output_cotangent, swap(output_cotangent, "core"))
    products = project("project_near", pos, near, query_weight, output_weight)

    own = jnp.stack([context_keys, context_values]).reshape(2, 8, 16, PIECE).transpose(2, 0, 1, 3)
    own = jnp.broadcast_to(own[:, None], (16, PLANES, 2, 8, PIECE)).reshape(128, 2, 8, PIECE)
    context = lax.all_to_all(after(own, near), HEADS + SEQ, 0, 0, tiled=True)
    keys = context[:, 0].reshape(4 * TOK, PIECE)
    values = context[:, 1].reshape(4 * TOK, PIECE)
    bias = context_bias(lengths, slot_passage)

    far_states, far_cotangent = after((far_states, far_cotangent), products, keys)
    far = (far_states, swap(far_states, "core"), far_cotangent, swap(far_cotangent, "core"))
    rows = project("project_far", pos, far, query_weight, output_weight, products)
    rows = lax.all_to_all(rows, "z", 0, 0, tiled=True)

    pairs = [(h * 4 + z, z * 4 + h) for h in range(4) for z in range(4)]
    both = jnp.stack(after((decoder_states, output_cotangent), far_states, far_cotangent))
    piece = lax.ppermute(both, HEADS + ("z",), pairs)
    piece = after(piece, rows)
    over_x = swap(piece, "xh")

    gathered, key_terms, value_terms = attention(pos, bias, rows, keys, values)
    left, right = shift(gathered, "z", 1), shift(gathered, "z", 3)
    half = PIECE // 2
    every = (gathered, left, right, shift(left[:, :half], "z", 1), shift(right[:, half:], "z", 3))

    piece, over_x = after((piece, over_x), gathered)
    group_states, group_cotangent = assemble(
        pos, (piece, swap(piece, "core"), over_x, swap(over_x, "core"))
    )

    terms = jnp.stack([key_terms.reshape(128, 8, PIECE), value_terms.reshape(128, 8, PIECE)], 1)
    moved = lax.all_to_all(after(terms, group_states), HEADS + SEQ, 0, 0, tiled=True)
    owned = jnp.sum(moved.reshape(16, PLANES, 2, 8, PIECE).astype(F32), axis=1)
    owned = owned.transpose(1, 2, 0, 3).reshape(2, 8, 16 * PIECE)

    terms = weight_terms(
        "output_weight_terms",
        output_grad_kernel,
        pos,
        0,
        every,
        group_cotangent,
        (2, BLOCK, 128),
        4,
        [pltpu.VMEM((PLANES, BLOCK, 128), BF16)],
    )
    total = terms[0].astype(F32)
    for d in range(1, 4):
        total = total + shift(terms[d], "y", d).astype(F32)
    kept, given = (lax.dynamic_index_in_dim(total, i, 0, False) for i in (pos[XL], 1 - pos[XL]))
    output_weight_grad = kept + swap(given.astype(BF16), "xl").astype(F32)

    (query_terms,) = weight_terms(
        "query_weight_terms",
        query_grad_kernel,
        pos,
        1,
        after(every, moved, terms),
        group_states,
        (BLOCK, BLOCK),
        1,
        [],
    )
    query_sums = lax.all_to_all(query_terms.reshape(PLANES, 128, BLOCK), ("y", "xl"), 0, 0, tiled=True)
    query_weight_grad = jnp.sum(query_sums.astype(F32), axis=0)

    give, keep = output_terms(pos, after(every, query_terms), output_weight)
    pair = keep + swap(give, "core").astype(F32)
    attended = (pair[0] + swap(pair[1].astype(BF16), "xh").astype(F32)).astype(BF16)
    return attended, query_weight_grad, output_weight_grad, owned[0], owned[1]


def solution(mesh):
    devices = mesh.devices.reshape([size for _, size in AXES])
    split = Mesh(devices, [name for name, _ in AXES])
    return jax.shard_map(
        on_device,
        mesh=split,
        in_specs=(
            P(SEQ, HEADS),
            P(None, HEADS),
            P(HEADS, None),
            P(HEADS + SEQ, None),
            P(HEADS + SEQ, None),
            P(),
            P(),
            P(SEQ, HEADS),
        ),
        out_specs=(
            P(SEQ, HEADS),
            P(SEQ, HEADS),
            P(HEADS, SEQ),
            P(HEADS + SEQ, None),
            P(HEADS + SEQ, None),
        ),
        check_vma=False,
    )
```

time: 281 us -> 274 us (0.975)
  waiting for transfers between devices: 98 us -> 133 us
  starting transfers between devices: 93.2 us -> 63.5 us
  Pallas kernels: 66.5 us -> 56.2 us
  local copies, waits for them, and re-layouts: 11.4 us -> 8.57 us
    ppermute x17 -> x8, starting transfers between devices: 27.6 us -> 8.23 us  [the longest x7 7.5 us: shift(): return lax.ppermute(x, axis, [(i, (i + d) % 4) for i in range(4)])]
    all_to_all x4, waiting for transfers between devices: 8.31 us -> 25.7 us  [the longest x1 18.6 us: on_device(): rows = lax.all_to_all(rows, 'z', 0, 0, tiled=True)]
    ppermute x10 -> x12, waiting for transfers between devices: 28.7 us -> 42.4 us  [swap(): return lax.ppermute(x, axis, SWAP)]
    pallas_call x10 -> x7, Pallas kernels: 66.5 us -> 56.2 us  [call(): pl.pallas_call(kernel, grid_spec=pltpu.PrefetchScalarGridSpec(num_scalar_...]
    ppermute x10 -> x12, starting transfers between devices: 30.6 us -> 22.2 us  [swap(): return lax.ppermute(x, axis, SWAP)]
    ppermute x17 -> x8, waiting for transfers between devices: 61 us -> 64.5 us  [the longest x7 64.5 us: shift(): return lax.ppermute(x, axis, [(i, (i + d) % 4) for i in range(4)])]
  transfers between devices with their start and end apart: 31 -> 24, of which waited for: 14 -> 14; matrix products, arithmetic and copies ran while one was open for 5% -> 5% of each run, Pallas kernels for 21% -> 15%
where the time goes in v8:
time: 274 us; the launch traced here: 273 us
  waiting for transfers between devices  133 us (49%)
  starting transfers between devices  63.5 us (23%)
  Pallas kernels  56.2 us (21%)
  other arithmetic  11.2 us (4%)
  local copies, waits for them, and re-layouts  8.57 us (3%)
    ppermute x7, waiting for transfers between devices, shift(): return lax.ppermute(x, axis, [(i, (i + d) % 4) for i in range(4)])  64.5 us
    pallas_call x7, Pallas kernels, call(): pl.pallas_call(kernel, grid_spec=pltpu.PrefetchScalarGridSpec(num_scalar_...  56.2 us
    ppermute x12, waiting for transfers between devices, swap(): return lax.ppermute(x, axis, SWAP)  42.4 us
    ppermute x12, starting transfers between devices, swap(): return lax.ppermute(x, axis, SWAP)  22.2 us
    all_to_all x1, waiting for transfers between devices, on_device(): rows = lax.all_to_all(rows, 'z', 0, 0, tiled=True)  18.6 us
    all_to_all x1, starting transfers between devices, on_device(): rows = lax.all_to_all(rows, 'z', 0, 0, tiled=True)  11.9 us
    all_to_all x1, starting transfers between devices, on_device(): context = lax.all_to_all(after(own, near), HEADS + SEQ, 0, 0, tiled=True)  11.1 us
    ppermute x7, starting transfers between devices, shift(): return lax.ppermute(x, axis, [(i, (i + d) % 4) for i in range(4)])  7.5 us
  transfers between devices with their start and end apart: 24, of which 14 were waited for; matrix products, arithmetic and copies ran while one was open for 5% of the time, Pallas kernels for 15%

profile of v8, /device:TPU:0, one launch (start us, length us, event | category | flops | bytes accessed | tf_op | source)
XLA Modules:
  0.0 272.9 jit_solution(723213507466772065)
XLA Ops:
  4.7 11.1 %all-to-all-start = ((bf16[128,2,8,256]{3,2,1,0:T(8,128)(2,1)}), bf16[128,2,8,256]{3,2,1,0:T(8,128)(2,1)S(1)}, u32[]{:S(2)}, u32[]{:S(2)}) async-start(bf16[128,2,8,256]{3,2,1,0:T(8,128)(2,1)} %bitcast.8), calls=%async_computation | async-start | bytes 2097152 | tf_op jit(solution)/shard_map/all_to_all | solution.py:312
  15.9 2.5 collective-permute-start.2
  20.1 8.4 %project_near.1.refs_1_ = f32[2,256,1024]{2,1,0:T(8,128)} custom-call(s32[5]{0:T(128)} %stack.44.refs_0_.pos, bf16[256,1024]{1,0:T(8,128)(2,1)} %refs_1_.1, bf16[256,1024]{1,0:T(8,128)(2,1)} %copy-done.12, bf16[256,1024]{1,0:T(8,128)(2,1)} %refs_3_.1, bf16[256,1024]{1,0:T(8,128)(2,1)} %copy-done.13, bf16[4096,1024]{1,0:T(8,128)(2,1)} %refs_6_.3, ...), custom_call_target="tpu_custom_call" | custom-call | flops 2147483648 | bytes 8388608 | tf_op jit(solution)/shard_map/project_near/pallas_call | solution.py:50
  28.5 7.0 %all-to-all-done = bf16[128,2,8,256]{3,2,1,0:T(8,128)(2,1)S(1)} async-done(((bf16[128,2,8,256]{3,2,1,0:T(8,128)(2,1)}), bf16[128,2,8,256]{3,2,1,0:T(8,128)(2,1)S(1)}, u32[]{:S(2)}, u32[]{:S(2)}) %all-to-all-start) | async-done | bytes 1048608 | tf_op jit(solution)/shard_map/all_to_all | solution.py:312
  36.6 5.0 %collective-permute-done.2.refs_2_ = bf16[256,1024]{1,0:T(8,128)(2,1)S(1)} collective-permute-done((bf16[256,1024]{1,0:T(8,128)(2,1)}, bf16[256,1024]{1,0:T(8,128)(2,1)S(1)}, u32[]{:S(2)}, u32[]{:S(2)}) %collective-permute-start.2) | collective-permute-done | bytes 524320 | tf_op jit(solution)/shard_map/ppermute | solution.py:301
  41.6 10.8 %collective-permute-done.3.refs_4_ = bf16[256,1024]{1,0:T(8,128)(2,1)S(1)} collective-permute-done((bf16[256,1024]{1,0:T(8,128)(2,1)}, bf16[256,1024]{1,0:T(8,128)(2,1)S(1)}, u32[]{:S(2)}, u32[]{:S(2)}) %collective-permute-start.3) | collective-permute-done | bytes 524320 | tf_op jit(solution)/shard_map/ppermute | solution.py:301
  56.5 9.3 %project_far.1 = bf16[4,2,256,256]{3,2,1,0:T(8,128)(2,1)} custom-call(s32[5]{0:T(128)} %stack.44.refs_0_.pos, f32[2,256,1024]{2,1,0:T(8,128)} %project_near.1.refs_1_, bf16[256,1024]{1,0:T(8,128)(2,1)} %copy-done.10, bf16[256,1024]{1,0:T(8,128)(2,1)} %copy-done.14, bf16[256,1024]{1,0:T(8,128)(2,1)} %copy-done.11, bf16[256,1024]{1,0:T(8,128)(2,1)} %copy-done.15, ...), custom_call_target="tpu_custom_call" | custom-call | flops 2147483648 | bytes 8388608 | tf_op jit(solution)/shard_map/project_far/pallas_call | solution.py:50
  65.8 11.9 %all-to-all-start.1 = ((bf16[4,2,256,256]{3,2,1,0:T(8,128)(2,1)}), bf16[4,2,256,256]{3,2,1,0:T(8,128)(2,1)S(1)}, u32[]{:S(2)}, u32[]{:S(2)}) async-start(bf16[4,2,256,256]{3,2,1,0:T(8,128)(2,1)} %project_far.1), calls=%async_computation.1 | async-start | bytes 2097152 | tf_op jit(solution)/shard_map/all_to_all | solution.py:320
  77.7 18.6 %all-to-all-done.1.rows = bf16[4,2,256,256]{3,2,1,0:T(8,128)(2,1)S(1)} async-done(((bf16[4,2,256,256]{3,2,1,0:T(8,128)(2,1)}), bf16[4,2,256,256]{3,2,1,0:T(8,128)(2,1)S(1)}, u32[]{:S(2)}, u32[]{:S(2)}) %all-to-all-start.1) | async-done | bytes 1048608 | tf_op jit(solution)/shard_map/all_to_all | solution.py:320
  96.4 8.8 %collective-permute-start.11 = (bf16[2,256,1024]{2,1,0:T(8,128)(2,1)S(1)}, bf16[2,256,1024]{2,1,0:T(8,128)(2,1)S(1)}, u32[]{:S(2)}, u32[]{:S(2)}) collective-permute-start(bf16[2,256,1024]{2,1,0:T(8,128)(2,1)S(1)} %collective-permute-done.10.p0), channel_id=1, source_target_pairs={{0,64},{64,0},{1,65},{65,1},{2,66},{66,2},{3,67},{67,3},{4,68},{68... | collective-permute-start | bytes 3145736 | tf_op jit(solution)/shard_map/ppermute | solution.py:301
  106.0 10.8 %attention.1 = (bf16[2,256,1024]{2,1,0:T(8,128)(2,1)}, bf16[1024,256]{1,0:T(8,128)(2,1)}, bf16[1024,256]{1,0:T(8,128)(2,1)}) custom-call(s32[5]{0:T(128)} %stack.44.refs_0_.pos, f32[1,1024]{1,0:T(1,128)} %bitcast.53, bf16[4,2,256,256]{3,2,1,0:T(8,128)(2,1)} %copy-done.9, bf16[1024,256]{1,0:T(8,128)(2,1)} %get-tuple-element.66.k_ref, ...), custom_call_target="tpu_custom_call" | custom-call | flops 8053063680 | bytes 4194304 | tf_op jit(solution)/shard_map/attention/pallas_call | solution.py:50
  116.8 11.7 %collective-permute-done.11.p2 = bf16[2,256,1024]{2,1,0:T(8,128)(2,1)S(1)} collective-permute-done((bf16[2,256,1024]{2,1,0:T(8,128)(2,1)S(1)}, bf16[2,256,1024]{2,1,0:T(8,128)(2,1)S(1)}, u32[]{:S(2)}, u32[]{:S(2)}) %collective-permute-start.11) | collective-permute-done | bytes 1048608 | tf_op jit(solution)/shard_map/ppermute | solution.py:301
  135.3 5.6 %column_blocks.1 = (bf16[1024,1024]{1,0:T(8,128)(2,1)}, bf16[1024,1024]{1,0:T(8,128)(2,1)}) custom-call(s32[5]{0:T(128)} %stack.44.refs_0_.pos, bf16[2,256,1024]{2,1,0:T(8,128)(2,1)} %copy-done.5, bf16[2,256,1024]{2,1,0:T(8,128)(2,1)} %copy-done.7, bf16[2,256,1024]{2,1,0:T(8,128)(2,1)} %copy-done.6, bf16[2,256,1024]{2,1,0:T(8,128)(2,1)} %copy-done.8), custom_call_target="tpu_custom_call" | custom-call | bytes 8388608 | tf_op jit(solution)/shard_map/column_blocks/pallas_call | solution.py:50
  140.9 5.8 %all-to-all-start.2 = ((bf16[128,2,8,256]{3,2,1,0:T(8,128)(2,1)}), bf16[128,2,8,256]{3,2,1,0:T(8,128)(2,1)S(1)}, u32[]{:S(2)}, u32[]{:S(2)}) async-start(bf16[128,2,8,256]{3,2,1,0:T(8,128)(2,1)} %pad_maximum_fusion), calls=%async_computation.2 | async-start | bytes 2097152 | tf_op jit(solution)/shard_map/all_to_all | solution.py:339
  146.7 18.7 %collective-permute-done.7.refs_2_ = bf16[2,256,1024]{2,1,0:T(8,128)(2,1)S(1)} collective-permute-done((bf16[2,256,1024]{2,1,0:T(8,128)(2,1)}, bf16[2,256,1024]{2,1,0:T(8,128)(2,1)S(1)}, u32[]{:S(2)}, u32[]{:S(2)}) %collective-permute-start.7) | collective-permute-done | bytes 1048608 | tf_op jit(solution)/shard_map/ppermute | solution.py:298
  167.7 10.8 %collective-permute-done.9.refs_4_ = bf16[2,128,1024]{2,1,0:T(8,128)(2,1)S(1)} collective-permute-done((bf16[2,128,1024]{2,1,0:T(8,128)(2,1)S(1)}, bf16[2,128,1024]{2,1,0:T(8,128)(2,1)S(1)}, u32[]{:S(2)}, u32[]{:S(2)}) %collective-permute-start.9) | collective-permute-done | bytes 524320 | tf_op jit(solution)/shard_map/ppermute | solution.py:298
  178.5 2.8 %collective-permute-done.8.refs_3_ = bf16[2,128,1024]{2,1,0:T(8,128)(2,1)S(1)} collective-permute-done((bf16[2,128,1024]{2,1,0:T(8,128)(2,1)S(1)}, bf16[2,128,1024]{2,1,0:T(8,128)(2,1)S(1)}, u32[]{:S(2)}, u32[]{:S(2)}) %collective-permute-start.8) | collective-permute-done | bytes 524320 | tf_op jit(solution)/shard_map/ppermute | solution.py:298
  182.0 6.8 %output_weight_terms.1 = (bf16[2,1024,128]{2,1,0:T(8,128)(2,1)}, bf16[2,1024,128]{2,1,0:T(8,128)(2,1)}, bf16[2,1024,128]{2,1,0:T(8,128)(2,1)}, bf16[2,1024,128]{2,1,0:T(8,128)(2,1)}) custom-call(s32[5]{0:T(128)} %stack.44.refs_0_.pos, bf16[2,256,1024]{2,1,0:T(8,128)(2,1)} %get-tuple-element.58.refs_0_, bf16[2,256,1024]{2,1,0:T(8,128)(2,1)} %copy-done.1, ...), custom_call_target="tpu_custom_call" | custom-call | flops 2147483648 | bytes 6291456 | tf_op jit(solution)/shard_map/output_weight_terms/pallas_call | solution.py:50
  188.8 7.2 %query_weight_terms.1 = bf16[1024,1024]{1,0:T(8,128)(2,1)} custom-call(s32[5]{0:T(128)} %stack.44.refs_0_.pos, bf16[2,256,1024]{2,1,0:T(8,128)(2,1)} %get-tuple-element.58.refs_0_, bf16[2,256,1024]{2,1,0:T(8,128)(2,1)} %copy-done.1, bf16[2,256,1024]{2,1,0:T(8,128)(2,1)} %copy-done, bf16[2,128,1024]{2,1,0:T(8,128)(2,1)} %copy-done.3, ...), custom_call_target="tpu_custom_call" | custom-call | flops 2147483648 | bytes 6291456 | tf_op jit(solution)/shard_map/query_weight_terms/pallas_call | solution.py:50
  196.0 8.1 %output_terms.1 = (bf16[2,256,1024]{2,1,0:T(8,128)(2,1)}, f32[2,256,1024]{2,1,0:T(8,128)}) custom-call(s32[5]{0:T(128)} %stack.44.refs_0_.pos, bf16[2,256,1024]{2,1,0:T(8,128)(2,1)} %get-tuple-element.58.refs_0_, bf16[2,256,1024]{2,1,0:T(8,128)(2,1)} %copy-done.1, bf16[2,256,1024]{2,1,0:T(8,128)(2,1)} %copy-done, bf16[2,128,1024]{2,1,0:T(8,128)(2,1)} %copy-done.3, ...), custom_call_target="tpu_custom_call" | custom-call | flops 2147483648 | bytes 8388608 | tf_op jit(solution)/shard_map/output_terms/pallas_call | solution.py:50
  207.6 4.2 %all-to-all-start.3 = ((bf16[8,128,1024]{2,1,0:T(8,128)(2,1)}), bf16[8,128,1024]{2,1,0:T(8,128)(2,1)S(1)}, u32[]{:S(2)}, u32[]{:S(2)}) async-start(bf16[8,128,1024]{2,1,0:T(8,128)(2,1)} %bitcast.45), calls=%async_computation.3 | async-start | bytes 4194304 | tf_op jit(solution)/shard_map/all_to_all | solution.py:371
  211.8 31.3 %collective-permute-done.16 = bf16[2,1024,128]{2,1,0:T(8,128)(2,1)} collective-permute-done((bf16[2,1024,128]{2,1,0:T(8,128)(2,1)}, bf16[2,1024,128]{2,1,0:T(8,128)(2,1)}, u32[]{:S(2)}, u32[]{:S(2)}) %collective-permute-start.16) | collective-permute-done | bytes 524320 | tf_op jit(solution)/shard_map/ppermute | solution.py:298
  247.7 8.1 %collective-permute-start.15 = (bf16[256,1024]{1,0:T(8,128)(2,1)S(1)}, bf16[256,1024]{1,0:T(8,128)(2,1)S(1)}, u32[]{:S(2)}, u32[]{:S(2)}) collective-permute-start(bf16[256,1024]{1,0:T(8,128)(2,1)S(1)} %fusion.2), channel_id=1, source_target_pairs={{0,64},{64,0},{1,65},{65,1},{2,66},{66,2},{3,67},{67,3},{4,68},{68... | collective-permute-start | bytes 1572872 | tf_op jit(solution)/shard_map/ppermute | solution.py:301
  257.5 13.3 %collective-permute-done.15 = bf16[256,1024]{1,0:T(8,128)(2,1)S(1)} collective-permute-done((bf16[256,1024]{1,0:T(8,128)(2,1)S(1)}, bf16[256,1024]{1,0:T(8,128)(2,1)S(1)}, u32[]{:S(2)}, u32[]{:S(2)}) %collective-permute-start.15) | collective-permute-done | bytes 524320 | tf_op jit(solution)/shard_map/ppermute | solution.py:301
  (88 shorter events, 33.4 us)
Async XLA Ops:
  0.6 2.2 collective-permute-start
  0.7 2.9 %collective-permute-start.1 = (bf16[256,1024]{1,0:T(8,128)(2,1)}, bf16[256,1024]{1,0:T(8,128)(2,1)S(1)}, u32[]{:S(2)}, u32[]{:S(2)}) collective-permute-start(bf16[256,1024]{1,0:T(8,128)(2,1)} %refs_3_.1), channel_id=1, source_target_pairs={{0,32},{32,0},{1,33},{33,1},{2,34},{34,2},{3,35},{35,3},{4,36},{36... | collective-permute-start | bytes 1572872 | tf_op jit(solution)/shard_map/ppermute | solution.py:301
  4.7 30.8 %all-to-all-start = ((bf16[128,2,8,256]{3,2,1,0:T(8,128)(2,1)}), bf16[128,2,8,256]{3,2,1,0:T(8,128)(2,1)S(1)}, u32[]{:S(2)}, u32[]{:S(2)}) async-start(bf16[128,2,8,256]{3,2,1,0:T(8,128)(2,1)} %bitcast.8), calls=%async_computation | async-start | bytes 2097152 | tf_op jit(solution)/shard_map/all_to_all | solution.py:312
  15.9 25.7 %collective-permute-start.2 = (bf16[256,1024]{1,0:T(8,128)(2,1)}, bf16[256,1024]{1,0:T(8,128)(2,1)S(1)}, u32[]{:S(2)}, u32[]{:S(2)}) collective-permute-start(bf16[256,1024]{1,0:T(8,128)(2,1)} %refs_1_.1), channel_id=1, source_target_pairs={{0,64},{64,0},{1,65},{65,1},{2,66},{66,2},{3,67},{67,3},{4,68},{68... | collective-permute-start | bytes 1572872 | tf_op jit(solution)/shard_map/ppermute | solution.py:301
  18.4 34.0 %collective-permute-start.3 = (bf16[256,1024]{1,0:T(8,128)(2,1)}, bf16[256,1024]{1,0:T(8,128)(2,1)S(1)}, u32[]{:S(2)}, u32[]{:S(2)}) collective-permute-start(bf16[256,1024]{1,0:T(8,128)(2,1)} %refs_3_.1), channel_id=1, source_target_pairs={{0,64},{64,0},{1,65},{65,1},{2,66},{66,2},{3,67},{67,3},{4,68},{68... | collective-permute-start | bytes 1572872 | tf_op jit(solution)/shard_map/ppermute | solution.py:301
  52.4 2.5 collective-permute-start.4
  52.4 2.7 collective-permute-start.5
  54.2 23.5 %collective-permute-start.10 = (bf16[2,256,1024]{2,1,0:T(8,128)(2,1)S(1)}, bf16[2,256,1024]{2,1,0:T(8,128)(2,1)S(1)}, u32[]{:S(2)}, u32[]{:S(2)}) collective-permute-start(bf16[2,256,1024]{2,1,0:T(8,128)(2,1)S(1)} %pad_maximum_fusion.1), channel_id=1, source_target_pairs={{0,0},{8,32},{16,64},{24,96},{32,8},{40,40},{48,72},{56,104},{64,1... | collective-permute-start | bytes 3145736 | tf_op jit(solution)/shard_map/ppermute | solution.py:324
  65.8 30.5 %all-to-all-start.1 = ((bf16[4,2,256,256]{3,2,1,0:T(8,128)(2,1)}), bf16[4,2,256,256]{3,2,1,0:T(8,128)(2,1)S(1)}, u32[]{:S(2)}, u32[]{:S(2)}) async-start(bf16[4,2,256,256]{3,2,1,0:T(8,128)(2,1)} %project_far.1), calls=%async_computation.1 | async-start | bytes 2097152 | tf_op jit(solution)/shard_map/all_to_all | solution.py:320
  96.4 32.1 %collective-permute-start.11 = (bf16[2,256,1024]{2,1,0:T(8,128)(2,1)S(1)}, bf16[2,256,1024]{2,1,0:T(8,128)(2,1)S(1)}, u32[]{:S(2)}, u32[]{:S(2)}) collective-permute-start(bf16[2,256,1024]{2,1,0:T(8,128)(2,1)S(1)} %collective-permute-done.10.p0), channel_id=1, source_target_pairs={{0,64},{64,0},{1,65},{65,1},{2,66},{66,2},{3,67},{67,3},{4,68},{68... | collective-permute-start | bytes 3145736 | tf_op jit(solution)/shard_map/ppermute | solution.py:301
  128.5 4.8 %collective-permute-start.12 = (bf16[2,256,1024]{2,1,0:T(8,128)(2,1)S(1)}, bf16[2,256,1024]{2,1,0:T(8,128)(2,1)S(1)}, u32[]{:S(2)}, u32[]{:S(2)}) collective-permute-start(bf16[2,256,1024]{2,1,0:T(8,128)(2,1)S(1)} %collective-permute-done.10.p0), channel_id=1, source_target_pairs={{0,32},{32,0},{1,33},{33,1},{2,34},{34,2},{3,35},{35,3},{4,36},{36... | collective-permute-start | bytes 3145736 | tf_op jit(solution)/shard_map/ppermute | solution.py:301
  128.5 4.8 %collective-permute-start.13 = (bf16[2,256,1024]{2,1,0:T(8,128)(2,1)S(1)}, bf16[2,256,1024]{2,1,0:T(8,128)(2,1)S(1)}, u32[]{:S(2)}, u32[]{:S(2)}) collective-permute-start(bf16[2,256,1024]{2,1,0:T(8,128)(2,1)S(1)} %collective-permute-done.11.p2), channel_id=1, source_target_pairs={{0,32},{32,0},{1,33},{33,1},{2,34},{34,2},{3,35},{35,3},{4,36},{36... | collective-permute-start | bytes 3145736 | tf_op jit(solution)/shard_map/ppermute | solution.py:301
  129.0 36.4 %collective-permute-start.7 = (bf16[2,256,1024]{2,1,0:T(8,128)(2,1)}, bf16[2,256,1024]{2,1,0:T(8,128)(2,1)S(1)}, u32[]{:S(2)}, u32[]{:S(2)}) collective-permute-start(bf16[2,256,1024]{2,1,0:T(8,128)(2,1)} %get-tuple-element.58.refs_0_), channel_id=1, source_target_pairs={{0,24},{8,0},{16,8},{24,16},{1,25},{9,1},{17,9},{25,17},{2,26},{10... | collective-permute-start | bytes 3145736 | tf_op jit(solution)/shard_map/ppermute | solution.py:298
  129.0 37.9 %collective-permute-start.6 = (bf16[2,256,1024]{2,1,0:T(8,128)(2,1)}, bf16[2,256,1024]{2,1,0:T(8,128)(2,1)S(1)}, u32[]{:S(2)}, u32[]{:S(2)}) collective-permute-start(bf16[2,256,1024]{2,1,0:T(8,128)(2,1)} %get-tuple-element.58.refs_0_), channel_id=1, source_target_pairs={{0,8},{8,16},{16,24},{24,0},{1,9},{9,17},{17,25},{25,1},{2,10},{10... | collective-permute-start | bytes 3145736 | tf_op jit(solution)/shard_map/ppermute | solution.py:298
  140.9 48.0 %all-to-all-start.2 = ((bf16[128,2,8,256]{3,2,1,0:T(8,128)(2,1)}), bf16[128,2,8,256]{3,2,1,0:T(8,128)(2,1)S(1)}, u32[]{:S(2)}, u32[]{:S(2)}) async-start(bf16[128,2,8,256]{3,2,1,0:T(8,128)(2,1)} %pad_maximum_fusion), calls=%async_computation.2 | async-start | bytes 2097152 | tf_op jit(solution)/shard_map/all_to_all | solution.py:339
  165.5 13.0 %collective-permute-start.9 = (bf16[2,128,1024]{2,1,0:T(8,128)(2,1)S(1)}, bf16[2,128,1024]{2,1,0:T(8,128)(2,1)S(1)}, u32[]{:S(2)}, u32[]{:S(2)}) collective-permute-start(bf16[2,128,1024]{2,1,0:T(8,128)(2,1)S(1)} %slice.38), channel_id=1, source_target_pairs={{0,24},{8,0},{16,8},{24,16},{1,25},{9,1},{17,9},{25,17},{2,26},{10... | collective-permute-start | bytes 1572872 | tf_op jit(solution)/shard_map/ppermute | solution.py:298
  166.9 14.3 %collective-permute-start.8 = (bf16[2,128,1024]{2,1,0:T(8,128)(2,1)S(1)}, bf16[2,128,1024]{2,1,0:T(8,128)(2,1)S(1)}, u32[]{:S(2)}, u32[]{:S(2)}) collective-permute-start(bf16[2,128,1024]{2,1,0:T(8,128)(2,1)S(1)} %slice.37), channel_id=1, source_target_pairs={{0,8},{8,16},{16,24},{24,0},{1,9},{9,17},{17,25},{25,1},{2,10},{10... | collective-permute-start | bytes 1572872 | tf_op jit(solution)/shard_map/ppermute | solution.py:298
  204.2 41.7 %collective-permute-start.14 = (bf16[2,256,1024]{2,1,0:T(8,128)(2,1)}, bf16[2,256,1024]{2,1,0:T(8,128)(2,1)}, u32[]{:S(2)}, u32[]{:S(2)}) collective-permute-start(bf16[2,256,1024]{2,1,0:T(8,128)(2,1)} %get-tuple-element.64), channel_id=1, source_target_pairs={{0,32},{32,0},{1,33},{33,1},{2,34},{34,2},{3,35},{35,3},{4,36},{36... | collective-permute-start | bytes 3145736 | tf_op jit(solution)/shard_map/ppermute | solution.py:301
  204.3 38.8 %collective-permute-start.16 = (bf16[2,1024,128]{2,1,0:T(8,128)(2,1)}, bf16[2,1024,128]{2,1,0:T(8,128)(2,1)}, u32[]{:S(2)}, u32[]{:S(2)}) collective-permute-start(bf16[2,1024,128]{2,1,0:T(8,128)(2,1)} %get-tuple-element.50), channel_id=1, source_target_pairs={{0,2},{2,4},{4,6},{6,0},{1,3},{3,5},{5,7},{7,1},{8,10},{10,12},{12... | collective-permute-start | bytes 1572872 | tf_op jit(solution)/shard_map/ppermute | solution.py:298
  204.5 38.6 %collective-permute-start.17 = (bf16[2,1024,128]{2,1,0:T(8,128)(2,1)}, bf16[2,1024,128]{2,1,0:T(8,128)(2,1)}, u32[]{:S(2)}, u32[]{:S(2)}) collective-permute-start(bf16[2,1024,128]{2,1,0:T(8,128)(2,1)} %get-tuple-element.51), channel_id=1, source_target_pairs={{0,4},{2,6},{4,0},{6,2},{1,5},{3,7},{5,1},{7,3},{8,12},{10,14},{12... | collective-permute-start | bytes 1572872 | tf_op jit(solution)/shard_map/ppermute | solution.py:298
  205.9 38.1 %collective-permute-start.18 = (bf16[2,1024,128]{2,1,0:T(8,128)(2,1)}, bf16[2,1024,128]{2,1,0:T(8,128)(2,1)}, u32[]{:S(2)}, u32[]{:S(2)}) collective-permute-start(bf16[2,1024,128]{2,1,0:T(8,128)(2,1)} %get-tuple-element.52), channel_id=1, source_target_pairs={{0,6},{2,0},{4,2},{6,4},{1,7},{3,1},{5,3},{7,5},{8,14},{10,8},{12,... | collective-permute-start | bytes 1572872 | tf_op jit(solution)/shard_map/ppermute | solution.py:298
  207.6 64.2 %all-to-all-start.3 = ((bf16[8,128,1024]{2,1,0:T(8,128)(2,1)}), bf16[8,128,1024]{2,1,0:T(8,128)(2,1)S(1)}, u32[]{:S(2)}, u32[]{:S(2)}) async-start(bf16[8,128,1024]{2,1,0:T(8,128)(2,1)} %bitcast.45), calls=%async_computation.3 | async-start | bytes 4194304 | tf_op jit(solution)/shard_map/all_to_all | solution.py:371
  245.8 10.0 %collective-permute-start.19 = (bf16[1024,128]{1,0:T(8,128)(2,1)S(1)}, bf16[1024,128]{1,0:T(8,128)(2,1)S(1)}, u32[]{:S(2)}, u32[]{:S(2)}) collective-permute-start(bf16[1024,128]{1,0:T(8,128)(2,1)S(1)} %fusion.3), channel_id=1, source_target_pairs={{0,1},{1,0},{2,3},{3,2},{4,5},{5,4},{6,7},{7,6},{8,9},{9,8},{10,11... | collective-permute-start | bytes 786440 | tf_op jit(solution)/shard_map/ppermute | solution.py:301
  247.7 23.1 %collective-permute-start.15 = (bf16[256,1024]{1,0:T(8,128)(2,1)S(1)}, bf16[256,1024]{1,0:T(8,128)(2,1)S(1)}, u32[]{:S(2)}, u32[]{:S(2)}) collective-permute-start(bf16[256,1024]{1,0:T(8,128)(2,1)S(1)} %fusion.2), channel_id=1, source_target_pairs={{0,64},{64,0},{1,65},{65,1},{2,66},{66,2},{3,67},{67,3},{4,68},{68... | collective-permute-start | bytes 1572872 | tf_op jit(solution)/shard_map/ppermute | solution.py:301
  (18 other events, 265.2 us)

commit v9 on v8

--- a/solution.py
+++ b/solution.py
@@ -134,9 +134,11 @@
 
 def assemble_kernel(pos, p0, p1, p2, p3, turned, straight):
     for i, piece in enumerate((p0, p1, p2, p3)):
-        token = pl.multiple_of(head_block(i, pos) * TOK, TOK)
-        turned[:, pl.ds(token, TOK)] = piece[0].T
-        straight[pl.ds(token, TOK), :] = piece[1]
+        col = pl.multiple_of(head_block(i, pos) * PIECE, PIECE)
+        for d in range(4):
+            token = pl.multiple_of(shifted(pos[Y], -d) * TOK, TOK)
+            turned[pl.ds(col, PIECE), pl.ds(token, TOK)] = piece[d, 0].T
+            straight[pl.ds(token, TOK), pl.ds(col, PIECE)] = piece[d, 1]
 
 
 def assemble(pos, pieces):
@@ -144,7 +146,7 @@
         assemble_kernel,
         "column_blocks",
         (1,),
-        [whole((2, TOK, BLOCK))] * 4,
+        [whole((4, 2, TOK, PIECE))] * 4,
         [whole((BLOCK, GROUP)), whole((GROUP, BLOCK))],
         [struct((BLOCK, GROUP)), struct((GROUP, BLOCK))],
         [],
@@ -203,34 +205,32 @@
 
 
 def output_grad_kernel(pos, *refs):
-    left, right, outs, held = refs[:5], refs[5], refs[6:10], refs[10]
+    left, right, out = refs[:5], refs[5], refs[6]
     for ref, (e, part) in zip(left, GATHERED):
         rows = ref.shape[1]
-        row = pl.multiple_of(shifted(pos[Z], -e) * PIECE + part * rows, rows)
+        row = pl.multiple_of(shifted(pos[Y], -e) * PIECE + part * rows, rows)
         product = dot(ref[0], right[...]).astype(BF16)
         for p in range(PLANES):
-            held[p, pl.ds(row, rows), :] = product[:, p * 128 : (p + 1) * 128]
-    for d in range(4):
-        outs[d][...] = held[pl.ds(shifted(pos[Y], d) * 2, 2)]
+            out[p, pl.ds(row, rows), :] = product[:, p * 128 : (p + 1) * 128]
 
 
 def query_grad_kernel(pos, *refs):
     right, left, out = refs[:5], refs[5], refs[6]
     for ref, (e, part) in zip(right, GATHERED):
         cols = ref.shape[1]
-        col = pl.multiple_of(shifted(pos[Z], -e) * PIECE + part * cols, cols)
+        col = pl.multiple_of(shifted(pos[Y], -e) * PIECE + part * cols, cols)
         out[:, pl.ds(col, cols)] = dot(left[...], ref[0], ((1,), (1,))).astype(BF16)
 
 
-def weight_terms(name, kernel, pos, which, gathered, block, out, count, scratch):
+def weight_terms(name, kernel, pos, which, gathered, block, out):
     return call(
         kernel,
         name,
         (1,),
         [pl.BlockSpec((1, *a.shape[1:]), lambda i, pos: (which, 0, 0)) for a in gathered] + [whole(block.shape)],
-        [whole(out)] * count,
-        [struct(out)] * count,
-        scratch,
+        whole(out),
+        struct(out),
+        [],
         2 * GROUP * BLOCK * BLOCK,
         6 * BLOCK * BLOCK,
         pos,
@@ -248,7 +248,7 @@
         product = jnp.zeros((TOK, BLOCK), F32)
         for ref, (e, part) in zip(rows, GATHERED):
             size = ref.shape[1]
-            row = pl.multiple_of(shifted(pos[Z], -e) * PIECE + part * size, size)
+            row = pl.multiple_of(shifted(pos[Y], -e) * PIECE + part * size, size)
             product = product + dot(ref[0], weights[n, pl.ds(row, size), :], ((0,), (0,)))
         if n < 2:
             give[n] = product.astype(BF16)
@@ -261,7 +261,7 @@
         output_kernel,
         "output_terms",
         (1,),
-        [pl.BlockSpec((1, a.shape[1], TOK), lambda n, pos: (0, 0, pos[Z])) for a in gathered] + [HBM],
+        [pl.BlockSpec((1, a.shape[1], TOK), lambda n, pos: (0, 0, pos[Y])) for a in gathered] + [HBM],
         [whole((2, TOK, BLOCK))] * 2,
         [struct((2, TOK, BLOCK)), struct((2, TOK, BLOCK), F32)],
         [pltpu.VMEM((4, BLOCK, BLOCK), BF16), pltpu.SemaphoreType.DMA((4,))],
@@ -307,71 +307,53 @@
     near = (decoder_states, swap(decoder_states, "core"), output_cotangent, swap(output_cotangent, "core"))
     products = project("project_near", pos, near, query_weight, output_weight)
 
-    own = jnp.stack([context_keys, context_values]).reshape(2, 8, 16, PIECE).transpose(2, 0, 1, 3)
-    own = jnp.broadcast_to(own[:, None], (16, PLANES, 2, 8, PIECE)).reshape(128, 2, 8, PIECE)
-    context = lax.all_to_all(after(own, near), HEADS + SEQ, 0, 0, tiled=True)
+    both = jnp.stack([decoder_states, output_cotangent]).reshape(2, TOK, 4, PIECE)
+    quarters = [lax.dynamic_index_in_dim(both, shifted(pos[Y], d), 2, False) for d in range(4)]
+    quarters = [shift(x, "y", d) if d else x for d, x in enumerate(quarters)]
+
+    own = jnp.stack([context_keys, context_values]).reshape(2, 8, 4, 4, PIECE).transpose(2, 3, 0, 1, 4)
+    own = jnp.broadcast_to(own[:, None, :, None], (4, 4, 4, 2, 2, 8, PIECE)).reshape(128, 2, 8, PIECE)
+    context = lax.all_to_all(after(own, products), HEADS + SEQ, 0, 0, tiled=True)
     keys = context[:, 0].reshape(4 * TOK, PIECE)
     values = context[:, 1].reshape(4 * TOK, PIECE)
     bias = context_bias(lengths, slot_passage)
 
-    far_states, far_cotangent = after((far_states, far_cotangent), products, keys)
+    far_states, far_cotangent = after((far_states, far_cotangent), products)
     far = (far_states, swap(far_states, "core"), far_cotangent, swap(far_cotangent, "core"))
-    rows = project("project_far", pos, far, query_weight, output_weight, products)
-    rows = lax.all_to_all(rows, "z", 0, 0, tiled=True)
-
-    pairs = [(h * 4 + z, z * 4 + h) for h in range(4) for z in range(4)]
-    both = jnp.stack(after((decoder_states, output_cotangent), far_states, far_cotangent))
-    piece = lax.ppermute(both, HEADS + ("z",), pairs)
-    piece = after(piece, rows)
+    rows = project("project_far", pos, far, query_weight, output_weight, after(products, keys, quarters))
+    rows = lax.all_to_all(rows, "y", 0, 0, tiled=True)
+
+    piece = jnp.stack(after(quarters, rows))
     over_x = swap(piece, "xh")
 
     gathered, key_terms, value_terms = attention(pos, bias, rows, keys, values)
-    left, right = shift(gathered, "z", 1), shift(gathered, "z", 3)
+    left, right = shift(gathered, "y", 1), shift(gathered, "y", 3)
     half = PIECE // 2
-    every = (gathered, left, right, shift(left[:, :half], "z", 1), shift(right[:, half:], "z", 3))
-
-    piece, over_x = after((piece, over_x), gathered)
+    every = (gathered, left, right, shift(left[:, :half], "y", 1), shift(right[:, half:], "y", 3))
+
+    terms = jnp.stack([key_terms.reshape(128, 8, PIECE), value_terms.reshape(128, 8, PIECE)], 1)
+    moved = lax.all_to_all(terms, HEADS + SEQ, 0, 0, tiled=True)
+    owned = jnp.sum(moved.reshape(4, 4, 4, 2, 2, 8, PIECE).astype(F32), axis=(1, 3))
+    owned = owned.transpose(2, 3, 0, 1, 4).reshape(2, 8, 16 * PIECE)
+
+    piece, over_x = after((piece, over_x), left, right, moved)
     group_states, group_cotangent = assemble(
         pos, (piece, swap(piece, "core"), over_x, swap(over_x, "core"))
     )
 
-    terms = jnp.stack([key_terms.reshape(128, 8, PIECE), value_terms.reshape(128, 8, PIECE)], 1)
-    moved = lax.all_to_all(after(terms, group_states), HEADS + SEQ, 0, 0, tiled=True)
-    owned = jnp.sum(moved.reshape(16, PLANES, 2, 8, PIECE).astype(F32), axis=1)
-    owned = owned.transpose(1, 2, 0, 3).reshape(2, 8, 16 * PIECE)
-
-    terms = weight_terms(
-        "output_weight_terms",
-        output_grad_kernel,
-        pos,
-        0,
-        every,
-        group_cotangent,
-        (2, BLOCK, 128),
-        4,
-        [pltpu.VMEM((PLANES, BLOCK, 128), BF16)],
-    )
-    total = terms[0].astype(F32)
-    for d in range(1, 4):
-        total = total + shift(terms[d], "y", d).astype(F32)
-    kept, given = (lax.dynamic_index_in_dim(total, i, 0, False) for i in (pos[XL], 1 - pos[XL]))
-    output_weight_grad = kept + swap(given.astype(BF16), "xl").astype(F32)
-
-    (query_terms,) = weight_terms(
-        "query_weight_terms",
-        query_grad_kernel,
-        pos,
-        1,
-        after(every, moved, terms),
-        group_states,
-        (BLOCK, BLOCK),
-        1,
-        [],
-    )
-    query_sums = lax.all_to_all(query_terms.reshape(PLANES, 128, BLOCK), ("y", "xl"), 0, 0, tiled=True)
-    query_weight_grad = jnp.sum(query_sums.astype(F32), axis=0)
-
-    give, keep = output_terms(pos, after(every, query_terms), output_weight)
+    def plane_sum(parts):
+        return jnp.sum(lax.all_to_all(parts, ("z", "xl"), 0, 0, tiled=True).astype(F32), axis=0)
+
+    output_parts = weight_terms(
+        "output_weight_terms", output_grad_kernel, pos, 0, every, group_cotangent, (PLANES, BLOCK, 128)
+    )
+    output_weight_grad = plane_sum(output_parts)
+    query_parts = weight_terms(
+        "query_weight_terms", query_grad_kernel, pos, 1, after(every, output_parts), group_states, (BLOCK, BLOCK)
+    )
+    query_weight_grad = plane_sum(after(query_parts, output_weight_grad).reshape(PLANES, 128, BLOCK))
+
+    give, keep = output_terms(pos, after(every, query_parts), output_weight)
     pair = keep + swap(give, "core").astype(F32)
     attended = (pair[0] + swap(pair[1].astype(BF16), "xh").astype(F32)).astype(BF16)
     return attended, query_weight_grad, output_weight_grad, owned[0], owned[1]

time: 274 us -> 262 us (0.956)
  blocking collectives: 0 us -> 39.8 us
  waiting for transfers between devices: 133 us -> 99.9 us
  starting transfers between devices: 63.5 us -> 40.3 us
  local copies, waits for them, and re-layouts: 8.57 us -> 15.7 us
  other arithmetic: 11.2 us -> 6.9 us
    ppermute x7, waiting for transfers between devices: 64.5 us -> 14.4 us  [shift(): return lax.ppermute(x, axis, [(i, (i + d) % 4) for i in range(4)])]
    all_to_all x0 -> x1, blocking collectives: none -> 39.8 us  [on_device(): moved = lax.all_to_all(terms, HEADS + SEQ, 0, 0, tiled=True)]
    ppermute x12 -> x11, waiting for transfers between devices: 42.4 us -> 60.7 us  [swap(): return lax.ppermute(x, axis, SWAP)]
    ppermute x12 -> x11, starting transfers between devices: 22.2 us -> 6.8 us  [swap(): return lax.ppermute(x, axis, SWAP)]
    all_to_all x4, starting transfers between devices: 33 us -> 22.5 us  [the longest x1 11.1 us: on_device(): lax.all_to_all(after(own, products), HEADS + SEQ, 0, 0, tiled=True)]
    ppermute x7, starting transfers between devices: 7.5 us -> 11 us  [shift(): return lax.ppermute(x, axis, [(i, (i + d) % 4) for i in range(4)])]
    another operation x0 -> x3, local copies, waits for them, and re-layouts: none -> 3.45 us  [on_device(): jnp.stack([decoder_states, output_cotangent]).reshape(2, TOK, 4, PIECE)]
    unnamed x37 -> x38, local copies, waits for them, and re-layouts: 4.85 us -> 6.9 us
  transfers between devices with their start and end apart: 24 -> 22, of which waited for: 14 -> 10; matrix products, arithmetic and copies ran while one was open for 5% -> 6% of each run, Pallas kernels for 15% -> 8%
where the time goes in v9:
time: 262 us; the launch traced here: 260 us
  waiting for transfers between devices  99.9 us (38%)
  Pallas kernels  56 us (21%)
  starting transfers between devices  40.3 us (15%)
  blocking collectives  39.8 us (15%)
  local copies, waits for them, and re-layouts  15.7 us (6%)
  other arithmetic  6.9 us (3%)
    ppermute x11, waiting for transfers between devices, swap(): return lax.ppermute(x, axis, SWAP)  60.7 us
    pallas_call x7, Pallas kernels, call(): pl.pallas_call(kernel, grid_spec=pltpu.PrefetchScalarGridSpec(num_scalar_...  56 us
    all_to_all x1, blocking collectives, on_device(): moved = lax.all_to_all(terms, HEADS + SEQ, 0, 0, tiled=True)  39.8 us
    ppermute x7, waiting for transfers between devices, shift(): return lax.ppermute(x, axis, [(i, (i + d) % 4) for i in range(4)])  14.4 us
    all_to_all x1, waiting for transfers between devices, on_device(): rows = lax.all_to_all(rows, 'y', 0, 0, tiled=True)  14 us
    all_to_all x1, starting transfers between devices, on_device(): lax.all_to_all(after(own, products), HEADS + SEQ, 0, 0, tiled=True)  11.1 us
    ppermute x7, starting transfers between devices, shift(): return lax.ppermute(x, axis, [(i, (i + d) % 4) for i in range(4)])  11 us
    all_to_all x2, waiting for transfers between devices, plane_sum(): lax.all_to_all(parts, ('z', 'xl'), 0, 0, tiled=True).astype(F32)  10.7 us
  transfers between devices with their start and end apart: 22, of which 10 were waited for; matrix products, arithmetic and copies ran while one was open for 6% of the time, Pallas kernels for 8%

profile of v9, /device:TPU:0, one launch (start us, length us, event | category | flops | bytes accessed | tf_op | source)
XLA Modules:
  0.0 259.5 jit_solution(1618384084883180850)
XLA Ops:
  4.4 8.4 %project_near.1.refs_1_ = f32[2,256,1024]{2,1,0:T(8,128)} custom-call(s32[5]{0:T(128)} %stack.59.refs_0_.pos, bf16[256,1024]{1,0:T(8,128)(2,1)} %refs_1_.1, bf16[256,1024]{1,0:T(8,128)(2,1)} %copy-done.12, bf16[256,1024]{1,0:T(8,128)(2,1)} %refs_3_.1, bf16[256,1024]{1,0:T(8,128)(2,1)} %copy-done.13, bf16[4096,1024]{1,0:T(8,128)(2,1)} %refs_6_.3, ...), custom_call_target="tpu_custom_call" | custom-call | flops 2147483648 | bytes 8388608 | tf_op jit(solution)/shard_map/project_near/pallas_call | solution.py:50
  13.9 11.1 %all-to-all-start = ((bf16[128,2,8,256]{3,2,1,0:T(8,128)(2,1)}), bf16[128,2,8,256]{3,2,1,0:T(8,128)(2,1)S(1)}, u32[]{:S(2)}, u32[]{:S(2)}) async-start(bf16[128,2,8,256]{3,2,1,0:T(8,128)(2,1)} %bitcast.8), calls=%async_computation | async-start | bytes 2097152 | tf_op jit(solution)/shard_map/all_to_all | solution.py:316
  25.1 2.5 collective-permute-start.5
  32.2 18.8 %collective-permute-done.5.refs_2_ = bf16[256,1024]{1,0:T(8,128)(2,1)} collective-permute-done((bf16[256,1024]{1,0:T(8,128)(2,1)S(1)}, bf16[256,1024]{1,0:T(8,128)(2,1)}, u32[]{:S(2)}, u32[]{:S(2)}) %collective-permute-start.5) | collective-permute-done | bytes 524320 | tf_op jit(solution)/shard_map/ppermute | solution.py:301
  50.9 10.8 %collective-permute-done.6.refs_4_ = bf16[256,1024]{1,0:T(8,128)(2,1)} collective-permute-done((bf16[256,1024]{1,0:T(8,128)(2,1)S(1)}, bf16[256,1024]{1,0:T(8,128)(2,1)}, u32[]{:S(2)}, u32[]{:S(2)}) %collective-permute-start.6) | collective-permute-done | bytes 524320 | tf_op jit(solution)/shard_map/ppermute | solution.py:301
  65.7 2.8 %collective-permute-start.3 = (bf16[2,256,256]{2,1,0:T(8,128)(2,1)}, bf16[2,256,256]{2,1,0:T(8,128)(2,1)S(1)}, u32[]{:S(2)}, u32[]{:S(2)}) collective-permute-start(bf16[2,256,256]{2,1,0:T(8,128)(2,1)} %get-tuple-element.64), channel_id=1, source_target_pairs={{0,4},{2,6},{4,0},{6,2},{1,5},{3,7},{5,1},{7,3},{8,12},{10,14},{12... | collective-permute-start | bytes 786440 | tf_op jit(solution)/shard_map/ppermute | solution.py:298
  70.9 3.0 %collective-permute-done.2 = bf16[2,256,256]{2,1,0:T(8,128)(2,1)S(1)} collective-permute-done((bf16[2,256,256]{2,1,0:T(8,128)(2,1)}, bf16[2,256,256]{2,1,0:T(8,128)(2,1)S(1)}, u32[]{:S(2)}, u32[]{:S(2)}) %collective-permute-start.2) | collective-permute-done | bytes 262176 | tf_op jit(solution)/shard_map/ppermute | solution.py:298
  73.9 6.6 %collective-permute-done.3 = bf16[2,256,256]{2,1,0:T(8,128)(2,1)S(1)} collective-permute-done((bf16[2,256,256]{2,1,0:T(8,128)(2,1)}, bf16[2,256,256]{2,1,0:T(8,128)(2,1)S(1)}, u32[]{:S(2)}, u32[]{:S(2)}) %collective-permute-start.3) | collective-permute-done | bytes 262176 | tf_op jit(solution)/shard_map/ppermute | solution.py:298
  82.1 9.2 %project_far.1 = bf16[4,2,256,256]{3,2,1,0:T(8,128)(2,1)} custom-call(s32[5]{0:T(128)} %stack.59.refs_0_.pos, f32[2,256,1024]{2,1,0:T(8,128)} %project_near.1.refs_1_, bf16[256,1024]{1,0:T(8,128)(2,1)} %collective-permute-done.5.refs_2_, bf16[256,1024]{1,0:T(8,128)(2,1)} %copy-done.10, bf16[256,1024]{1,0:T(8,128)(2,1)} %collective-permute-done.6.refs_4_, ...), custom_call_target="tpu_custom_call" | custom-call | flops 2147483648 | bytes 8388608 | tf_op jit(solution)/shard_map/project_far/pallas_call | solution.py:50
  91.4 3.9 %all-to-all-start.1 = ((bf16[4,2,256,256]{3,2,1,0:T(8,128)(2,1)}), bf16[4,2,256,256]{3,2,1,0:T(8,128)(2,1)S(1)}, u32[]{:S(2)}, u32[]{:S(2)}) async-start(bf16[4,2,256,256]{3,2,1,0:T(8,128)(2,1)} %project_far.1), calls=%async_computation.1 | async-start | bytes 2097152 | tf_op jit(solution)/shard_map/all_to_all | solution.py:324
  96.1 14.0 %all-to-all-done.1.rows = bf16[4,2,256,256]{3,2,1,0:T(8,128)(2,1)S(1)} async-done(((bf16[4,2,256,256]{3,2,1,0:T(8,128)(2,1)}), bf16[4,2,256,256]{3,2,1,0:T(8,128)(2,1)S(1)}, u32[]{:S(2)}, u32[]{:S(2)}) %all-to-all-start.1) | async-done | bytes 1048608 | tf_op jit(solution)/shard_map/all_to_all | solution.py:324
  111.1 10.8 %attention.1 = (bf16[2,256,1024]{2,1,0:T(8,128)(2,1)}, bf16[1024,256]{1,0:T(8,128)(2,1)}, bf16[1024,256]{1,0:T(8,128)(2,1)}) custom-call(s32[5]{0:T(128)} %stack.59.refs_0_.pos, f32[1,1024]{1,0:T(1,128)} %bitcast.63, bf16[4,2,256,256]{3,2,1,0:T(8,128)(2,1)} %copy-done.9, bf16[1024,256]{1,0:T(8,128)(2,1)} %get-tuple-element.62.k_ref, ...), custom_call_target="tpu_custom_call" | custom-call | flops 8053063680 | bytes 4194304 | tf_op jit(solution)/shard_map/attention/pallas_call | solution.py:50
  124.7 39.8 %all_to_all.25 = bf16[128,2,8,256]{3,2,1,0:T(8,128)(2,1)S(1)} all-to-all(bf16[128,2,8,256]{3,2,1,0:T(8,128)(2,1)S(1)} %pad_maximum_fusion.1), channel_id=1, replica_groups=mesh['xh'=2,'core'=2,'z'=4,'y'=4,'xl'=2] {'xh','core','z','y','xl'}, dimensions={0} | all-to-all | bytes 2097152 | tf_op jit(solution)/shard_map/all_to_all | solution.py:335
  166.3 3.0 %collective-permute-start.12 = (bf16[2,128,1024]{2,1,0:T(8,128)(2,1)}, bf16[2,128,1024]{2,1,0:T(8,128)(2,1)S(1)}, u32[]{:S(2)}, u32[]{:S(2)}) collective-permute-start(bf16[2,128,1024]{2,1,0:T(8,128)(2,1)} %slice.38), channel_id=1, source_target_pairs={{0,6},{2,0},{4,2},{6,4},{1,7},{3,1},{5,3},{7,5},{8,14},{10,8},{12,... | collective-permute-start | bytes 1572872 | tf_op jit(solution)/shard_map/ppermute | solution.py:298
  170.3 5.6 %column_blocks.1 = (bf16[1024,1024]{1,0:T(8,128)(2,1)}, bf16[1024,1024]{1,0:T(8,128)(2,1)}) custom-call(s32[5]{0:T(128)} %stack.59.refs_0_.pos, bf16[4,2,256,256]{3,2,1,0:T(8,128)(2,1)} %copy-done.4, bf16[4,2,256,256]{3,2,1,0:T(8,128)(2,1)} %copy-done.8, bf16[4,2,256,256]{3,2,1,0:T(8,128)(2,1)} %copy-done.7, bf16[4,2,256,256]{3,2,1,0:T(8,128)(2,1)} %collective-permute-done.15.p3), custom_call_target="tpu_custom_call" | custom-call | bytes 8388608 | tf_op jit(solution)/shard_map/column_blocks/pallas_call | solution.py:50
  175.9 4.4 %collective-permute-done.11.refs_3_ = bf16[2,128,1024]{2,1,0:T(8,128)(2,1)S(1)} collective-permute-done((bf16[2,128,1024]{2,1,0:T(8,128)(2,1)S(1)}, bf16[2,128,1024]{2,1,0:T(8,128)(2,1)S(1)}, u32[]{:S(2)}, u32[]{:S(2)}) %collective-permute-start.11) | collective-permute-done | bytes 524320 | tf_op jit(solution)/shard_map/ppermute | solution.py:298
  181.6 6.6 %output_weight_terms.1 = bf16[8,1024,128]{2,1,0:T(8,128)(2,1)} custom-call(s32[5]{0:T(128)} %stack.59.refs_0_.pos, bf16[2,256,1024]{2,1,0:T(8,128)(2,1)} %get-tuple-element.53.refs_0_, bf16[2,256,1024]{2,1,0:T(8,128)(2,1)} %copy-done.1, bf16[2,256,1024]{2,1,0:T(8,128)(2,1)} %copy-done, bf16[2,128,1024]{2,1,0:T(8,128)(2,1)} %copy-done.2, ...), custom_call_target="tpu_custom_call" | custom-call | flops 2147483648 | bytes 6291456 | tf_op jit(solution)/shard_map/output_weight_terms/pallas_call | solution.py:50
  188.2 3.8 %all-to-all-start.3 = ((bf16[8,1024,128]{2,1,0:T(8,128)(2,1)}), bf16[8,1024,128]{2,1,0:T(8,128)(2,1)S(1)}, u32[]{:S(2)}, u32[]{:S(2)}) async-start(bf16[8,1024,128]{2,1,0:T(8,128)(2,1)} %output_weight_terms.1), calls=%async_computation.3 | async-start | bytes 4194304 | tf_op jit(solution)/shard_map/all_to_all | solution.py:345
  192.0 7.2 %query_weight_terms.1 = bf16[1024,1024]{1,0:T(8,128)(2,1)} custom-call(s32[5]{0:T(128)} %stack.59.refs_0_.pos, bf16[2,256,1024]{2,1,0:T(8,128)(2,1)} %get-tuple-element.53.refs_0_, bf16[2,256,1024]{2,1,0:T(8,128)(2,1)} %copy-done.1, bf16[2,256,1024]{2,1,0:T(8,128)(2,1)} %copy-done, bf16[2,128,1024]{2,1,0:T(8,128)(2,1)} %copy-done.2, ...), custom_call_target="tpu_custom_call" | custom-call | flops 2147483648 | bytes 6291456 | tf_op jit(solution)/shard_map/query_weight_terms/pallas_call | solution.py:50
  199.2 8.2 %output_terms.1 = (bf16[2,256,1024]{2,1,0:T(8,128)(2,1)}, f32[2,256,1024]{2,1,0:T(8,128)}) custom-call(s32[5]{0:T(128)} %stack.59.refs_0_.pos, bf16[2,256,1024]{2,1,0:T(8,128)(2,1)} %get-tuple-element.53.refs_0_, bf16[2,256,1024]{2,1,0:T(8,128)(2,1)} %copy-done.1, bf16[2,256,1024]{2,1,0:T(8,128)(2,1)} %copy-done, bf16[2,128,1024]{2,1,0:T(8,128)(2,1)} %copy-done.2, ...), custom_call_target="tpu_custom_call" | custom-call | flops 2147483648 | bytes 8388608 | tf_op jit(solution)/shard_map/output_terms/pallas_call | solution.py:50
  207.5 10.7 %all-to-all-done.3 = bf16[8,1024,128]{2,1,0:T(8,128)(2,1)S(1)} async-done(((bf16[8,1024,128]{2,1,0:T(8,128)(2,1)}), bf16[8,1024,128]{2,1,0:T(8,128)(2,1)S(1)}, u32[]{:S(2)}, u32[]{:S(2)}) %all-to-all-start.3) | async-done | bytes 2097184 | tf_op jit(solution)/shard_map/all_to_all | solution.py:345
  219.2 3.6 %all-to-all-start.4 = ((bf16[8,128,1024]{2,1,0:T(8,128)(2,1)}), bf16[8,128,1024]{2,1,0:T(8,128)(2,1)S(1)}, u32[]{:S(2)}, u32[]{:S(2)}) async-start(bf16[8,128,1024]{2,1,0:T(8,128)(2,1)} %bitcast.50), calls=%async_computation.4 | async-start | bytes 4194304 | tf_op jit(solution)/shard_map/all_to_all | solution.py:345
  222.9 2.2 convert_add_fusion
  227.0 30.4 %collective-permute-done.17 = bf16[256,1024]{1,0:T(8,128)(2,1)S(1)} collective-permute-done((bf16[256,1024]{1,0:T(8,128)(2,1)S(1)}, bf16[256,1024]{1,0:T(8,128)(2,1)S(1)}, u32[]{:S(2)}, u32[]{:S(2)}) %collective-permute-start.17) | collective-permute-done | bytes 524320 | tf_op jit(solution)/shard_map/ppermute | solution.py:301
  (88 shorter events, 31.2 us)
Async XLA Ops:
  0.6 2.2 collective-permute-start
  0.7 2.9 %collective-permute-start.1 = (bf16[256,1024]{1,0:T(8,128)(2,1)}, bf16[256,1024]{1,0:T(8,128)(2,1)S(1)}, u32[]{:S(2)}, u32[]{:S(2)}) collective-permute-start(bf16[256,1024]{1,0:T(8,128)(2,1)} %refs_3_.1), channel_id=1, source_target_pairs={{0,32},{32,0},{1,33},{33,1},{2,34},{34,2},{3,35},{35,3},{4,36},{36... | collective-permute-start | bytes 1572872 | tf_op jit(solution)/shard_map/ppermute | solution.py:301
  12.8 14.8 %copy-start.6 = (bf16[256,1024]{1,0:T(8,128)(2,1)S(1)}, bf16[256,1024]{1,0:T(8,128)(2,1)}, u32[]{:S(2)}) copy-start(bf16[256,1024]{1,0:T(8,128)(2,1)} %refs_3_.1) | copy-start | bytes 1572868
  13.9 55.9 %all-to-all-start = ((bf16[128,2,8,256]{3,2,1,0:T(8,128)(2,1)}), bf16[128,2,8,256]{3,2,1,0:T(8,128)(2,1)S(1)}, u32[]{:S(2)}, u32[]{:S(2)}) async-start(bf16[128,2,8,256]{3,2,1,0:T(8,128)(2,1)} %bitcast.8), calls=%async_computation | async-start | bytes 2097152 | tf_op jit(solution)/shard_map/all_to_all | solution.py:316
  25.1 25.8 %collective-permute-start.5 = (bf16[256,1024]{1,0:T(8,128)(2,1)S(1)}, bf16[256,1024]{1,0:T(8,128)(2,1)}, u32[]{:S(2)}, u32[]{:S(2)}) collective-permute-start(bf16[256,1024]{1,0:T(8,128)(2,1)S(1)} %copy-done.5), channel_id=1, source_target_pairs={{0,64},{64,0},{1,65},{65,1},{2,66},{66,2},{3,67},{67,3},{4,68},{68... | collective-permute-start | bytes 1572872 | tf_op jit(solution)/shard_map/ppermute | solution.py:301
  27.6 34.1 %collective-permute-start.6 = (bf16[256,1024]{1,0:T(8,128)(2,1)S(1)}, bf16[256,1024]{1,0:T(8,128)(2,1)}, u32[]{:S(2)}, u32[]{:S(2)}) collective-permute-start(bf16[256,1024]{1,0:T(8,128)(2,1)S(1)} %copy-done.6), channel_id=1, source_target_pairs={{0,64},{64,0},{1,65},{65,1},{2,66},{66,2},{3,67},{67,3},{4,68},{68... | collective-permute-start | bytes 1572872 | tf_op jit(solution)/shard_map/ppermute | solution.py:301
  61.7 18.8 %collective-permute-start.7 = (bf16[256,1024]{1,0:T(8,128)(2,1)}, bf16[256,1024]{1,0:T(8,128)(2,1)S(1)}, u32[]{:S(2)}, u32[]{:S(2)}) collective-permute-start(bf16[256,1024]{1,0:T(8,128)(2,1)} %collective-permute-done.5.refs_2_), channel_id=1, source_target_pairs={{0,32},{32,0},{1,33},{33,1},{2,34},{34,2},{3,35},{35,3},{4,36},{36... | collective-permute-start | bytes 1572872 | tf_op jit(solution)/shard_map/ppermute | solution.py:301
  61.7 18.8 %collective-permute-start.8 = (bf16[256,1024]{1,0:T(8,128)(2,1)}, bf16[256,1024]{1,0:T(8,128)(2,1)S(1)}, u32[]{:S(2)}, u32[]{:S(2)}) collective-permute-start(bf16[256,1024]{1,0:T(8,128)(2,1)} %collective-permute-done.6.refs_4_), channel_id=1, source_target_pairs={{0,32},{32,0},{1,33},{33,1},{2,34},{34,2},{3,35},{35,3},{4,36},{36... | collective-permute-start | bytes 1572872 | tf_op jit(solution)/shard_map/ppermute | solution.py:301
  64.3 9.6 %collective-permute-start.2 = (bf16[2,256,256]{2,1,0:T(8,128)(2,1)}, bf16[2,256,256]{2,1,0:T(8,128)(2,1)S(1)}, u32[]{:S(2)}, u32[]{:S(2)}) collective-permute-start(bf16[2,256,256]{2,1,0:T(8,128)(2,1)} %get-tuple-element.65), channel_id=1, source_target_pairs={{0,2},{2,4},{4,6},{6,0},{1,3},{3,5},{5,7},{7,1},{8,10},{10,12},{12... | collective-permute-start | bytes 786440 | tf_op jit(solution)/shard_map/ppermute | solution.py:298
  65.7 14.8 %collective-permute-start.3 = (bf16[2,256,256]{2,1,0:T(8,128)(2,1)}, bf16[2,256,256]{2,1,0:T(8,128)(2,1)S(1)}, u32[]{:S(2)}, u32[]{:S(2)}) collective-permute-start(bf16[2,256,256]{2,1,0:T(8,128)(2,1)} %get-tuple-element.64), channel_id=1, source_target_pairs={{0,4},{2,6},{4,0},{6,2},{1,5},{3,7},{5,1},{7,3},{8,12},{10,14},{12... | collective-permute-start | bytes 786440 | tf_op jit(solution)/shard_map/ppermute | solution.py:298
  68.5 12.0 %collective-permute-start.4 = (bf16[2,256,256]{2,1,0:T(8,128)(2,1)}, bf16[2,256,256]{2,1,0:T(8,128)(2,1)S(1)}, u32[]{:S(2)}, u32[]{:S(2)}) collective-permute-start(bf16[2,256,256]{2,1,0:T(8,128)(2,1)} %get-tuple-element.63), channel_id=1, source_target_pairs={{0,6},{2,0},{4,2},{6,4},{1,7},{3,1},{5,3},{7,5},{8,14},{10,8},{12,... | collective-permute-start | bytes 786440 | tf_op jit(solution)/shard_map/ppermute | solution.py:298
  91.4 18.8 %all-to-all-start.1 = ((bf16[4,2,256,256]{3,2,1,0:T(8,128)(2,1)}), bf16[4,2,256,256]{3,2,1,0:T(8,128)(2,1)S(1)}, u32[]{:S(2)}, u32[]{:S(2)}) async-start(bf16[4,2,256,256]{3,2,1,0:T(8,128)(2,1)} %project_far.1), calls=%async_computation.1 | async-start | bytes 2097152 | tf_op jit(solution)/shard_map/all_to_all | solution.py:324
  121.9 42.6 %collective-permute-start.10 = (bf16[2,256,1024]{2,1,0:T(8,128)(2,1)}, bf16[2,256,1024]{2,1,0:T(8,128)(2,1)S(1)}, u32[]{:S(2)}, u32[]{:S(2)}) collective-permute-start(bf16[2,256,1024]{2,1,0:T(8,128)(2,1)} %get-tuple-element.53.refs_0_), channel_id=1, source_target_pairs={{0,6},{2,0},{4,2},{6,4},{1,7},{3,1},{5,3},{7,5},{8,14},{10,8},{12,... | collective-permute-start | bytes 3145736 | tf_op jit(solution)/shard_map/ppermute | solution.py:298
  123.1 41.4 %collective-permute-start.9 = (bf16[2,256,1024]{2,1,0:T(8,128)(2,1)}, bf16[2,256,1024]{2,1,0:T(8,128)(2,1)S(1)}, u32[]{:S(2)}, u32[]{:S(2)}) collective-permute-start(bf16[2,256,1024]{2,1,0:T(8,128)(2,1)} %get-tuple-element.53.refs_0_), channel_id=1, source_target_pairs={{0,2},{2,4},{4,6},{6,0},{1,3},{3,5},{5,7},{7,1},{8,10},{10,12},{12... | collective-permute-start | bytes 3145736 | tf_op jit(solution)/shard_map/ppermute | solution.py:298
  124.1 40.4 %copy-start.4 = (bf16[4,2,256,256]{3,2,1,0:T(8,128)(2,1)}, bf16[4,2,256,256]{3,2,1,0:T(8,128)(2,1)S(1)}, u32[]{:S(2)}) copy-start(bf16[4,2,256,256]{3,2,1,0:T(8,128)(2,1)S(1)} %pad_maximum_fusion.p0) | copy-start | bytes 3145732
  124.2 40.3 %collective-permute-start.13 = (bf16[4,2,256,256]{3,2,1,0:T(8,128)(2,1)S(1)}, bf16[4,2,256,256]{3,2,1,0:T(8,128)(2,1)S(1)}, u32[]{:S(2)}, u32[]{:S(2)}) collective-permute-start(bf16[4,2,256,256]{3,2,1,0:T(8,128)(2,1)S(1)} %pad_maximum_fusion.p0), channel_id=1, source_target_pairs={{0,64},{64,0},{1,65},{65,1},{2,66},{66,2},{3,67},{67,3},{4,68},{68... | collective-permute-start | bytes 3145736 | tf_op jit(solution)/shard_map/ppermute | solution.py:301
  164.5 4.8 %collective-permute-start.14 = (bf16[4,2,256,256]{3,2,1,0:T(8,128)(2,1)S(1)}, bf16[4,2,256,256]{3,2,1,0:T(8,128)(2,1)S(1)}, u32[]{:S(2)}, u32[]{:S(2)}) collective-permute-start(bf16[4,2,256,256]{3,2,1,0:T(8,128)(2,1)S(1)} %pad_maximum_fusion.p0), channel_id=1, source_target_pairs={{0,32},{32,0},{1,33},{33,1},{2,34},{34,2},{3,35},{35,3},{4,36},{36... | collective-permute-start | bytes 3145736 | tf_op jit(solution)/shard_map/ppermute | solution.py:301
  164.6 4.7 %collective-permute-start.15 = (bf16[4,2,256,256]{3,2,1,0:T(8,128)(2,1)S(1)}, bf16[4,2,256,256]{3,2,1,0:T(8,128)(2,1)}, u32[]{:S(2)}, u32[]{:S(2)}) collective-permute-start(bf16[4,2,256,256]{3,2,1,0:T(8,128)(2,1)S(1)} %collective-permute-done.13.p2), channel_id=1, source_target_pairs={{0,32},{32,0},{1,33},{33,1},{2,34},{34,2},{3,35},{35,3},{4,36},{36... | collective-permute-start | bytes 3145736 | tf_op jit(solution)/shard_map/ppermute | solution.py:301
  165.2 15.2 %collective-permute-start.11 = (bf16[2,128,1024]{2,1,0:T(8,128)(2,1)S(1)}, bf16[2,128,1024]{2,1,0:T(8,128)(2,1)S(1)}, u32[]{:S(2)}, u32[]{:S(2)}) collective-permute-start(bf16[2,128,1024]{2,1,0:T(8,128)(2,1)S(1)} %slice.37), channel_id=1, source_target_pairs={{0,2},{2,4},{4,6},{6,0},{1,3},{3,5},{5,7},{7,1},{8,10},{10,12},{12... | collective-permute-start | bytes 1572872 | tf_op jit(solution)/shard_map/ppermute | solution.py:298
  166.3 14.5 %collective-permute-start.12 = (bf16[2,128,1024]{2,1,0:T(8,128)(2,1)}, bf16[2,128,1024]{2,1,0:T(8,128)(2,1)S(1)}, u32[]{:S(2)}, u32[]{:S(2)}) collective-permute-start(bf16[2,128,1024]{2,1,0:T(8,128)(2,1)} %slice.38), channel_id=1, source_target_pairs={{0,6},{2,0},{4,2},{6,4},{1,7},{3,1},{5,3},{7,5},{8,14},{10,8},{12,... | collective-permute-start | bytes 1572872 | tf_op jit(solution)/shard_map/ppermute | solution.py:298
  188.2 30.0 %all-to-all-start.3 = ((bf16[8,1024,128]{2,1,0:T(8,128)(2,1)}), bf16[8,1024,128]{2,1,0:T(8,128)(2,1)S(1)}, u32[]{:S(2)}, u32[]{:S(2)}) async-start(bf16[8,1024,128]{2,1,0:T(8,128)(2,1)} %output_weight_terms.1), calls=%async_computation.3 | async-start | bytes 4194304 | tf_op jit(solution)/shard_map/all_to_all | solution.py:345
  207.4 15.5 %collective-permute-start.16 = (bf16[2,256,1024]{2,1,0:T(8,128)(2,1)}, bf16[2,256,1024]{2,1,0:T(8,128)(2,1)}, u32[]{:S(2)}, u32[]{:S(2)}) collective-permute-start(bf16[2,256,1024]{2,1,0:T(8,128)(2,1)} %get-tuple-element.59), channel_id=1, source_target_pairs={{0,32},{32,0},{1,33},{33,1},{2,34},{34,2},{3,35},{35,3},{4,36},{36... | collective-permute-start | bytes 3145736 | tf_op jit(solution)/shard_map/ppermute | solution.py:301
  219.2 39.1 %all-to-all-start.4 = ((bf16[8,128,1024]{2,1,0:T(8,128)(2,1)}), bf16[8,128,1024]{2,1,0:T(8,128)(2,1)S(1)}, u32[]{:S(2)}, u32[]{:S(2)}) async-start(bf16[8,128,1024]{2,1,0:T(8,128)(2,1)} %bitcast.50), calls=%async_computation.4 | async-start | bytes 4194304 | tf_op jit(solution)/shard_map/all_to_all | solution.py:345
  225.1 32.3 %collective-permute-start.17 = (bf16[256,1024]{1,0:T(8,128)(2,1)S(1)}, bf16[256,1024]{1,0:T(8,128)(2,1)S(1)}, u32[]{:S(2)}, u32[]{:S(2)}) collective-permute-start(bf16[256,1024]{1,0:T(8,128)(2,1)S(1)} %fusion.2), channel_id=1, source_target_pairs={{0,64},{64,0},{1,65},{65,1},{2,66},{66,2},{3,67},{67,3},{4,68},{68... | collective-permute-start | bytes 1572872 | tf_op jit(solution)/shard_map/ppermute | solution.py:301
  (16 other events, 81.5 us)

commit v10 on v9

--- a/solution.py
+++ b/solution.py
@@ -313,14 +313,13 @@
 
     own = jnp.stack([context_keys, context_values]).reshape(2, 8, 4, 4, PIECE).transpose(2, 3, 0, 1, 4)
     own = jnp.broadcast_to(own[:, None, :, None], (4, 4, 4, 2, 2, 8, PIECE)).reshape(128, 2, 8, PIECE)
-    context = lax.all_to_all(after(own, products), HEADS + SEQ, 0, 0, tiled=True)
+    context = lax.all_to_all(after(own, products, far_states, far_cotangent, quarters), HEADS + SEQ, 0, 0, tiled=True)
     keys = context[:, 0].reshape(4 * TOK, PIECE)
     values = context[:, 1].reshape(4 * TOK, PIECE)
     bias = context_bias(lengths, slot_passage)
 
-    far_states, far_cotangent = after((far_states, far_cotangent), products)
     far = (far_states, swap(far_states, "core"), far_cotangent, swap(far_cotangent, "core"))
-    rows = project("project_far", pos, far, query_weight, output_weight, after(products, keys, quarters))
+    rows = project("project_far", pos, far, query_weight, output_weight, products)
     rows = lax.all_to_all(rows, "y", 0, 0, tiled=True)
 
     piece = jnp.stack(after(quarters, rows))
@@ -336,7 +335,7 @@
     owned = jnp.sum(moved.reshape(4, 4, 4, 2, 2, 8, PIECE).astype(F32), axis=(1, 3))
     owned = owned.transpose(2, 3, 0, 1, 4).reshape(2, 8, 16 * PIECE)
 
-    piece, over_x = after((piece, over_x), left, right, moved)
+    piece, over_x = after((piece, over_x), left, right)
     group_states, group_cotangent = assemble(
         pos, (piece, swap(piece, "core"), over_x, swap(over_x, "core"))
     )
@@ -345,17 +344,18 @@
         return jnp.sum(lax.all_to_all(parts, ("z", "xl"), 0, 0, tiled=True).astype(F32), axis=0)
 
     output_parts = weight_terms(
-        "output_weight_terms", output_grad_kernel, pos, 0, every, group_cotangent, (PLANES, BLOCK, 128)
+        "output_weight_terms", output_grad_kernel, pos, 0, after(every, moved), group_cotangent, (PLANES, BLOCK, 128)
     )
     output_weight_grad = plane_sum(output_parts)
     query_parts = weight_terms(
         "query_weight_terms", query_grad_kernel, pos, 1, after(every, output_parts), group_states, (BLOCK, BLOCK)
     )
-    query_weight_grad = plane_sum(after(query_parts, output_weight_grad).reshape(PLANES, 128, BLOCK))
-
     give, keep = output_terms(pos, after(every, query_parts), output_weight)
     pair = keep + swap(give, "core").astype(F32)
-    attended = (pair[0] + swap(pair[1].astype(BF16), "xh").astype(F32)).astype(BF16)
+    pair_far = pair[1].astype(BF16)
+    attended = (pair[0] + swap(pair_far, "xh").astype(F32)).astype(BF16)
+    query_parts = after(query_parts, output_weight_grad, pair_far)
+    query_weight_grad = plane_sum(query_parts.reshape(PLANES, 128, BLOCK))
     return attended, query_weight_grad, output_weight_grad, owned[0], owned[1]
 
 

time: 262 us -> 240 us (0.916)
  blocking collectives: 39.8 us -> 0 us
  waiting for transfers between devices: 99.9 us -> 111 us
  starting transfers between devices: 40.3 us -> 49.3 us
  local copies, waits for them, and re-layouts: 15.7 us -> 11.3 us
  other arithmetic: 6.9 us -> 10.3 us
    all_to_all x1 -> x0, blocking collectives: 39.8 us -> none  [on_device(): moved = lax.all_to_all(terms, HEADS + SEQ, 0, 0, tiled=True)]
    all_to_all x1 -> x2, waiting for transfers between devices: 0.01 us -> 21.4 us  [the longest x1 15.1 us: on_device(): moved = lax.all_to_all(terms, HEADS + SEQ, 0, 0, tiled=True)]
    ppermute x11, waiting for transfers between devices: 60.7 us -> 53 us  [swap(): return lax.ppermute(x, axis, SWAP)]
    all_to_all x2, waiting for transfers between devices: 10.7 us -> 4.45 us  [plane_sum(): lax.all_to_all(parts, ('z', 'xl'), 0, 0, tiled=True).astype(F32)]
    ppermute x7, waiting for transfers between devices: 14.4 us -> 19.6 us  [shift(): return lax.ppermute(x, axis, [(i, (i + d) % 4) for i in range(4)])]
    all_to_all x1 -> x2, starting transfers between devices: 11.1 us -> 16.1 us  [the longest x1 11.1 us: on_device(): lax.all_to_all(after(own, products, far_states, far_cotangent, quarters),...]
    unnamed x38 -> x42, local copies, waits for them, and re-layouts: 6.9 us -> 2.95 us
  transfers between devices with their start and end apart: 22 -> 23, of which waited for: 10 -> 14; matrix products, arithmetic and copies ran while one was open for 6% -> 6% of each run, Pallas kernels for 8% -> 18%
where the time goes in v10:
time: 240 us; the launch traced here: 239 us
  waiting for transfers between devices  111 us (46%)
  Pallas kernels  56 us (23%)
  starting transfers between devices  49.3 us (21%)
  local copies, waits for them, and re-layouts  11.3 us (5%)
  other arithmetic  10.3 us (4%)
    pallas_call x7, Pallas kernels, call(): pl.pallas_call(kernel, grid_spec=pltpu.PrefetchScalarGridSpec(num_scalar_...  56 us
    ppermute x11, waiting for transfers between devices, swap(): return lax.ppermute(x, axis, SWAP)  53 us
    ppermute x7, waiting for transfers between devices, shift(): return lax.ppermute(x, axis, [(i, (i + d) % 4) for i in range(4)])  19.6 us
    all_to_all x1, waiting for transfers between devices, on_device(): moved = lax.all_to_all(terms, HEADS + SEQ, 0, 0, tiled=True)  15.1 us
    all_to_all x1, waiting for transfers between devices, on_device(): rows = lax.all_to_all(rows, 'y', 0, 0, tiled=True)  13.1 us
    ppermute x7, starting transfers between devices, shift(): return lax.ppermute(x, axis, [(i, (i + d) % 4) for i in range(4)])  11.3 us
    all_to_all x1, starting transfers between devices, on_device(): lax.all_to_all(after(own, products, far_states, far_cotangent, quarters),...  11.1 us
    all_to_all x2, starting transfers between devices, plane_sum(): lax.all_to_all(parts, ('z', 'xl'), 0, 0, tiled=True).astype(F32)  9.3 us
  transfers between devices with their start and end apart: 23, of which 14 were waited for; matrix products, arithmetic and copies ran while one was open for 6% of the time, Pallas kernels for 18%

profile of v10, /device:TPU:0, one launch (start us, length us, event | category | flops | bytes accessed | tf_op | source)
XLA Modules:
  0.0 239.4 jit_solution(18439106055604386582)
XLA Ops:
  0.7 3.2 %collective-permute-start.2 = (bf16[256,1024]{1,0:T(8,128)(2,1)}, bf16[256,1024]{1,0:T(8,128)(2,1)S(1)}, u32[]{:S(2)}, u32[]{:S(2)}) collective-permute-start(bf16[256,1024]{1,0:T(8,128)(2,1)} %refs_1_.1), channel_id=1, source_target_pairs={{0,64},{64,0},{1,65},{65,1},{2,66},{66,2},{3,67},{67,3},{4,68},{68... | collective-permute-start | bytes 1572872 | tf_op jit(solution)/shard_map/ppermute | solution.py:301
  9.4 2.9 %collective-permute-start.7 = (bf16[2,256,256]{2,1,0:T(8,128)(2,1)S(1)}, bf16[2,256,256]{2,1,0:T(8,128)(2,1)S(1)}, u32[]{:S(2)}, u32[]{:S(2)}) collective-permute-start(bf16[2,256,256]{2,1,0:T(8,128)(2,1)S(1)} %get-tuple-element.68), channel_id=1, source_target_pairs={{0,4},{2,6},{4,0},{6,2},{1,5},{3,7},{5,1},{7,3},{8,12},{10,14},{12... | collective-permute-start | bytes 786440 | tf_op jit(solution)/shard_map/ppermute | solution.py:298
  14.4 8.4 %project_near.1.refs_1_ = f32[2,256,1024]{2,1,0:T(8,128)} custom-call(s32[5]{0:T(128)} %stack.59.refs_0_.pos, bf16[256,1024]{1,0:T(8,128)(2,1)} %refs_1_.1, bf16[256,1024]{1,0:T(8,128)(2,1)} %collective-permute-done.refs_2_, bf16[256,1024]{1,0:T(8,128)(2,1)} %refs_3_.1, bf16[256,1024]{1,0:T(8,128)(2,1)} %collective-permute-done.1.refs_4_, ...), custom_call_target="tpu_custom_call" | custom-call | flops 2147483648 | bytes 8388608 | tf_op jit(solution)/shard_map/project_near/pallas_call | solution.py:50
  24.2 3.8 %collective-permute-done.4.refs_4_ = bf16[256,1024]{1,0:T(8,128)(2,1)S(1)} collective-permute-done((bf16[256,1024]{1,0:T(8,128)(2,1)}, bf16[256,1024]{1,0:T(8,128)(2,1)S(1)}, u32[]{:S(2)}, u32[]{:S(2)}) %collective-permute-start.4) | collective-permute-done | bytes 524320 | tf_op jit(solution)/shard_map/ppermute | solution.py:301
  29.2 11.1 %all-to-all-start.1 = ((bf16[128,2,8,256]{3,2,1,0:T(8,128)(2,1)}), bf16[128,2,8,256]{3,2,1,0:T(8,128)(2,1)S(1)}, u32[]{:S(2)}, u32[]{:S(2)}) async-start(bf16[128,2,8,256]{3,2,1,0:T(8,128)(2,1)} %bitcast.8), calls=%async_computation.1 | async-start | bytes 2097152 | tf_op jit(solution)/shard_map/all_to_all | solution.py:316
  43.9 9.3 %project_far.1 = bf16[4,2,256,256]{3,2,1,0:T(8,128)(2,1)} custom-call(s32[5]{0:T(128)} %stack.59.refs_0_.pos, f32[2,256,1024]{2,1,0:T(8,128)} %project_near.1.refs_1_, bf16[256,1024]{1,0:T(8,128)(2,1)} %copy-done.6, bf16[256,1024]{1,0:T(8,128)(2,1)} %copy-done.8, bf16[256,1024]{1,0:T(8,128)(2,1)} %copy-done.7, bf16[256,1024]{1,0:T(8,128)(2,1)} %copy-done.9, ...), custom_call_target="tpu_custom_call" | custom-call | flops 2147483648 | bytes 8388608 | tf_op jit(solution)/shard_map/project_far/pallas_call | solution.py:50
  53.3 6.3 %all-to-all-done.1 = bf16[128,2,8,256]{3,2,1,0:T(8,128)(2,1)S(1)} async-done(((bf16[128,2,8,256]{3,2,1,0:T(8,128)(2,1)}), bf16[128,2,8,256]{3,2,1,0:T(8,128)(2,1)S(1)}, u32[]{:S(2)}, u32[]{:S(2)}) %all-to-all-start.1) | async-done | bytes 1048608 | tf_op jit(solution)/shard_map/all_to_all | solution.py:316
  59.6 3.5 %all-to-all-start = ((bf16[4,2,256,256]{3,2,1,0:T(8,128)(2,1)}), bf16[4,2,256,256]{3,2,1,0:T(8,128)(2,1)S(1)}, u32[]{:S(2)}, u32[]{:S(2)}) async-start(bf16[4,2,256,256]{3,2,1,0:T(8,128)(2,1)} %project_far.1), calls=%async_computation | async-start | bytes 2097152 | tf_op jit(solution)/shard_map/all_to_all | solution.py:323
  65.0 13.1 %all-to-all-done.rows = bf16[4,2,256,256]{3,2,1,0:T(8,128)(2,1)S(1)} async-done(((bf16[4,2,256,256]{3,2,1,0:T(8,128)(2,1)}), bf16[4,2,256,256]{3,2,1,0:T(8,128)(2,1)S(1)}, u32[]{:S(2)}, u32[]{:S(2)}) %all-to-all-start) | async-done | bytes 1048608 | tf_op jit(solution)/shard_map/all_to_all | solution.py:323
  80.5 10.8 %attention.1 = (bf16[2,256,1024]{2,1,0:T(8,128)(2,1)}, bf16[1024,256]{1,0:T(8,128)(2,1)}, bf16[1024,256]{1,0:T(8,128)(2,1)}) custom-call(s32[5]{0:T(128)} %stack.59.refs_0_.pos, f32[1,1024]{1,0:T(1,128)} %bitcast.63, bf16[4,2,256,256]{3,2,1,0:T(8,128)(2,1)} %copy-done.5, bf16[1024,256]{1,0:T(8,128)(2,1)} %get-tuple-element.66.k_ref, ...), custom_call_target="tpu_custom_call" | custom-call | flops 8053063680 | bytes 4194304 | tf_op jit(solution)/shard_map/attention/pallas_call | solution.py:50
  93.3 11.5 %collective-permute-done.13.p2 = bf16[4,2,256,256]{3,2,1,0:T(8,128)(2,1)} collective-permute-done((bf16[4,2,256,256]{3,2,1,0:T(8,128)(2,1)}, bf16[4,2,256,256]{3,2,1,0:T(8,128)(2,1)}, u32[]{:S(2)}, u32[]{:S(2)}) %collective-permute-start.13) | collective-permute-done | bytes 1048608 | tf_op jit(solution)/shard_map/ppermute | solution.py:301
  104.8 10.4 %collective-permute-done.10.refs_2_ = bf16[2,256,1024]{2,1,0:T(8,128)(2,1)S(1)} collective-permute-done((bf16[2,256,1024]{2,1,0:T(8,128)(2,1)}, bf16[2,256,1024]{2,1,0:T(8,128)(2,1)S(1)}, u32[]{:S(2)}, u32[]{:S(2)}) %collective-permute-start.10) | collective-permute-done | bytes 1048608 | tf_op jit(solution)/shard_map/ppermute | solution.py:298
  120.1 5.0 %all-to-all-start.2 = ((bf16[128,2,8,256]{3,2,1,0:T(8,128)(2,1)}), bf16[128,2,8,256]{3,2,1,0:T(8,128)(2,1)S(1)}, u32[]{:S(2)}, u32[]{:S(2)}) async-start(bf16[128,2,8,256]{3,2,1,0:T(8,128)(2,1)} %pad_maximum_fusion), calls=%async_computation.2 | async-start | bytes 2097152 | tf_op jit(solution)/shard_map/all_to_all | solution.py:334
  129.2 15.1 %all-to-all-done.2 = bf16[128,2,8,256]{3,2,1,0:T(8,128)(2,1)S(1)} async-done(((bf16[128,2,8,256]{3,2,1,0:T(8,128)(2,1)}), bf16[128,2,8,256]{3,2,1,0:T(8,128)(2,1)S(1)}, u32[]{:S(2)}, u32[]{:S(2)}) %all-to-all-start.2) | async-done | bytes 1048608 | tf_op jit(solution)/shard_map/all_to_all | solution.py:334
  144.3 5.8 %collective-permute-done.11.refs_3_ = bf16[2,128,1024]{2,1,0:T(8,128)(2,1)S(1)} collective-permute-done((bf16[2,128,1024]{2,1,0:T(8,128)(2,1)}, bf16[2,128,1024]{2,1,0:T(8,128)(2,1)S(1)}, u32[]{:S(2)}, u32[]{:S(2)}) %collective-permute-start.11) | collective-permute-done | bytes 524320 | tf_op jit(solution)/shard_map/ppermute | solution.py:298
  150.1 5.6 %column_blocks.1 = (bf16[1024,1024]{1,0:T(8,128)(2,1)}, bf16[1024,1024]{1,0:T(8,128)(2,1)}) custom-call(s32[5]{0:T(128)} %stack.59.refs_0_.pos, bf16[4,2,256,256]{3,2,1,0:T(8,128)(2,1)} %pad_maximum_fusion.1.p0, bf16[4,2,256,256]{3,2,1,0:T(8,128)(2,1)} %collective-permute-done.14.p1, bf16[4,2,256,256]{3,2,1,0:T(8,128)(2,1)} %collective-permute-done.13.p2, ...), custom_call_target="tpu_custom_call" | custom-call | bytes 8388608 | tf_op jit(solution)/shard_map/column_blocks/pallas_call | solution.py:50
  155.7 6.6 %output_weight_terms.1 = bf16[8,1024,128]{2,1,0:T(8,128)(2,1)} custom-call(s32[5]{0:T(128)} %stack.59.refs_0_.pos, bf16[2,256,1024]{2,1,0:T(8,128)(2,1)} %get-tuple-element.57.refs_0_, bf16[2,256,1024]{2,1,0:T(8,128)(2,1)} %copy-done.1, bf16[2,256,1024]{2,1,0:T(8,128)(2,1)} %copy-done, bf16[2,128,1024]{2,1,0:T(8,128)(2,1)} %copy-done.3, ...), custom_call_target="tpu_custom_call" | custom-call | flops 2147483648 | bytes 6291456 | tf_op jit(solution)/shard_map/output_weight_terms/pallas_call | solution.py:50
  162.3 5.7 %all-to-all-start.3 = ((bf16[8,1024,128]{2,1,0:T(8,128)(2,1)}), bf16[8,1024,128]{2,1,0:T(8,128)(2,1)S(1)}, u32[]{:S(2)}, u32[]{:S(2)}) async-start(bf16[8,1024,128]{2,1,0:T(8,128)(2,1)} %output_weight_terms.1), calls=%async_computation.3 | async-start | bytes 4194304 | tf_op jit(solution)/shard_map/all_to_all | solution.py:344
  168.0 7.2 %query_weight_terms.1 = bf16[1024,1024]{1,0:T(8,128)(2,1)} custom-call(s32[5]{0:T(128)} %stack.59.refs_0_.pos, bf16[2,256,1024]{2,1,0:T(8,128)(2,1)} %get-tuple-element.57.refs_0_, bf16[2,256,1024]{2,1,0:T(8,128)(2,1)} %copy-done.1, bf16[2,256,1024]{2,1,0:T(8,128)(2,1)} %copy-done, bf16[2,128,1024]{2,1,0:T(8,128)(2,1)} %copy-done.3, ...), custom_call_target="tpu_custom_call" | custom-call | flops 2147483648 | bytes 6291456 | tf_op jit(solution)/shard_map/query_weight_terms/pallas_call | solution.py:50
  175.2 8.2 %output_terms.1 = (bf16[2,256,1024]{2,1,0:T(8,128)(2,1)}, f32[2,256,1024]{2,1,0:T(8,128)}) custom-call(s32[5]{0:T(128)} %stack.59.refs_0_.pos, bf16[2,256,1024]{2,1,0:T(8,128)(2,1)} %get-tuple-element.57.refs_0_, bf16[2,256,1024]{2,1,0:T(8,128)(2,1)} %copy-done.1, bf16[2,256,1024]{2,1,0:T(8,128)(2,1)} %copy-done, bf16[2,128,1024]{2,1,0:T(8,128)(2,1)} %copy-done.3, ...), custom_call_target="tpu_custom_call" | custom-call | flops 2147483648 | bytes 8388608 | tf_op jit(solution)/shard_map/output_terms/pallas_call | solution.py:50
  183.5 2.9 %collective-permute-done.16 = bf16[2,256,1024]{2,1,0:T(8,128)(2,1)S(1)} collective-permute-done((bf16[2,256,1024]{2,1,0:T(8,128)(2,1)}, bf16[2,256,1024]{2,1,0:T(8,128)(2,1)S(1)}, u32[]{:S(2)}, u32[]{:S(2)}) %collective-permute-start.16) | collective-permute-done | bytes 1048608 | tf_op jit(solution)/shard_map/ppermute | solution.py:301
  190.5 4.4 %all-to-all-done.3 = bf16[8,1024,128]{2,1,0:T(8,128)(2,1)S(1)} async-done(((bf16[8,1024,128]{2,1,0:T(8,128)(2,1)}), bf16[8,1024,128]{2,1,0:T(8,128)(2,1)S(1)}, u32[]{:S(2)}, u32[]{:S(2)}) %all-to-all-start.3) | async-done | bytes 2097184 | tf_op jit(solution)/shard_map/all_to_all | solution.py:344
  196.1 3.6 %all-to-all-start.4 = ((bf16[8,128,1024]{2,1,0:T(8,128)(2,1)}), bf16[8,128,1024]{2,1,0:T(8,128)(2,1)S(1)}, u32[]{:S(2)}, u32[]{:S(2)}) async-start(bf16[8,128,1024]{2,1,0:T(8,128)(2,1)} %bitcast.50), calls=%async_computation.4 | async-start | bytes 4194304 | tf_op jit(solution)/shard_map/all_to_all | solution.py:344
  203.4 32.7 %collective-permute-done.17 = bf16[256,1024]{1,0:T(8,128)(2,1)S(1)} collective-permute-done((bf16[256,1024]{1,0:T(8,128)(2,1)}, bf16[256,1024]{1,0:T(8,128)(2,1)S(1)}, u32[]{:S(2)}, u32[]{:S(2)}) %collective-permute-start.17) | collective-permute-done | bytes 524320 | tf_op jit(solution)/shard_map/ppermute | solution.py:301
  (93 shorter events, 41.5 us)
Async XLA Ops:
  0.6 8.8 %collective-permute-start = (bf16[256,1024]{1,0:T(8,128)(2,1)}, bf16[256,1024]{1,0:T(8,128)(2,1)}, u32[]{:S(2)}, u32[]{:S(2)}) collective-permute-start(bf16[256,1024]{1,0:T(8,128)(2,1)} %refs_1_.1), channel_id=1, source_target_pairs={{0,32},{32,0},{1,33},{33,1},{2,34},{34,2},{3,35},{35,3},{4,36},{36... | collective-permute-start | bytes 1572872 | tf_op jit(solution)/shard_map/ppermute | solution.py:301
  0.7 23.5 %collective-permute-start.2 = (bf16[256,1024]{1,0:T(8,128)(2,1)}, bf16[256,1024]{1,0:T(8,128)(2,1)S(1)}, u32[]{:S(2)}, u32[]{:S(2)}) collective-permute-start(bf16[256,1024]{1,0:T(8,128)(2,1)} %refs_1_.1), channel_id=1, source_target_pairs={{0,64},{64,0},{1,65},{65,1},{2,66},{66,2},{3,67},{67,3},{4,68},{68... | collective-permute-start | bytes 1572872 | tf_op jit(solution)/shard_map/ppermute | solution.py:301
  3.9 8.4 %collective-permute-start.1 = (bf16[256,1024]{1,0:T(8,128)(2,1)}, bf16[256,1024]{1,0:T(8,128)(2,1)}, u32[]{:S(2)}, u32[]{:S(2)}) collective-permute-start(bf16[256,1024]{1,0:T(8,128)(2,1)} %refs_3_.1), channel_id=1, source_target_pairs={{0,32},{32,0},{1,33},{33,1},{2,34},{34,2},{3,35},{35,3},{4,36},{36... | collective-permute-start | bytes 1572872 | tf_op jit(solution)/shard_map/ppermute | solution.py:301
  4.1 24.0 %collective-permute-start.4 = (bf16[256,1024]{1,0:T(8,128)(2,1)}, bf16[256,1024]{1,0:T(8,128)(2,1)S(1)}, u32[]{:S(2)}, u32[]{:S(2)}) collective-permute-start(bf16[256,1024]{1,0:T(8,128)(2,1)} %refs_3_.1), channel_id=1, source_target_pairs={{0,64},{64,0},{1,65},{65,1},{2,66},{66,2},{3,67},{67,3},{4,68},{68... | collective-permute-start | bytes 1572872 | tf_op jit(solution)/shard_map/ppermute | solution.py:301
  7.7 15.1 %collective-permute-start.6 = (bf16[2,256,256]{2,1,0:T(8,128)(2,1)S(1)}, bf16[2,256,256]{2,1,0:T(8,128)(2,1)S(1)}, u32[]{:S(2)}, u32[]{:S(2)}) collective-permute-start(bf16[2,256,256]{2,1,0:T(8,128)(2,1)S(1)} %get-tuple-element.69), channel_id=1, source_target_pairs={{0,2},{2,4},{4,6},{6,0},{1,3},{3,5},{5,7},{7,1},{8,10},{10,12},{12... | collective-permute-start | bytes 786440 | tf_op jit(solution)/shard_map/ppermute | solution.py:298
  9.4 14.8 %collective-permute-start.7 = (bf16[2,256,256]{2,1,0:T(8,128)(2,1)S(1)}, bf16[2,256,256]{2,1,0:T(8,128)(2,1)S(1)}, u32[]{:S(2)}, u32[]{:S(2)}) collective-permute-start(bf16[2,256,256]{2,1,0:T(8,128)(2,1)S(1)} %get-tuple-element.68), channel_id=1, source_target_pairs={{0,4},{2,6},{4,0},{6,2},{1,5},{3,7},{5,1},{7,3},{8,12},{10,14},{12... | collective-permute-start | bytes 786440 | tf_op jit(solution)/shard_map/ppermute | solution.py:298
  12.3 11.9 %collective-permute-start.8 = (bf16[2,256,256]{2,1,0:T(8,128)(2,1)S(1)}, bf16[2,256,256]{2,1,0:T(8,128)(2,1)S(1)}, u32[]{:S(2)}, u32[]{:S(2)}) collective-permute-start(bf16[2,256,256]{2,1,0:T(8,128)(2,1)S(1)} %get-tuple-element.67), channel_id=1, source_target_pairs={{0,6},{2,0},{4,2},{6,4},{1,7},{3,1},{5,3},{7,5},{8,14},{10,8},{12,... | collective-permute-start | bytes 786440 | tf_op jit(solution)/shard_map/ppermute | solution.py:298
  29.2 30.4 %all-to-all-start.1 = ((bf16[128,2,8,256]{3,2,1,0:T(8,128)(2,1)}), bf16[128,2,8,256]{3,2,1,0:T(8,128)(2,1)S(1)}, u32[]{:S(2)}, u32[]{:S(2)}) async-start(bf16[128,2,8,256]{3,2,1,0:T(8,128)(2,1)} %bitcast.8), calls=%async_computation.1 | async-start | bytes 2097152 | tf_op jit(solution)/shard_map/all_to_all | solution.py:316
  40.4 2.0 collective-permute-start.3
  40.4 2.6 %collective-permute-start.5 = (bf16[256,1024]{1,0:T(8,128)(2,1)S(1)}, bf16[256,1024]{1,0:T(8,128)(2,1)S(1)}, u32[]{:S(2)}, u32[]{:S(2)}) collective-permute-start(bf16[256,1024]{1,0:T(8,128)(2,1)S(1)} %collective-permute-done.4.refs_4_), channel_id=1, source_target_pairs={{0,32},{32,0},{1,33},{33,1},{2,34},{34,2},{3,35},{35,3},{4,36},{36... | collective-permute-start | bytes 1572872 | tf_op jit(solution)/shard_map/ppermute | solution.py:301
  53.2 24.9 %copy-start.11 = (bf16[2,256,256]{2,1,0:T(8,128)(2,1)S(1)}, bf16[2,256,256]{2,1,0:T(8,128)(2,1)}, u32[]{:S(2)}) copy-start(bf16[2,256,256]{2,1,0:T(8,128)(2,1)} %copy-done.10) | copy-start | bytes 786436
  59.6 18.5 %all-to-all-start = ((bf16[4,2,256,256]{3,2,1,0:T(8,128)(2,1)}), bf16[4,2,256,256]{3,2,1,0:T(8,128)(2,1)S(1)}, u32[]{:S(2)}, u32[]{:S(2)}) async-start(bf16[4,2,256,256]{3,2,1,0:T(8,128)(2,1)} %project_far.1), calls=%async_computation | async-start | bytes 2097152 | tf_op jit(solution)/shard_map/all_to_all | solution.py:323
  79.4 25.4 %collective-permute-start.13 = (bf16[4,2,256,256]{3,2,1,0:T(8,128)(2,1)}, bf16[4,2,256,256]{3,2,1,0:T(8,128)(2,1)}, u32[]{:S(2)}, u32[]{:S(2)}) collective-permute-start(bf16[4,2,256,256]{3,2,1,0:T(8,128)(2,1)} %pad_maximum_fusion.1.p0), channel_id=1, source_target_pairs={{0,64},{64,0},{1,65},{65,1},{2,66},{66,2},{3,67},{67,3},{4,68},{68... | collective-permute-start | bytes 3145736 | tf_op jit(solution)/shard_map/ppermute | solution.py:301
  91.3 23.8 %collective-permute-start.10 = (bf16[2,256,1024]{2,1,0:T(8,128)(2,1)}, bf16[2,256,1024]{2,1,0:T(8,128)(2,1)S(1)}, u32[]{:S(2)}, u32[]{:S(2)}) collective-permute-start(bf16[2,256,1024]{2,1,0:T(8,128)(2,1)} %get-tuple-element.57.refs_0_), channel_id=1, source_target_pairs={{0,6},{2,0},{4,2},{6,4},{1,7},{3,1},{5,3},{7,5},{8,14},{10,8},{12,... | collective-permute-start | bytes 3145736 | tf_op jit(solution)/shard_map/ppermute | solution.py:298
  92.5 24.8 %collective-permute-start.9 = (bf16[2,256,1024]{2,1,0:T(8,128)(2,1)}, bf16[2,256,1024]{2,1,0:T(8,128)(2,1)S(1)}, u32[]{:S(2)}, u32[]{:S(2)}) collective-permute-start(bf16[2,256,1024]{2,1,0:T(8,128)(2,1)} %get-tuple-element.57.refs_0_), channel_id=1, source_target_pairs={{0,2},{2,4},{4,6},{6,0},{1,3},{3,5},{5,7},{7,1},{8,10},{10,12},{12... | collective-permute-start | bytes 3145736 | tf_op jit(solution)/shard_map/ppermute | solution.py:298
  117.3 32.8 %collective-permute-start.14 = (bf16[4,2,256,256]{3,2,1,0:T(8,128)(2,1)}, bf16[4,2,256,256]{3,2,1,0:T(8,128)(2,1)}, u32[]{:S(2)}, u32[]{:S(2)}) collective-permute-start(bf16[4,2,256,256]{3,2,1,0:T(8,128)(2,1)} %pad_maximum_fusion.1.p0), channel_id=1, source_target_pairs={{0,32},{32,0},{1,33},{33,1},{2,34},{34,2},{3,35},{35,3},{4,36},{36... | collective-permute-start | bytes 3145736 | tf_op jit(solution)/shard_map/ppermute | solution.py:301
  117.3 32.8 %collective-permute-start.15 = (bf16[4,2,256,256]{3,2,1,0:T(8,128)(2,1)}, bf16[4,2,256,256]{3,2,1,0:T(8,128)(2,1)}, u32[]{:S(2)}, u32[]{:S(2)}) collective-permute-start(bf16[4,2,256,256]{3,2,1,0:T(8,128)(2,1)} %collective-permute-done.13.p2), channel_id=1, source_target_pairs={{0,32},{32,0},{1,33},{33,1},{2,34},{34,2},{3,35},{35,3},{4,36},{36... | collective-permute-start | bytes 3145736 | tf_op jit(solution)/shard_map/ppermute | solution.py:301
  120.1 24.2 %all-to-all-start.2 = ((bf16[128,2,8,256]{3,2,1,0:T(8,128)(2,1)}), bf16[128,2,8,256]{3,2,1,0:T(8,128)(2,1)S(1)}, u32[]{:S(2)}, u32[]{:S(2)}) async-start(bf16[128,2,8,256]{3,2,1,0:T(8,128)(2,1)} %pad_maximum_fusion), calls=%async_computation.2 | async-start | bytes 2097152 | tf_op jit(solution)/shard_map/all_to_all | solution.py:334
  125.9 24.2 %collective-permute-start.11 = (bf16[2,128,1024]{2,1,0:T(8,128)(2,1)}, bf16[2,128,1024]{2,1,0:T(8,128)(2,1)S(1)}, u32[]{:S(2)}, u32[]{:S(2)}) collective-permute-start(bf16[2,128,1024]{2,1,0:T(8,128)(2,1)} %slice.37), channel_id=1, source_target_pairs={{0,2},{2,4},{4,6},{6,0},{1,3},{3,5},{5,7},{7,1},{8,10},{10,12},{12... | collective-permute-start | bytes 1572872 | tf_op jit(solution)/shard_map/ppermute | solution.py:298
  126.9 23.2 %collective-permute-start.12 = (bf16[2,128,1024]{2,1,0:T(8,128)(2,1)S(1)}, bf16[2,128,1024]{2,1,0:T(8,128)(2,1)S(1)}, u32[]{:S(2)}, u32[]{:S(2)}) collective-permute-start(bf16[2,128,1024]{2,1,0:T(8,128)(2,1)S(1)} %slice.38), channel_id=1, source_target_pairs={{0,6},{2,0},{4,2},{6,4},{1,7},{3,1},{5,3},{7,5},{8,14},{10,8},{12,... | collective-permute-start | bytes 1572872 | tf_op jit(solution)/shard_map/ppermute | solution.py:298
  162.3 32.6 %all-to-all-start.3 = ((bf16[8,1024,128]{2,1,0:T(8,128)(2,1)}), bf16[8,1024,128]{2,1,0:T(8,128)(2,1)S(1)}, u32[]{:S(2)}, u32[]{:S(2)}) async-start(bf16[8,1024,128]{2,1,0:T(8,128)(2,1)} %output_weight_terms.1), calls=%async_computation.3 | async-start | bytes 4194304 | tf_op jit(solution)/shard_map/all_to_all | solution.py:344
  183.4 3.0 %collective-permute-start.16 = (bf16[2,256,1024]{2,1,0:T(8,128)(2,1)}, bf16[2,256,1024]{2,1,0:T(8,128)(2,1)S(1)}, u32[]{:S(2)}, u32[]{:S(2)}) collective-permute-start(bf16[2,256,1024]{2,1,0:T(8,128)(2,1)} %get-tuple-element.63), channel_id=1, source_target_pairs={{0,32},{32,0},{1,33},{33,1},{2,34},{34,2},{3,35},{35,3},{4,36},{36... | collective-permute-start | bytes 3145736 | tf_op jit(solution)/shard_map/ppermute | solution.py:301
  196.1 42.2 %all-to-all-start.4 = ((bf16[8,128,1024]{2,1,0:T(8,128)(2,1)}), bf16[8,128,1024]{2,1,0:T(8,128)(2,1)S(1)}, u32[]{:S(2)}, u32[]{:S(2)}) async-start(bf16[8,128,1024]{2,1,0:T(8,128)(2,1)} %bitcast.50), calls=%async_computation.4 | async-start | bytes 4194304 | tf_op jit(solution)/shard_map/all_to_all | solution.py:344
  199.7 36.4 %collective-permute-start.17 = (bf16[256,1024]{1,0:T(8,128)(2,1)}, bf16[256,1024]{1,0:T(8,128)(2,1)S(1)}, u32[]{:S(2)}, u32[]{:S(2)}) collective-permute-start(bf16[256,1024]{1,0:T(8,128)(2,1)} %fusion.2), channel_id=1, source_target_pairs={{0,64},{64,0},{1,65},{65,1},{2,66},{66,2},{3,67},{67,3},{4,68},{68... | collective-permute-start | bytes 1572872 | tf_op jit(solution)/shard_map/ppermute | solution.py:301
  (19 other events, 179.8 us)

commit v11 on v10

--- a/solution.py
+++ b/solution.py
@@ -222,12 +222,16 @@
         out[:, pl.ds(col, cols)] = dot(left[...], ref[0], ((1,), (1,))).astype(BF16)
 
 
+def one_of(pair, which):
+    return pl.BlockSpec((1, *pair.shape[1:]), lambda i, pos: (which if pair.shape[0] == 2 else 0, 0, 0))
+
+
 def weight_terms(name, kernel, pos, which, gathered, block, out):
     return call(
         kernel,
         name,
         (1,),
-        [pl.BlockSpec((1, *a.shape[1:]), lambda i, pos: (which, 0, 0)) for a in gathered] + [whole(block.shape)],
+        [one_of(a, which) for a in gathered] + [whole(block.shape)],
         whole(out),
         struct(out),
         [],
@@ -328,7 +332,12 @@
     gathered, key_terms, value_terms = attention(pos, bias, rows, keys, values)
     left, right = shift(gathered, "y", 1), shift(gathered, "y", 3)
     half = PIECE // 2
-    every = (gathered, left, right, shift(left[:, :half], "y", 1), shift(right[:, half:], "y", 3))
+
+    def far_halves(i):
+        return shift(left[i : i + 1, :half], "y", 1), shift(right[i : i + 1, half:], "y", 3)
+
+    every_out = (gathered, left, right, *far_halves(0))
+    every_grad = (gathered, left, right, *far_halves(1))
 
     terms = jnp.stack([key_terms.reshape(128, 8, PIECE), value_terms.reshape(128, 8, PIECE)], 1)
     moved = lax.all_to_all(terms, HEADS + SEQ, 0, 0, tiled=True)
@@ -337,24 +346,36 @@
 
     piece, over_x = after((piece, over_x), left, right)
     group_states, group_cotangent = assemble(
-        pos, (piece, swap(piece, "core"), over_x, swap(over_x, "core"))
-    )
+        pos, after((piece, swap(piece, "core"), over_x, swap(over_x, "core")), moved)
+    )
+
+    give, keep = output_terms(pos, every_out, output_weight)
+    pair = keep + swap(give, "core").astype(F32)
+    attended = (pair[0] + swap(pair[1].astype(BF16), "xh").astype(F32)).astype(BF16)
 
     def plane_sum(parts):
         return jnp.sum(lax.all_to_all(parts, ("z", "xl"), 0, 0, tiled=True).astype(F32), axis=0)
 
     output_parts = weight_terms(
-        "output_weight_terms", output_grad_kernel, pos, 0, after(every, moved), group_cotangent, (PLANES, BLOCK, 128)
+        "output_weight_terms",
+        output_grad_kernel,
+        pos,
+        0,
+        after(every_out, give),
+        group_cotangent,
+        (PLANES, BLOCK, 128),
     )
     output_weight_grad = plane_sum(output_parts)
     query_parts = weight_terms(
-        "query_weight_terms", query_grad_kernel, pos, 1, after(every, output_parts), group_states, (BLOCK, BLOCK)
-    )
-    give, keep = output_terms(pos, after(every, query_parts), output_weight)
-    pair = keep + swap(give, "core").astype(F32)
-    pair_far = pair[1].astype(BF16)
-    attended = (pair[0] + swap(pair_far, "xh").astype(F32)).astype(BF16)
-    query_parts = after(query_parts, output_weight_grad, pair_far)
+        "query_weight_terms",
+        query_grad_kernel,
+        pos,
+        1,
+        after(every_grad, output_parts, attended),
+        group_states,
+        (BLOCK, BLOCK),
+    )
+    query_parts = after(query_parts, output_weight_grad)
     query_weight_grad = plane_sum(query_parts.reshape(PLANES, 128, BLOCK))
     return attended, query_weight_grad, output_weight_grad, owned[0], owned[1]
 

time: 240 us -> 240 us (level)
  other arithmetic: 10.3 us -> 7.08 us
  waiting for transfers between devices: 111 us -> 114 us
    all_to_all x2, waiting for transfers between devices: 4.45 us -> 25.1 us  [plane_sum(): lax.all_to_all(parts, ('z', 'xl'), 0, 0, tiled=True).astype(F32)]
    ppermute x11, waiting for transfers between devices: 53 us -> 34.6 us  [swap(): return lax.ppermute(x, axis, SWAP)]
    ppermute x7 -> x9, waiting for transfers between devices: 19.6 us -> 24.8 us  [shift(): return lax.ppermute(x, axis, [(i, (i + d) % 4) for i in range(4)])]
    all_to_all x1, waiting for transfers between devices: 15.1 us -> 10 us  [on_device(): moved = lax.all_to_all(terms, HEADS + SEQ, 0, 0, tiled=True)]
    ppermute x7 -> x9, starting transfers between devices: 11.3 us -> 11.2 us  [shift(): return lax.ppermute(x, axis, [(i, (i + d) % 4) for i in range(4)])]
  transfers between devices with their start and end apart: 23 -> 25, of which waited for: 14 -> 11; matrix products, arithmetic and copies ran while one was open for 6% -> 5% of each run, Pallas kernels for 18% -> 19%
where the time goes in v11:
time: 240 us
  waiting for transfers between devices  114 us (48%)
  Pallas kernels  56.2 us (23%)
  starting transfers between devices  48.7 us (20%)
  local copies, waits for them, and re-layouts  12.8 us (5%)
  other arithmetic  7.08 us (3%)
    pallas_call x7, Pallas kernels, call(): pl.pallas_call(kernel, grid_spec=pltpu.PrefetchScalarGridSpec(num_scalar_...  56.2 us
    ppermute x11, waiting for transfers between devices, swap(): return lax.ppermute(x, axis, SWAP)  34.6 us
    all_to_all x2, waiting for transfers between devices, plane_sum(): lax.all_to_all(parts, ('z', 'xl'), 0, 0, tiled=True).astype(F32)  25.1 us
    ppermute x9, waiting for transfers between devices, shift(): return lax.ppermute(x, axis, [(i, (i + d) % 4) for i in range(4)])  24.8 us
    all_to_all x1, waiting for transfers between devices, on_device(): rows = lax.all_to_all(rows, 'y', 0, 0, tiled=True)  12.9 us
    ppermute x9, starting transfers between devices, shift(): return lax.ppermute(x, axis, [(i, (i + d) % 4) for i in range(4)])  11.2 us
    all_to_all x1, starting transfers between devices, on_device(): lax.all_to_all(after(own, products, far_states, far_cotangent, quarters),...  11.1 us
    all_to_all x1, waiting for transfers between devices, on_device(): moved = lax.all_to_all(terms, HEADS + SEQ, 0, 0, tiled=True)  10 us
  transfers between devices with their start and end apart: 25, of which 11 were waited for; matrix products, arithmetic and copies ran while one was open for 5% of the time, Pallas kernels for 19%

profile of v11, /device:TPU:0, one launch (start us, length us, event | category | flops | bytes accessed | tf_op | source)
XLA Modules:
  0.0 239.6 jit_solution(17608402292582035933)
XLA Ops:
  0.7 3.2 %collective-permute-start.2 = (bf16[256,1024]{1,0:T(8,128)(2,1)}, bf16[256,1024]{1,0:T(8,128)(2,1)S(1)}, u32[]{:S(2)}, u32[]{:S(2)}) collective-permute-start(bf16[256,1024]{1,0:T(8,128)(2,1)} %refs_1_.1), channel_id=1, source_target_pairs={{0,64},{64,0},{1,65},{65,1},{2,66},{66,2},{3,67},{67,3},{4,68},{68... | collective-permute-start | bytes 1572872 | tf_op jit(solution)/shard_map/ppermute | solution.py:305
  7.7 3.2 %collective-permute-start.8 = (bf16[2,256,256]{2,1,0:T(8,128)(2,1)S(1)}, bf16[2,256,256]{2,1,0:T(8,128)(2,1)S(1)}, u32[]{:S(2)}, u32[]{:S(2)}) collective-permute-start(bf16[2,256,256]{2,1,0:T(8,128)(2,1)S(1)} %get-tuple-element.69), channel_id=1, source_target_pairs={{0,6},{2,0},{4,2},{6,4},{1,7},{3,1},{5,3},{7,5},{8,14},{10,8},{12,... | collective-permute-start | bytes 786440 | tf_op jit(solution)/shard_map/ppermute | solution.py:302
  13.2 8.4 %project_near.1.refs_1_ = f32[2,256,1024]{2,1,0:T(8,128)} custom-call(s32[5]{0:T(128)} %stack.59.refs_0_.pos, bf16[256,1024]{1,0:T(8,128)(2,1)} %refs_1_.1, bf16[256,1024]{1,0:T(8,128)(2,1)} %collective-permute-done.refs_2_, bf16[256,1024]{1,0:T(8,128)(2,1)} %refs_3_.1, bf16[256,1024]{1,0:T(8,128)(2,1)} %collective-permute-done.1.refs_4_, ...), custom_call_target="tpu_custom_call" | custom-call | flops 2147483648 | bytes 8388608 | tf_op jit(solution)/shard_map/project_near/pallas_call | solution.py:50
  22.3 3.7 %collective-permute-done.6 = bf16[2,256,256]{2,1,0:T(8,128)(2,1)S(1)} collective-permute-done((bf16[2,256,256]{2,1,0:T(8,128)(2,1)S(1)}, bf16[2,256,256]{2,1,0:T(8,128)(2,1)S(1)}, u32[]{:S(2)}, u32[]{:S(2)}) %collective-permute-start.6) | collective-permute-done | bytes 262176 | tf_op jit(solution)/shard_map/ppermute | solution.py:302
  26.0 2.0 collective-permute-done.4.refs_4_
  29.2 11.1 %all-to-all-start.1 = ((bf16[128,2,8,256]{3,2,1,0:T(8,128)(2,1)}), bf16[128,2,8,256]{3,2,1,0:T(8,128)(2,1)S(1)}, u32[]{:S(2)}, u32[]{:S(2)}) async-start(bf16[128,2,8,256]{3,2,1,0:T(8,128)(2,1)} %bitcast.8), calls=%async_computation.1 | async-start | bytes 2097152 | tf_op jit(solution)/shard_map/all_to_all | solution.py:320
  43.9 9.2 %project_far.1 = bf16[4,2,256,256]{3,2,1,0:T(8,128)(2,1)} custom-call(s32[5]{0:T(128)} %stack.59.refs_0_.pos, f32[2,256,1024]{2,1,0:T(8,128)} %project_near.1.refs_1_, bf16[256,1024]{1,0:T(8,128)(2,1)} %copy-done.5, bf16[256,1024]{1,0:T(8,128)(2,1)} %copy-done.7, bf16[256,1024]{1,0:T(8,128)(2,1)} %copy-done.6, bf16[256,1024]{1,0:T(8,128)(2,1)} %copy-done.8, ...), custom_call_target="tpu_custom_call" | custom-call | flops 2147483648 | bytes 8388608 | tf_op jit(solution)/shard_map/project_far/pallas_call | solution.py:50
  53.2 6.4 %all-to-all-done.1 = bf16[128,2,8,256]{3,2,1,0:T(8,128)(2,1)S(1)} async-done(((bf16[128,2,8,256]{3,2,1,0:T(8,128)(2,1)}), bf16[128,2,8,256]{3,2,1,0:T(8,128)(2,1)S(1)}, u32[]{:S(2)}, u32[]{:S(2)}) %all-to-all-start.1) | async-done | bytes 1048608 | tf_op jit(solution)/shard_map/all_to_all | solution.py:320
  59.5 3.7 %all-to-all-start = ((bf16[4,2,256,256]{3,2,1,0:T(8,128)(2,1)}), bf16[4,2,256,256]{3,2,1,0:T(8,128)(2,1)S(1)}, u32[]{:S(2)}, u32[]{:S(2)}) async-start(bf16[4,2,256,256]{3,2,1,0:T(8,128)(2,1)} %project_far.1), calls=%async_computation | async-start | bytes 2097152 | tf_op jit(solution)/shard_map/all_to_all | solution.py:327
  65.2 12.9 %all-to-all-done.rows = bf16[4,2,256,256]{3,2,1,0:T(8,128)(2,1)S(1)} async-done(((bf16[4,2,256,256]{3,2,1,0:T(8,128)(2,1)}), bf16[4,2,256,256]{3,2,1,0:T(8,128)(2,1)S(1)}, u32[]{:S(2)}, u32[]{:S(2)}) %all-to-all-start) | async-done | bytes 1048608 | tf_op jit(solution)/shard_map/all_to_all | solution.py:327
  79.1 11.1 %attention.1 = (bf16[2,256,1024]{2,1,0:T(8,128)(2,1)}, bf16[1024,256]{1,0:T(8,128)(2,1)}, bf16[1024,256]{1,0:T(8,128)(2,1)}) custom-call(s32[5]{0:T(128)} %stack.59.refs_0_.pos, f32[1,1024]{1,0:T(1,128)} %bitcast.63, bf16[4,2,256,256]{3,2,1,0:T(8,128)(2,1)} %copy-done.4, bf16[1024,256]{1,0:T(8,128)(2,1)} %get-tuple-element.68.k_ref, ...), custom_call_target="tpu_custom_call" | custom-call | flops 8053063680 | bytes 4194304 | tf_op jit(solution)/shard_map/attention/pallas_call | solution.py:50
  93.5 20.4 %collective-permute-done.10.refs_2_ = bf16[2,256,1024]{2,1,0:T(8,128)(2,1)S(1)} collective-permute-done((bf16[2,256,1024]{2,1,0:T(8,128)(2,1)}, bf16[2,256,1024]{2,1,0:T(8,128)(2,1)S(1)}, u32[]{:S(2)}, u32[]{:S(2)}) %collective-permute-start.10) | collective-permute-done | bytes 1048608 | tf_op jit(solution)/shard_map/ppermute | solution.py:302
  114.8 2.4 collective-permute-start.12
  120.0 6.5 %all-to-all-start.2 = ((bf16[128,2,8,256]{3,2,1,0:T(8,128)(2,1)}), bf16[128,2,8,256]{3,2,1,0:T(8,128)(2,1)S(1)}, u32[]{:S(2)}, u32[]{:S(2)}) async-start(bf16[128,2,8,256]{3,2,1,0:T(8,128)(2,1)} %pad_maximum_fusion.1), calls=%async_computation.2 | async-start | bytes 2097152 | tf_op jit(solution)/shard_map/all_to_all | solution.py:343
  127.2 8.2 %output_terms.1 = (bf16[2,256,1024]{2,1,0:T(8,128)(2,1)}, f32[2,256,1024]{2,1,0:T(8,128)}) custom-call(s32[5]{0:T(128)} %stack.59.refs_0_.pos, bf16[2,256,1024]{2,1,0:T(8,128)(2,1)} %get-tuple-element.56.refs_0_, bf16[2,256,1024]{2,1,0:T(8,128)(2,1)} %copy-done.2, bf16[2,256,1024]{2,1,0:T(8,128)(2,1)} %copy-done.1, ...), custom_call_target="tpu_custom_call" | custom-call | flops 2147483648 | bytes 8388608 | tf_op jit(solution)/shard_map/output_terms/pallas_call | solution.py:50
  135.7 10.0 %all-to-all-done.2 = bf16[128,2,8,256]{3,2,1,0:T(8,128)(2,1)S(1)} async-done(((bf16[128,2,8,256]{3,2,1,0:T(8,128)(2,1)}), bf16[128,2,8,256]{3,2,1,0:T(8,128)(2,1)S(1)}, u32[]{:S(2)}, u32[]{:S(2)}) %all-to-all-start.2) | async-done | bytes 1048608 | tf_op jit(solution)/shard_map/all_to_all | solution.py:343
  145.8 5.7 %column_blocks.1 = (bf16[1024,1024]{1,0:T(8,128)(2,1)}, bf16[1024,1024]{1,0:T(8,128)(2,1)}) custom-call(s32[5]{0:T(128)} %stack.59.refs_0_.pos, bf16[4,2,256,256]{3,2,1,0:T(8,128)(2,1)} %copy-done, bf16[4,2,256,256]{3,2,1,0:T(8,128)(2,1)} %collective-permute-done.18.p1, bf16[4,2,256,256]{3,2,1,0:T(8,128)(2,1)} %copy-done.3, ...), custom_call_target="tpu_custom_call" | custom-call | bytes 8388608 | tf_op jit(solution)/shard_map/column_blocks/pallas_call | solution.py:50
  151.4 6.6 %output_weight_terms.1 = bf16[8,1024,128]{2,1,0:T(8,128)(2,1)} custom-call(s32[5]{0:T(128)} %stack.59.refs_0_.pos, bf16[2,256,1024]{2,1,0:T(8,128)(2,1)} %get-tuple-element.56.refs_0_, bf16[2,256,1024]{2,1,0:T(8,128)(2,1)} %copy-done.2, bf16[2,256,1024]{2,1,0:T(8,128)(2,1)} %copy-done.1, bf16[1,128,1024]{2,1,0:T(8,128)(2,1)} %collective-permute-done.11.refs_3_, ...), custom_call_target="tpu_custom_call" | custom-call | flops 2147483648 | bytes 6291456 | tf_op jit(solution)/shard_map/output_weight_terms/pallas_call | solution.py:50
  158.0 3.6 %all-to-all-start.3 = ((bf16[8,1024,128]{2,1,0:T(8,128)(2,1)}), bf16[8,1024,128]{2,1,0:T(8,128)(2,1)S(1)}, u32[]{:S(2)}, u32[]{:S(2)}) async-start(bf16[8,1024,128]{2,1,0:T(8,128)(2,1)} %output_weight_terms.1), calls=%async_computation.3 | async-start | bytes 4194304 | tf_op jit(solution)/shard_map/all_to_all | solution.py:357
  161.7 2.2 convert_add_fusion
  167.0 30.4 %collective-permute-done.14 = bf16[256,1024]{1,0:T(8,128)(2,1)S(1)} collective-permute-done((bf16[256,1024]{1,0:T(8,128)(2,1)S(1)}, bf16[256,1024]{1,0:T(8,128)(2,1)S(1)}, u32[]{:S(2)}, u32[]{:S(2)}) %collective-permute-start.14) | collective-permute-done | bytes 524320 | tf_op jit(solution)/shard_map/ppermute | solution.py:305
  199.1 7.1 %query_weight_terms.1 = bf16[1024,1024]{1,0:T(8,128)(2,1)} custom-call(s32[5]{0:T(128)} %stack.59.refs_0_.pos, bf16[2,256,1024]{2,1,0:T(8,128)(2,1)} %get-tuple-element.56.refs_0_, bf16[2,256,1024]{2,1,0:T(8,128)(2,1)} %copy-done.2, bf16[2,256,1024]{2,1,0:T(8,128)(2,1)} %copy-done.1, bf16[1,128,1024]{2,1,0:T(8,128)(2,1)} %copy-done.23, ...), custom_call_target="tpu_custom_call" | custom-call | flops 2147483648 | bytes 6291456 | tf_op jit(solution)/shard_map/query_weight_terms/pallas_call | solution.py:50
  207.3 5.1 %all-to-all-start.4 = ((bf16[8,128,1024]{2,1,0:T(8,128)(2,1)}), bf16[8,128,1024]{2,1,0:T(8,128)(2,1)S(1)}, u32[]{:S(2)}, u32[]{:S(2)}) async-start(bf16[8,128,1024]{2,1,0:T(8,128)(2,1)} %bitcast.51), calls=%async_computation.4 | async-start | bytes 4194304 | tf_op jit(solution)/shard_map/all_to_all | solution.py:357
  213.4 25.1 %all-to-all-done.4 = bf16[8,128,1024]{2,1,0:T(8,128)(2,1)S(1)} async-done(((bf16[8,128,1024]{2,1,0:T(8,128)(2,1)}), bf16[8,128,1024]{2,1,0:T(8,128)(2,1)S(1)}, u32[]{:S(2)}, u32[]{:S(2)}) %all-to-all-start.4) | async-done | bytes 2097184 | tf_op jit(solution)/shard_map/all_to_all | solution.py:357
  (109 shorter events, 30.4 us)
Async XLA Ops:
  0.6 10.2 %collective-permute-start = (bf16[256,1024]{1,0:T(8,128)(2,1)}, bf16[256,1024]{1,0:T(8,128)(2,1)}, u32[]{:S(2)}, u32[]{:S(2)}) collective-permute-start(bf16[256,1024]{1,0:T(8,128)(2,1)} %refs_1_.1), channel_id=1, source_target_pairs={{0,32},{32,0},{1,33},{33,1},{2,34},{34,2},{3,35},{35,3},{4,36},{36... | collective-permute-start | bytes 1572872 | tf_op jit(solution)/shard_map/ppermute | solution.py:305
  0.7 25.2 %collective-permute-start.2 = (bf16[256,1024]{1,0:T(8,128)(2,1)}, bf16[256,1024]{1,0:T(8,128)(2,1)S(1)}, u32[]{:S(2)}, u32[]{:S(2)}) collective-permute-start(bf16[256,1024]{1,0:T(8,128)(2,1)} %refs_1_.1), channel_id=1, source_target_pairs={{0,64},{64,0},{1,65},{65,1},{2,66},{66,2},{3,67},{67,3},{4,68},{68... | collective-permute-start | bytes 1572872 | tf_op jit(solution)/shard_map/ppermute | solution.py:305
  3.9 7.6 %collective-permute-start.1 = (bf16[256,1024]{1,0:T(8,128)(2,1)}, bf16[256,1024]{1,0:T(8,128)(2,1)}, u32[]{:S(2)}, u32[]{:S(2)}) collective-permute-start(bf16[256,1024]{1,0:T(8,128)(2,1)} %refs_3_.1), channel_id=1, source_target_pairs={{0,32},{32,0},{1,33},{33,1},{2,34},{34,2},{3,35},{35,3},{4,36},{36... | collective-permute-start | bytes 1572872 | tf_op jit(solution)/shard_map/ppermute | solution.py:305
  4.1 24.0 %collective-permute-start.4 = (bf16[256,1024]{1,0:T(8,128)(2,1)}, bf16[256,1024]{1,0:T(8,128)(2,1)S(1)}, u32[]{:S(2)}, u32[]{:S(2)}) collective-permute-start(bf16[256,1024]{1,0:T(8,128)(2,1)} %refs_3_.1), channel_id=1, source_target_pairs={{0,64},{64,0},{1,65},{65,1},{2,66},{66,2},{3,67},{67,3},{4,68},{68... | collective-permute-start | bytes 1572872 | tf_op jit(solution)/shard_map/ppermute | solution.py:305
  7.7 14.6 %collective-permute-start.8 = (bf16[2,256,256]{2,1,0:T(8,128)(2,1)S(1)}, bf16[2,256,256]{2,1,0:T(8,128)(2,1)S(1)}, u32[]{:S(2)}, u32[]{:S(2)}) collective-permute-start(bf16[2,256,256]{2,1,0:T(8,128)(2,1)S(1)} %get-tuple-element.69), channel_id=1, source_target_pairs={{0,6},{2,0},{4,2},{6,4},{1,7},{3,1},{5,3},{7,5},{8,14},{10,8},{12,... | collective-permute-start | bytes 786440 | tf_op jit(solution)/shard_map/ppermute | solution.py:302
  10.8 11.4 %collective-permute-start.7 = (bf16[2,256,256]{2,1,0:T(8,128)(2,1)S(1)}, bf16[2,256,256]{2,1,0:T(8,128)(2,1)S(1)}, u32[]{:S(2)}, u32[]{:S(2)}) collective-permute-start(bf16[2,256,256]{2,1,0:T(8,128)(2,1)S(1)} %get-tuple-element.70), channel_id=1, source_target_pairs={{0,4},{2,6},{4,0},{6,2},{1,5},{3,7},{5,1},{7,3},{8,12},{10,14},{12... | collective-permute-start | bytes 786440 | tf_op jit(solution)/shard_map/ppermute | solution.py:302
  11.5 14.5 %collective-permute-start.6 = (bf16[2,256,256]{2,1,0:T(8,128)(2,1)S(1)}, bf16[2,256,256]{2,1,0:T(8,128)(2,1)S(1)}, u32[]{:S(2)}, u32[]{:S(2)}) collective-permute-start(bf16[2,256,256]{2,1,0:T(8,128)(2,1)S(1)} %get-tuple-element.71), channel_id=1, source_target_pairs={{0,2},{2,4},{4,6},{6,0},{1,3},{3,5},{5,7},{7,1},{8,10},{10,12},{12... | collective-permute-start | bytes 786440 | tf_op jit(solution)/shard_map/ppermute | solution.py:302
  29.2 30.4 %all-to-all-start.1 = ((bf16[128,2,8,256]{3,2,1,0:T(8,128)(2,1)}), bf16[128,2,8,256]{3,2,1,0:T(8,128)(2,1)S(1)}, u32[]{:S(2)}, u32[]{:S(2)}) async-start(bf16[128,2,8,256]{3,2,1,0:T(8,128)(2,1)} %bitcast.8), calls=%async_computation.1 | async-start | bytes 2097152 | tf_op jit(solution)/shard_map/all_to_all | solution.py:320
  40.4 2.6 %collective-permute-start.5 = (bf16[256,1024]{1,0:T(8,128)(2,1)S(1)}, bf16[256,1024]{1,0:T(8,128)(2,1)S(1)}, u32[]{:S(2)}, u32[]{:S(2)}) collective-permute-start(bf16[256,1024]{1,0:T(8,128)(2,1)S(1)} %collective-permute-done.4.refs_4_), channel_id=1, source_target_pairs={{0,32},{32,0},{1,33},{33,1},{2,34},{34,2},{3,35},{35,3},{4,36},{36... | collective-permute-start | bytes 1572872 | tf_op jit(solution)/shard_map/ppermute | solution.py:305
  59.5 18.5 %all-to-all-start = ((bf16[4,2,256,256]{3,2,1,0:T(8,128)(2,1)}), bf16[4,2,256,256]{3,2,1,0:T(8,128)(2,1)S(1)}, u32[]{:S(2)}, u32[]{:S(2)}) async-start(bf16[4,2,256,256]{3,2,1,0:T(8,128)(2,1)} %project_far.1), calls=%async_computation | async-start | bytes 2097152 | tf_op jit(solution)/shard_map/all_to_all | solution.py:327
  90.1 23.8 %collective-permute-start.10 = (bf16[2,256,1024]{2,1,0:T(8,128)(2,1)}, bf16[2,256,1024]{2,1,0:T(8,128)(2,1)S(1)}, u32[]{:S(2)}, u32[]{:S(2)}) collective-permute-start(bf16[2,256,1024]{2,1,0:T(8,128)(2,1)} %get-tuple-element.56.refs_0_), channel_id=1, source_target_pairs={{0,6},{2,0},{4,2},{6,4},{1,7},{3,1},{5,3},{7,5},{8,14},{10,8},{12,... | collective-permute-start | bytes 3145736 | tf_op jit(solution)/shard_map/ppermute | solution.py:302
  91.3 25.9 %collective-permute-start.9 = (bf16[2,256,1024]{2,1,0:T(8,128)(2,1)}, bf16[2,256,1024]{2,1,0:T(8,128)(2,1)S(1)}, u32[]{:S(2)}, u32[]{:S(2)}) collective-permute-start(bf16[2,256,1024]{2,1,0:T(8,128)(2,1)} %get-tuple-element.56.refs_0_), channel_id=1, source_target_pairs={{0,2},{2,4},{4,6},{6,0},{1,3},{3,5},{5,7},{7,1},{8,10},{10,12},{12... | collective-permute-start | bytes 3145736 | tf_op jit(solution)/shard_map/ppermute | solution.py:302
  92.3 25.8 %collective-permute-start.17 = (bf16[4,2,256,256]{3,2,1,0:T(8,128)(2,1)S(1)}, bf16[4,2,256,256]{3,2,1,0:T(8,128)(2,1)S(1)}, u32[]{:S(2)}, u32[]{:S(2)}) collective-permute-start(bf16[4,2,256,256]{3,2,1,0:T(8,128)(2,1)S(1)} %pad_maximum_fusion.p0), channel_id=1, source_target_pairs={{0,64},{64,0},{1,65},{65,1},{2,66},{66,2},{3,67},{67,3},{4,68},{68... | collective-permute-start | bytes 3145736 | tf_op jit(solution)/shard_map/ppermute | solution.py:305
  114.8 11.7 %collective-permute-start.12 = (bf16[1,128,1024]{2,1,0:T(8,128)(2,1)}, bf16[1,128,1024]{2,1,0:T(8,128)(2,1)S(1)}, u32[]{:S(2)}, u32[]{:S(2)}) collective-permute-start(bf16[1,128,1024]{2,1,0:T(8,128)(2,1)} %get-tuple-element.64), channel_id=1, source_target_pairs={{0,6},{2,0},{4,2},{6,4},{1,7},{3,1},{5,3},{7,5},{8,14},{10,8},{12,... | collective-permute-start | bytes 786440 | tf_op jit(solution)/shard_map/ppermute | solution.py:302
  118.1 8.4 %collective-permute-start.11 = (bf16[1,128,1024]{2,1,0:T(8,128)(2,1)}, bf16[1,128,1024]{2,1,0:T(8,128)(2,1)}, u32[]{:S(2)}, u32[]{:S(2)}) collective-permute-start(bf16[1,128,1024]{2,1,0:T(8,128)(2,1)} %get-tuple-element.66), channel_id=1, source_target_pairs={{0,2},{2,4},{4,6},{6,0},{1,3},{3,5},{5,7},{7,1},{8,10},{10,12},{12... | collective-permute-start | bytes 786440 | tf_op jit(solution)/shard_map/ppermute | solution.py:302
  118.4 27.4 %collective-permute-start.18 = (bf16[4,2,256,256]{3,2,1,0:T(8,128)(2,1)S(1)}, bf16[4,2,256,256]{3,2,1,0:T(8,128)(2,1)}, u32[]{:S(2)}, u32[]{:S(2)}) collective-permute-start(bf16[4,2,256,256]{3,2,1,0:T(8,128)(2,1)S(1)} %pad_maximum_fusion.p0), channel_id=1, source_target_pairs={{0,32},{32,0},{1,33},{33,1},{2,34},{34,2},{3,35},{35,3},{4,36},{36... | collective-permute-start | bytes 3145736 | tf_op jit(solution)/shard_map/ppermute | solution.py:305
  118.4 27.4 %collective-permute-start.19 = (bf16[4,2,256,256]{3,2,1,0:T(8,128)(2,1)S(1)}, bf16[4,2,256,256]{3,2,1,0:T(8,128)(2,1)}, u32[]{:S(2)}, u32[]{:S(2)}) collective-permute-start(bf16[4,2,256,256]{3,2,1,0:T(8,128)(2,1)S(1)} %collective-permute-done.17.p2), channel_id=1, source_target_pairs={{0,32},{32,0},{1,33},{33,1},{2,34},{34,2},{3,35},{35,3},{4,36},{36... | collective-permute-start | bytes 3145736 | tf_op jit(solution)/shard_map/ppermute | solution.py:305
  120.0 25.7 %all-to-all-start.2 = ((bf16[128,2,8,256]{3,2,1,0:T(8,128)(2,1)}), bf16[128,2,8,256]{3,2,1,0:T(8,128)(2,1)S(1)}, u32[]{:S(2)}, u32[]{:S(2)}) async-start(bf16[128,2,8,256]{3,2,1,0:T(8,128)(2,1)} %pad_maximum_fusion.1), calls=%async_computation.2 | async-start | bytes 2097152 | tf_op jit(solution)/shard_map/all_to_all | solution.py:343
  135.4 26.2 %collective-permute-start.13 = (bf16[2,256,1024]{2,1,0:T(8,128)(2,1)}, bf16[2,256,1024]{2,1,0:T(8,128)(2,1)}, u32[]{:S(2)}, u32[]{:S(2)}) collective-permute-start(bf16[2,256,1024]{2,1,0:T(8,128)(2,1)} %get-tuple-element.37), channel_id=1, source_target_pairs={{0,32},{32,0},{1,33},{33,1},{2,34},{34,2},{3,35},{35,3},{4,36},{36... | collective-permute-start | bytes 3145736 | tf_op jit(solution)/shard_map/ppermute | solution.py:305
  158.0 48.2 %all-to-all-start.3 = ((bf16[8,1024,128]{2,1,0:T(8,128)(2,1)}), bf16[8,1024,128]{2,1,0:T(8,128)(2,1)S(1)}, u32[]{:S(2)}, u32[]{:S(2)}) async-start(bf16[8,1024,128]{2,1,0:T(8,128)(2,1)} %output_weight_terms.1), calls=%async_computation.3 | async-start | bytes 4194304 | tf_op jit(solution)/shard_map/all_to_all | solution.py:357
  164.0 33.4 %collective-permute-start.14 = (bf16[256,1024]{1,0:T(8,128)(2,1)S(1)}, bf16[256,1024]{1,0:T(8,128)(2,1)S(1)}, u32[]{:S(2)}, u32[]{:S(2)}) collective-permute-start(bf16[256,1024]{1,0:T(8,128)(2,1)S(1)} %fusion.2), channel_id=1, source_target_pairs={{0,64},{64,0},{1,65},{65,1},{2,66},{66,2},{3,67},{67,3},{4,68},{68... | collective-permute-start | bytes 1572872 | tf_op jit(solution)/shard_map/ppermute | solution.py:305
  164.9 33.4 %collective-permute-start.16 = (bf16[1,128,1024]{2,1,0:T(8,128)(2,1)S(1)}, bf16[1,128,1024]{2,1,0:T(8,128)(2,1)S(1)}, u32[]{:S(2)}, u32[]{:S(2)}) collective-permute-start(bf16[1,128,1024]{2,1,0:T(8,128)(2,1)S(1)} %copy-done.12), channel_id=1, source_target_pairs={{0,6},{2,0},{4,2},{6,4},{1,7},{3,1},{5,3},{7,5},{8,14},{10,8},{12,... | collective-permute-start | bytes 786440 | tf_op jit(solution)/shard_map/ppermute | solution.py:302
  165.7 32.6 %collective-permute-start.15 = (bf16[1,128,1024]{2,1,0:T(8,128)(2,1)S(1)}, bf16[1,128,1024]{2,1,0:T(8,128)(2,1)S(1)}, u32[]{:S(2)}, u32[]{:S(2)}) collective-permute-start(bf16[1,128,1024]{2,1,0:T(8,128)(2,1)S(1)} %copy-done.13), channel_id=1, source_target_pairs={{0,2},{2,4},{4,6},{6,0},{1,3},{3,5},{5,7},{7,1},{8,10},{10,12},{12... | collective-permute-start | bytes 786440 | tf_op jit(solution)/shard_map/ppermute | solution.py:302
  207.3 31.2 %all-to-all-start.4 = ((bf16[8,128,1024]{2,1,0:T(8,128)(2,1)}), bf16[8,128,1024]{2,1,0:T(8,128)(2,1)S(1)}, u32[]{:S(2)}, u32[]{:S(2)}) async-start(bf16[8,128,1024]{2,1,0:T(8,128)(2,1)} %bitcast.51), calls=%async_computation.4 | async-start | bytes 4194304 | tf_op jit(solution)/shard_map/all_to_all | solution.py:357
  (27 other events, 234.0 us)

commit v12 on v11

--- a/solution.py
+++ b/solution.py
@@ -365,13 +365,13 @@
         group_cotangent,
         (PLANES, BLOCK, 128),
     )
-    output_weight_grad = plane_sum(output_parts)
+    output_weight_grad = plane_sum(after(output_parts, attended))
     query_parts = weight_terms(
         "query_weight_terms",
         query_grad_kernel,
         pos,
         1,
-        after(every_grad, output_parts, attended),
+        after(every_grad, output_parts),
         group_states,
         (BLOCK, BLOCK),
     )

time: 240 us -> 257 us (1.071)
  the two profiles are of different devices: /device:TPU:0 before, /device:TPU:4 now
where the time goes in v12:
time: 257 us
  waiting for transfers between devices  118 us (46%)
  starting transfers between devices  58.5 us (23%)
  Pallas kernels  56 us (22%)
  local copies, waits for them, and re-layouts  14.1 us (5%)
  other arithmetic  9.27 us (4%)
    pallas_call x7, Pallas kernels, call(): pl.pallas_call(kernel, grid_spec=pltpu.PrefetchScalarGridSpec(num_scalar_...  56 us
    ppermute x9, waiting for transfers between devices, shift(): return lax.ppermute(x, axis, [(i, (i + d) % 4) for i in range(4)])  40.8 us
    all_to_all x2, waiting for transfers between devices, plane_sum(): lax.all_to_all(parts, ('z', 'xl'), 0, 0, tiled=True).astype(F32)  34.3 us
    all_to_all x2, starting transfers between devices, plane_sum(): lax.all_to_all(parts, ('z', 'xl'), 0, 0, tiled=True).astype(F32)  16.4 us
    all_to_all x1, waiting for transfers between devices, on_device(): rows = lax.all_to_all(rows, 'y', 0, 0, tiled=True)  13.2 us
    ppermute x11, waiting for transfers between devices, swap(): return lax.ppermute(x, axis, SWAP)  12.4 us
    all_to_all x1, waiting for transfers between devices, on_device(): moved = lax.all_to_all(terms, HEADS + SEQ, 0, 0, tiled=True)  12.4 us
    ppermute x9, starting transfers between devices, shift(): return lax.ppermute(x, axis, [(i, (i + d) % 4) for i in range(4)])  11.3 us
  transfers between devices with their start and end apart: 25, of which 16 were waited for; matrix products, arithmetic and copies ran while one was open for 5% of the time, Pallas kernels for 18%

profile of v12, /device:TPU:4, one launch (start us, length us, event | category | flops | bytes accessed | tf_op | source)
XLA Modules:
  0.0 256.7 jit_solution(2216956196499205379)
XLA Ops:
  1.4 3.1 %collective-permute-start.4 = (bf16[256,1024]{1,0:T(8,128)(2,1)}, bf16[256,1024]{1,0:T(8,128)(2,1)S(1)}, u32[]{:S(2)}, u32[]{:S(2)}) collective-permute-start(bf16[256,1024]{1,0:T(8,128)(2,1)} %refs_3_.1), channel_id=1, source_target_pairs={{0,64},{64,0},{1,65},{65,1},{2,66},{66,2},{3,67},{67,3},{4,68},{68... | collective-permute-start | bytes 1572872 | tf_op jit(solution)/shard_map/ppermute | solution.py:305
  7.7 3.1 %collective-permute-start.8 = (bf16[2,256,256]{2,1,0:T(8,128)(2,1)S(1)}, bf16[2,256,256]{2,1,0:T(8,128)(2,1)S(1)}, u32[]{:S(2)}, u32[]{:S(2)}) collective-permute-start(bf16[2,256,256]{2,1,0:T(8,128)(2,1)S(1)} %get-tuple-element.71), channel_id=1, source_target_pairs={{0,6},{2,0},{4,2},{6,4},{1,7},{3,1},{5,3},{7,5},{8,14},{10,8},{12,... | collective-permute-start | bytes 786440 | tf_op jit(solution)/shard_map/ppermute | solution.py:302
  13.1 8.4 %project_near.1.refs_1_ = f32[2,256,1024]{2,1,0:T(8,128)} custom-call(s32[5]{0:T(128)} %stack.59.refs_0_.pos, bf16[256,1024]{1,0:T(8,128)(2,1)} %refs_1_.1, bf16[256,1024]{1,0:T(8,128)(2,1)} %collective-permute-done.refs_2_, bf16[256,1024]{1,0:T(8,128)(2,1)} %refs_3_.1, bf16[256,1024]{1,0:T(8,128)(2,1)} %collective-permute-done.1.refs_4_, ...), custom_call_target="tpu_custom_call" | custom-call | flops 2147483648 | bytes 8388608 | tf_op jit(solution)/shard_map/project_near/pallas_call | solution.py:50
  22.2 3.7 %collective-permute-done.6 = bf16[2,256,256]{2,1,0:T(8,128)(2,1)S(1)} collective-permute-done((bf16[2,256,256]{2,1,0:T(8,128)(2,1)S(1)}, bf16[2,256,256]{2,1,0:T(8,128)(2,1)S(1)}, u32[]{:S(2)}, u32[]{:S(2)}) %collective-permute-start.6) | collective-permute-done | bytes 262176 | tf_op jit(solution)/shard_map/ppermute | solution.py:302
  29.2 10.5 %all-to-all-start.1 = ((bf16[128,2,8,256]{3,2,1,0:T(8,128)(2,1)}), bf16[128,2,8,256]{3,2,1,0:T(8,128)(2,1)S(1)}, u32[]{:S(2)}, u32[]{:S(2)}) async-start(bf16[128,2,8,256]{3,2,1,0:T(8,128)(2,1)} %bitcast.8), calls=%async_computation.1 | async-start | bytes 2097152 | tf_op jit(solution)/shard_map/all_to_all | solution.py:320
  43.2 9.2 %project_far.1 = bf16[4,2,256,256]{3,2,1,0:T(8,128)(2,1)} custom-call(s32[5]{0:T(128)} %stack.59.refs_0_.pos, f32[2,256,1024]{2,1,0:T(8,128)} %project_near.1.refs_1_, bf16[256,1024]{1,0:T(8,128)(2,1)} %copy-done.5, bf16[256,1024]{1,0:T(8,128)(2,1)} %copy-done.7, bf16[256,1024]{1,0:T(8,128)(2,1)} %copy-done.6, bf16[256,1024]{1,0:T(8,128)(2,1)} %copy-done.8, ...), custom_call_target="tpu_custom_call" | custom-call | flops 2147483648 | bytes 8388608 | tf_op jit(solution)/shard_map/project_far/pallas_call | solution.py:50
  52.5 4.8 %all-to-all-done.1 = bf16[128,2,8,256]{3,2,1,0:T(8,128)(2,1)S(1)} async-done(((bf16[128,2,8,256]{3,2,1,0:T(8,128)(2,1)}), bf16[128,2,8,256]{3,2,1,0:T(8,128)(2,1)S(1)}, u32[]{:S(2)}, u32[]{:S(2)}) %all-to-all-start.1) | async-done | bytes 1048608 | tf_op jit(solution)/shard_map/all_to_all | solution.py:320
  57.3 3.7 %all-to-all-start = ((bf16[4,2,256,256]{3,2,1,0:T(8,128)(2,1)}), bf16[4,2,256,256]{3,2,1,0:T(8,128)(2,1)S(1)}, u32[]{:S(2)}, u32[]{:S(2)}) async-start(bf16[4,2,256,256]{3,2,1,0:T(8,128)(2,1)} %project_far.1), calls=%async_computation | async-start | bytes 2097152 | tf_op jit(solution)/shard_map/all_to_all | solution.py:327
  62.9 13.2 %all-to-all-done.rows = bf16[4,2,256,256]{3,2,1,0:T(8,128)(2,1)S(1)} async-done(((bf16[4,2,256,256]{3,2,1,0:T(8,128)(2,1)}), bf16[4,2,256,256]{3,2,1,0:T(8,128)(2,1)S(1)}, u32[]{:S(2)}, u32[]{:S(2)}) %all-to-all-start) | async-done | bytes 1048608 | tf_op jit(solution)/shard_map/all_to_all | solution.py:327
  77.1 10.9 %attention.1 = (bf16[2,256,1024]{2,1,0:T(8,128)(2,1)}, bf16[1024,256]{1,0:T(8,128)(2,1)}, bf16[1024,256]{1,0:T(8,128)(2,1)}) custom-call(s32[5]{0:T(128)} %stack.59.refs_0_.pos, f32[1,1024]{1,0:T(1,128)} %bitcast.62, bf16[4,2,256,256]{3,2,1,0:T(8,128)(2,1)} %copy-done.4, bf16[1024,256]{1,0:T(8,128)(2,1)} %get-tuple-element.70.k_ref, ...), custom_call_target="tpu_custom_call" | custom-call | flops 8053063680 | bytes 4194304 | tf_op jit(solution)/shard_map/attention/pallas_call | solution.py:50
  90.1 22.1 %collective-permute-done.10.refs_2_ = bf16[2,256,1024]{2,1,0:T(8,128)(2,1)S(1)} collective-permute-done((bf16[2,256,1024]{2,1,0:T(8,128)(2,1)}, bf16[2,256,1024]{2,1,0:T(8,128)(2,1)S(1)}, u32[]{:S(2)}, u32[]{:S(2)}) %collective-permute-start.10) | collective-permute-done | bytes 1048608 | tf_op jit(solution)/shard_map/ppermute | solution.py:302
  119.4 4.4 %collective-permute-done.11.refs_3_ = bf16[1,128,1024]{2,1,0:T(8,128)(2,1)S(1)} collective-permute-done((bf16[1,128,1024]{2,1,0:T(8,128)(2,1)S(1)}, bf16[1,128,1024]{2,1,0:T(8,128)(2,1)S(1)}, u32[]{:S(2)}, u32[]{:S(2)}) %collective-permute-start.11) | collective-permute-done | bytes 262176 | tf_op jit(solution)/shard_map/ppermute | solution.py:302
  124.5 8.1 %output_terms.1 = (bf16[2,256,1024]{2,1,0:T(8,128)(2,1)}, f32[2,256,1024]{2,1,0:T(8,128)}) custom-call(s32[5]{0:T(128)} %stack.59.refs_0_.pos, bf16[2,256,1024]{2,1,0:T(8,128)(2,1)} %get-tuple-element.57.refs_0_, bf16[2,256,1024]{2,1,0:T(8,128)(2,1)} %copy-done.2, bf16[2,256,1024]{2,1,0:T(8,128)(2,1)} %copy-done.1, bf16[1,128,1024]{2,1,0:T(8,128)(2,1)} %copy-done.12, ...), custom_call_target="tpu_custom_call" | custom-call | flops 2147483648 | bytes 8388608 | tf_op jit(solution)/shard_map/output_terms/pallas_call | solution.py:50
  132.7 8.1 %collective-permute-done.17.p2 = bf16[4,2,256,256]{3,2,1,0:T(8,128)(2,1)} collective-permute-done((bf16[4,2,256,256]{3,2,1,0:T(8,128)(2,1)S(1)}, bf16[4,2,256,256]{3,2,1,0:T(8,128)(2,1)}, u32[]{:S(2)}, u32[]{:S(2)}) %collective-permute-start.17) | collective-permute-done | bytes 1048608 | tf_op jit(solution)/shard_map/ppermute | solution.py:305
  142.4 8.3 %all-to-all-start.2 = ((bf16[128,2,8,256]{3,2,1,0:T(8,128)(2,1)}), bf16[128,2,8,256]{3,2,1,0:T(8,128)(2,1)}, u32[]{:S(2)}, u32[]{:S(2)}) async-start(bf16[128,2,8,256]{3,2,1,0:T(8,128)(2,1)} %pad_maximum_fusion.1), calls=%async_computation.2 | async-start | bytes 2097152 | tf_op jit(solution)/shard_map/all_to_all | solution.py:343
  155.9 12.4 %all-to-all-done.2 = bf16[128,2,8,256]{3,2,1,0:T(8,128)(2,1)} async-done(((bf16[128,2,8,256]{3,2,1,0:T(8,128)(2,1)}), bf16[128,2,8,256]{3,2,1,0:T(8,128)(2,1)}, u32[]{:S(2)}, u32[]{:S(2)}) %all-to-all-start.2) | async-done | bytes 1048608 | tf_op jit(solution)/shard_map/all_to_all | solution.py:343
  168.2 5.6 %column_blocks.1 = (bf16[1024,1024]{1,0:T(8,128)(2,1)}, bf16[1024,1024]{1,0:T(8,128)(2,1)}) custom-call(s32[5]{0:T(128)} %stack.59.refs_0_.pos, bf16[4,2,256,256]{3,2,1,0:T(8,128)(2,1)} %copy-done, bf16[4,2,256,256]{3,2,1,0:T(8,128)(2,1)} %collective-permute-done.18.p1, bf16[4,2,256,256]{3,2,1,0:T(8,128)(2,1)} %collective-permute-done.17.p2, ...), custom_call_target="tpu_custom_call" | custom-call | bytes 8388608 | tf_op jit(solution)/shard_map/column_blocks/pallas_call | solution.py:50
  173.9 6.6 %output_weight_terms.1 = bf16[8,1024,128]{2,1,0:T(8,128)(2,1)} custom-call(s32[5]{0:T(128)} %stack.59.refs_0_.pos, bf16[2,256,1024]{2,1,0:T(8,128)(2,1)} %get-tuple-element.57.refs_0_, bf16[2,256,1024]{2,1,0:T(8,128)(2,1)} %copy-done.2, bf16[2,256,1024]{2,1,0:T(8,128)(2,1)} %copy-done.1, bf16[1,128,1024]{2,1,0:T(8,128)(2,1)} %copy-done.12, ...), custom_call_target="tpu_custom_call" | custom-call | flops 2147483648 | bytes 6291456 | tf_op jit(solution)/shard_map/output_weight_terms/pallas_call | solution.py:50
  182.4 12.8 %all-to-all-start.3 = ((bf16[8,1024,128]{2,1,0:T(8,128)(2,1)}), bf16[8,1024,128]{2,1,0:T(8,128)(2,1)S(1)}, u32[]{:S(2)}, u32[]{:S(2)}) async-start(bf16[8,1024,128]{2,1,0:T(8,128)(2,1)} %output_weight_terms.1), calls=%async_computation.3 | async-start | bytes 4194304 | tf_op jit(solution)/shard_map/all_to_all | solution.py:357
  197.3 6.6 %collective-permute-done.16.refs_4_ = bf16[1,128,1024]{2,1,0:T(8,128)(2,1)S(1)} collective-permute-done((bf16[1,128,1024]{2,1,0:T(8,128)(2,1)S(1)}, bf16[1,128,1024]{2,1,0:T(8,128)(2,1)S(1)}, u32[]{:S(2)}, u32[]{:S(2)}) %collective-permute-start.16) | collective-permute-done | bytes 262176 | tf_op jit(solution)/shard_map/ppermute | solution.py:302
  207.1 7.2 %query_weight_terms.1 = bf16[1024,1024]{1,0:T(8,128)(2,1)} custom-call(s32[5]{0:T(128)} %stack.59.refs_0_.pos, bf16[2,256,1024]{2,1,0:T(8,128)(2,1)} %get-tuple-element.57.refs_0_, bf16[2,256,1024]{2,1,0:T(8,128)(2,1)} %copy-done.2, bf16[2,256,1024]{2,1,0:T(8,128)(2,1)} %copy-done.1, bf16[1,128,1024]{2,1,0:T(8,128)(2,1)} %copy-done.24, ...), custom_call_target="tpu_custom_call" | custom-call | flops 2147483648 | bytes 6291456 | tf_op jit(solution)/shard_map/query_weight_terms/pallas_call | solution.py:50
  214.3 8.8 %all-to-all-done.3 = bf16[8,1024,128]{2,1,0:T(8,128)(2,1)S(1)} async-done(((bf16[8,1024,128]{2,1,0:T(8,128)(2,1)}), bf16[8,1024,128]{2,1,0:T(8,128)(2,1)S(1)}, u32[]{:S(2)}, u32[]{:S(2)}) %all-to-all-start.3) | async-done | bytes 2097184 | tf_op jit(solution)/shard_map/all_to_all | solution.py:357
  224.2 3.6 %all-to-all-start.4 = ((bf16[8,128,1024]{2,1,0:T(8,128)(2,1)}), bf16[8,128,1024]{2,1,0:T(8,128)(2,1)S(1)}, u32[]{:S(2)}, u32[]{:S(2)}) async-start(bf16[8,128,1024]{2,1,0:T(8,128)(2,1)} %bitcast.50), calls=%async_computation.4 | async-start | bytes 4194304 | tf_op jit(solution)/shard_map/all_to_all | solution.py:357
  230.0 25.5 %all-to-all-done.4 = bf16[8,128,1024]{2,1,0:T(8,128)(2,1)S(1)} async-done(((bf16[8,128,1024]{2,1,0:T(8,128)(2,1)}), bf16[8,128,1024]{2,1,0:T(8,128)(2,1)S(1)}, u32[]{:S(2)}, u32[]{:S(2)}) %all-to-all-start.4) | async-done | bytes 2097184 | tf_op jit(solution)/shard_map/all_to_all | solution.py:357
  (111 shorter events, 45.0 us)
Async XLA Ops:
  0.6 10.1 %collective-permute-start = (bf16[256,1024]{1,0:T(8,128)(2,1)}, bf16[256,1024]{1,0:T(8,128)(2,1)}, u32[]{:S(2)}, u32[]{:S(2)}) collective-permute-start(bf16[256,1024]{1,0:T(8,128)(2,1)} %refs_1_.1), channel_id=1, source_target_pairs={{0,32},{32,0},{1,33},{33,1},{2,34},{34,2},{3,35},{35,3},{4,36},{36... | collective-permute-start | bytes 1572872 | tf_op jit(solution)/shard_map/ppermute | solution.py:305
  0.7 25.2 %collective-permute-start.2 = (bf16[256,1024]{1,0:T(8,128)(2,1)}, bf16[256,1024]{1,0:T(8,128)(2,1)S(1)}, u32[]{:S(2)}, u32[]{:S(2)}) collective-permute-start(bf16[256,1024]{1,0:T(8,128)(2,1)} %refs_1_.1), channel_id=1, source_target_pairs={{0,64},{64,0},{1,65},{65,1},{2,66},{66,2},{3,67},{67,3},{4,68},{68... | collective-permute-start | bytes 1572872 | tf_op jit(solution)/shard_map/ppermute | solution.py:305
  1.2 10.2 %collective-permute-start.1 = (bf16[256,1024]{1,0:T(8,128)(2,1)}, bf16[256,1024]{1,0:T(8,128)(2,1)}, u32[]{:S(2)}, u32[]{:S(2)}) collective-permute-start(bf16[256,1024]{1,0:T(8,128)(2,1)} %refs_3_.1), channel_id=1, source_target_pairs={{0,32},{32,0},{1,33},{33,1},{2,34},{34,2},{3,35},{35,3},{4,36},{36... | collective-permute-start | bytes 1572872 | tf_op jit(solution)/shard_map/ppermute | solution.py:305
  1.4 26.6 %collective-permute-start.4 = (bf16[256,1024]{1,0:T(8,128)(2,1)}, bf16[256,1024]{1,0:T(8,128)(2,1)S(1)}, u32[]{:S(2)}, u32[]{:S(2)}) collective-permute-start(bf16[256,1024]{1,0:T(8,128)(2,1)} %refs_3_.1), channel_id=1, source_target_pairs={{0,64},{64,0},{1,65},{65,1},{2,66},{66,2},{3,67},{67,3},{4,68},{68... | collective-permute-start | bytes 1572872 | tf_op jit(solution)/shard_map/ppermute | solution.py:305
  7.7 14.5 %collective-permute-start.8 = (bf16[2,256,256]{2,1,0:T(8,128)(2,1)S(1)}, bf16[2,256,256]{2,1,0:T(8,128)(2,1)S(1)}, u32[]{:S(2)}, u32[]{:S(2)}) collective-permute-start(bf16[2,256,256]{2,1,0:T(8,128)(2,1)S(1)} %get-tuple-element.71), channel_id=1, source_target_pairs={{0,6},{2,0},{4,2},{6,4},{1,7},{3,1},{5,3},{7,5},{8,14},{10,8},{12,... | collective-permute-start | bytes 786440 | tf_op jit(solution)/shard_map/ppermute | solution.py:302
  10.8 11.4 %collective-permute-start.7 = (bf16[2,256,256]{2,1,0:T(8,128)(2,1)S(1)}, bf16[2,256,256]{2,1,0:T(8,128)(2,1)S(1)}, u32[]{:S(2)}, u32[]{:S(2)}) collective-permute-start(bf16[2,256,256]{2,1,0:T(8,128)(2,1)S(1)} %get-tuple-element.72), channel_id=1, source_target_pairs={{0,4},{2,6},{4,0},{6,2},{1,5},{3,7},{5,1},{7,3},{8,12},{10,14},{12... | collective-permute-start | bytes 786440 | tf_op jit(solution)/shard_map/ppermute | solution.py:302
  11.4 14.5 %collective-permute-start.6 = (bf16[2,256,256]{2,1,0:T(8,128)(2,1)S(1)}, bf16[2,256,256]{2,1,0:T(8,128)(2,1)S(1)}, u32[]{:S(2)}, u32[]{:S(2)}) collective-permute-start(bf16[2,256,256]{2,1,0:T(8,128)(2,1)S(1)} %get-tuple-element.73), channel_id=1, source_target_pairs={{0,2},{2,4},{4,6},{6,0},{1,3},{3,5},{5,7},{7,1},{8,10},{10,12},{12... | collective-permute-start | bytes 786440 | tf_op jit(solution)/shard_map/ppermute | solution.py:302
  29.2 28.1 %all-to-all-start.1 = ((bf16[128,2,8,256]{3,2,1,0:T(8,128)(2,1)}), bf16[128,2,8,256]{3,2,1,0:T(8,128)(2,1)S(1)}, u32[]{:S(2)}, u32[]{:S(2)}) async-start(bf16[128,2,8,256]{3,2,1,0:T(8,128)(2,1)} %bitcast.8), calls=%async_computation.1 | async-start | bytes 2097152 | tf_op jit(solution)/shard_map/all_to_all | solution.py:320
  39.9 2.5 collective-permute-start.5
  57.3 18.8 %all-to-all-start = ((bf16[4,2,256,256]{3,2,1,0:T(8,128)(2,1)}), bf16[4,2,256,256]{3,2,1,0:T(8,128)(2,1)S(1)}, u32[]{:S(2)}, u32[]{:S(2)}) async-start(bf16[4,2,256,256]{3,2,1,0:T(8,128)(2,1)} %project_far.1), calls=%async_computation | async-start | bytes 2097152 | tf_op jit(solution)/shard_map/all_to_all | solution.py:327
  88.0 24.2 %collective-permute-start.10 = (bf16[2,256,1024]{2,1,0:T(8,128)(2,1)}, bf16[2,256,1024]{2,1,0:T(8,128)(2,1)S(1)}, u32[]{:S(2)}, u32[]{:S(2)}) collective-permute-start(bf16[2,256,1024]{2,1,0:T(8,128)(2,1)} %get-tuple-element.57.refs_0_), channel_id=1, source_target_pairs={{0,6},{2,0},{4,2},{6,4},{1,7},{3,1},{5,3},{7,5},{8,14},{10,8},{12,... | collective-permute-start | bytes 3145736 | tf_op jit(solution)/shard_map/ppermute | solution.py:302
  89.2 26.2 %collective-permute-start.9 = (bf16[2,256,1024]{2,1,0:T(8,128)(2,1)}, bf16[2,256,1024]{2,1,0:T(8,128)(2,1)S(1)}, u32[]{:S(2)}, u32[]{:S(2)}) collective-permute-start(bf16[2,256,1024]{2,1,0:T(8,128)(2,1)} %get-tuple-element.57.refs_0_), channel_id=1, source_target_pairs={{0,2},{2,4},{4,6},{6,0},{1,3},{3,5},{5,7},{7,1},{8,10},{10,12},{12... | collective-permute-start | bytes 3145736 | tf_op jit(solution)/shard_map/ppermute | solution.py:302
  113.0 6.4 %collective-permute-start.12 = (bf16[1,128,1024]{2,1,0:T(8,128)(2,1)S(1)}, bf16[1,128,1024]{2,1,0:T(8,128)(2,1)S(1)}, u32[]{:S(2)}, u32[]{:S(2)}) collective-permute-start(bf16[1,128,1024]{2,1,0:T(8,128)(2,1)S(1)} %get-tuple-element.66), channel_id=1, source_target_pairs={{0,6},{2,0},{4,2},{6,4},{1,7},{3,1},{5,3},{7,5},{8,14},{10,8},{12,... | collective-permute-start | bytes 786440 | tf_op jit(solution)/shard_map/ppermute | solution.py:302
  116.2 7.6 %collective-permute-start.11 = (bf16[1,128,1024]{2,1,0:T(8,128)(2,1)S(1)}, bf16[1,128,1024]{2,1,0:T(8,128)(2,1)S(1)}, u32[]{:S(2)}, u32[]{:S(2)}) collective-permute-start(bf16[1,128,1024]{2,1,0:T(8,128)(2,1)S(1)} %get-tuple-element.68), channel_id=1, source_target_pairs={{0,2},{2,4},{4,6},{6,0},{1,3},{3,5},{5,7},{7,1},{8,10},{10,12},{12... | collective-permute-start | bytes 786440 | tf_op jit(solution)/shard_map/ppermute | solution.py:302
  116.4 24.4 %collective-permute-start.17 = (bf16[4,2,256,256]{3,2,1,0:T(8,128)(2,1)S(1)}, bf16[4,2,256,256]{3,2,1,0:T(8,128)(2,1)}, u32[]{:S(2)}, u32[]{:S(2)}) collective-permute-start(bf16[4,2,256,256]{3,2,1,0:T(8,128)(2,1)S(1)} %pad_maximum_fusion.p0), channel_id=1, source_target_pairs={{0,64},{64,0},{1,65},{65,1},{2,66},{66,2},{3,67},{67,3},{4,68},{68... | collective-permute-start | bytes 3145736 | tf_op jit(solution)/shard_map/ppermute | solution.py:305
  132.6 18.1 %collective-permute-start.13 = (bf16[2,256,1024]{2,1,0:T(8,128)(2,1)}, bf16[2,256,1024]{2,1,0:T(8,128)(2,1)S(1)}, u32[]{:S(2)}, u32[]{:S(2)}) collective-permute-start(bf16[2,256,1024]{2,1,0:T(8,128)(2,1)} %get-tuple-element.38), channel_id=1, source_target_pairs={{0,32},{32,0},{1,33},{33,1},{2,34},{34,2},{3,35},{35,3},{4,36},{36... | collective-permute-start | bytes 3145736 | tf_op jit(solution)/shard_map/ppermute | solution.py:305
  140.8 27.4 %collective-permute-start.18 = (bf16[4,2,256,256]{3,2,1,0:T(8,128)(2,1)S(1)}, bf16[4,2,256,256]{3,2,1,0:T(8,128)(2,1)}, u32[]{:S(2)}, u32[]{:S(2)}) collective-permute-start(bf16[4,2,256,256]{3,2,1,0:T(8,128)(2,1)S(1)} %pad_maximum_fusion.p0), channel_id=1, source_target_pairs={{0,32},{32,0},{1,33},{33,1},{2,34},{34,2},{3,35},{35,3},{4,36},{36... | collective-permute-start | bytes 3145736 | tf_op jit(solution)/shard_map/ppermute | solution.py:305
  140.8 27.4 %collective-permute-start.19 = (bf16[4,2,256,256]{3,2,1,0:T(8,128)(2,1)}, bf16[4,2,256,256]{3,2,1,0:T(8,128)(2,1)}, u32[]{:S(2)}, u32[]{:S(2)}) collective-permute-start(bf16[4,2,256,256]{3,2,1,0:T(8,128)(2,1)} %collective-permute-done.17.p2), channel_id=1, source_target_pairs={{0,32},{32,0},{1,33},{33,1},{2,34},{34,2},{3,35},{35,3},{4,36},{36... | collective-permute-start | bytes 3145736 | tf_op jit(solution)/shard_map/ppermute | solution.py:305
  142.4 25.8 %all-to-all-start.2 = ((bf16[128,2,8,256]{3,2,1,0:T(8,128)(2,1)}), bf16[128,2,8,256]{3,2,1,0:T(8,128)(2,1)}, u32[]{:S(2)}, u32[]{:S(2)}) async-start(bf16[128,2,8,256]{3,2,1,0:T(8,128)(2,1)} %pad_maximum_fusion.1), calls=%async_computation.2 | async-start | bytes 2097152 | tf_op jit(solution)/shard_map/all_to_all | solution.py:343
  154.7 25.7 %collective-permute-start.14 = (bf16[256,1024]{1,0:T(8,128)(2,1)}, bf16[256,1024]{1,0:T(8,128)(2,1)}, u32[]{:S(2)}, u32[]{:S(2)}) collective-permute-start(bf16[256,1024]{1,0:T(8,128)(2,1)} %fusion.2), channel_id=1, source_target_pairs={{0,64},{64,0},{1,65},{65,1},{2,66},{66,2},{3,67},{67,3},{4,68},{68... | collective-permute-start | bytes 1572872 | tf_op jit(solution)/shard_map/ppermute | solution.py:305
  182.4 40.7 %all-to-all-start.3 = ((bf16[8,1024,128]{2,1,0:T(8,128)(2,1)}), bf16[8,1024,128]{2,1,0:T(8,128)(2,1)S(1)}, u32[]{:S(2)}, u32[]{:S(2)}) async-start(bf16[8,1024,128]{2,1,0:T(8,128)(2,1)} %output_weight_terms.1), calls=%async_computation.3 | async-start | bytes 4194304 | tf_op jit(solution)/shard_map/all_to_all | solution.py:357
  195.2 8.7 %collective-permute-start.16 = (bf16[1,128,1024]{2,1,0:T(8,128)(2,1)S(1)}, bf16[1,128,1024]{2,1,0:T(8,128)(2,1)S(1)}, u32[]{:S(2)}, u32[]{:S(2)}) collective-permute-start(bf16[1,128,1024]{2,1,0:T(8,128)(2,1)S(1)} %copy-done.13), channel_id=1, source_target_pairs={{0,6},{2,0},{4,2},{6,4},{1,7},{3,1},{5,3},{7,5},{8,14},{10,8},{12,... | collective-permute-start | bytes 786440 | tf_op jit(solution)/shard_map/ppermute | solution.py:302
  196.4 10.0 %collective-permute-start.15 = (bf16[1,128,1024]{2,1,0:T(8,128)(2,1)S(1)}, bf16[1,128,1024]{2,1,0:T(8,128)(2,1)S(1)}, u32[]{:S(2)}, u32[]{:S(2)}) collective-permute-start(bf16[1,128,1024]{2,1,0:T(8,128)(2,1)S(1)} %copy-done.14), channel_id=1, source_target_pairs={{0,2},{2,4},{4,6},{6,0},{1,3},{3,5},{5,7},{7,1},{8,10},{10,12},{12... | collective-permute-start | bytes 786440 | tf_op jit(solution)/shard_map/ppermute | solution.py:302
  224.2 31.3 %all-to-all-start.4 = ((bf16[8,128,1024]{2,1,0:T(8,128)(2,1)}), bf16[8,128,1024]{2,1,0:T(8,128)(2,1)S(1)}, u32[]{:S(2)}, u32[]{:S(2)}) async-start(bf16[8,128,1024]{2,1,0:T(8,128)(2,1)} %bitcast.50), calls=%async_computation.4 | async-start | bytes 4194304 | tf_op jit(solution)/shard_map/all_to_all | solution.py:357
  (28 other events, 298.0 us)

commit v13 on v12

--- a/solution.py
+++ b/solution.py
@@ -336,6 +336,7 @@
     def far_halves(i):
         return shift(left[i : i + 1, :half], "y", 1), shift(right[i : i + 1, half:], "y", 3)
 
+    left, right = after((left, right), over_x)
     every_out = (gathered, left, right, *far_halves(0))
     every_grad = (gathered, left, right, *far_halves(1))
 
@@ -351,7 +352,8 @@
 
     give, keep = output_terms(pos, every_out, output_weight)
     pair = keep + swap(give, "core").astype(F32)
-    attended = (pair[0] + swap(pair[1].astype(BF16), "xh").astype(F32)).astype(BF16)
+    pair_far = pair[1].astype(BF16)
+    attended = (pair[0] + swap(pair_far, "xh").astype(F32)).astype(BF16)
 
     def plane_sum(parts):
         return jnp.sum(lax.all_to_all(parts, ("z", "xl"), 0, 0, tiled=True).astype(F32), axis=0)
@@ -365,7 +367,7 @@
         group_cotangent,
         (PLANES, BLOCK, 128),
     )
-    output_weight_grad = plane_sum(after(output_parts, attended))
+    output_weight_grad = plane_sum(output_parts)
     query_parts = weight_terms(
         "query_weight_terms",
         query_grad_kernel,
@@ -375,7 +377,7 @@
         group_states,
         (BLOCK, BLOCK),
     )
-    query_parts = after(query_parts, output_weight_grad)
+    query_parts = after(query_parts, output_weight_grad, pair_far)
     query_weight_grad = plane_sum(query_parts.reshape(PLANES, 128, BLOCK))
     return attended, query_weight_grad, output_weight_grad, owned[0], owned[1]
 

time: 257 us -> 244 us (0.949)
  the two profiles are of different devices: /device:TPU:4 before, /device:TPU:0 now
where the time goes in v13:
time: 244 us; the launch traced here: 243 us
  waiting for transfers between devices  108 us (44%)
  Pallas kernels  56.4 us (23%)
  starting transfers between devices  52.5 us (22%)
  local copies, waits for them, and re-layouts  17.1 us (7%)
  other arithmetic  7.73 us (3%)
    pallas_call x7, Pallas kernels, call(): pl.pallas_call(kernel, grid_spec=pltpu.PrefetchScalarGridSpec(num_scalar_...  56.4 us
    ppermute x9, waiting for transfers between devices, shift(): return lax.ppermute(x, axis, [(i, (i + d) % 4) for i in range(4)])  47.2 us
    ppermute x11, waiting for transfers between devices, swap(): return lax.ppermute(x, axis, SWAP)  37.9 us
    ppermute x9, starting transfers between devices, shift(): return lax.ppermute(x, axis, [(i, (i + d) % 4) for i in range(4)])  13.4 us
    all_to_all x1, waiting for transfers between devices, on_device(): rows = lax.all_to_all(rows, 'y', 0, 0, tiled=True)  12.9 us
    all_to_all x1, starting transfers between devices, on_device(): lax.all_to_all(after(own, products, far_states, far_cotangent, quarters),...  11.1 us
    all_to_all x2, starting transfers between devices, plane_sum(): lax.all_to_all(parts, ('z', 'xl'), 0, 0, tiled=True).astype(F32)  9.43 us
    ppermute x11, starting transfers between devices, swap(): return lax.ppermute(x, axis, SWAP)  9 us
  transfers between devices with their start and end apart: 25, of which 14 were waited for; matrix products, arithmetic and copies ran while one was open for 6% of the time, Pallas kernels for 14%

profile of v13, /device:TPU:0, one launch (start us, length us, event | category | flops | bytes accessed | tf_op | source)
XLA Modules:
  0.0 243.1 jit_solution(7684068942284365561)
XLA Ops:
  0.7 3.2 %collective-permute-start.2 = (bf16[256,1024]{1,0:T(8,128)(2,1)}, bf16[256,1024]{1,0:T(8,128)(2,1)S(1)}, u32[]{:S(2)}, u32[]{:S(2)}) collective-permute-start(bf16[256,1024]{1,0:T(8,128)(2,1)} %refs_1_.1), channel_id=1, source_target_pairs={{0,64},{64,0},{1,65},{65,1},{2,66},{66,2},{3,67},{67,3},{4,68},{68... | collective-permute-start | bytes 1572872 | tf_op jit(solution)/shard_map/ppermute | solution.py:305
  7.7 3.2 %collective-permute-start.8 = (bf16[2,256,256]{2,1,0:T(8,128)(2,1)S(1)}, bf16[2,256,256]{2,1,0:T(8,128)(2,1)S(1)}, u32[]{:S(2)}, u32[]{:S(2)}) collective-permute-start(bf16[2,256,256]{2,1,0:T(8,128)(2,1)S(1)} %get-tuple-element.73), channel_id=1, source_target_pairs={{0,6},{2,0},{4,2},{6,4},{1,7},{3,1},{5,3},{7,5},{8,14},{10,8},{12,... | collective-permute-start | bytes 786440 | tf_op jit(solution)/shard_map/ppermute | solution.py:302
  13.2 8.4 %project_near.1.refs_1_ = f32[2,256,1024]{2,1,0:T(8,128)} custom-call(s32[5]{0:T(128)} %stack.59.refs_0_.pos, bf16[256,1024]{1,0:T(8,128)(2,1)} %refs_1_.1, bf16[256,1024]{1,0:T(8,128)(2,1)} %collective-permute-done.refs_2_, bf16[256,1024]{1,0:T(8,128)(2,1)} %refs_3_.1, bf16[256,1024]{1,0:T(8,128)(2,1)} %collective-permute-done.1.refs_4_, ...), custom_call_target="tpu_custom_call" | custom-call | flops 2147483648 | bytes 8388608 | tf_op jit(solution)/shard_map/project_near/pallas_call | solution.py:50
  22.3 3.7 %collective-permute-done.6 = bf16[2,256,256]{2,1,0:T(8,128)(2,1)S(1)} collective-permute-done((bf16[2,256,256]{2,1,0:T(8,128)(2,1)S(1)}, bf16[2,256,256]{2,1,0:T(8,128)(2,1)S(1)}, u32[]{:S(2)}, u32[]{:S(2)}) %collective-permute-start.6) | collective-permute-done | bytes 262176 | tf_op jit(solution)/shard_map/ppermute | solution.py:302
  29.2 11.1 %all-to-all-start.1 = ((bf16[128,2,8,256]{3,2,1,0:T(8,128)(2,1)}), bf16[128,2,8,256]{3,2,1,0:T(8,128)(2,1)S(1)}, u32[]{:S(2)}, u32[]{:S(2)}) async-start(bf16[128,2,8,256]{3,2,1,0:T(8,128)(2,1)} %bitcast.8), calls=%async_computation.1 | async-start | bytes 2097152 | tf_op jit(solution)/shard_map/all_to_all | solution.py:320
  43.9 9.2 %project_far.1 = bf16[4,2,256,256]{3,2,1,0:T(8,128)(2,1)} custom-call(s32[5]{0:T(128)} %stack.59.refs_0_.pos, f32[2,256,1024]{2,1,0:T(8,128)} %project_near.1.refs_1_, bf16[256,1024]{1,0:T(8,128)(2,1)} %copy-done.7, bf16[256,1024]{1,0:T(8,128)(2,1)} %copy-done.9, bf16[256,1024]{1,0:T(8,128)(2,1)} %copy-done.8, bf16[256,1024]{1,0:T(8,128)(2,1)} %copy-done.10, ...), custom_call_target="tpu_custom_call" | custom-call | flops 2147483648 | bytes 8388608 | tf_op jit(solution)/shard_map/project_far/pallas_call | solution.py:50
  53.2 6.4 %all-to-all-done.1 = bf16[128,2,8,256]{3,2,1,0:T(8,128)(2,1)S(1)} async-done(((bf16[128,2,8,256]{3,2,1,0:T(8,128)(2,1)}), bf16[128,2,8,256]{3,2,1,0:T(8,128)(2,1)S(1)}, u32[]{:S(2)}, u32[]{:S(2)}) %all-to-all-start.1) | async-done | bytes 1048608 | tf_op jit(solution)/shard_map/all_to_all | solution.py:320
  59.5 3.7 %all-to-all-start = ((bf16[4,2,256,256]{3,2,1,0:T(8,128)(2,1)}), bf16[4,2,256,256]{3,2,1,0:T(8,128)(2,1)S(1)}, u32[]{:S(2)}, u32[]{:S(2)}) async-start(bf16[4,2,256,256]{3,2,1,0:T(8,128)(2,1)} %project_far.1), calls=%async_computation | async-start | bytes 2097152 | tf_op jit(solution)/shard_map/all_to_all | solution.py:327
  65.1 12.9 %all-to-all-done.rows = bf16[4,2,256,256]{3,2,1,0:T(8,128)(2,1)S(1)} async-done(((bf16[4,2,256,256]{3,2,1,0:T(8,128)(2,1)}), bf16[4,2,256,256]{3,2,1,0:T(8,128)(2,1)S(1)}, u32[]{:S(2)}, u32[]{:S(2)}) %all-to-all-start) | async-done | bytes 1048608 | tf_op jit(solution)/shard_map/all_to_all | solution.py:327
  79.0 11.1 %attention.1 = (bf16[2,256,1024]{2,1,0:T(8,128)(2,1)}, bf16[1024,256]{1,0:T(8,128)(2,1)}, bf16[1024,256]{1,0:T(8,128)(2,1)}) custom-call(s32[5]{0:T(128)} %stack.59.refs_0_.pos, f32[1,1024]{1,0:T(1,128)} %bitcast.63, bf16[4,2,256,256]{3,2,1,0:T(8,128)(2,1)} %copy-done.6, bf16[1024,256]{1,0:T(8,128)(2,1)} %get-tuple-element.72.k_ref, ...), custom_call_target="tpu_custom_call" | custom-call | flops 8053063680 | bytes 4194304 | tf_op jit(solution)/shard_map/attention/pallas_call | solution.py:50
  93.6 20.4 %collective-permute-done.10.refs_2_ = bf16[2,256,1024]{2,1,0:T(8,128)(2,1)S(1)} collective-permute-done((bf16[2,256,1024]{2,1,0:T(8,128)(2,1)}, bf16[2,256,1024]{2,1,0:T(8,128)(2,1)S(1)}, u32[]{:S(2)}, u32[]{:S(2)}) %collective-permute-start.10) | collective-permute-done | bytes 1048608 | tf_op jit(solution)/shard_map/ppermute | solution.py:302
  118.7 5.9 %all-to-all-start.2 = ((bf16[128,2,8,256]{3,2,1,0:T(8,128)(2,1)}), bf16[128,2,8,256]{3,2,1,0:T(8,128)(2,1)S(1)}, u32[]{:S(2)}, u32[]{:S(2)}) async-start(bf16[128,2,8,256]{3,2,1,0:T(8,128)(2,1)} %pad_maximum_fusion.1), calls=%async_computation.2 | async-start | bytes 2097152 | tf_op jit(solution)/shard_map/all_to_all | solution.py:344
  130.3 13.7 %collective-permute-done.12.refs_3_ = bf16[1,128,1024]{2,1,0:T(8,128)(2,1)S(1)} collective-permute-done((bf16[1,128,1024]{2,1,0:T(8,128)(2,1)S(1)}, bf16[1,128,1024]{2,1,0:T(8,128)(2,1)S(1)}, u32[]{:S(2)}, u32[]{:S(2)}) %collective-permute-start.12) | collective-permute-done | bytes 262176 | tf_op jit(solution)/shard_map/ppermute | solution.py:302
  145.4 8.2 %output_terms.1 = (bf16[2,256,1024]{2,1,0:T(8,128)(2,1)}, f32[2,256,1024]{2,1,0:T(8,128)}) custom-call(s32[5]{0:T(128)} %stack.59.refs_0_.pos, bf16[2,256,1024]{2,1,0:T(8,128)(2,1)} %get-tuple-element.60.refs_0_, bf16[2,256,1024]{2,1,0:T(8,128)(2,1)} %copy-done.3, bf16[2,256,1024]{2,1,0:T(8,128)(2,1)} %copy-done.2, bf16[1,128,1024]{2,1,0:T(8,128)(2,1)} %copy-done.13, ...), custom_call_target="tpu_custom_call" | custom-call | flops 2147483648 | bytes 8388608 | tf_op jit(solution)/shard_map/output_terms/pallas_call | solution.py:50
  153.6 5.6 %column_blocks.1 = (bf16[1024,1024]{1,0:T(8,128)(2,1)}, bf16[1024,1024]{1,0:T(8,128)(2,1)}) custom-call(s32[5]{0:T(128)} %stack.59.refs_0_.pos, bf16[4,2,256,256]{3,2,1,0:T(8,128)(2,1)} %copy-done.1, bf16[4,2,256,256]{3,2,1,0:T(8,128)(2,1)} %collective-permute-done.18.p1, bf16[4,2,256,256]{3,2,1,0:T(8,128)(2,1)} %collective-permute-done.11.p2, ...), custom_call_target="tpu_custom_call" | custom-call | bytes 8388608 | tf_op jit(solution)/shard_map/column_blocks/pallas_call | solution.py:50
  159.3 6.6 %output_weight_terms.1 = bf16[8,1024,128]{2,1,0:T(8,128)(2,1)} custom-call(s32[5]{0:T(128)} %stack.59.refs_0_.pos, bf16[2,256,1024]{2,1,0:T(8,128)(2,1)} %get-tuple-element.60.refs_0_, bf16[2,256,1024]{2,1,0:T(8,128)(2,1)} %copy-done.3, bf16[2,256,1024]{2,1,0:T(8,128)(2,1)} %copy-done.2, bf16[1,128,1024]{2,1,0:T(8,128)(2,1)} %copy-done.13, ...), custom_call_target="tpu_custom_call" | custom-call | flops 2147483648 | bytes 6291456 | tf_op jit(solution)/shard_map/output_weight_terms/pallas_call | solution.py:50
  165.9 5.8 %all-to-all-start.3 = ((bf16[8,1024,128]{2,1,0:T(8,128)(2,1)}), bf16[8,1024,128]{2,1,0:T(8,128)(2,1)S(1)}, u32[]{:S(2)}, u32[]{:S(2)}) async-start(bf16[8,1024,128]{2,1,0:T(8,128)(2,1)} %output_weight_terms.1), calls=%async_computation.3 | async-start | bytes 4194304 | tf_op jit(solution)/shard_map/all_to_all | solution.py:359
  171.8 3.2 %collective-permute-start.17 = (bf16[1,128,1024]{2,1,0:T(8,128)(2,1)}, bf16[1,128,1024]{2,1,0:T(8,128)(2,1)S(1)}, u32[]{:S(2)}, u32[]{:S(2)}) collective-permute-start(bf16[1,128,1024]{2,1,0:T(8,128)(2,1)} %get-tuple-element.67), channel_id=1, source_target_pairs={{0,6},{2,0},{4,2},{6,4},{1,7},{3,1},{5,3},{7,5},{8,14},{10,8},{12,... | collective-permute-start | bytes 786440 | tf_op jit(solution)/shard_map/ppermute | solution.py:302
  175.0 6.6 %collective-permute-done.16.refs_3_ = bf16[1,128,1024]{2,1,0:T(8,128)(2,1)S(1)} collective-permute-done((bf16[1,128,1024]{2,1,0:T(8,128)(2,1)S(1)}, bf16[1,128,1024]{2,1,0:T(8,128)(2,1)S(1)}, u32[]{:S(2)}, u32[]{:S(2)}) %collective-permute-start.16) | collective-permute-done | bytes 262176 | tf_op jit(solution)/shard_map/ppermute | solution.py:302
  182.4 7.3 %query_weight_terms.1 = bf16[1024,1024]{1,0:T(8,128)(2,1)} custom-call(s32[5]{0:T(128)} %stack.59.refs_0_.pos, bf16[2,256,1024]{2,1,0:T(8,128)(2,1)} %get-tuple-element.60.refs_0_, bf16[2,256,1024]{2,1,0:T(8,128)(2,1)} %copy-done.3, bf16[2,256,1024]{2,1,0:T(8,128)(2,1)} %copy-done.2, bf16[1,128,1024]{2,1,0:T(8,128)(2,1)} %copy-done.24, ...), custom_call_target="tpu_custom_call" | custom-call | flops 2147483648 | bytes 6291456 | tf_op jit(solution)/shard_map/query_weight_terms/pallas_call | solution.py:50
  194.7 4.0 %all-to-all-done.3 = bf16[8,1024,128]{2,1,0:T(8,128)(2,1)S(1)} async-done(((bf16[8,1024,128]{2,1,0:T(8,128)(2,1)}), bf16[8,1024,128]{2,1,0:T(8,128)(2,1)S(1)}, u32[]{:S(2)}, u32[]{:S(2)}) %all-to-all-start.3) | async-done | bytes 2097184 | tf_op jit(solution)/shard_map/all_to_all | solution.py:359
  199.7 3.6 %all-to-all-start.4 = ((bf16[8,128,1024]{2,1,0:T(8,128)(2,1)}), bf16[8,128,1024]{2,1,0:T(8,128)(2,1)S(1)}, u32[]{:S(2)}, u32[]{:S(2)}) async-start(bf16[8,128,1024]{2,1,0:T(8,128)(2,1)} %bitcast.51), calls=%async_computation.4 | async-start | bytes 4194304 | tf_op jit(solution)/shard_map/all_to_all | solution.py:359
  203.4 2.8 %collective-permute-start.15 = (bf16[256,1024]{1,0:T(8,128)(2,1)}, bf16[256,1024]{1,0:T(8,128)(2,1)S(1)}, u32[]{:S(2)}, u32[]{:S(2)}) collective-permute-start(bf16[256,1024]{1,0:T(8,128)(2,1)} %fusion.2), channel_id=1, source_target_pairs={{0,64},{64,0},{1,65},{65,1},{2,66},{66,2},{3,67},{67,3},{4,68},{68... | collective-permute-start | bytes 1572872 | tf_op jit(solution)/shard_map/ppermute | solution.py:305
  207.1 32.7 %collective-permute-done.15 = bf16[256,1024]{1,0:T(8,128)(2,1)S(1)} collective-permute-done((bf16[256,1024]{1,0:T(8,128)(2,1)}, bf16[256,1024]{1,0:T(8,128)(2,1)S(1)}, u32[]{:S(2)}, u32[]{:S(2)}) %collective-permute-start.15) | collective-permute-done | bytes 524320 | tf_op jit(solution)/shard_map/ppermute | solution.py:305
  (113 shorter events, 42.8 us)
Async XLA Ops:
  0.6 10.2 %collective-permute-start = (bf16[256,1024]{1,0:T(8,128)(2,1)}, bf16[256,1024]{1,0:T(8,128)(2,1)}, u32[]{:S(2)}, u32[]{:S(2)}) collective-permute-start(bf16[256,1024]{1,0:T(8,128)(2,1)} %refs_1_.1), channel_id=1, source_target_pairs={{0,32},{32,0},{1,33},{33,1},{2,34},{34,2},{3,35},{35,3},{4,36},{36... | collective-permute-start | bytes 1572872 | tf_op jit(solution)/shard_map/ppermute | solution.py:305
  0.7 25.2 %collective-permute-start.2 = (bf16[256,1024]{1,0:T(8,128)(2,1)}, bf16[256,1024]{1,0:T(8,128)(2,1)S(1)}, u32[]{:S(2)}, u32[]{:S(2)}) collective-permute-start(bf16[256,1024]{1,0:T(8,128)(2,1)} %refs_1_.1), channel_id=1, source_target_pairs={{0,64},{64,0},{1,65},{65,1},{2,66},{66,2},{3,67},{67,3},{4,68},{68... | collective-permute-start | bytes 1572872 | tf_op jit(solution)/shard_map/ppermute | solution.py:305
  3.9 7.6 %collective-permute-start.1 = (bf16[256,1024]{1,0:T(8,128)(2,1)}, bf16[256,1024]{1,0:T(8,128)(2,1)}, u32[]{:S(2)}, u32[]{:S(2)}) collective-permute-start(bf16[256,1024]{1,0:T(8,128)(2,1)} %refs_3_.1), channel_id=1, source_target_pairs={{0,32},{32,0},{1,33},{33,1},{2,34},{34,2},{3,35},{35,3},{4,36},{36... | collective-permute-start | bytes 1572872 | tf_op jit(solution)/shard_map/ppermute | solution.py:305
  4.1 24.0 %collective-permute-start.4 = (bf16[256,1024]{1,0:T(8,128)(2,1)}, bf16[256,1024]{1,0:T(8,128)(2,1)S(1)}, u32[]{:S(2)}, u32[]{:S(2)}) collective-permute-start(bf16[256,1024]{1,0:T(8,128)(2,1)} %refs_3_.1), channel_id=1, source_target_pairs={{0,64},{64,0},{1,65},{65,1},{2,66},{66,2},{3,67},{67,3},{4,68},{68... | collective-permute-start | bytes 1572872 | tf_op jit(solution)/shard_map/ppermute | solution.py:305
  7.7 14.6 %collective-permute-start.8 = (bf16[2,256,256]{2,1,0:T(8,128)(2,1)S(1)}, bf16[2,256,256]{2,1,0:T(8,128)(2,1)S(1)}, u32[]{:S(2)}, u32[]{:S(2)}) collective-permute-start(bf16[2,256,256]{2,1,0:T(8,128)(2,1)S(1)} %get-tuple-element.73), channel_id=1, source_target_pairs={{0,6},{2,0},{4,2},{6,4},{1,7},{3,1},{5,3},{7,5},{8,14},{10,8},{12,... | collective-permute-start | bytes 786440 | tf_op jit(solution)/shard_map/ppermute | solution.py:302
  10.8 11.4 %collective-permute-start.7 = (bf16[2,256,256]{2,1,0:T(8,128)(2,1)S(1)}, bf16[2,256,256]{2,1,0:T(8,128)(2,1)S(1)}, u32[]{:S(2)}, u32[]{:S(2)}) collective-permute-start(bf16[2,256,256]{2,1,0:T(8,128)(2,1)S(1)} %get-tuple-element.74), channel_id=1, source_target_pairs={{0,4},{2,6},{4,0},{6,2},{1,5},{3,7},{5,1},{7,3},{8,12},{10,14},{12... | collective-permute-start | bytes 786440 | tf_op jit(solution)/shard_map/ppermute | solution.py:302
  11.5 14.5 %collective-permute-start.6 = (bf16[2,256,256]{2,1,0:T(8,128)(2,1)S(1)}, bf16[2,256,256]{2,1,0:T(8,128)(2,1)S(1)}, u32[]{:S(2)}, u32[]{:S(2)}) collective-permute-start(bf16[2,256,256]{2,1,0:T(8,128)(2,1)S(1)} %get-tuple-element.75), channel_id=1, source_target_pairs={{0,2},{2,4},{4,6},{6,0},{1,3},{3,5},{5,7},{7,1},{8,10},{10,12},{12... | collective-permute-start | bytes 786440 | tf_op jit(solution)/shard_map/ppermute | solution.py:302
  29.2 30.4 %all-to-all-start.1 = ((bf16[128,2,8,256]{3,2,1,0:T(8,128)(2,1)}), bf16[128,2,8,256]{3,2,1,0:T(8,128)(2,1)S(1)}, u32[]{:S(2)}, u32[]{:S(2)}) async-start(bf16[128,2,8,256]{3,2,1,0:T(8,128)(2,1)} %bitcast.8), calls=%async_computation.1 | async-start | bytes 2097152 | tf_op jit(solution)/shard_map/all_to_all | solution.py:320
  40.4 2.6 %collective-permute-start.5 = (bf16[256,1024]{1,0:T(8,128)(2,1)S(1)}, bf16[256,1024]{1,0:T(8,128)(2,1)S(1)}, u32[]{:S(2)}, u32[]{:S(2)}) collective-permute-start(bf16[256,1024]{1,0:T(8,128)(2,1)S(1)} %collective-permute-done.4.refs_4_), channel_id=1, source_target_pairs={{0,32},{32,0},{1,33},{33,1},{2,34},{34,2},{3,35},{35,3},{4,36},{36... | collective-permute-start | bytes 1572872 | tf_op jit(solution)/shard_map/ppermute | solution.py:305
  59.5 18.5 %all-to-all-start = ((bf16[4,2,256,256]{3,2,1,0:T(8,128)(2,1)}), bf16[4,2,256,256]{3,2,1,0:T(8,128)(2,1)S(1)}, u32[]{:S(2)}, u32[]{:S(2)}) async-start(bf16[4,2,256,256]{3,2,1,0:T(8,128)(2,1)} %project_far.1), calls=%async_computation | async-start | bytes 2097152 | tf_op jit(solution)/shard_map/all_to_all | solution.py:327
  90.1 23.9 %collective-permute-start.10 = (bf16[2,256,1024]{2,1,0:T(8,128)(2,1)}, bf16[2,256,1024]{2,1,0:T(8,128)(2,1)S(1)}, u32[]{:S(2)}, u32[]{:S(2)}) collective-permute-start(bf16[2,256,1024]{2,1,0:T(8,128)(2,1)} %get-tuple-element.60.refs_0_), channel_id=1, source_target_pairs={{0,6},{2,0},{4,2},{6,4},{1,7},{3,1},{5,3},{7,5},{8,14},{10,8},{12,... | collective-permute-start | bytes 3145736 | tf_op jit(solution)/shard_map/ppermute | solution.py:302
  91.3 24.8 %collective-permute-start.9 = (bf16[2,256,1024]{2,1,0:T(8,128)(2,1)}, bf16[2,256,1024]{2,1,0:T(8,128)(2,1)S(1)}, u32[]{:S(2)}, u32[]{:S(2)}) collective-permute-start(bf16[2,256,1024]{2,1,0:T(8,128)(2,1)} %get-tuple-element.60.refs_0_), channel_id=1, source_target_pairs={{0,2},{2,4},{4,6},{6,0},{1,3},{3,5},{5,7},{7,1},{8,10},{10,12},{12... | collective-permute-start | bytes 3145736 | tf_op jit(solution)/shard_map/ppermute | solution.py:302
  92.4 24.7 %collective-permute-start.11 = (bf16[4,2,256,256]{3,2,1,0:T(8,128)(2,1)S(1)}, bf16[4,2,256,256]{3,2,1,0:T(8,128)(2,1)}, u32[]{:S(2)}, u32[]{:S(2)}) collective-permute-start(bf16[4,2,256,256]{3,2,1,0:T(8,128)(2,1)S(1)} %pad_maximum_fusion.p0), channel_id=1, source_target_pairs={{0,64},{64,0},{1,65},{65,1},{2,66},{66,2},{3,67},{67,3},{4,68},{68... | collective-permute-start | bytes 3145736 | tf_op jit(solution)/shard_map/ppermute | solution.py:305
  117.1 36.5 %collective-permute-start.18 = (bf16[4,2,256,256]{3,2,1,0:T(8,128)(2,1)S(1)}, bf16[4,2,256,256]{3,2,1,0:T(8,128)(2,1)}, u32[]{:S(2)}, u32[]{:S(2)}) collective-permute-start(bf16[4,2,256,256]{3,2,1,0:T(8,128)(2,1)S(1)} %pad_maximum_fusion.p0), channel_id=1, source_target_pairs={{0,32},{32,0},{1,33},{33,1},{2,34},{34,2},{3,35},{35,3},{4,36},{36... | collective-permute-start | bytes 3145736 | tf_op jit(solution)/shard_map/ppermute | solution.py:305
  117.1 36.5 %collective-permute-start.19 = (bf16[4,2,256,256]{3,2,1,0:T(8,128)(2,1)}, bf16[4,2,256,256]{3,2,1,0:T(8,128)(2,1)}, u32[]{:S(2)}, u32[]{:S(2)}) collective-permute-start(bf16[4,2,256,256]{3,2,1,0:T(8,128)(2,1)} %collective-permute-done.11.p2), channel_id=1, source_target_pairs={{0,32},{32,0},{1,33},{33,1},{2,34},{34,2},{3,35},{35,3},{4,36},{36... | collective-permute-start | bytes 3145736 | tf_op jit(solution)/shard_map/ppermute | solution.py:305
  118.7 34.9 %all-to-all-start.2 = ((bf16[128,2,8,256]{3,2,1,0:T(8,128)(2,1)}), bf16[128,2,8,256]{3,2,1,0:T(8,128)(2,1)S(1)}, u32[]{:S(2)}, u32[]{:S(2)}) async-start(bf16[128,2,8,256]{3,2,1,0:T(8,128)(2,1)} %pad_maximum_fusion.1), calls=%async_computation.2 | async-start | bytes 2097152 | tf_op jit(solution)/shard_map/all_to_all | solution.py:344
  126.4 17.6 %collective-permute-start.12 = (bf16[1,128,1024]{2,1,0:T(8,128)(2,1)S(1)}, bf16[1,128,1024]{2,1,0:T(8,128)(2,1)S(1)}, u32[]{:S(2)}, u32[]{:S(2)}) collective-permute-start(bf16[1,128,1024]{2,1,0:T(8,128)(2,1)S(1)} %get-tuple-element.70), channel_id=1, source_target_pairs={{0,2},{2,4},{4,6},{6,0},{1,3},{3,5},{5,7},{7,1},{8,10},{10,12},{12... | collective-permute-start | bytes 786440 | tf_op jit(solution)/shard_map/ppermute | solution.py:302
  128.1 15.9 %collective-permute-start.13 = (bf16[1,128,1024]{2,1,0:T(8,128)(2,1)S(1)}, bf16[1,128,1024]{2,1,0:T(8,128)(2,1)S(1)}, u32[]{:S(2)}, u32[]{:S(2)}) collective-permute-start(bf16[1,128,1024]{2,1,0:T(8,128)(2,1)S(1)} %get-tuple-element.68), channel_id=1, source_target_pairs={{0,6},{2,0},{4,2},{6,4},{1,7},{3,1},{5,3},{7,5},{8,14},{10,8},{12,... | collective-permute-start | bytes 786440 | tf_op jit(solution)/shard_map/ppermute | solution.py:302
  165.9 32.8 %all-to-all-start.3 = ((bf16[8,1024,128]{2,1,0:T(8,128)(2,1)}), bf16[8,1024,128]{2,1,0:T(8,128)(2,1)S(1)}, u32[]{:S(2)}, u32[]{:S(2)}) async-start(bf16[8,1024,128]{2,1,0:T(8,128)(2,1)} %output_weight_terms.1), calls=%async_computation.3 | async-start | bytes 4194304 | tf_op jit(solution)/shard_map/all_to_all | solution.py:359
  171.7 18.1 %collective-permute-start.14 = (bf16[2,256,1024]{2,1,0:T(8,128)(2,1)}, bf16[2,256,1024]{2,1,0:T(8,128)(2,1)S(1)}, u32[]{:S(2)}, u32[]{:S(2)}) collective-permute-start(bf16[2,256,1024]{2,1,0:T(8,128)(2,1)} %get-tuple-element.45), channel_id=1, source_target_pairs={{0,32},{32,0},{1,33},{33,1},{2,34},{34,2},{3,35},{35,3},{4,36},{36... | collective-permute-start | bytes 3145736 | tf_op jit(solution)/shard_map/ppermute | solution.py:305
  171.7 9.9 %collective-permute-start.16 = (bf16[1,128,1024]{2,1,0:T(8,128)(2,1)S(1)}, bf16[1,128,1024]{2,1,0:T(8,128)(2,1)S(1)}, u32[]{:S(2)}, u32[]{:S(2)}) collective-permute-start(bf16[1,128,1024]{2,1,0:T(8,128)(2,1)S(1)} %copy-done.15), channel_id=1, source_target_pairs={{0,2},{2,4},{4,6},{6,0},{1,3},{3,5},{5,7},{7,1},{8,10},{10,12},{12... | collective-permute-start | bytes 786440 | tf_op jit(solution)/shard_map/ppermute | solution.py:302
  171.8 9.9 %collective-permute-start.17 = (bf16[1,128,1024]{2,1,0:T(8,128)(2,1)}, bf16[1,128,1024]{2,1,0:T(8,128)(2,1)S(1)}, u32[]{:S(2)}, u32[]{:S(2)}) collective-permute-start(bf16[1,128,1024]{2,1,0:T(8,128)(2,1)} %get-tuple-element.67), channel_id=1, source_target_pairs={{0,6},{2,0},{4,2},{6,4},{1,7},{3,1},{5,3},{7,5},{8,14},{10,8},{12,... | collective-permute-start | bytes 786440 | tf_op jit(solution)/shard_map/ppermute | solution.py:302
  199.7 42.2 %all-to-all-start.4 = ((bf16[8,128,1024]{2,1,0:T(8,128)(2,1)}), bf16[8,128,1024]{2,1,0:T(8,128)(2,1)S(1)}, u32[]{:S(2)}, u32[]{:S(2)}) async-start(bf16[8,128,1024]{2,1,0:T(8,128)(2,1)} %bitcast.51), calls=%async_computation.4 | async-start | bytes 4194304 | tf_op jit(solution)/shard_map/all_to_all | solution.py:359
  203.4 36.4 %collective-permute-start.15 = (bf16[256,1024]{1,0:T(8,128)(2,1)}, bf16[256,1024]{1,0:T(8,128)(2,1)S(1)}, u32[]{:S(2)}, u32[]{:S(2)}) collective-permute-start(bf16[256,1024]{1,0:T(8,128)(2,1)} %fusion.2), channel_id=1, source_target_pairs={{0,64},{64,0},{1,65},{65,1},{2,66},{66,2},{3,67},{67,3},{4,68},{68... | collective-permute-start | bytes 1572872 | tf_op jit(solution)/shard_map/ppermute | solution.py:305
  (29 other events, 249.8 us)

commit v14 on v13

--- a/solution.py
+++ b/solution.py
@@ -340,20 +340,10 @@
     every_out = (gathered, left, right, *far_halves(0))
     every_grad = (gathered, left, right, *far_halves(1))
 
-    terms = jnp.stack([key_terms.reshape(128, 8, PIECE), value_terms.reshape(128, 8, PIECE)], 1)
-    moved = lax.all_to_all(terms, HEADS + SEQ, 0, 0, tiled=True)
-    owned = jnp.sum(moved.reshape(4, 4, 4, 2, 2, 8, PIECE).astype(F32), axis=(1, 3))
-    owned = owned.transpose(2, 3, 0, 1, 4).reshape(2, 8, 16 * PIECE)
-
     piece, over_x = after((piece, over_x), left, right)
     group_states, group_cotangent = assemble(
-        pos, after((piece, swap(piece, "core"), over_x, swap(over_x, "core")), moved)
-    )
-
-    give, keep = output_terms(pos, every_out, output_weight)
-    pair = keep + swap(give, "core").astype(F32)
-    pair_far = pair[1].astype(BF16)
-    attended = (pair[0] + swap(pair_far, "xh").astype(F32)).astype(BF16)
+        pos, (piece, swap(piece, "core"), over_x, swap(over_x, "core"))
+    )
 
     def plane_sum(parts):
         return jnp.sum(lax.all_to_all(parts, ("z", "xl"), 0, 0, tiled=True).astype(F32), axis=0)
@@ -363,11 +353,21 @@
         output_grad_kernel,
         pos,
         0,
-        after(every_out, give),
+        every_out,
         group_cotangent,
         (PLANES, BLOCK, 128),
     )
     output_weight_grad = plane_sum(output_parts)
+
+    give, keep = output_terms(pos, after(every_out, output_parts), output_weight)
+    pair = keep + swap(give, "core").astype(F32)
+    attended = (pair[0] + swap(pair[1].astype(BF16), "xh").astype(F32)).astype(BF16)
+
+    terms = jnp.stack([key_terms.reshape(128, 8, PIECE), value_terms.reshape(128, 8, PIECE)], 1)
+    moved = lax.all_to_all(after(terms, output_weight_grad), HEADS + SEQ, 0, 0, tiled=True)
+    owned = jnp.sum(moved.reshape(4, 4, 4, 2, 2, 8, PIECE).astype(F32), axis=(1, 3))
+    owned = owned.transpose(2, 3, 0, 1, 4).reshape(2, 8, 16 * PIECE)
+
     query_parts = weight_terms(
         "query_weight_terms",
         query_grad_kernel,
@@ -377,7 +377,7 @@
         group_states,
         (BLOCK, BLOCK),
     )
-    query_parts = after(query_parts, output_weight_grad, pair_far)
+    query_parts = after(query_parts, moved, attended)
     query_weight_grad = plane_sum(query_parts.reshape(PLANES, 128, BLOCK))
     return attended, query_weight_grad, output_weight_grad, owned[0], owned[1]
 

time: 244 us -> 235 us (0.963)
  local copies, waits for them, and re-layouts: 17.1 us -> 12.5 us
    all_to_all x2, waiting for transfers between devices: 3.99 us -> 39.9 us  [plane_sum(): lax.all_to_all(parts, ('z', 'xl'), 0, 0, tiled=True).astype(F32)]
    ppermute x9, waiting for transfers between devices: 47.2 us -> 27.7 us  [shift(): return lax.ppermute(x, axis, [(i, (i + d) % 4) for i in range(4)])]
    ppermute x11, waiting for transfers between devices: 37.9 us -> 18.9 us  [swap(): return lax.ppermute(x, axis, SWAP)]
    unnamed x58 -> x60, local copies, waits for them, and re-layouts: 7.1 us -> 5.03 us
  transfers between devices with their start and end apart: 25 -> 25, of which waited for: 14 -> 13; matrix products, arithmetic and copies ran while one was open for 6% -> 5% of each run, Pallas kernels for 14% -> 21%
where the time goes in v14:
time: 235 us
  waiting for transfers between devices  106 us (45%)
  Pallas kernels  56.1 us (24%)
  starting transfers between devices  52.7 us (22%)
  local copies, waits for them, and re-layouts  12.5 us (5%)
  other arithmetic  6.48 us (3%)
    pallas_call x7, Pallas kernels, call(): pl.pallas_call(kernel, grid_spec=pltpu.PrefetchScalarGridSpec(num_scalar_...  56.1 us
    all_to_all x2, waiting for transfers between devices, plane_sum(): lax.all_to_all(parts, ('z', 'xl'), 0, 0, tiled=True).astype(F32)  39.9 us
    ppermute x9, waiting for transfers between devices, shift(): return lax.ppermute(x, axis, [(i, (i + d) % 4) for i in range(4)])  27.7 us
    ppermute x11, waiting for transfers between devices, swap(): return lax.ppermute(x, axis, SWAP)  18.9 us
    ppermute x9, starting transfers between devices, shift(): return lax.ppermute(x, axis, [(i, (i + d) % 4) for i in range(4)])  14.5 us
    all_to_all x1, waiting for transfers between devices, on_device(): rows = lax.all_to_all(rows, 'y', 0, 0, tiled=True)  13.1 us
    all_to_all x1, starting transfers between devices, on_device(): lax.all_to_all(after(own, products, far_states, far_cotangent, quarters),...  11.1 us
    all_to_all x2, starting transfers between devices, plane_sum(): lax.all_to_all(parts, ('z', 'xl'), 0, 0, tiled=True).astype(F32)  9.29 us
  transfers between devices with their start and end apart: 25, of which 13 were waited for; matrix products, arithmetic and copies ran while one was open for 5% of the time, Pallas kernels for 21%

profile of v14, /device:TPU:0, one launch (start us, length us, event | category | flops | bytes accessed | tf_op | source)
XLA Modules:
  0.0 234.8 jit_solution(8529135480424049656)
XLA Ops:
  0.7 3.2 %collective-permute-start.2 = (bf16[256,1024]{1,0:T(8,128)(2,1)}, bf16[256,1024]{1,0:T(8,128)(2,1)S(1)}, u32[]{:S(2)}, u32[]{:S(2)}) collective-permute-start(bf16[256,1024]{1,0:T(8,128)(2,1)} %refs_1_.1), channel_id=1, source_target_pairs={{0,64},{64,0},{1,65},{65,1},{2,66},{66,2},{3,67},{67,3},{4,68},{68... | collective-permute-start | bytes 1572872 | tf_op jit(solution)/shard_map/ppermute | solution.py:305
  9.4 2.9 %collective-permute-start.7 = (bf16[2,256,256]{2,1,0:T(8,128)(2,1)S(1)}, bf16[2,256,256]{2,1,0:T(8,128)(2,1)S(1)}, u32[]{:S(2)}, u32[]{:S(2)}) collective-permute-start(bf16[2,256,256]{2,1,0:T(8,128)(2,1)S(1)} %get-tuple-element.68), channel_id=1, source_target_pairs={{0,4},{2,6},{4,0},{6,2},{1,5},{3,7},{5,1},{7,3},{8,12},{10,14},{12... | collective-permute-start | bytes 786440 | tf_op jit(solution)/shard_map/ppermute | solution.py:302
  14.4 8.4 %project_near.1.refs_1_ = f32[2,256,1024]{2,1,0:T(8,128)} custom-call(s32[5]{0:T(128)} %stack.59.refs_0_.pos, bf16[256,1024]{1,0:T(8,128)(2,1)} %refs_1_.1, bf16[256,1024]{1,0:T(8,128)(2,1)} %collective-permute-done.refs_2_, bf16[256,1024]{1,0:T(8,128)(2,1)} %refs_3_.1, bf16[256,1024]{1,0:T(8,128)(2,1)} %collective-permute-done.1.refs_4_, ...), custom_call_target="tpu_custom_call" | custom-call | flops 2147483648 | bytes 8388608 | tf_op jit(solution)/shard_map/project_near/pallas_call | solution.py:50
  24.2 3.8 %collective-permute-done.4.refs_4_ = bf16[256,1024]{1,0:T(8,128)(2,1)S(1)} collective-permute-done((bf16[256,1024]{1,0:T(8,128)(2,1)}, bf16[256,1024]{1,0:T(8,128)(2,1)S(1)}, u32[]{:S(2)}, u32[]{:S(2)}) %collective-permute-start.4) | collective-permute-done | bytes 524320 | tf_op jit(solution)/shard_map/ppermute | solution.py:305
  29.2 11.1 %all-to-all-start.1 = ((bf16[128,2,8,256]{3,2,1,0:T(8,128)(2,1)}), bf16[128,2,8,256]{3,2,1,0:T(8,128)(2,1)S(1)}, u32[]{:S(2)}, u32[]{:S(2)}) async-start(bf16[128,2,8,256]{3,2,1,0:T(8,128)(2,1)} %bitcast.8), calls=%async_computation.1 | async-start | bytes 2097152 | tf_op jit(solution)/shard_map/all_to_all | solution.py:320
  43.9 9.2 %project_far.1 = bf16[4,2,256,256]{3,2,1,0:T(8,128)(2,1)} custom-call(s32[5]{0:T(128)} %stack.59.refs_0_.pos, f32[2,256,1024]{2,1,0:T(8,128)} %project_near.1.refs_1_, bf16[256,1024]{1,0:T(8,128)(2,1)} %copy-done.9, bf16[256,1024]{1,0:T(8,128)(2,1)} %copy-done.11, bf16[256,1024]{1,0:T(8,128)(2,1)} %copy-done.10, bf16[256,1024]{1,0:T(8,128)(2,1)} %copy-done.12, ...), custom_call_target="tpu_custom_call" | custom-call | flops 2147483648 | bytes 8388608 | tf_op jit(solution)/shard_map/project_far/pallas_call | solution.py:50
  53.2 6.3 %all-to-all-done.1 = bf16[128,2,8,256]{3,2,1,0:T(8,128)(2,1)S(1)} async-done(((bf16[128,2,8,256]{3,2,1,0:T(8,128)(2,1)}), bf16[128,2,8,256]{3,2,1,0:T(8,128)(2,1)S(1)}, u32[]{:S(2)}, u32[]{:S(2)}) %all-to-all-start.1) | async-done | bytes 1048608 | tf_op jit(solution)/shard_map/all_to_all | solution.py:320
  59.5 3.5 %all-to-all-start = ((bf16[4,2,256,256]{3,2,1,0:T(8,128)(2,1)}), bf16[4,2,256,256]{3,2,1,0:T(8,128)(2,1)S(1)}, u32[]{:S(2)}, u32[]{:S(2)}) async-start(bf16[4,2,256,256]{3,2,1,0:T(8,128)(2,1)} %project_far.1), calls=%async_computation | async-start | bytes 2097152 | tf_op jit(solution)/shard_map/all_to_all | solution.py:327
  65.0 13.1 %all-to-all-done.rows = bf16[4,2,256,256]{3,2,1,0:T(8,128)(2,1)S(1)} async-done(((bf16[4,2,256,256]{3,2,1,0:T(8,128)(2,1)}), bf16[4,2,256,256]{3,2,1,0:T(8,128)(2,1)S(1)}, u32[]{:S(2)}, u32[]{:S(2)}) %all-to-all-start) | async-done | bytes 1048608 | tf_op jit(solution)/shard_map/all_to_all | solution.py:327
  79.6 10.8 %attention.1 = (bf16[2,256,1024]{2,1,0:T(8,128)(2,1)}, bf16[1024,256]{1,0:T(8,128)(2,1)}, bf16[1024,256]{1,0:T(8,128)(2,1)}) custom-call(s32[5]{0:T(128)} %stack.59.refs_0_.pos, f32[1,1024]{1,0:T(1,128)} %bitcast.63, bf16[4,2,256,256]{3,2,1,0:T(8,128)(2,1)} %copy-done.8, bf16[1024,256]{1,0:T(8,128)(2,1)} %get-tuple-element.66.k_ref, ...), custom_call_target="tpu_custom_call" | custom-call | flops 8053063680 | bytes 4194304 | tf_op jit(solution)/shard_map/attention/pallas_call | solution.py:50
  92.4 11.2 %collective-permute-done.11.p2 = bf16[4,2,256,256]{3,2,1,0:T(8,128)(2,1)S(1)} collective-permute-done((bf16[4,2,256,256]{3,2,1,0:T(8,128)(2,1)S(1)}, bf16[4,2,256,256]{3,2,1,0:T(8,128)(2,1)S(1)}, u32[]{:S(2)}, u32[]{:S(2)}) %collective-permute-start.11) | collective-permute-done | bytes 1048608 | tf_op jit(solution)/shard_map/ppermute | solution.py:305
  103.6 10.6 %collective-permute-done.10.refs_2_ = bf16[2,256,1024]{2,1,0:T(8,128)(2,1)S(1)} collective-permute-done((bf16[2,256,1024]{2,1,0:T(8,128)(2,1)}, bf16[2,256,1024]{2,1,0:T(8,128)(2,1)S(1)}, u32[]{:S(2)}, u32[]{:S(2)}) %collective-permute-start.10) | collective-permute-done | bytes 1048608 | tf_op jit(solution)/shard_map/ppermute | solution.py:302
  117.7 3.2 %collective-permute-start.13 = (bf16[1,128,1024]{2,1,0:T(8,128)(2,1)S(1)}, bf16[1,128,1024]{2,1,0:T(8,128)(2,1)S(1)}, u32[]{:S(2)}, u32[]{:S(2)}) collective-permute-start(bf16[1,128,1024]{2,1,0:T(8,128)(2,1)S(1)} %get-tuple-element.62), channel_id=1, source_target_pairs={{0,6},{2,0},{4,2},{6,4},{1,7},{3,1},{5,3},{7,5},{8,14},{10,8},{12,... | collective-permute-start | bytes 786440 | tf_op jit(solution)/shard_map/ppermute | solution.py:302
  122.9 5.6 %column_blocks.1 = (bf16[1024,1024]{1,0:T(8,128)(2,1)}, bf16[1024,1024]{1,0:T(8,128)(2,1)}) custom-call(s32[5]{0:T(128)} %stack.59.refs_0_.pos, bf16[4,2,256,256]{3,2,1,0:T(8,128)(2,1)} %copy-done.1, bf16[4,2,256,256]{3,2,1,0:T(8,128)(2,1)} %copy-done.6, bf16[4,2,256,256]{3,2,1,0:T(8,128)(2,1)} %copy-done.5, bf16[4,2,256,256]{3,2,1,0:T(8,128)(2,1)} %copy-done.7), custom_call_target="tpu_custom_call" | custom-call | bytes 8388608 | tf_op jit(solution)/shard_map/column_blocks/pallas_call | solution.py:50
  129.3 6.6 %output_weight_terms.1 = bf16[8,1024,128]{2,1,0:T(8,128)(2,1)} custom-call(s32[5]{0:T(128)} %stack.59.refs_0_.pos, bf16[2,256,1024]{2,1,0:T(8,128)(2,1)} %get-tuple-element.51.refs_0_, bf16[2,256,1024]{2,1,0:T(8,128)(2,1)} %copy-done.3, bf16[2,256,1024]{2,1,0:T(8,128)(2,1)} %copy-done.2, bf16[1,128,1024]{2,1,0:T(8,128)(2,1)} %copy-done.15, ...), custom_call_target="tpu_custom_call" | custom-call | flops 2147483648 | bytes 6291456 | tf_op jit(solution)/shard_map/output_weight_terms/pallas_call | solution.py:50
  135.9 3.6 %all-to-all-start.2 = ((bf16[8,1024,128]{2,1,0:T(8,128)(2,1)}), bf16[8,1024,128]{2,1,0:T(8,128)(2,1)S(1)}, u32[]{:S(2)}, u32[]{:S(2)}) async-start(bf16[8,1024,128]{2,1,0:T(8,128)(2,1)} %output_weight_terms.1), calls=%async_computation.2 | async-start | bytes 4194304 | tf_op jit(solution)/shard_map/all_to_all | solution.py:349
  139.5 8.3 %output_terms.1 = (bf16[2,256,1024]{2,1,0:T(8,128)(2,1)}, f32[2,256,1024]{2,1,0:T(8,128)}) custom-call(s32[5]{0:T(128)} %stack.59.refs_0_.pos, bf16[2,256,1024]{2,1,0:T(8,128)(2,1)} %get-tuple-element.51.refs_0_, bf16[2,256,1024]{2,1,0:T(8,128)(2,1)} %copy-done.3, bf16[2,256,1024]{2,1,0:T(8,128)(2,1)} %copy-done.2, bf16[1,128,1024]{2,1,0:T(8,128)(2,1)} %copy-done.15, ...), custom_call_target="tpu_custom_call" | custom-call | flops 2147483648 | bytes 8388608 | tf_op jit(solution)/shard_map/output_terms/pallas_call | solution.py:50
  152.5 13.9 %all-to-all-done.2 = bf16[8,1024,128]{2,1,0:T(8,128)(2,1)S(1)} async-done(((bf16[8,1024,128]{2,1,0:T(8,128)(2,1)}), bf16[8,1024,128]{2,1,0:T(8,128)(2,1)S(1)}, u32[]{:S(2)}, u32[]{:S(2)}) %all-to-all-start.2) | async-done | bytes 2097184 | tf_op jit(solution)/shard_map/all_to_all | solution.py:349
  167.5 5.3 %all-to-all-start.3 = ((bf16[128,2,8,256]{3,2,1,0:T(8,128)(2,1)}), bf16[128,2,8,256]{3,2,1,0:T(8,128)(2,1)S(1)}, u32[]{:S(2)}, u32[]{:S(2)}) async-start(bf16[128,2,8,256]{3,2,1,0:T(8,128)(2,1)} %pad_maximum_fusion.1), calls=%async_computation.3 | async-start | bytes 2097152 | tf_op jit(solution)/shard_map/all_to_all | solution.py:367
  172.8 2.5 %collective-permute-start.17 = (bf16[256,1024]{1,0:T(8,128)(2,1)S(1)}, bf16[256,1024]{1,0:T(8,128)(2,1)S(1)}, u32[]{:S(2)}, u32[]{:S(2)}) collective-permute-start(bf16[256,1024]{1,0:T(8,128)(2,1)S(1)} %fusion.2), channel_id=1, source_target_pairs={{0,64},{64,0},{1,65},{65,1},{2,66},{66,2},{3,67},{67,3},{4,68},{68... | collective-permute-start | bytes 1572872 | tf_op jit(solution)/shard_map/ppermute | solution.py:305
  178.6 13.5 %collective-permute-done.18.refs_3_ = bf16[1,128,1024]{2,1,0:T(8,128)(2,1)S(1)} collective-permute-done((bf16[1,128,1024]{2,1,0:T(8,128)(2,1)S(1)}, bf16[1,128,1024]{2,1,0:T(8,128)(2,1)S(1)}, u32[]{:S(2)}, u32[]{:S(2)}) %collective-permute-start.18) | collective-permute-done | bytes 262176 | tf_op jit(solution)/shard_map/ppermute | solution.py:302
  192.9 7.2 %query_weight_terms.1 = bf16[1024,1024]{1,0:T(8,128)(2,1)} custom-call(s32[5]{0:T(128)} %stack.59.refs_0_.pos, bf16[2,256,1024]{2,1,0:T(8,128)(2,1)} %get-tuple-element.51.refs_0_, bf16[2,256,1024]{2,1,0:T(8,128)(2,1)} %copy-done.3, bf16[2,256,1024]{2,1,0:T(8,128)(2,1)} %copy-done.2, bf16[1,128,1024]{2,1,0:T(8,128)(2,1)} %copy-done.25, ...), custom_call_target="tpu_custom_call" | custom-call | flops 2147483648 | bytes 6291456 | tf_op jit(solution)/shard_map/query_weight_terms/pallas_call | solution.py:50
  201.0 5.7 %all-to-all-start.4 = ((bf16[8,128,1024]{2,1,0:T(8,128)(2,1)}), bf16[8,128,1024]{2,1,0:T(8,128)(2,1)S(1)}, u32[]{:S(2)}, u32[]{:S(2)}) async-start(bf16[8,128,1024]{2,1,0:T(8,128)(2,1)} %bitcast.51), calls=%async_computation.4 | async-start | bytes 4194304 | tf_op jit(solution)/shard_map/all_to_all | solution.py:349
  207.6 26.0 %all-to-all-done.4 = bf16[8,128,1024]{2,1,0:T(8,128)(2,1)S(1)} async-done(((bf16[8,128,1024]{2,1,0:T(8,128)(2,1)}), bf16[8,128,1024]{2,1,0:T(8,128)(2,1)S(1)}, u32[]{:S(2)}, u32[]{:S(2)}) %all-to-all-start.4) | async-done | bytes 2097184 | tf_op jit(solution)/shard_map/all_to_all | solution.py:349
  (115 shorter events, 38.1 us)
Async XLA Ops:
  0.6 8.8 %collective-permute-start = (bf16[256,1024]{1,0:T(8,128)(2,1)}, bf16[256,1024]{1,0:T(8,128)(2,1)}, u32[]{:S(2)}, u32[]{:S(2)}) collective-permute-start(bf16[256,1024]{1,0:T(8,128)(2,1)} %refs_1_.1), channel_id=1, source_target_pairs={{0,32},{32,0},{1,33},{33,1},{2,34},{34,2},{3,35},{35,3},{4,36},{36... | collective-permute-start | bytes 1572872 | tf_op jit(solution)/shard_map/ppermute | solution.py:305
  0.7 23.5 %collective-permute-start.2 = (bf16[256,1024]{1,0:T(8,128)(2,1)}, bf16[256,1024]{1,0:T(8,128)(2,1)S(1)}, u32[]{:S(2)}, u32[]{:S(2)}) collective-permute-start(bf16[256,1024]{1,0:T(8,128)(2,1)} %refs_1_.1), channel_id=1, source_target_pairs={{0,64},{64,0},{1,65},{65,1},{2,66},{66,2},{3,67},{67,3},{4,68},{68... | collective-permute-start | bytes 1572872 | tf_op jit(solution)/shard_map/ppermute | solution.py:305
  3.9 8.4 %collective-permute-start.1 = (bf16[256,1024]{1,0:T(8,128)(2,1)}, bf16[256,1024]{1,0:T(8,128)(2,1)}, u32[]{:S(2)}, u32[]{:S(2)}) collective-permute-start(bf16[256,1024]{1,0:T(8,128)(2,1)} %refs_3_.1), channel_id=1, source_target_pairs={{0,32},{32,0},{1,33},{33,1},{2,34},{34,2},{3,35},{35,3},{4,36},{36... | collective-permute-start | bytes 1572872 | tf_op jit(solution)/shard_map/ppermute | solution.py:305
  4.1 24.0 %collective-permute-start.4 = (bf16[256,1024]{1,0:T(8,128)(2,1)}, bf16[256,1024]{1,0:T(8,128)(2,1)S(1)}, u32[]{:S(2)}, u32[]{:S(2)}) collective-permute-start(bf16[256,1024]{1,0:T(8,128)(2,1)} %refs_3_.1), channel_id=1, source_target_pairs={{0,64},{64,0},{1,65},{65,1},{2,66},{66,2},{3,67},{67,3},{4,68},{68... | collective-permute-start | bytes 1572872 | tf_op jit(solution)/shard_map/ppermute | solution.py:305
  7.7 15.1 %collective-permute-start.6 = (bf16[2,256,256]{2,1,0:T(8,128)(2,1)S(1)}, bf16[2,256,256]{2,1,0:T(8,128)(2,1)S(1)}, u32[]{:S(2)}, u32[]{:S(2)}) collective-permute-start(bf16[2,256,256]{2,1,0:T(8,128)(2,1)S(1)} %get-tuple-element.69), channel_id=1, source_target_pairs={{0,2},{2,4},{4,6},{6,0},{1,3},{3,5},{5,7},{7,1},{8,10},{10,12},{12... | collective-permute-start | bytes 786440 | tf_op jit(solution)/shard_map/ppermute | solution.py:302
  9.4 14.8 %collective-permute-start.7 = (bf16[2,256,256]{2,1,0:T(8,128)(2,1)S(1)}, bf16[2,256,256]{2,1,0:T(8,128)(2,1)S(1)}, u32[]{:S(2)}, u32[]{:S(2)}) collective-permute-start(bf16[2,256,256]{2,1,0:T(8,128)(2,1)S(1)} %get-tuple-element.68), channel_id=1, source_target_pairs={{0,4},{2,6},{4,0},{6,2},{1,5},{3,7},{5,1},{7,3},{8,12},{10,14},{12... | collective-permute-start | bytes 786440 | tf_op jit(solution)/shard_map/ppermute | solution.py:302
  12.3 11.9 %collective-permute-start.8 = (bf16[2,256,256]{2,1,0:T(8,128)(2,1)S(1)}, bf16[2,256,256]{2,1,0:T(8,128)(2,1)S(1)}, u32[]{:S(2)}, u32[]{:S(2)}) collective-permute-start(bf16[2,256,256]{2,1,0:T(8,128)(2,1)S(1)} %get-tuple-element.67), channel_id=1, source_target_pairs={{0,6},{2,0},{4,2},{6,4},{1,7},{3,1},{5,3},{7,5},{8,14},{10,8},{12,... | collective-permute-start | bytes 786440 | tf_op jit(solution)/shard_map/ppermute | solution.py:302
  29.2 30.4 %all-to-all-start.1 = ((bf16[128,2,8,256]{3,2,1,0:T(8,128)(2,1)}), bf16[128,2,8,256]{3,2,1,0:T(8,128)(2,1)S(1)}, u32[]{:S(2)}, u32[]{:S(2)}) async-start(bf16[128,2,8,256]{3,2,1,0:T(8,128)(2,1)} %bitcast.8), calls=%async_computation.1 | async-start | bytes 2097152 | tf_op jit(solution)/shard_map/all_to_all | solution.py:320
  40.4 2.6 %collective-permute-start.5 = (bf16[256,1024]{1,0:T(8,128)(2,1)S(1)}, bf16[256,1024]{1,0:T(8,128)(2,1)S(1)}, u32[]{:S(2)}, u32[]{:S(2)}) collective-permute-start(bf16[256,1024]{1,0:T(8,128)(2,1)S(1)} %collective-permute-done.4.refs_4_), channel_id=1, source_target_pairs={{0,32},{32,0},{1,33},{33,1},{2,34},{34,2},{3,35},{35,3},{4,36},{36... | collective-permute-start | bytes 1572872 | tf_op jit(solution)/shard_map/ppermute | solution.py:305
  59.5 18.5 %all-to-all-start = ((bf16[4,2,256,256]{3,2,1,0:T(8,128)(2,1)}), bf16[4,2,256,256]{3,2,1,0:T(8,128)(2,1)S(1)}, u32[]{:S(2)}, u32[]{:S(2)}) async-start(bf16[4,2,256,256]{3,2,1,0:T(8,128)(2,1)} %project_far.1), calls=%async_computation | async-start | bytes 2097152 | tf_op jit(solution)/shard_map/all_to_all | solution.py:327
  78.2 25.4 %collective-permute-start.11 = (bf16[4,2,256,256]{3,2,1,0:T(8,128)(2,1)S(1)}, bf16[4,2,256,256]{3,2,1,0:T(8,128)(2,1)S(1)}, u32[]{:S(2)}, u32[]{:S(2)}) collective-permute-start(bf16[4,2,256,256]{3,2,1,0:T(8,128)(2,1)S(1)} %pad_maximum_fusion.p0), channel_id=1, source_target_pairs={{0,64},{64,0},{1,65},{65,1},{2,66},{66,2},{3,67},{67,3},{4,68},{68... | collective-permute-start | bytes 3145736 | tf_op jit(solution)/shard_map/ppermute | solution.py:305
  90.4 23.9 %collective-permute-start.10 = (bf16[2,256,1024]{2,1,0:T(8,128)(2,1)}, bf16[2,256,1024]{2,1,0:T(8,128)(2,1)S(1)}, u32[]{:S(2)}, u32[]{:S(2)}) collective-permute-start(bf16[2,256,1024]{2,1,0:T(8,128)(2,1)} %get-tuple-element.51.refs_0_), channel_id=1, source_target_pairs={{0,6},{2,0},{4,2},{6,4},{1,7},{3,1},{5,3},{7,5},{8,14},{10,8},{12,... | collective-permute-start | bytes 3145736 | tf_op jit(solution)/shard_map/ppermute | solution.py:302
  91.6 24.8 %collective-permute-start.9 = (bf16[2,256,1024]{2,1,0:T(8,128)(2,1)}, bf16[2,256,1024]{2,1,0:T(8,128)(2,1)S(1)}, u32[]{:S(2)}, u32[]{:S(2)}) collective-permute-start(bf16[2,256,1024]{2,1,0:T(8,128)(2,1)} %get-tuple-element.51.refs_0_), channel_id=1, source_target_pairs={{0,2},{2,4},{4,6},{6,0},{1,3},{3,5},{5,7},{7,1},{8,10},{10,12},{12... | collective-permute-start | bytes 3145736 | tf_op jit(solution)/shard_map/ppermute | solution.py:302
  116.3 4.6 %collective-permute-start.14 = (bf16[4,2,256,256]{3,2,1,0:T(8,128)(2,1)S(1)}, bf16[4,2,256,256]{3,2,1,0:T(8,128)(2,1)S(1)}, u32[]{:S(2)}, u32[]{:S(2)}) collective-permute-start(bf16[4,2,256,256]{3,2,1,0:T(8,128)(2,1)S(1)} %pad_maximum_fusion.p0), channel_id=1, source_target_pairs={{0,32},{32,0},{1,33},{33,1},{2,34},{34,2},{3,35},{35,3},{4,36},{36... | collective-permute-start | bytes 3145736 | tf_op jit(solution)/shard_map/ppermute | solution.py:305
  116.3 4.6 %collective-permute-start.15 = (bf16[4,2,256,256]{3,2,1,0:T(8,128)(2,1)S(1)}, bf16[4,2,256,256]{3,2,1,0:T(8,128)(2,1)S(1)}, u32[]{:S(2)}, u32[]{:S(2)}) collective-permute-start(bf16[4,2,256,256]{3,2,1,0:T(8,128)(2,1)S(1)} %collective-permute-done.11.p2), channel_id=1, source_target_pairs={{0,32},{32,0},{1,33},{33,1},{2,34},{34,2},{3,35},{35,3},{4,36},{36... | collective-permute-start | bytes 3145736 | tf_op jit(solution)/shard_map/ppermute | solution.py:305
  116.9 11.6 %collective-permute-start.12 = (bf16[1,128,1024]{2,1,0:T(8,128)(2,1)S(1)}, bf16[1,128,1024]{2,1,0:T(8,128)(2,1)S(1)}, u32[]{:S(2)}, u32[]{:S(2)}) collective-permute-start(bf16[1,128,1024]{2,1,0:T(8,128)(2,1)S(1)} %get-tuple-element.64), channel_id=1, source_target_pairs={{0,2},{2,4},{4,6},{6,0},{1,3},{3,5},{5,7},{7,1},{8,10},{10,12},{12... | collective-permute-start | bytes 786440 | tf_op jit(solution)/shard_map/ppermute | solution.py:302
  117.7 10.8 %collective-permute-start.13 = (bf16[1,128,1024]{2,1,0:T(8,128)(2,1)S(1)}, bf16[1,128,1024]{2,1,0:T(8,128)(2,1)S(1)}, u32[]{:S(2)}, u32[]{:S(2)}) collective-permute-start(bf16[1,128,1024]{2,1,0:T(8,128)(2,1)S(1)} %get-tuple-element.62), channel_id=1, source_target_pairs={{0,6},{2,0},{4,2},{6,4},{1,7},{3,1},{5,3},{7,5},{8,14},{10,8},{12,... | collective-permute-start | bytes 786440 | tf_op jit(solution)/shard_map/ppermute | solution.py:302
  135.9 30.5 %all-to-all-start.2 = ((bf16[8,1024,128]{2,1,0:T(8,128)(2,1)}), bf16[8,1024,128]{2,1,0:T(8,128)(2,1)S(1)}, u32[]{:S(2)}, u32[]{:S(2)}) async-start(bf16[8,1024,128]{2,1,0:T(8,128)(2,1)} %output_weight_terms.1), calls=%async_computation.2 | async-start | bytes 4194304 | tf_op jit(solution)/shard_map/all_to_all | solution.py:349
  147.8 3.0 %collective-permute-start.16 = (bf16[2,256,1024]{2,1,0:T(8,128)(2,1)}, bf16[2,256,1024]{2,1,0:T(8,128)(2,1)S(1)}, u32[]{:S(2)}, u32[]{:S(2)}) collective-permute-start(bf16[2,256,1024]{2,1,0:T(8,128)(2,1)} %get-tuple-element.50), channel_id=1, source_target_pairs={{0,32},{32,0},{1,33},{33,1},{2,34},{34,2},{3,35},{35,3},{4,36},{36... | collective-permute-start | bytes 3145736 | tf_op jit(solution)/shard_map/ppermute | solution.py:305
  167.5 33.6 %all-to-all-start.3 = ((bf16[128,2,8,256]{3,2,1,0:T(8,128)(2,1)}), bf16[128,2,8,256]{3,2,1,0:T(8,128)(2,1)S(1)}, u32[]{:S(2)}, u32[]{:S(2)}) async-start(bf16[128,2,8,256]{3,2,1,0:T(8,128)(2,1)} %pad_maximum_fusion.1), calls=%async_computation.3 | async-start | bytes 2097152 | tf_op jit(solution)/shard_map/all_to_all | solution.py:367
  172.8 27.3 %collective-permute-start.17 = (bf16[256,1024]{1,0:T(8,128)(2,1)S(1)}, bf16[256,1024]{1,0:T(8,128)(2,1)S(1)}, u32[]{:S(2)}, u32[]{:S(2)}) collective-permute-start(bf16[256,1024]{1,0:T(8,128)(2,1)S(1)} %fusion.2), channel_id=1, source_target_pairs={{0,64},{64,0},{1,65},{65,1},{2,66},{66,2},{3,67},{67,3},{4,68},{68... | collective-permute-start | bytes 1572872 | tf_op jit(solution)/shard_map/ppermute | solution.py:305
  175.4 16.8 %collective-permute-start.18 = (bf16[1,128,1024]{2,1,0:T(8,128)(2,1)S(1)}, bf16[1,128,1024]{2,1,0:T(8,128)(2,1)S(1)}, u32[]{:S(2)}, u32[]{:S(2)}) collective-permute-start(bf16[1,128,1024]{2,1,0:T(8,128)(2,1)S(1)} %get-tuple-element.63), channel_id=1, source_target_pairs={{0,2},{2,4},{4,6},{6,0},{1,3},{3,5},{5,7},{7,1},{8,10},{10,12},{12... | collective-permute-start | bytes 786440 | tf_op jit(solution)/shard_map/ppermute | solution.py:302
  176.8 15.3 %collective-permute-start.19 = (bf16[1,128,1024]{2,1,0:T(8,128)(2,1)}, bf16[1,128,1024]{2,1,0:T(8,128)(2,1)S(1)}, u32[]{:S(2)}, u32[]{:S(2)}) collective-permute-start(bf16[1,128,1024]{2,1,0:T(8,128)(2,1)} %get-tuple-element.61), channel_id=1, source_target_pairs={{0,6},{2,0},{4,2},{6,4},{1,7},{3,1},{5,3},{7,5},{8,14},{10,8},{12,... | collective-permute-start | bytes 786440 | tf_op jit(solution)/shard_map/ppermute | solution.py:302
  201.0 32.6 %all-to-all-start.4 = ((bf16[8,128,1024]{2,1,0:T(8,128)(2,1)}), bf16[8,128,1024]{2,1,0:T(8,128)(2,1)S(1)}, u32[]{:S(2)}, u32[]{:S(2)}) async-start(bf16[8,128,1024]{2,1,0:T(8,128)(2,1)} %bitcast.51), calls=%async_computation.4 | async-start | bytes 4194304 | tf_op jit(solution)/shard_map/all_to_all | solution.py:349
  (30 other events, 285.5 us)

commit v15 on v14

--- a/solution.py
+++ b/solution.py
@@ -157,7 +157,7 @@
     )
 
 
-def attention_kernel(pos, bias, rows, k_ref, v_ref, out, dk_ref, dv_ref, dk_sum, dv_sum):
+def attention_kernel(pos, bias, rows, k_ref, v_ref, out, dq_ref, dk_ref, dv_ref, dk_sum, dv_sum):
     k, v = k_ref[...], v_ref[...]
     for layer in range(4):
         q = rows[layer, 0]
@@ -172,7 +172,7 @@
         g = (rows[layer, 1].astype(F32) * (share * SCALE)).astype(BF16)
         delta = jnp.sum(g.astype(F32) * heads_out.astype(F32), axis=1, keepdims=True)
         score_grad = (low.astype(F32) * (dot(g, v, ((1,), (1,))) - delta)).astype(BF16)
-        out[1, :, token] = dot(score_grad, k).astype(BF16).T
+        dq_ref[0, :, token] = dot(score_grad, k).astype(BF16).T
         dk_term, dv_term = dot(q, score_grad, ((0,), (0,))), dot(g, low, ((0,), (0,)))
         dk_sum[...] = dk_term if layer == 0 else dk_sum[...] + dk_term
         dv_sum[...] = dv_term if layer == 0 else dv_sum[...] + dv_term
@@ -188,8 +188,8 @@
         "attention",
         (PIECE // HEAD,),
         [whole((1, context)), pl.BlockSpec((4, 2, TOK, HEAD), lambda h, pos: (0, 0, 0, h))] + [column] * 2,
-        [pl.BlockSpec((2, HEAD, GROUP), lambda h, pos: (0, h, 0))] + [column] * 2,
-        [struct((2, PIECE, GROUP))] + [struct((GROUP, PIECE))] * 2,
+        [pl.BlockSpec((1, HEAD, GROUP), lambda h, pos: (0, h, 0))] * 2 + [column] * 2,
+        [struct((1, PIECE, GROUP))] * 2 + [struct((GROUP, PIECE))] * 2,
         [pltpu.VMEM((HEAD, context), F32)] * 2,
         30 * GROUP * PIECE * context,
         16 * GROUP * PIECE,
@@ -222,16 +222,12 @@
         out[:, pl.ds(col, cols)] = dot(left[...], ref[0], ((1,), (1,))).astype(BF16)
 
 
-def one_of(pair, which):
-    return pl.BlockSpec((1, *pair.shape[1:]), lambda i, pos: (which if pair.shape[0] == 2 else 0, 0, 0))
-
-
-def weight_terms(name, kernel, pos, which, gathered, block, out):
+def weight_terms(name, kernel, pos, gathered, block, out):
     return call(
         kernel,
         name,
         (1,),
-        [one_of(a, which) for a in gathered] + [whole(block.shape)],
+        [whole(a.shape) for a in gathered] + [whole(block.shape)],
         whole(out),
         struct(out),
         [],
@@ -329,18 +325,16 @@
     piece = jnp.stack(after(quarters, rows))
     over_x = swap(piece, "xh")
 
-    gathered, key_terms, value_terms = attention(pos, bias, rows, keys, values)
-    left, right = shift(gathered, "y", 1), shift(gathered, "y", 3)
+    heads_out, query_grad, key_terms, value_terms = attention(pos, bias, rows, keys, values)
     half = PIECE // 2
 
-    def far_halves(i):
-        return shift(left[i : i + 1, :half], "y", 1), shift(right[i : i + 1, half:], "y", 3)
-
-    left, right = after((left, right), over_x)
-    every_out = (gathered, left, right, *far_halves(0))
-    every_grad = (gathered, left, right, *far_halves(1))
-
-    piece, over_x = after((piece, over_x), left, right)
+    def ring(x, *others):
+        left, right = after((shift(x, "y", 1), shift(x, "y", 3)), *others)
+        return x, left, right, shift(left[:, :half], "y", 1), shift(right[:, half:], "y", 3)
+
+    every_out = ring(heads_out, over_x)
+
+    piece, over_x = after((piece, over_x), *every_out[:3])
     group_states, group_cotangent = assemble(
         pos, (piece, swap(piece, "core"), over_x, swap(over_x, "core"))
     )
@@ -352,31 +346,31 @@
         "output_weight_terms",
         output_grad_kernel,
         pos,
-        0,
         every_out,
         group_cotangent,
         (PLANES, BLOCK, 128),
     )
+    every_grad = ring(after(query_grad, every_out), output_parts)
     output_weight_grad = plane_sum(output_parts)
 
     give, keep = output_terms(pos, after(every_out, output_parts), output_weight)
     pair = keep + swap(give, "core").astype(F32)
     attended = (pair[0] + swap(pair[1].astype(BF16), "xh").astype(F32)).astype(BF16)
 
-    terms = jnp.stack([key_terms.reshape(128, 8, PIECE), value_terms.reshape(128, 8, PIECE)], 1)
-    moved = lax.all_to_all(after(terms, output_weight_grad), HEADS + SEQ, 0, 0, tiled=True)
-    owned = jnp.sum(moved.reshape(4, 4, 4, 2, 2, 8, PIECE).astype(F32), axis=(1, 3))
-    owned = owned.transpose(2, 3, 0, 1, 4).reshape(2, 8, 16 * PIECE)
-
     query_parts = weight_terms(
         "query_weight_terms",
         query_grad_kernel,
         pos,
-        1,
         after(every_grad, output_parts),
         group_states,
         (BLOCK, BLOCK),
     )
+
+    terms = jnp.stack([key_terms.reshape(128, 8, PIECE), value_terms.reshape(128, 8, PIECE)], 1)
+    moved = lax.all_to_all(after(terms, output_weight_grad, query_parts), HEADS + SEQ, 0, 0, tiled=True)
+    owned = jnp.sum(moved.reshape(4, 4, 4, 2, 2, 8, PIECE).astype(F32), axis=(1, 3))
+    owned = owned.transpose(2, 3, 0, 1, 4).reshape(2, 8, 16 * PIECE)
+
     query_parts = after(query_parts, moved, attended)
     query_weight_grad = plane_sum(query_parts.reshape(PLANES, 128, BLOCK))
     return attended, query_weight_grad, output_weight_grad, owned[0], owned[1]

time: 235 us -> 239 us (1.017)
  waiting for transfers between devices: 106 us -> 111 us
    all_to_all x2, waiting for transfers between devices: 39.9 us -> 25.9 us  [plane_sum(): lax.all_to_all(parts, ('z', 'xl'), 0, 0, tiled=True).astype(F32)]
    ppermute x9 -> x11, waiting for transfers between devices: 27.7 us -> 37.1 us  [shift(): return lax.ppermute(x, axis, [(i, (i + d) % 4) for i in range(4)])]
    ppermute x11, waiting for transfers between devices: 18.9 us -> 28.3 us  [swap(): return lax.ppermute(x, axis, SWAP)]
    ppermute x9 -> x11, starting transfers between devices: 14.5 us -> 13.2 us  [shift(): return lax.ppermute(x, axis, [(i, (i + d) % 4) for i in range(4)])]
    unnamed x60 -> x66, local copies, waits for them, and re-layouts: 5.03 us -> 4.15 us
  transfers between devices with their start and end apart: 25 -> 27, of which waited for: 13 -> 16; matrix products, arithmetic and copies ran while one was open for 5% -> 4% of each run, Pallas kernels for 21% -> 21%
where the time goes in v15:
time: 239 us; the launch traced here: 238 us
  waiting for transfers between devices  111 us (46%)
  Pallas kernels  56 us (23%)
  starting transfers between devices  52.3 us (22%)
  local copies, waits for them, and re-layouts  10.9 us (5%)
  other arithmetic  6.63 us (3%)
    pallas_call x7, Pallas kernels, call(): pl.pallas_call(kernel, grid_spec=pltpu.PrefetchScalarGridSpec(num_scalar_...  56 us
    ppermute x11, waiting for transfers between devices, shift(): return lax.ppermute(x, axis, [(i, (i + d) % 4) for i in range(4)])  37.1 us
    ppermute x11, waiting for transfers between devices, swap(): return lax.ppermute(x, axis, SWAP)  28.3 us
    all_to_all x2, waiting for transfers between devices, plane_sum(): lax.all_to_all(parts, ('z', 'xl'), 0, 0, tiled=True).astype(F32)  25.9 us
    ppermute x11, starting transfers between devices, shift(): return lax.ppermute(x, axis, [(i, (i + d) % 4) for i in range(4)])  13.2 us
    all_to_all x1, waiting for transfers between devices, on_device(): rows = lax.all_to_all(rows, 'y', 0, 0, tiled=True)  13.1 us
    all_to_all x1, starting transfers between devices, on_device(): lax.all_to_all(after(own, products, far_states, far_cotangent, quarters),...  11.1 us
    ppermute x11, starting transfers between devices, swap(): return lax.ppermute(x, axis, SWAP)  9.18 us
  transfers between devices with their start and end apart: 27, of which 16 were waited for; matrix products, arithmetic and copies ran while one was open for 4% of the time, Pallas kernels for 21%

profile of v15, /device:TPU:0, one launch (start us, length us, event | category | flops | bytes accessed | tf_op | source)
XLA Modules:
  0.0 237.6 jit_solution(13597573732382805089)
XLA Ops:
  0.7 3.2 %collective-permute-start.2 = (bf16[256,1024]{1,0:T(8,128)(2,1)}, bf16[256,1024]{1,0:T(8,128)(2,1)S(1)}, u32[]{:S(2)}, u32[]{:S(2)}) collective-permute-start(bf16[256,1024]{1,0:T(8,128)(2,1)} %refs_1_.1), channel_id=1, source_target_pairs={{0,64},{64,0},{1,65},{65,1},{2,66},{66,2},{3,67},{67,3},{4,68},{68... | collective-permute-start | bytes 1572872 | tf_op jit(solution)/shard_map/ppermute | solution.py:301
  7.7 3.2 %collective-permute-start.8 = (bf16[2,256,256]{2,1,0:T(8,128)(2,1)S(1)}, bf16[2,256,256]{2,1,0:T(8,128)(2,1)S(1)}, u32[]{:S(2)}, u32[]{:S(2)}) collective-permute-start(bf16[2,256,256]{2,1,0:T(8,128)(2,1)S(1)} %get-tuple-element.71), channel_id=1, source_target_pairs={{0,6},{2,0},{4,2},{6,4},{1,7},{3,1},{5,3},{7,5},{8,14},{10,8},{12,... | collective-permute-start | bytes 786440 | tf_op jit(solution)/shard_map/ppermute | solution.py:298
  13.2 8.4 %project_near.1.refs_1_ = f32[2,256,1024]{2,1,0:T(8,128)} custom-call(s32[5]{0:T(128)} %stack.59.refs_0_.pos, bf16[256,1024]{1,0:T(8,128)(2,1)} %refs_1_.1, bf16[256,1024]{1,0:T(8,128)(2,1)} %collective-permute-done.refs_2_, bf16[256,1024]{1,0:T(8,128)(2,1)} %refs_3_.1, bf16[256,1024]{1,0:T(8,128)(2,1)} %collective-permute-done.1.refs_4_, ...), custom_call_target="tpu_custom_call" | custom-call | flops 2147483648 | bytes 8388608 | tf_op jit(solution)/shard_map/project_near/pallas_call | solution.py:50
  22.3 3.7 %collective-permute-done.6 = bf16[2,256,256]{2,1,0:T(8,128)(2,1)S(1)} collective-permute-done((bf16[2,256,256]{2,1,0:T(8,128)(2,1)S(1)}, bf16[2,256,256]{2,1,0:T(8,128)(2,1)S(1)}, u32[]{:S(2)}, u32[]{:S(2)}) %collective-permute-start.6) | collective-permute-done | bytes 262176 | tf_op jit(solution)/shard_map/ppermute | solution.py:298
  29.2 11.1 %all-to-all-start.1 = ((bf16[128,2,8,256]{3,2,1,0:T(8,128)(2,1)}), bf16[128,2,8,256]{3,2,1,0:T(8,128)(2,1)S(1)}, u32[]{:S(2)}, u32[]{:S(2)}) async-start(bf16[128,2,8,256]{3,2,1,0:T(8,128)(2,1)} %bitcast.8), calls=%async_computation.1 | async-start | bytes 2097152 | tf_op jit(solution)/shard_map/all_to_all | solution.py:316
  43.9 9.2 %project_far.1 = bf16[4,2,256,256]{3,2,1,0:T(8,128)(2,1)} custom-call(s32[5]{0:T(128)} %stack.59.refs_0_.pos, f32[2,256,1024]{2,1,0:T(8,128)} %project_near.1.refs_1_, bf16[256,1024]{1,0:T(8,128)(2,1)} %copy-done.9, bf16[256,1024]{1,0:T(8,128)(2,1)} %copy-done.11, bf16[256,1024]{1,0:T(8,128)(2,1)} %copy-done.10, bf16[256,1024]{1,0:T(8,128)(2,1)} %copy-done.12, ...), custom_call_target="tpu_custom_call" | custom-call | flops 2147483648 | bytes 8388608 | tf_op jit(solution)/shard_map/project_far/pallas_call | solution.py:50
  53.2 6.3 %all-to-all-done.1 = bf16[128,2,8,256]{3,2,1,0:T(8,128)(2,1)S(1)} async-done(((bf16[128,2,8,256]{3,2,1,0:T(8,128)(2,1)}), bf16[128,2,8,256]{3,2,1,0:T(8,128)(2,1)S(1)}, u32[]{:S(2)}, u32[]{:S(2)}) %all-to-all-start.1) | async-done | bytes 1048608 | tf_op jit(solution)/shard_map/all_to_all | solution.py:316
  59.5 3.5 %all-to-all-start = ((bf16[4,2,256,256]{3,2,1,0:T(8,128)(2,1)}), bf16[4,2,256,256]{3,2,1,0:T(8,128)(2,1)S(1)}, u32[]{:S(2)}, u32[]{:S(2)}) async-start(bf16[4,2,256,256]{3,2,1,0:T(8,128)(2,1)} %project_far.1), calls=%async_computation | async-start | bytes 2097152 | tf_op jit(solution)/shard_map/all_to_all | solution.py:323
  65.0 13.1 %all-to-all-done.rows = bf16[4,2,256,256]{3,2,1,0:T(8,128)(2,1)S(1)} async-done(((bf16[4,2,256,256]{3,2,1,0:T(8,128)(2,1)}), bf16[4,2,256,256]{3,2,1,0:T(8,128)(2,1)S(1)}, u32[]{:S(2)}, u32[]{:S(2)}) %all-to-all-start) | async-done | bytes 1048608 | tf_op jit(solution)/shard_map/all_to_all | solution.py:323
  79.6 10.6 %attention.1 = (bf16[1,256,1024]{2,1,0:T(8,128)(2,1)}, bf16[1,256,1024]{2,1,0:T(8,128)(2,1)}, bf16[1024,256]{1,0:T(8,128)(2,1)}, bf16[1024,256]{1,0:T(8,128)(2,1)}) custom-call(s32[5]{0:T(128)} %stack.59.refs_0_.pos, f32[1,1024]{1,0:T(1,128)} %bitcast.63, bf16[4,2,256,256]{3,2,1,0:T(8,128)(2,1)} %copy-done.8, bf16[1024,256]{1,0:T(8,128)(2,1)} %get-tuple-element.70.k_ref, ...), custom_call_target="tpu_custom_call" | custom-call | flops 8053063680 | bytes 4194304 | tf_op jit(solution)/shard_map/attention/pallas_call | solution.py:50
  92.2 10.6 %collective-permute-done.10.refs_2_ = bf16[1,256,1024]{2,1,0:T(8,128)(2,1)S(1)} collective-permute-done((bf16[1,256,1024]{2,1,0:T(8,128)(2,1)}, bf16[1,256,1024]{2,1,0:T(8,128)(2,1)S(1)}, u32[]{:S(2)}, u32[]{:S(2)}) %collective-permute-start.10) | collective-permute-done | bytes 524320 | tf_op jit(solution)/shard_map/ppermute | solution.py:298
  102.8 2.1 collective-permute-done.9.refs_1_
  110.2 5.6 %column_blocks.1 = (bf16[1024,1024]{1,0:T(8,128)(2,1)}, bf16[1024,1024]{1,0:T(8,128)(2,1)}) custom-call(s32[5]{0:T(128)} %stack.59.refs_0_.pos, bf16[4,2,256,256]{3,2,1,0:T(8,128)(2,1)} %copy-done.1, bf16[4,2,256,256]{3,2,1,0:T(8,128)(2,1)} %copy-done.6, bf16[4,2,256,256]{3,2,1,0:T(8,128)(2,1)} %copy-done.5, bf16[4,2,256,256]{3,2,1,0:T(8,128)(2,1)} %copy-done.7), custom_call_target="tpu_custom_call" | custom-call | bytes 8388608 | tf_op jit(solution)/shard_map/column_blocks/pallas_call | solution.py:50
  116.7 6.6 %output_weight_terms.1 = bf16[8,1024,128]{2,1,0:T(8,128)(2,1)} custom-call(s32[5]{0:T(128)} %stack.59.refs_0_.pos, bf16[1,256,1024]{2,1,0:T(8,128)(2,1)} %get-tuple-element.48.refs_0_, bf16[1,256,1024]{2,1,0:T(8,128)(2,1)} %copy-done.4, bf16[1,256,1024]{2,1,0:T(8,128)(2,1)} %copy-done.3, bf16[1,128,1024]{2,1,0:T(8,128)(2,1)} %copy-done.22, ...), custom_call_target="tpu_custom_call" | custom-call | flops 2147483648 | bytes 6291456 | tf_op jit(solution)/shard_map/output_weight_terms/pallas_call | solution.py:50
  123.3 3.6 %all-to-all-start.2 = ((bf16[8,1024,128]{2,1,0:T(8,128)(2,1)}), bf16[8,1024,128]{2,1,0:T(8,128)(2,1)S(1)}, u32[]{:S(2)}, u32[]{:S(2)}) async-start(bf16[8,1024,128]{2,1,0:T(8,128)(2,1)} %output_weight_terms.1), calls=%async_computation.2 | async-start | bytes 4194304 | tf_op jit(solution)/shard_map/all_to_all | solution.py:343
  126.9 8.3 %output_terms.1 = (bf16[2,256,1024]{2,1,0:T(8,128)(2,1)}, f32[2,256,1024]{2,1,0:T(8,128)}) custom-call(s32[5]{0:T(128)} %stack.59.refs_0_.pos, bf16[1,256,1024]{2,1,0:T(8,128)(2,1)} %get-tuple-element.48.refs_0_, bf16[1,256,1024]{2,1,0:T(8,128)(2,1)} %copy-done.4, bf16[1,256,1024]{2,1,0:T(8,128)(2,1)} %copy-done.3, bf16[1,128,1024]{2,1,0:T(8,128)(2,1)} %copy-done.22, ...), custom_call_target="tpu_custom_call" | custom-call | flops 2147483648 | bytes 8388608 | tf_op jit(solution)/shard_map/output_terms/pallas_call | solution.py:50
  137.5 12.2 %collective-permute-done.19.refs_2_ = bf16[1,256,1024]{2,1,0:T(8,128)(2,1)S(1)} collective-permute-done((bf16[1,256,1024]{2,1,0:T(8,128)(2,1)S(1)}, bf16[1,256,1024]{2,1,0:T(8,128)(2,1)S(1)}, u32[]{:S(2)}, u32[]{:S(2)}) %collective-permute-start.19) | collective-permute-done | bytes 524320 | tf_op jit(solution)/shard_map/ppermute | solution.py:298
  155.0 4.4 %collective-permute-done.21.refs_4_ = bf16[1,128,1024]{2,1,0:T(8,128)(2,1)S(1)} collective-permute-done((bf16[1,128,1024]{2,1,0:T(8,128)(2,1)S(1)}, bf16[1,128,1024]{2,1,0:T(8,128)(2,1)S(1)}, u32[]{:S(2)}, u32[]{:S(2)}) %collective-permute-start.21) | collective-permute-done | bytes 262176 | tf_op jit(solution)/shard_map/ppermute | solution.py:298
  161.7 7.3 %query_weight_terms.1 = bf16[1024,1024]{1,0:T(8,128)(2,1)} custom-call(s32[5]{0:T(128)} %stack.59.refs_0_.pos, bf16[1,256,1024]{2,1,0:T(8,128)(2,1)} %get-tuple-element.59.refs_0_, bf16[1,256,1024]{2,1,0:T(8,128)(2,1)} %copy-done.24, bf16[1,256,1024]{2,1,0:T(8,128)(2,1)} %copy-done.23, bf16[1,128,1024]{2,1,0:T(8,128)(2,1)} %copy-done.29, ...), custom_call_target="tpu_custom_call" | custom-call | flops 2147483648 | bytes 6291456 | tf_op jit(solution)/shard_map/query_weight_terms/pallas_call | solution.py:50
  171.9 6.9 %all-to-all-start.3 = ((bf16[128,2,8,256]{3,2,1,0:T(8,128)(2,1)}), bf16[128,2,8,256]{3,2,1,0:T(8,128)(2,1)S(1)}, u32[]{:S(2)}, u32[]{:S(2)}) async-start(bf16[128,2,8,256]{3,2,1,0:T(8,128)(2,1)} %pad_maximum_fusion.1), calls=%async_computation.3 | async-start | bytes 2097152 | tf_op jit(solution)/shard_map/all_to_all | solution.py:370
  178.9 2.5 %collective-permute-start.17 = (bf16[256,1024]{1,0:T(8,128)(2,1)S(1)}, bf16[256,1024]{1,0:T(8,128)(2,1)S(1)}, u32[]{:S(2)}, u32[]{:S(2)}) collective-permute-start(bf16[256,1024]{1,0:T(8,128)(2,1)S(1)} %fusion.2), channel_id=1, source_target_pairs={{0,64},{64,0},{1,65},{65,1},{2,66},{66,2},{3,67},{67,3},{4,68},{68... | collective-permute-start | bytes 1572872 | tf_op jit(solution)/shard_map/ppermute | solution.py:301
  181.4 22.6 %collective-permute-done.17 = bf16[256,1024]{1,0:T(8,128)(2,1)S(1)} collective-permute-done((bf16[256,1024]{1,0:T(8,128)(2,1)S(1)}, bf16[256,1024]{1,0:T(8,128)(2,1)S(1)}, u32[]{:S(2)}, u32[]{:S(2)}) %collective-permute-start.17) | collective-permute-done | bytes 524320 | tf_op jit(solution)/shard_map/ppermute | solution.py:301
  205.0 4.7 %all-to-all-start.4 = ((bf16[8,128,1024]{2,1,0:T(8,128)(2,1)}), bf16[8,128,1024]{2,1,0:T(8,128)(2,1)S(1)}, u32[]{:S(2)}, u32[]{:S(2)}) async-start(bf16[8,128,1024]{2,1,0:T(8,128)(2,1)} %bitcast.51), calls=%async_computation.4 | async-start | bytes 4194304 | tf_op jit(solution)/shard_map/all_to_all | solution.py:343
  210.6 25.9 %all-to-all-done.4 = bf16[8,128,1024]{2,1,0:T(8,128)(2,1)S(1)} async-done(((bf16[8,128,1024]{2,1,0:T(8,128)(2,1)}), bf16[8,128,1024]{2,1,0:T(8,128)(2,1)S(1)}, u32[]{:S(2)}, u32[]{:S(2)}) %all-to-all-start.4) | async-done | bytes 2097184 | tf_op jit(solution)/shard_map/all_to_all | solution.py:343
  (127 shorter events, 40.9 us)
Async XLA Ops:
  0.6 10.2 %collective-permute-start = (bf16[256,1024]{1,0:T(8,128)(2,1)}, bf16[256,1024]{1,0:T(8,128)(2,1)}, u32[]{:S(2)}, u32[]{:S(2)}) collective-permute-start(bf16[256,1024]{1,0:T(8,128)(2,1)} %refs_1_.1), channel_id=1, source_target_pairs={{0,32},{32,0},{1,33},{33,1},{2,34},{34,2},{3,35},{35,3},{4,36},{36... | collective-permute-start | bytes 1572872 | tf_op jit(solution)/shard_map/ppermute | solution.py:301
  0.7 25.2 %collective-permute-start.2 = (bf16[256,1024]{1,0:T(8,128)(2,1)}, bf16[256,1024]{1,0:T(8,128)(2,1)S(1)}, u32[]{:S(2)}, u32[]{:S(2)}) collective-permute-start(bf16[256,1024]{1,0:T(8,128)(2,1)} %refs_1_.1), channel_id=1, source_target_pairs={{0,64},{64,0},{1,65},{65,1},{2,66},{66,2},{3,67},{67,3},{4,68},{68... | collective-permute-start | bytes 1572872 | tf_op jit(solution)/shard_map/ppermute | solution.py:301
  3.9 7.6 %collective-permute-start.1 = (bf16[256,1024]{1,0:T(8,128)(2,1)}, bf16[256,1024]{1,0:T(8,128)(2,1)}, u32[]{:S(2)}, u32[]{:S(2)}) collective-permute-start(bf16[256,1024]{1,0:T(8,128)(2,1)} %refs_3_.1), channel_id=1, source_target_pairs={{0,32},{32,0},{1,33},{33,1},{2,34},{34,2},{3,35},{35,3},{4,36},{36... | collective-permute-start | bytes 1572872 | tf_op jit(solution)/shard_map/ppermute | solution.py:301
  4.1 24.0 %collective-permute-start.4 = (bf16[256,1024]{1,0:T(8,128)(2,1)}, bf16[256,1024]{1,0:T(8,128)(2,1)S(1)}, u32[]{:S(2)}, u32[]{:S(2)}) collective-permute-start(bf16[256,1024]{1,0:T(8,128)(2,1)} %refs_3_.1), channel_id=1, source_target_pairs={{0,64},{64,0},{1,65},{65,1},{2,66},{66,2},{3,67},{67,3},{4,68},{68... | collective-permute-start | bytes 1572872 | tf_op jit(solution)/shard_map/ppermute | solution.py:301
  7.7 14.6 %collective-permute-start.8 = (bf16[2,256,256]{2,1,0:T(8,128)(2,1)S(1)}, bf16[2,256,256]{2,1,0:T(8,128)(2,1)S(1)}, u32[]{:S(2)}, u32[]{:S(2)}) collective-permute-start(bf16[2,256,256]{2,1,0:T(8,128)(2,1)S(1)} %get-tuple-element.71), channel_id=1, source_target_pairs={{0,6},{2,0},{4,2},{6,4},{1,7},{3,1},{5,3},{7,5},{8,14},{10,8},{12,... | collective-permute-start | bytes 786440 | tf_op jit(solution)/shard_map/ppermute | solution.py:298
  10.8 11.4 %collective-permute-start.7 = (bf16[2,256,256]{2,1,0:T(8,128)(2,1)S(1)}, bf16[2,256,256]{2,1,0:T(8,128)(2,1)S(1)}, u32[]{:S(2)}, u32[]{:S(2)}) collective-permute-start(bf16[2,256,256]{2,1,0:T(8,128)(2,1)S(1)} %get-tuple-element.72), channel_id=1, source_target_pairs={{0,4},{2,6},{4,0},{6,2},{1,5},{3,7},{5,1},{7,3},{8,12},{10,14},{12... | collective-permute-start | bytes 786440 | tf_op jit(solution)/shard_map/ppermute | solution.py:298
  11.5 14.5 %collective-permute-start.6 = (bf16[2,256,256]{2,1,0:T(8,128)(2,1)S(1)}, bf16[2,256,256]{2,1,0:T(8,128)(2,1)S(1)}, u32[]{:S(2)}, u32[]{:S(2)}) collective-permute-start(bf16[2,256,256]{2,1,0:T(8,128)(2,1)S(1)} %get-tuple-element.73), channel_id=1, source_target_pairs={{0,2},{2,4},{4,6},{6,0},{1,3},{3,5},{5,7},{7,1},{8,10},{10,12},{12... | collective-permute-start | bytes 786440 | tf_op jit(solution)/shard_map/ppermute | solution.py:298
  29.2 30.4 %all-to-all-start.1 = ((bf16[128,2,8,256]{3,2,1,0:T(8,128)(2,1)}), bf16[128,2,8,256]{3,2,1,0:T(8,128)(2,1)S(1)}, u32[]{:S(2)}, u32[]{:S(2)}) async-start(bf16[128,2,8,256]{3,2,1,0:T(8,128)(2,1)} %bitcast.8), calls=%async_computation.1 | async-start | bytes 2097152 | tf_op jit(solution)/shard_map/all_to_all | solution.py:316
  59.5 18.5 %all-to-all-start = ((bf16[4,2,256,256]{3,2,1,0:T(8,128)(2,1)}), bf16[4,2,256,256]{3,2,1,0:T(8,128)(2,1)S(1)}, u32[]{:S(2)}, u32[]{:S(2)}) async-start(bf16[4,2,256,256]{3,2,1,0:T(8,128)(2,1)} %project_far.1), calls=%async_computation | async-start | bytes 2097152 | tf_op jit(solution)/shard_map/all_to_all | solution.py:323
  78.2 26.7 %collective-permute-start.11 = (bf16[4,2,256,256]{3,2,1,0:T(8,128)(2,1)S(1)}, bf16[4,2,256,256]{3,2,1,0:T(8,128)(2,1)S(1)}, u32[]{:S(2)}, u32[]{:S(2)}) collective-permute-start(bf16[4,2,256,256]{3,2,1,0:T(8,128)(2,1)S(1)} %pad_maximum_fusion.p0), channel_id=1, source_target_pairs={{0,64},{64,0},{1,65},{65,1},{2,66},{66,2},{3,67},{67,3},{4,68},{68... | collective-permute-start | bytes 3145736 | tf_op jit(solution)/shard_map/ppermute | solution.py:301
  90.2 12.6 %collective-permute-start.10 = (bf16[1,256,1024]{2,1,0:T(8,128)(2,1)}, bf16[1,256,1024]{2,1,0:T(8,128)(2,1)S(1)}, u32[]{:S(2)}, u32[]{:S(2)}) collective-permute-start(bf16[1,256,1024]{2,1,0:T(8,128)(2,1)} %get-tuple-element.48.refs_0_), channel_id=1, source_target_pairs={{0,6},{2,0},{4,2},{6,4},{1,7},{3,1},{5,3},{7,5},{8,14},{10,8},{12,... | collective-permute-start | bytes 1572872 | tf_op jit(solution)/shard_map/ppermute | solution.py:298
  91.4 13.6 %collective-permute-start.9 = (bf16[1,256,1024]{2,1,0:T(8,128)(2,1)}, bf16[1,256,1024]{2,1,0:T(8,128)(2,1)S(1)}, u32[]{:S(2)}, u32[]{:S(2)}) collective-permute-start(bf16[1,256,1024]{2,1,0:T(8,128)(2,1)} %get-tuple-element.48.refs_0_), channel_id=1, source_target_pairs={{0,2},{2,4},{4,6},{6,0},{1,3},{3,5},{5,7},{7,1},{8,10},{10,12},{12... | collective-permute-start | bytes 1572872 | tf_op jit(solution)/shard_map/ppermute | solution.py:298
  105.0 4.1 %collective-permute-start.15 = (bf16[4,2,256,256]{3,2,1,0:T(8,128)(2,1)S(1)}, bf16[4,2,256,256]{3,2,1,0:T(8,128)(2,1)S(1)}, u32[]{:S(2)}, u32[]{:S(2)}) collective-permute-start(bf16[4,2,256,256]{3,2,1,0:T(8,128)(2,1)S(1)} %collective-permute-done.11.p2), channel_id=1, source_target_pairs={{0,32},{32,0},{1,33},{33,1},{2,34},{34,2},{3,35},{35,3},{4,36},{36... | collective-permute-start | bytes 3145736 | tf_op jit(solution)/shard_map/ppermute | solution.py:301
  105.6 10.3 %collective-permute-start.13 = (bf16[1,128,1024]{2,1,0:T(8,128)(2,1)S(1)}, bf16[1,128,1024]{2,1,0:T(8,128)(2,1)S(1)}, u32[]{:S(2)}, u32[]{:S(2)}) collective-permute-start(bf16[1,128,1024]{2,1,0:T(8,128)(2,1)S(1)} %slice.36), channel_id=1, source_target_pairs={{0,6},{2,0},{4,2},{6,4},{1,7},{3,1},{5,3},{7,5},{8,14},{10,8},{12,... | collective-permute-start | bytes 786440 | tf_op jit(solution)/shard_map/ppermute | solution.py:298
  106.0 9.9 %collective-permute-start.12 = (bf16[1,128,1024]{2,1,0:T(8,128)(2,1)S(1)}, bf16[1,128,1024]{2,1,0:T(8,128)(2,1)S(1)}, u32[]{:S(2)}, u32[]{:S(2)}) collective-permute-start(bf16[1,128,1024]{2,1,0:T(8,128)(2,1)S(1)} %slice.35), channel_id=1, source_target_pairs={{0,2},{2,4},{4,6},{6,0},{1,3},{3,5},{5,7},{7,1},{8,10},{10,12},{12... | collective-permute-start | bytes 786440 | tf_op jit(solution)/shard_map/ppermute | solution.py:298
  123.3 47.6 %all-to-all-start.2 = ((bf16[8,1024,128]{2,1,0:T(8,128)(2,1)}), bf16[8,1024,128]{2,1,0:T(8,128)(2,1)S(1)}, u32[]{:S(2)}, u32[]{:S(2)}) async-start(bf16[8,1024,128]{2,1,0:T(8,128)(2,1)} %output_weight_terms.1), calls=%async_computation.2 | async-start | bytes 4194304 | tf_op jit(solution)/shard_map/all_to_all | solution.py:343
  135.2 33.8 %collective-permute-start.16 = (bf16[2,256,1024]{2,1,0:T(8,128)(2,1)}, bf16[2,256,1024]{2,1,0:T(8,128)(2,1)S(1)}, u32[]{:S(2)}, u32[]{:S(2)}) collective-permute-start(bf16[2,256,1024]{2,1,0:T(8,128)(2,1)} %get-tuple-element.54), channel_id=1, source_target_pairs={{0,32},{32,0},{1,33},{33,1},{2,34},{34,2},{3,35},{35,3},{4,36},{36... | collective-permute-start | bytes 3145736 | tf_op jit(solution)/shard_map/ppermute | solution.py:301
  135.4 14.2 %collective-permute-start.19 = (bf16[1,256,1024]{2,1,0:T(8,128)(2,1)S(1)}, bf16[1,256,1024]{2,1,0:T(8,128)(2,1)S(1)}, u32[]{:S(2)}, u32[]{:S(2)}) collective-permute-start(bf16[1,256,1024]{2,1,0:T(8,128)(2,1)S(1)} %copy-done.27), channel_id=1, source_target_pairs={{0,6},{2,0},{4,2},{6,4},{1,7},{3,1},{5,3},{7,5},{8,14},{10,8},{12,... | collective-permute-start | bytes 1572872 | tf_op jit(solution)/shard_map/ppermute | solution.py:298
  136.4 15.2 %collective-permute-start.18 = (bf16[1,256,1024]{2,1,0:T(8,128)(2,1)S(1)}, bf16[1,256,1024]{2,1,0:T(8,128)(2,1)S(1)}, u32[]{:S(2)}, u32[]{:S(2)}) collective-permute-start(bf16[1,256,1024]{2,1,0:T(8,128)(2,1)S(1)} %copy-done.27), channel_id=1, source_target_pairs={{0,2},{2,4},{4,6},{6,0},{1,3},{3,5},{5,7},{7,1},{8,10},{10,12},{12... | collective-permute-start | bytes 1572872 | tf_op jit(solution)/shard_map/ppermute | solution.py:298
  151.6 7.8 %collective-permute-start.21 = (bf16[1,128,1024]{2,1,0:T(8,128)(2,1)S(1)}, bf16[1,128,1024]{2,1,0:T(8,128)(2,1)S(1)}, u32[]{:S(2)}, u32[]{:S(2)}) collective-permute-start(bf16[1,128,1024]{2,1,0:T(8,128)(2,1)S(1)} %slice.40), channel_id=1, source_target_pairs={{0,6},{2,0},{4,2},{6,4},{1,7},{3,1},{5,3},{7,5},{8,14},{10,8},{12,... | collective-permute-start | bytes 786440 | tf_op jit(solution)/shard_map/ppermute | solution.py:298
  152.2 8.8 %collective-permute-start.20 = (bf16[1,128,1024]{2,1,0:T(8,128)(2,1)S(1)}, bf16[1,128,1024]{2,1,0:T(8,128)(2,1)S(1)}, u32[]{:S(2)}, u32[]{:S(2)}) collective-permute-start(bf16[1,128,1024]{2,1,0:T(8,128)(2,1)S(1)} %slice.39), channel_id=1, source_target_pairs={{0,2},{2,4},{4,6},{6,0},{1,3},{3,5},{5,7},{7,1},{8,10},{10,12},{12... | collective-permute-start | bytes 786440 | tf_op jit(solution)/shard_map/ppermute | solution.py:298
  171.9 33.1 %all-to-all-start.3 = ((bf16[128,2,8,256]{3,2,1,0:T(8,128)(2,1)}), bf16[128,2,8,256]{3,2,1,0:T(8,128)(2,1)S(1)}, u32[]{:S(2)}, u32[]{:S(2)}) async-start(bf16[128,2,8,256]{3,2,1,0:T(8,128)(2,1)} %pad_maximum_fusion.1), calls=%async_computation.3 | async-start | bytes 2097152 | tf_op jit(solution)/shard_map/all_to_all | solution.py:370
  178.9 25.2 %collective-permute-start.17 = (bf16[256,1024]{1,0:T(8,128)(2,1)S(1)}, bf16[256,1024]{1,0:T(8,128)(2,1)S(1)}, u32[]{:S(2)}, u32[]{:S(2)}) collective-permute-start(bf16[256,1024]{1,0:T(8,128)(2,1)S(1)} %fusion.2), channel_id=1, source_target_pairs={{0,64},{64,0},{1,65},{65,1},{2,66},{66,2},{3,67},{67,3},{4,68},{68... | collective-permute-start | bytes 1572872 | tf_op jit(solution)/shard_map/ppermute | solution.py:301
  205.0 31.5 %all-to-all-start.4 = ((bf16[8,128,1024]{2,1,0:T(8,128)(2,1)}), bf16[8,128,1024]{2,1,0:T(8,128)(2,1)S(1)}, u32[]{:S(2)}, u32[]{:S(2)}) async-start(bf16[8,128,1024]{2,1,0:T(8,128)(2,1)} %bitcast.51), calls=%async_computation.4 | async-start | bytes 4194304 | tf_op jit(solution)/shard_map/all_to_all | solution.py:343
  (35 other events, 336.4 us)

commit v16 on v15

--- a/solution.py
+++ b/solution.py
@@ -355,7 +355,8 @@
 
     give, keep = output_terms(pos, after(every_out, output_parts), output_weight)
     pair = keep + swap(give, "core").astype(F32)
-    attended = (pair[0] + swap(pair[1].astype(BF16), "xh").astype(F32)).astype(BF16)
+    pair_far = pair[1].astype(BF16)
+    attended = (pair[0] + swap(pair_far, "xh").astype(F32)).astype(BF16)
 
     query_parts = weight_terms(
         "query_weight_terms",
@@ -367,7 +368,7 @@
     )
 
     terms = jnp.stack([key_terms.reshape(128, 8, PIECE), value_terms.reshape(128, 8, PIECE)], 1)
-    moved = lax.all_to_all(after(terms, output_weight_grad, query_parts), HEADS + SEQ, 0, 0, tiled=True)
+    moved = lax.all_to_all(after(terms, output_weight_grad, pair_far), HEADS + SEQ, 0, 0, tiled=True)
     owned = jnp.sum(moved.reshape(4, 4, 4, 2, 2, 8, PIECE).astype(F32), axis=(1, 3))
     owned = owned.transpose(2, 3, 0, 1, 4).reshape(2, 8, 16 * PIECE)
 

time: 239 us -> 224 us (0.937)
  waiting for transfers between devices: 111 us -> 95.8 us
  local copies, waits for them, and re-layouts: 10.9 us -> 13.4 us
    ppermute x11, waiting for transfers between devices: 28.3 us -> 5.7 us  [swap(): return lax.ppermute(x, axis, SWAP)]
    all_to_all x2, waiting for transfers between devices: 25.9 us -> 40.2 us  [plane_sum(): lax.all_to_all(parts, ('z', 'xl'), 0, 0, tiled=True).astype(F32)]
    ppermute x11, waiting for transfers between devices: 37.1 us -> 30.5 us  [shift(): return lax.ppermute(x, axis, [(i, (i + d) % 4) for i in range(4)])]
    unnamed x66 -> x64, local copies, waits for them, and re-layouts: 4.15 us -> 5.5 us
  transfers between devices with their start and end apart: 27 -> 27, of which waited for: 16 -> 14; matrix products, arithmetic and copies ran while one was open for 4% -> 5% of each run, Pallas kernels for 21% -> 22%
where the time goes in v16:
time: 224 us; the launch traced here: 223 us
  waiting for transfers between devices  95.8 us (43%)
  Pallas kernels  56 us (25%)
  starting transfers between devices  51.3 us (23%)
  local copies, waits for them, and re-layouts  13.4 us (6%)
  other arithmetic  5.26 us (2%)
    pallas_call x7, Pallas kernels, call(): pl.pallas_call(kernel, grid_spec=pltpu.PrefetchScalarGridSpec(num_scalar_...  56 us
    all_to_all x2, waiting for transfers between devices, plane_sum(): lax.all_to_all(parts, ('z', 'xl'), 0, 0, tiled=True).astype(F32)  40.2 us
    ppermute x11, waiting for transfers between devices, shift(): return lax.ppermute(x, axis, [(i, (i + d) % 4) for i in range(4)])  30.5 us
    ppermute x11, starting transfers between devices, shift(): return lax.ppermute(x, axis, [(i, (i + d) % 4) for i in range(4)])  13.8 us
    all_to_all x1, waiting for transfers between devices, on_device(): rows = lax.all_to_all(rows, 'y', 0, 0, tiled=True)  13.1 us
    all_to_all x1, starting transfers between devices, on_device(): lax.all_to_all(after(own, products, far_states, far_cotangent, quarters),...  11.1 us
    ppermute x11, starting transfers between devices, swap(): return lax.ppermute(x, axis, SWAP)  9.19 us
    all_to_all x2, starting transfers between devices, plane_sum(): lax.all_to_all(parts, ('z', 'xl'), 0, 0, tiled=True).astype(F32)  8.77 us
  transfers between devices with their start and end apart: 27, of which 14 were waited for; matrix products, arithmetic and copies ran while one was open for 5% of the time, Pallas kernels for 22%

profile of v16, /device:TPU:0, one launch (start us, length us, event | category | flops | bytes accessed | tf_op | source)
XLA Modules:
  0.0 222.8 jit_solution(13398408994657387040)
XLA Ops:
  0.7 3.2 %collective-permute-start.2 = (bf16[256,1024]{1,0:T(8,128)(2,1)}, bf16[256,1024]{1,0:T(8,128)(2,1)S(1)}, u32[]{:S(2)}, u32[]{:S(2)}) collective-permute-start(bf16[256,1024]{1,0:T(8,128)(2,1)} %refs_1_.1), channel_id=1, source_target_pairs={{0,64},{64,0},{1,65},{65,1},{2,66},{66,2},{3,67},{67,3},{4,68},{68... | collective-permute-start | bytes 1572872 | tf_op jit(solution)/shard_map/ppermute | solution.py:301
  7.7 3.2 %collective-permute-start.8 = (bf16[2,256,256]{2,1,0:T(8,128)(2,1)S(1)}, bf16[2,256,256]{2,1,0:T(8,128)(2,1)S(1)}, u32[]{:S(2)}, u32[]{:S(2)}) collective-permute-start(bf16[2,256,256]{2,1,0:T(8,128)(2,1)S(1)} %get-tuple-element.71), channel_id=1, source_target_pairs={{0,6},{2,0},{4,2},{6,4},{1,7},{3,1},{5,3},{7,5},{8,14},{10,8},{12,... | collective-permute-start | bytes 786440 | tf_op jit(solution)/shard_map/ppermute | solution.py:298
  13.2 8.4 %project_near.1.refs_1_ = f32[2,256,1024]{2,1,0:T(8,128)} custom-call(s32[5]{0:T(128)} %stack.59.refs_0_.pos, bf16[256,1024]{1,0:T(8,128)(2,1)} %refs_1_.1, bf16[256,1024]{1,0:T(8,128)(2,1)} %collective-permute-done.refs_2_, bf16[256,1024]{1,0:T(8,128)(2,1)} %refs_3_.1, bf16[256,1024]{1,0:T(8,128)(2,1)} %collective-permute-done.1.refs_4_, ...), custom_call_target="tpu_custom_call" | custom-call | flops 2147483648 | bytes 8388608 | tf_op jit(solution)/shard_map/project_near/pallas_call | solution.py:50
  22.3 3.7 %collective-permute-done.6 = bf16[2,256,256]{2,1,0:T(8,128)(2,1)S(1)} collective-permute-done((bf16[2,256,256]{2,1,0:T(8,128)(2,1)S(1)}, bf16[2,256,256]{2,1,0:T(8,128)(2,1)S(1)}, u32[]{:S(2)}, u32[]{:S(2)}) %collective-permute-start.6) | collective-permute-done | bytes 262176 | tf_op jit(solution)/shard_map/ppermute | solution.py:298
  29.2 11.1 %all-to-all-start.1 = ((bf16[128,2,8,256]{3,2,1,0:T(8,128)(2,1)}), bf16[128,2,8,256]{3,2,1,0:T(8,128)(2,1)S(1)}, u32[]{:S(2)}, u32[]{:S(2)}) async-start(bf16[128,2,8,256]{3,2,1,0:T(8,128)(2,1)} %bitcast.8), calls=%async_computation.1 | async-start | bytes 2097152 | tf_op jit(solution)/shard_map/all_to_all | solution.py:316
  43.9 9.2 %project_far.1 = bf16[4,2,256,256]{3,2,1,0:T(8,128)(2,1)} custom-call(s32[5]{0:T(128)} %stack.59.refs_0_.pos, f32[2,256,1024]{2,1,0:T(8,128)} %project_near.1.refs_1_, bf16[256,1024]{1,0:T(8,128)(2,1)} %copy-done.10, bf16[256,1024]{1,0:T(8,128)(2,1)} %copy-done.12, bf16[256,1024]{1,0:T(8,128)(2,1)} %copy-done.11, bf16[256,1024]{1,0:T(8,128)(2,1)} %copy-done.13, ...), custom_call_target="tpu_custom_call" | custom-call | flops 2147483648 | bytes 8388608 | tf_op jit(solution)/shard_map/project_far/pallas_call | solution.py:50
  53.2 6.3 %all-to-all-done.1 = bf16[128,2,8,256]{3,2,1,0:T(8,128)(2,1)S(1)} async-done(((bf16[128,2,8,256]{3,2,1,0:T(8,128)(2,1)}), bf16[128,2,8,256]{3,2,1,0:T(8,128)(2,1)S(1)}, u32[]{:S(2)}, u32[]{:S(2)}) %all-to-all-start.1) | async-done | bytes 1048608 | tf_op jit(solution)/shard_map/all_to_all | solution.py:316
  59.6 3.5 %all-to-all-start = ((bf16[4,2,256,256]{3,2,1,0:T(8,128)(2,1)}), bf16[4,2,256,256]{3,2,1,0:T(8,128)(2,1)S(1)}, u32[]{:S(2)}, u32[]{:S(2)}) async-start(bf16[4,2,256,256]{3,2,1,0:T(8,128)(2,1)} %project_far.1), calls=%async_computation | async-start | bytes 2097152 | tf_op jit(solution)/shard_map/all_to_all | solution.py:323
  65.0 13.1 %all-to-all-done.rows = bf16[4,2,256,256]{3,2,1,0:T(8,128)(2,1)S(1)} async-done(((bf16[4,2,256,256]{3,2,1,0:T(8,128)(2,1)}), bf16[4,2,256,256]{3,2,1,0:T(8,128)(2,1)S(1)}, u32[]{:S(2)}, u32[]{:S(2)}) %all-to-all-start) | async-done | bytes 1048608 | tf_op jit(solution)/shard_map/all_to_all | solution.py:323
  79.6 10.5 %attention.1 = (bf16[1,256,1024]{2,1,0:T(8,128)(2,1)}, bf16[1,256,1024]{2,1,0:T(8,128)(2,1)}, bf16[1024,256]{1,0:T(8,128)(2,1)}, bf16[1024,256]{1,0:T(8,128)(2,1)}) custom-call(s32[5]{0:T(128)} %stack.59.refs_0_.pos, f32[1,1024]{1,0:T(1,128)} %bitcast.63, bf16[4,2,256,256]{3,2,1,0:T(8,128)(2,1)} %copy-done.9, bf16[1024,256]{1,0:T(8,128)(2,1)} %get-tuple-element.70.k_ref, ...), custom_call_target="tpu_custom_call" | custom-call | flops 8053063680 | bytes 4194304 | tf_op jit(solution)/shard_map/attention/pallas_call | solution.py:50
  92.2 10.6 %collective-permute-done.10.refs_2_ = bf16[1,256,1024]{2,1,0:T(8,128)(2,1)S(1)} collective-permute-done((bf16[1,256,1024]{2,1,0:T(8,128)(2,1)}, bf16[1,256,1024]{2,1,0:T(8,128)(2,1)S(1)}, u32[]{:S(2)}, u32[]{:S(2)}) %collective-permute-start.10) | collective-permute-done | bytes 524320 | tf_op jit(solution)/shard_map/ppermute | solution.py:298
  102.8 2.1 collective-permute-done.9.refs_1_
  110.2 5.6 %column_blocks.1 = (bf16[1024,1024]{1,0:T(8,128)(2,1)}, bf16[1024,1024]{1,0:T(8,128)(2,1)}) custom-call(s32[5]{0:T(128)} %stack.59.refs_0_.pos, bf16[4,2,256,256]{3,2,1,0:T(8,128)(2,1)} %copy-done.2, bf16[4,2,256,256]{3,2,1,0:T(8,128)(2,1)} %copy-done.7, bf16[4,2,256,256]{3,2,1,0:T(8,128)(2,1)} %copy-done.6, bf16[4,2,256,256]{3,2,1,0:T(8,128)(2,1)} %copy-done.8), custom_call_target="tpu_custom_call" | custom-call | bytes 8388608 | tf_op jit(solution)/shard_map/column_blocks/pallas_call | solution.py:50
  116.6 6.6 %output_weight_terms.1 = bf16[8,1024,128]{2,1,0:T(8,128)(2,1)} custom-call(s32[5]{0:T(128)} %stack.59.refs_0_.pos, bf16[1,256,1024]{2,1,0:T(8,128)(2,1)} %get-tuple-element.48.refs_0_, bf16[1,256,1024]{2,1,0:T(8,128)(2,1)} %copy-done.5, bf16[1,256,1024]{2,1,0:T(8,128)(2,1)} %copy-done.4, bf16[1,128,1024]{2,1,0:T(8,128)(2,1)} %copy-done.23, ...), custom_call_target="tpu_custom_call" | custom-call | flops 2147483648 | bytes 6291456 | tf_op jit(solution)/shard_map/output_weight_terms/pallas_call | solution.py:50
  123.3 3.6 %all-to-all-start.2 = ((bf16[8,1024,128]{2,1,0:T(8,128)(2,1)}), bf16[8,1024,128]{2,1,0:T(8,128)(2,1)S(1)}, u32[]{:S(2)}, u32[]{:S(2)}) async-start(bf16[8,1024,128]{2,1,0:T(8,128)(2,1)} %output_weight_terms.1), calls=%async_computation.2 | async-start | bytes 4194304 | tf_op jit(solution)/shard_map/all_to_all | solution.py:343
  126.9 8.3 %output_terms.1 = (bf16[2,256,1024]{2,1,0:T(8,128)(2,1)}, f32[2,256,1024]{2,1,0:T(8,128)}) custom-call(s32[5]{0:T(128)} %stack.59.refs_0_.pos, bf16[1,256,1024]{2,1,0:T(8,128)(2,1)} %get-tuple-element.48.refs_0_, bf16[1,256,1024]{2,1,0:T(8,128)(2,1)} %copy-done.5, bf16[1,256,1024]{2,1,0:T(8,128)(2,1)} %copy-done.4, bf16[1,128,1024]{2,1,0:T(8,128)(2,1)} %copy-done.23, ...), custom_call_target="tpu_custom_call" | custom-call | flops 2147483648 | bytes 8388608 | tf_op jit(solution)/shard_map/output_terms/pallas_call | solution.py:50
  140.4 13.9 %all-to-all-done.2 = bf16[8,1024,128]{2,1,0:T(8,128)(2,1)S(1)} async-done(((bf16[8,1024,128]{2,1,0:T(8,128)(2,1)}), bf16[8,1024,128]{2,1,0:T(8,128)(2,1)S(1)}, u32[]{:S(2)}, u32[]{:S(2)}) %all-to-all-start.2) | async-done | bytes 2097184 | tf_op jit(solution)/shard_map/all_to_all | solution.py:343
  155.4 5.0 %all-to-all-start.3 = ((bf16[128,2,8,256]{3,2,1,0:T(8,128)(2,1)}), bf16[128,2,8,256]{3,2,1,0:T(8,128)(2,1)S(1)}, u32[]{:S(2)}, u32[]{:S(2)}) async-start(bf16[128,2,8,256]{3,2,1,0:T(8,128)(2,1)} %pad_maximum_fusion.1), calls=%async_computation.3 | async-start | bytes 2097152 | tf_op jit(solution)/shard_map/all_to_all | solution.py:371
  160.4 2.5 %collective-permute-start.17 = (bf16[256,1024]{1,0:T(8,128)(2,1)S(1)}, bf16[256,1024]{1,0:T(8,128)(2,1)S(1)}, u32[]{:S(2)}, u32[]{:S(2)}) collective-permute-start(bf16[256,1024]{1,0:T(8,128)(2,1)S(1)} %fusion.2), channel_id=1, source_target_pairs={{0,64},{64,0},{1,65},{65,1},{2,66},{66,2},{3,67},{67,3},{4,68},{68... | collective-permute-start | bytes 1572872 | tf_op jit(solution)/shard_map/ppermute | solution.py:301
  164.1 2.8 %collective-permute-start.21 = (bf16[1,128,1024]{2,1,0:T(8,128)(2,1)S(1)}, bf16[1,128,1024]{2,1,0:T(8,128)(2,1)S(1)}, u32[]{:S(2)}, u32[]{:S(2)}) collective-permute-start(bf16[1,128,1024]{2,1,0:T(8,128)(2,1)S(1)} %slice.40), channel_id=1, source_target_pairs={{0,6},{2,0},{4,2},{6,4},{1,7},{3,1},{5,3},{7,5},{8,14},{10,8},{12,... | collective-permute-start | bytes 786440 | tf_op jit(solution)/shard_map/ppermute | solution.py:298
  167.0 11.6 %collective-permute-done.21.refs_4_ = bf16[1,128,1024]{2,1,0:T(8,128)(2,1)S(1)} collective-permute-done((bf16[1,128,1024]{2,1,0:T(8,128)(2,1)S(1)}, bf16[1,128,1024]{2,1,0:T(8,128)(2,1)S(1)}, u32[]{:S(2)}, u32[]{:S(2)}) %collective-permute-start.21) | collective-permute-done | bytes 262176 | tf_op jit(solution)/shard_map/ppermute | solution.py:298
  181.1 7.3 %query_weight_terms.1 = bf16[1024,1024]{1,0:T(8,128)(2,1)} custom-call(s32[5]{0:T(128)} %stack.59.refs_0_.pos, bf16[1,256,1024]{2,1,0:T(8,128)(2,1)} %get-tuple-element.59.refs_0_, bf16[1,256,1024]{2,1,0:T(8,128)(2,1)} %collective-permute-done.18.refs_1_, bf16[1,256,1024]{2,1,0:T(8,128)(2,1)} %copy-done.24, bf16[1,128,1024]{2,1,0:T(8,128)(2,1)} %copy-done.28, ...), custom_call_target="tpu_custom_call" | custom-call | flops 2147483648 | bytes 6291456 | tf_op jit(solution)/shard_map/query_weight_terms/pallas_call | solution.py:50
  189.3 5.2 %all-to-all-start.4 = ((bf16[8,128,1024]{2,1,0:T(8,128)(2,1)}), bf16[8,128,1024]{2,1,0:T(8,128)(2,1)S(1)}, u32[]{:S(2)}, u32[]{:S(2)}) async-start(bf16[8,128,1024]{2,1,0:T(8,128)(2,1)} %bitcast.51), calls=%async_computation.4 | async-start | bytes 4194304 | tf_op jit(solution)/shard_map/all_to_all | solution.py:343
  195.4 26.3 %all-to-all-done.4 = bf16[8,128,1024]{2,1,0:T(8,128)(2,1)S(1)} async-done(((bf16[8,128,1024]{2,1,0:T(8,128)(2,1)}), bf16[8,128,1024]{2,1,0:T(8,128)(2,1)S(1)}, u32[]{:S(2)}, u32[]{:S(2)}) %all-to-all-start.4) | async-done | bytes 2097184 | tf_op jit(solution)/shard_map/all_to_all | solution.py:343
  (125 shorter events, 38.1 us)
Async XLA Ops:
  0.6 10.2 %collective-permute-start = (bf16[256,1024]{1,0:T(8,128)(2,1)}, bf16[256,1024]{1,0:T(8,128)(2,1)}, u32[]{:S(2)}, u32[]{:S(2)}) collective-permute-start(bf16[256,1024]{1,0:T(8,128)(2,1)} %refs_1_.1), channel_id=1, source_target_pairs={{0,32},{32,0},{1,33},{33,1},{2,34},{34,2},{3,35},{35,3},{4,36},{36... | collective-permute-start | bytes 1572872 | tf_op jit(solution)/shard_map/ppermute | solution.py:301
  0.7 25.2 %collective-permute-start.2 = (bf16[256,1024]{1,0:T(8,128)(2,1)}, bf16[256,1024]{1,0:T(8,128)(2,1)S(1)}, u32[]{:S(2)}, u32[]{:S(2)}) collective-permute-start(bf16[256,1024]{1,0:T(8,128)(2,1)} %refs_1_.1), channel_id=1, source_target_pairs={{0,64},{64,0},{1,65},{65,1},{2,66},{66,2},{3,67},{67,3},{4,68},{68... | collective-permute-start | bytes 1572872 | tf_op jit(solution)/shard_map/ppermute | solution.py:301
  3.9 7.6 %collective-permute-start.1 = (bf16[256,1024]{1,0:T(8,128)(2,1)}, bf16[256,1024]{1,0:T(8,128)(2,1)}, u32[]{:S(2)}, u32[]{:S(2)}) collective-permute-start(bf16[256,1024]{1,0:T(8,128)(2,1)} %refs_3_.1), channel_id=1, source_target_pairs={{0,32},{32,0},{1,33},{33,1},{2,34},{34,2},{3,35},{35,3},{4,36},{36... | collective-permute-start | bytes 1572872 | tf_op jit(solution)/shard_map/ppermute | solution.py:301
  4.1 24.0 %collective-permute-start.4 = (bf16[256,1024]{1,0:T(8,128)(2,1)}, bf16[256,1024]{1,0:T(8,128)(2,1)S(1)}, u32[]{:S(2)}, u32[]{:S(2)}) collective-permute-start(bf16[256,1024]{1,0:T(8,128)(2,1)} %refs_3_.1), channel_id=1, source_target_pairs={{0,64},{64,0},{1,65},{65,1},{2,66},{66,2},{3,67},{67,3},{4,68},{68... | collective-permute-start | bytes 1572872 | tf_op jit(solution)/shard_map/ppermute | solution.py:301
  7.7 14.6 %collective-permute-start.8 = (bf16[2,256,256]{2,1,0:T(8,128)(2,1)S(1)}, bf16[2,256,256]{2,1,0:T(8,128)(2,1)S(1)}, u32[]{:S(2)}, u32[]{:S(2)}) collective-permute-start(bf16[2,256,256]{2,1,0:T(8,128)(2,1)S(1)} %get-tuple-element.71), channel_id=1, source_target_pairs={{0,6},{2,0},{4,2},{6,4},{1,7},{3,1},{5,3},{7,5},{8,14},{10,8},{12,... | collective-permute-start | bytes 786440 | tf_op jit(solution)/shard_map/ppermute | solution.py:298
  10.8 11.4 %collective-permute-start.7 = (bf16[2,256,256]{2,1,0:T(8,128)(2,1)S(1)}, bf16[2,256,256]{2,1,0:T(8,128)(2,1)S(1)}, u32[]{:S(2)}, u32[]{:S(2)}) collective-permute-start(bf16[2,256,256]{2,1,0:T(8,128)(2,1)S(1)} %get-tuple-element.72), channel_id=1, source_target_pairs={{0,4},{2,6},{4,0},{6,2},{1,5},{3,7},{5,1},{7,3},{8,12},{10,14},{12... | collective-permute-start | bytes 786440 | tf_op jit(solution)/shard_map/ppermute | solution.py:298
  11.5 14.5 %collective-permute-start.6 = (bf16[2,256,256]{2,1,0:T(8,128)(2,1)S(1)}, bf16[2,256,256]{2,1,0:T(8,128)(2,1)S(1)}, u32[]{:S(2)}, u32[]{:S(2)}) collective-permute-start(bf16[2,256,256]{2,1,0:T(8,128)(2,1)S(1)} %get-tuple-element.73), channel_id=1, source_target_pairs={{0,2},{2,4},{4,6},{6,0},{1,3},{3,5},{5,7},{7,1},{8,10},{10,12},{12... | collective-permute-start | bytes 786440 | tf_op jit(solution)/shard_map/ppermute | solution.py:298
  29.2 30.4 %all-to-all-start.1 = ((bf16[128,2,8,256]{3,2,1,0:T(8,128)(2,1)}), bf16[128,2,8,256]{3,2,1,0:T(8,128)(2,1)S(1)}, u32[]{:S(2)}, u32[]{:S(2)}) async-start(bf16[128,2,8,256]{3,2,1,0:T(8,128)(2,1)} %bitcast.8), calls=%async_computation.1 | async-start | bytes 2097152 | tf_op jit(solution)/shard_map/all_to_all | solution.py:316
  59.6 18.5 %all-to-all-start = ((bf16[4,2,256,256]{3,2,1,0:T(8,128)(2,1)}), bf16[4,2,256,256]{3,2,1,0:T(8,128)(2,1)S(1)}, u32[]{:S(2)}, u32[]{:S(2)}) async-start(bf16[4,2,256,256]{3,2,1,0:T(8,128)(2,1)} %project_far.1), calls=%async_computation | async-start | bytes 2097152 | tf_op jit(solution)/shard_map/all_to_all | solution.py:323
  78.2 26.7 %collective-permute-start.11 = (bf16[4,2,256,256]{3,2,1,0:T(8,128)(2,1)S(1)}, bf16[4,2,256,256]{3,2,1,0:T(8,128)(2,1)S(1)}, u32[]{:S(2)}, u32[]{:S(2)}) collective-permute-start(bf16[4,2,256,256]{3,2,1,0:T(8,128)(2,1)S(1)} %pad_maximum_fusion.p0), channel_id=1, source_target_pairs={{0,64},{64,0},{1,65},{65,1},{2,66},{66,2},{3,67},{67,3},{4,68},{68... | collective-permute-start | bytes 3145736 | tf_op jit(solution)/shard_map/ppermute | solution.py:301
  90.2 12.6 %collective-permute-start.10 = (bf16[1,256,1024]{2,1,0:T(8,128)(2,1)}, bf16[1,256,1024]{2,1,0:T(8,128)(2,1)S(1)}, u32[]{:S(2)}, u32[]{:S(2)}) collective-permute-start(bf16[1,256,1024]{2,1,0:T(8,128)(2,1)} %get-tuple-element.48.refs_0_), channel_id=1, source_target_pairs={{0,6},{2,0},{4,2},{6,4},{1,7},{3,1},{5,3},{7,5},{8,14},{10,8},{12,... | collective-permute-start | bytes 1572872 | tf_op jit(solution)/shard_map/ppermute | solution.py:298
  91.3 13.5 %collective-permute-start.9 = (bf16[1,256,1024]{2,1,0:T(8,128)(2,1)}, bf16[1,256,1024]{2,1,0:T(8,128)(2,1)S(1)}, u32[]{:S(2)}, u32[]{:S(2)}) collective-permute-start(bf16[1,256,1024]{2,1,0:T(8,128)(2,1)} %get-tuple-element.48.refs_0_), channel_id=1, source_target_pairs={{0,2},{2,4},{4,6},{6,0},{1,3},{3,5},{5,7},{7,1},{8,10},{10,12},{12... | collective-permute-start | bytes 1572872 | tf_op jit(solution)/shard_map/ppermute | solution.py:298
  105.0 4.1 %collective-permute-start.15 = (bf16[4,2,256,256]{3,2,1,0:T(8,128)(2,1)S(1)}, bf16[4,2,256,256]{3,2,1,0:T(8,128)(2,1)S(1)}, u32[]{:S(2)}, u32[]{:S(2)}) collective-permute-start(bf16[4,2,256,256]{3,2,1,0:T(8,128)(2,1)S(1)} %collective-permute-done.11.p2), channel_id=1, source_target_pairs={{0,32},{32,0},{1,33},{33,1},{2,34},{34,2},{3,35},{35,3},{4,36},{36... | collective-permute-start | bytes 3145736 | tf_op jit(solution)/shard_map/ppermute | solution.py:301
  105.5 10.3 %collective-permute-start.13 = (bf16[1,128,1024]{2,1,0:T(8,128)(2,1)S(1)}, bf16[1,128,1024]{2,1,0:T(8,128)(2,1)S(1)}, u32[]{:S(2)}, u32[]{:S(2)}) collective-permute-start(bf16[1,128,1024]{2,1,0:T(8,128)(2,1)S(1)} %slice.36), channel_id=1, source_target_pairs={{0,6},{2,0},{4,2},{6,4},{1,7},{3,1},{5,3},{7,5},{8,14},{10,8},{12,... | collective-permute-start | bytes 786440 | tf_op jit(solution)/shard_map/ppermute | solution.py:298
  105.9 9.9 %collective-permute-start.12 = (bf16[1,128,1024]{2,1,0:T(8,128)(2,1)S(1)}, bf16[1,128,1024]{2,1,0:T(8,128)(2,1)S(1)}, u32[]{:S(2)}, u32[]{:S(2)}) collective-permute-start(bf16[1,128,1024]{2,1,0:T(8,128)(2,1)S(1)} %slice.35), channel_id=1, source_target_pairs={{0,2},{2,4},{4,6},{6,0},{1,3},{3,5},{5,7},{7,1},{8,10},{10,12},{12... | collective-permute-start | bytes 786440 | tf_op jit(solution)/shard_map/ppermute | solution.py:298
  123.3 31.1 %all-to-all-start.2 = ((bf16[8,1024,128]{2,1,0:T(8,128)(2,1)}), bf16[8,1024,128]{2,1,0:T(8,128)(2,1)S(1)}, u32[]{:S(2)}, u32[]{:S(2)}) async-start(bf16[8,1024,128]{2,1,0:T(8,128)(2,1)} %output_weight_terms.1), calls=%async_computation.2 | async-start | bytes 4194304 | tf_op jit(solution)/shard_map/all_to_all | solution.py:343
  135.2 3.3 %collective-permute-start.16 = (bf16[2,256,1024]{2,1,0:T(8,128)(2,1)}, bf16[2,256,1024]{2,1,0:T(8,128)(2,1)S(1)}, u32[]{:S(2)}, u32[]{:S(2)}) collective-permute-start(bf16[2,256,1024]{2,1,0:T(8,128)(2,1)} %get-tuple-element.54), channel_id=1, source_target_pairs={{0,32},{32,0},{1,33},{33,1},{2,34},{34,2},{3,35},{35,3},{4,36},{36... | collective-permute-start | bytes 3145736 | tf_op jit(solution)/shard_map/ppermute | solution.py:301
  136.5 26.5 %collective-permute-start.19 = (bf16[1,256,1024]{2,1,0:T(8,128)(2,1)}, bf16[1,256,1024]{2,1,0:T(8,128)(2,1)S(1)}, u32[]{:S(2)}, u32[]{:S(2)}) collective-permute-start(bf16[1,256,1024]{2,1,0:T(8,128)(2,1)} %get-tuple-element.59.refs_0_), channel_id=1, source_target_pairs={{0,6},{2,0},{4,2},{6,4},{1,7},{3,1},{5,3},{7,5},{8,14},{10,8},{12,... | collective-permute-start | bytes 1572872 | tf_op jit(solution)/shard_map/ppermute | solution.py:298
  137.4 25.6 %collective-permute-start.18 = (bf16[1,256,1024]{2,1,0:T(8,128)(2,1)}, bf16[1,256,1024]{2,1,0:T(8,128)(2,1)}, u32[]{:S(2)}, u32[]{:S(2)}) collective-permute-start(bf16[1,256,1024]{2,1,0:T(8,128)(2,1)} %get-tuple-element.59.refs_0_), channel_id=1, source_target_pairs={{0,2},{2,4},{4,6},{6,0},{1,3},{3,5},{5,7},{7,1},{8,10},{10,12},{12... | collective-permute-start | bytes 1572872 | tf_op jit(solution)/shard_map/ppermute | solution.py:298
  155.4 33.9 %all-to-all-start.3 = ((bf16[128,2,8,256]{3,2,1,0:T(8,128)(2,1)}), bf16[128,2,8,256]{3,2,1,0:T(8,128)(2,1)S(1)}, u32[]{:S(2)}, u32[]{:S(2)}) async-start(bf16[128,2,8,256]{3,2,1,0:T(8,128)(2,1)} %pad_maximum_fusion.1), calls=%async_computation.3 | async-start | bytes 2097152 | tf_op jit(solution)/shard_map/all_to_all | solution.py:371
  160.4 28.0 %collective-permute-start.17 = (bf16[256,1024]{1,0:T(8,128)(2,1)S(1)}, bf16[256,1024]{1,0:T(8,128)(2,1)S(1)}, u32[]{:S(2)}, u32[]{:S(2)}) collective-permute-start(bf16[256,1024]{1,0:T(8,128)(2,1)S(1)} %fusion.2), channel_id=1, source_target_pairs={{0,64},{64,0},{1,65},{65,1},{2,66},{66,2},{3,67},{67,3},{4,68},{68... | collective-permute-start | bytes 1572872 | tf_op jit(solution)/shard_map/ppermute | solution.py:301
  164.1 14.4 %collective-permute-start.21 = (bf16[1,128,1024]{2,1,0:T(8,128)(2,1)S(1)}, bf16[1,128,1024]{2,1,0:T(8,128)(2,1)S(1)}, u32[]{:S(2)}, u32[]{:S(2)}) collective-permute-start(bf16[1,128,1024]{2,1,0:T(8,128)(2,1)S(1)} %slice.40), channel_id=1, source_target_pairs={{0,6},{2,0},{4,2},{6,4},{1,7},{3,1},{5,3},{7,5},{8,14},{10,8},{12,... | collective-permute-start | bytes 786440 | tf_op jit(solution)/shard_map/ppermute | solution.py:298
  167.0 13.4 %collective-permute-start.20 = (bf16[1,128,1024]{2,1,0:T(8,128)(2,1)S(1)}, bf16[1,128,1024]{2,1,0:T(8,128)(2,1)S(1)}, u32[]{:S(2)}, u32[]{:S(2)}) collective-permute-start(bf16[1,128,1024]{2,1,0:T(8,128)(2,1)S(1)} %slice.39), channel_id=1, source_target_pairs={{0,2},{2,4},{4,6},{6,0},{1,3},{3,5},{5,7},{7,1},{8,10},{10,12},{12... | collective-permute-start | bytes 786440 | tf_op jit(solution)/shard_map/ppermute | solution.py:298
  189.3 32.3 %all-to-all-start.4 = ((bf16[8,128,1024]{2,1,0:T(8,128)(2,1)}), bf16[8,128,1024]{2,1,0:T(8,128)(2,1)S(1)}, u32[]{:S(2)}, u32[]{:S(2)}) async-start(bf16[8,128,1024]{2,1,0:T(8,128)(2,1)} %bitcast.51), calls=%async_computation.4 | async-start | bytes 4194304 | tf_op jit(solution)/shard_map/all_to_all | solution.py:343
  (34 other events, 283.4 us)

commit v17 on v16

--- a/solution.py
+++ b/solution.py
@@ -353,7 +353,7 @@
     every_grad = ring(after(query_grad, every_out), output_parts)
     output_weight_grad = plane_sum(output_parts)
 
-    give, keep = output_terms(pos, after(every_out, output_parts), output_weight)
+    give, keep = output_terms(pos, after(every_out, output_parts, *every_grad[:3]), output_weight)
     pair = keep + swap(give, "core").astype(F32)
     pair_far = pair[1].astype(BF16)
     attended = (pair[0] + swap(pair_far, "xh").astype(F32)).astype(BF16)

time: 224 us -> 231 us (1.031)
  starting transfers between devices: 51.3 us -> 57.4 us
    ppermute x11, starting transfers between devices: 13.8 us -> 19.1 us  [shift(): return lax.ppermute(x, axis, [(i, (i + d) % 4) for i in range(4)])]
    unnamed x64 -> x62, local copies, waits for them, and re-layouts: 5.5 us -> 5.77 us
  transfers between devices with their start and end apart: 27 -> 27, of which waited for: 14 -> 12; matrix products, arithmetic and copies ran while one was open for 5% -> 5% of each run, Pallas kernels for 22% -> 24%
where the time goes in v17:
time: 231 us; the launch traced here: 230 us
  waiting for transfers between devices  96 us (42%)
  starting transfers between devices  57.4 us (25%)
  Pallas kernels  56 us (24%)
  local copies, waits for them, and re-layouts  14.3 us (6%)
  other arithmetic  5.26 us (2%)
    pallas_call x7, Pallas kernels, call(): pl.pallas_call(kernel, grid_spec=pltpu.PrefetchScalarGridSpec(num_scalar_...  56 us
    all_to_all x2, waiting for transfers between devices, plane_sum(): lax.all_to_all(parts, ('z', 'xl'), 0, 0, tiled=True).astype(F32)  38.7 us
    ppermute x11, waiting for transfers between devices, shift(): return lax.ppermute(x, axis, [(i, (i + d) % 4) for i in range(4)])  30.1 us
    ppermute x11, starting transfers between devices, shift(): return lax.ppermute(x, axis, [(i, (i + d) % 4) for i in range(4)])  19.1 us
    all_to_all x1, waiting for transfers between devices, on_device(): rows = lax.all_to_all(rows, 'y', 0, 0, tiled=True)  13.1 us
    all_to_all x1, starting transfers between devices, on_device(): lax.all_to_all(after(own, products, far_states, far_cotangent, quarters),...  11.1 us
    ppermute x11, starting transfers between devices, swap(): return lax.ppermute(x, axis, SWAP)  9.28 us
    all_to_all x2, starting transfers between devices, plane_sum(): lax.all_to_all(parts, ('z', 'xl'), 0, 0, tiled=True).astype(F32)  9.15 us
  transfers between devices with their start and end apart: 27, of which 12 were waited for; matrix products, arithmetic and copies ran while one was open for 5% of the time, Pallas kernels for 24%

profile of v17, /device:TPU:0, one launch (start us, length us, event | category | flops | bytes accessed | tf_op | source)
XLA Modules:
  0.0 230.1 jit_solution(3168847901413869414)
XLA Ops:
  0.7 3.2 %collective-permute-start.2 = (bf16[256,1024]{1,0:T(8,128)(2,1)}, bf16[256,1024]{1,0:T(8,128)(2,1)S(1)}, u32[]{:S(2)}, u32[]{:S(2)}) collective-permute-start(bf16[256,1024]{1,0:T(8,128)(2,1)} %refs_1_.1), channel_id=1, source_target_pairs={{0,64},{64,0},{1,65},{65,1},{2,66},{66,2},{3,67},{67,3},{4,68},{68... | collective-permute-start | bytes 1572872 | tf_op jit(solution)/shard_map/ppermute | solution.py:301
  9.4 2.9 %collective-permute-start.7 = (bf16[2,256,256]{2,1,0:T(8,128)(2,1)S(1)}, bf16[2,256,256]{2,1,0:T(8,128)(2,1)S(1)}, u32[]{:S(2)}, u32[]{:S(2)}) collective-permute-start(bf16[2,256,256]{2,1,0:T(8,128)(2,1)S(1)} %get-tuple-element.72), channel_id=1, source_target_pairs={{0,4},{2,6},{4,0},{6,2},{1,5},{3,7},{5,1},{7,3},{8,12},{10,14},{12... | collective-permute-start | bytes 786440 | tf_op jit(solution)/shard_map/ppermute | solution.py:298
  14.3 8.4 %project_near.1.refs_1_ = f32[2,256,1024]{2,1,0:T(8,128)} custom-call(s32[5]{0:T(128)} %stack.59.refs_0_.pos, bf16[256,1024]{1,0:T(8,128)(2,1)} %refs_1_.1, bf16[256,1024]{1,0:T(8,128)(2,1)} %collective-permute-done.refs_2_, bf16[256,1024]{1,0:T(8,128)(2,1)} %refs_3_.1, bf16[256,1024]{1,0:T(8,128)(2,1)} %collective-permute-done.1.refs_4_, ...), custom_call_target="tpu_custom_call" | custom-call | flops 2147483648 | bytes 8388608 | tf_op jit(solution)/shard_map/project_near/pallas_call | solution.py:50
  24.2 3.8 %collective-permute-done.4.refs_4_ = bf16[256,1024]{1,0:T(8,128)(2,1)S(1)} collective-permute-done((bf16[256,1024]{1,0:T(8,128)(2,1)}, bf16[256,1024]{1,0:T(8,128)(2,1)S(1)}, u32[]{:S(2)}, u32[]{:S(2)}) %collective-permute-start.4) | collective-permute-done | bytes 524320 | tf_op jit(solution)/shard_map/ppermute | solution.py:301
  29.2 11.1 %all-to-all-start.1 = ((bf16[128,2,8,256]{3,2,1,0:T(8,128)(2,1)}), bf16[128,2,8,256]{3,2,1,0:T(8,128)(2,1)S(1)}, u32[]{:S(2)}, u32[]{:S(2)}) async-start(bf16[128,2,8,256]{3,2,1,0:T(8,128)(2,1)} %bitcast.8), calls=%async_computation.1 | async-start | bytes 2097152 | tf_op jit(solution)/shard_map/all_to_all | solution.py:316
  43.9 9.2 %project_far.1 = bf16[4,2,256,256]{3,2,1,0:T(8,128)(2,1)} custom-call(s32[5]{0:T(128)} %stack.59.refs_0_.pos, f32[2,256,1024]{2,1,0:T(8,128)} %project_near.1.refs_1_, bf16[256,1024]{1,0:T(8,128)(2,1)} %copy-done.10, bf16[256,1024]{1,0:T(8,128)(2,1)} %copy-done.12, bf16[256,1024]{1,0:T(8,128)(2,1)} %copy-done.11, bf16[256,1024]{1,0:T(8,128)(2,1)} %copy-done.13, ...), custom_call_target="tpu_custom_call" | custom-call | flops 2147483648 | bytes 8388608 | tf_op jit(solution)/shard_map/project_far/pallas_call | solution.py:50
  53.2 6.3 %all-to-all-done.1 = bf16[128,2,8,256]{3,2,1,0:T(8,128)(2,1)S(1)} async-done(((bf16[128,2,8,256]{3,2,1,0:T(8,128)(2,1)}), bf16[128,2,8,256]{3,2,1,0:T(8,128)(2,1)S(1)}, u32[]{:S(2)}, u32[]{:S(2)}) %all-to-all-start.1) | async-done | bytes 1048608 | tf_op jit(solution)/shard_map/all_to_all | solution.py:316
  59.6 3.5 %all-to-all-start = ((bf16[4,2,256,256]{3,2,1,0:T(8,128)(2,1)}), bf16[4,2,256,256]{3,2,1,0:T(8,128)(2,1)S(1)}, u32[]{:S(2)}, u32[]{:S(2)}) async-start(bf16[4,2,256,256]{3,2,1,0:T(8,128)(2,1)} %project_far.1), calls=%async_computation | async-start | bytes 2097152 | tf_op jit(solution)/shard_map/all_to_all | solution.py:323
  65.0 13.1 %all-to-all-done.rows = bf16[4,2,256,256]{3,2,1,0:T(8,128)(2,1)S(1)} async-done(((bf16[4,2,256,256]{3,2,1,0:T(8,128)(2,1)}), bf16[4,2,256,256]{3,2,1,0:T(8,128)(2,1)S(1)}, u32[]{:S(2)}, u32[]{:S(2)}) %all-to-all-start) | async-done | bytes 1048608 | tf_op jit(solution)/shard_map/all_to_all | solution.py:323
  79.6 10.5 %attention.1 = (bf16[1,256,1024]{2,1,0:T(8,128)(2,1)}, bf16[1,256,1024]{2,1,0:T(8,128)(2,1)}, bf16[1024,256]{1,0:T(8,128)(2,1)}, bf16[1024,256]{1,0:T(8,128)(2,1)}) custom-call(s32[5]{0:T(128)} %stack.59.refs_0_.pos, f32[1,1024]{1,0:T(1,128)} %bitcast.63, bf16[4,2,256,256]{3,2,1,0:T(8,128)(2,1)} %copy-done.9, bf16[1024,256]{1,0:T(8,128)(2,1)} %get-tuple-element.70.k_ref, ...), custom_call_target="tpu_custom_call" | custom-call | flops 8053063680 | bytes 4194304 | tf_op jit(solution)/shard_map/attention/pallas_call | solution.py:50
  90.8 2.7 %collective-permute-start.10 = (bf16[1,256,1024]{2,1,0:T(8,128)(2,1)}, bf16[1,256,1024]{2,1,0:T(8,128)(2,1)S(1)}, u32[]{:S(2)}, u32[]{:S(2)}) collective-permute-start(bf16[1,256,1024]{2,1,0:T(8,128)(2,1)} %get-tuple-element.52.refs_0_), channel_id=1, source_target_pairs={{0,6},{2,0},{4,2},{6,4},{1,7},{3,1},{5,3},{7,5},{8,14},{10,8},{12,... | collective-permute-start | bytes 1572872 | tf_op jit(solution)/shard_map/ppermute | solution.py:298
  93.4 10.6 %collective-permute-done.9.refs_1_ = bf16[1,256,1024]{2,1,0:T(8,128)(2,1)S(1)} collective-permute-done((bf16[1,256,1024]{2,1,0:T(8,128)(2,1)}, bf16[1,256,1024]{2,1,0:T(8,128)(2,1)S(1)}, u32[]{:S(2)}, u32[]{:S(2)}) %collective-permute-start.9) | collective-permute-done | bytes 524320 | tf_op jit(solution)/shard_map/ppermute | solution.py:298
  104.8 3.2 %collective-permute-start.13 = (bf16[1,128,1024]{2,1,0:T(8,128)(2,1)S(1)}, bf16[1,128,1024]{2,1,0:T(8,128)(2,1)S(1)}, u32[]{:S(2)}, u32[]{:S(2)}) collective-permute-start(bf16[1,128,1024]{2,1,0:T(8,128)(2,1)S(1)} %slice.36), channel_id=1, source_target_pairs={{0,6},{2,0},{4,2},{6,4},{1,7},{3,1},{5,3},{7,5},{8,14},{10,8},{12,... | collective-permute-start | bytes 786440 | tf_op jit(solution)/shard_map/ppermute | solution.py:298
  108.0 6.3 %collective-permute-done.12.refs_3_ = bf16[1,128,1024]{2,1,0:T(8,128)(2,1)S(1)} collective-permute-done((bf16[1,128,1024]{2,1,0:T(8,128)(2,1)S(1)}, bf16[1,128,1024]{2,1,0:T(8,128)(2,1)S(1)}, u32[]{:S(2)}, u32[]{:S(2)}) %collective-permute-start.12) | collective-permute-done | bytes 262176 | tf_op jit(solution)/shard_map/ppermute | solution.py:298
  119.6 5.6 %column_blocks.1 = (bf16[1024,1024]{1,0:T(8,128)(2,1)}, bf16[1024,1024]{1,0:T(8,128)(2,1)}) custom-call(s32[5]{0:T(128)} %stack.59.refs_0_.pos, bf16[4,2,256,256]{3,2,1,0:T(8,128)(2,1)} %copy-done.2, bf16[4,2,256,256]{3,2,1,0:T(8,128)(2,1)} %copy-done.7, bf16[4,2,256,256]{3,2,1,0:T(8,128)(2,1)} %copy-done.6, bf16[4,2,256,256]{3,2,1,0:T(8,128)(2,1)} %copy-done.8), custom_call_target="tpu_custom_call" | custom-call | bytes 8388608 | tf_op jit(solution)/shard_map/column_blocks/pallas_call | solution.py:50
  125.2 6.6 %output_weight_terms.1 = bf16[8,1024,128]{2,1,0:T(8,128)(2,1)} custom-call(s32[5]{0:T(128)} %stack.59.refs_0_.pos, bf16[1,256,1024]{2,1,0:T(8,128)(2,1)} %get-tuple-element.52.refs_0_, bf16[1,256,1024]{2,1,0:T(8,128)(2,1)} %copy-done.4, bf16[1,256,1024]{2,1,0:T(8,128)(2,1)} %copy-done.5, bf16[1,128,1024]{2,1,0:T(8,128)(2,1)} %copy-done.22, ...), custom_call_target="tpu_custom_call" | custom-call | flops 2147483648 | bytes 6291456 | tf_op jit(solution)/shard_map/output_weight_terms/pallas_call | solution.py:50
  131.8 3.6 %all-to-all-start.2 = ((bf16[8,1024,128]{2,1,0:T(8,128)(2,1)}), bf16[8,1024,128]{2,1,0:T(8,128)(2,1)S(1)}, u32[]{:S(2)}, u32[]{:S(2)}) async-start(bf16[8,1024,128]{2,1,0:T(8,128)(2,1)} %output_weight_terms.1), calls=%async_computation.2 | async-start | bytes 4194304 | tf_op jit(solution)/shard_map/all_to_all | solution.py:343
  135.5 8.3 %output_terms.1 = (bf16[2,256,1024]{2,1,0:T(8,128)(2,1)}, f32[2,256,1024]{2,1,0:T(8,128)}) custom-call(s32[5]{0:T(128)} %stack.59.refs_0_.pos, bf16[1,256,1024]{2,1,0:T(8,128)(2,1)} %get-tuple-element.52.refs_0_, bf16[1,256,1024]{2,1,0:T(8,128)(2,1)} %copy-done.4, bf16[1,256,1024]{2,1,0:T(8,128)(2,1)} %copy-done.5, bf16[1,128,1024]{2,1,0:T(8,128)(2,1)} %copy-done.22, ...), custom_call_target="tpu_custom_call" | custom-call | flops 2147483648 | bytes 8388608 | tf_op jit(solution)/shard_map/output_terms/pallas_call | solution.py:50
  148.9 12.6 %all-to-all-done.2 = bf16[8,1024,128]{2,1,0:T(8,128)(2,1)S(1)} async-done(((bf16[8,1024,128]{2,1,0:T(8,128)(2,1)}), bf16[8,1024,128]{2,1,0:T(8,128)(2,1)S(1)}, u32[]{:S(2)}, u32[]{:S(2)}) %all-to-all-start.2) | async-done | bytes 2097184 | tf_op jit(solution)/shard_map/all_to_all | solution.py:343
  162.6 5.2 %all-to-all-start.3 = ((bf16[128,2,8,256]{3,2,1,0:T(8,128)(2,1)}), bf16[128,2,8,256]{3,2,1,0:T(8,128)(2,1)S(1)}, u32[]{:S(2)}, u32[]{:S(2)}) async-start(bf16[128,2,8,256]{3,2,1,0:T(8,128)(2,1)} %pad_maximum_fusion.1), calls=%async_computation.3 | async-start | bytes 2097152 | tf_op jit(solution)/shard_map/all_to_all | solution.py:371
  175.6 11.8 %collective-permute-done.20.refs_3_ = bf16[1,128,1024]{2,1,0:T(8,128)(2,1)S(1)} collective-permute-done((bf16[1,128,1024]{2,1,0:T(8,128)(2,1)S(1)}, bf16[1,128,1024]{2,1,0:T(8,128)(2,1)S(1)}, u32[]{:S(2)}, u32[]{:S(2)}) %collective-permute-start.20) | collective-permute-done | bytes 262176 | tf_op jit(solution)/shard_map/ppermute | solution.py:298
  188.2 7.3 %query_weight_terms.1 = bf16[1024,1024]{1,0:T(8,128)(2,1)} custom-call(s32[5]{0:T(128)} %stack.59.refs_0_.pos, bf16[1,256,1024]{2,1,0:T(8,128)(2,1)} %get-tuple-element.59.refs_0_, bf16[1,256,1024]{2,1,0:T(8,128)(2,1)} %collective-permute-done.16.refs_1_, bf16[1,256,1024]{2,1,0:T(8,128)(2,1)} %collective-permute-done.17.refs_2_, ...), custom_call_target="tpu_custom_call" | custom-call | flops 2147483648 | bytes 6291456 | tf_op jit(solution)/shard_map/query_weight_terms/pallas_call | solution.py:50
  196.4 5.5 %all-to-all-start.4 = ((bf16[8,128,1024]{2,1,0:T(8,128)(2,1)}), bf16[8,128,1024]{2,1,0:T(8,128)(2,1)S(1)}, u32[]{:S(2)}, u32[]{:S(2)}) async-start(bf16[8,128,1024]{2,1,0:T(8,128)(2,1)} %bitcast.51), calls=%async_computation.4 | async-start | bytes 4194304 | tf_op jit(solution)/shard_map/all_to_all | solution.py:343
  202.9 26.1 %all-to-all-done.4 = bf16[8,128,1024]{2,1,0:T(8,128)(2,1)S(1)} async-done(((bf16[8,128,1024]{2,1,0:T(8,128)(2,1)}), bf16[8,128,1024]{2,1,0:T(8,128)(2,1)S(1)}, u32[]{:S(2)}, u32[]{:S(2)}) %all-to-all-start.4) | async-done | bytes 2097184 | tf_op jit(solution)/shard_map/all_to_all | solution.py:343
  (123 shorter events, 41.5 us)
Async XLA Ops:
  0.6 8.8 %collective-permute-start = (bf16[256,1024]{1,0:T(8,128)(2,1)}, bf16[256,1024]{1,0:T(8,128)(2,1)}, u32[]{:S(2)}, u32[]{:S(2)}) collective-permute-start(bf16[256,1024]{1,0:T(8,128)(2,1)} %refs_1_.1), channel_id=1, source_target_pairs={{0,32},{32,0},{1,33},{33,1},{2,34},{34,2},{3,35},{35,3},{4,36},{36... | collective-permute-start | bytes 1572872 | tf_op jit(solution)/shard_map/ppermute | solution.py:301
  0.7 23.5 %collective-permute-start.2 = (bf16[256,1024]{1,0:T(8,128)(2,1)}, bf16[256,1024]{1,0:T(8,128)(2,1)S(1)}, u32[]{:S(2)}, u32[]{:S(2)}) collective-permute-start(bf16[256,1024]{1,0:T(8,128)(2,1)} %refs_1_.1), channel_id=1, source_target_pairs={{0,64},{64,0},{1,65},{65,1},{2,66},{66,2},{3,67},{67,3},{4,68},{68... | collective-permute-start | bytes 1572872 | tf_op jit(solution)/shard_map/ppermute | solution.py:301
  3.9 8.4 %collective-permute-start.1 = (bf16[256,1024]{1,0:T(8,128)(2,1)}, bf16[256,1024]{1,0:T(8,128)(2,1)}, u32[]{:S(2)}, u32[]{:S(2)}) collective-permute-start(bf16[256,1024]{1,0:T(8,128)(2,1)} %refs_3_.1), channel_id=1, source_target_pairs={{0,32},{32,0},{1,33},{33,1},{2,34},{34,2},{3,35},{35,3},{4,36},{36... | collective-permute-start | bytes 1572872 | tf_op jit(solution)/shard_map/ppermute | solution.py:301
  4.1 24.0 %collective-permute-start.4 = (bf16[256,1024]{1,0:T(8,128)(2,1)}, bf16[256,1024]{1,0:T(8,128)(2,1)S(1)}, u32[]{:S(2)}, u32[]{:S(2)}) collective-permute-start(bf16[256,1024]{1,0:T(8,128)(2,1)} %refs_3_.1), channel_id=1, source_target_pairs={{0,64},{64,0},{1,65},{65,1},{2,66},{66,2},{3,67},{67,3},{4,68},{68... | collective-permute-start | bytes 1572872 | tf_op jit(solution)/shard_map/ppermute | solution.py:301
  7.7 15.0 %collective-permute-start.6 = (bf16[2,256,256]{2,1,0:T(8,128)(2,1)S(1)}, bf16[2,256,256]{2,1,0:T(8,128)(2,1)S(1)}, u32[]{:S(2)}, u32[]{:S(2)}) collective-permute-start(bf16[2,256,256]{2,1,0:T(8,128)(2,1)S(1)} %get-tuple-element.73), channel_id=1, source_target_pairs={{0,2},{2,4},{4,6},{6,0},{1,3},{3,5},{5,7},{7,1},{8,10},{10,12},{12... | collective-permute-start | bytes 786440 | tf_op jit(solution)/shard_map/ppermute | solution.py:298
  9.4 14.8 %collective-permute-start.7 = (bf16[2,256,256]{2,1,0:T(8,128)(2,1)S(1)}, bf16[2,256,256]{2,1,0:T(8,128)(2,1)S(1)}, u32[]{:S(2)}, u32[]{:S(2)}) collective-permute-start(bf16[2,256,256]{2,1,0:T(8,128)(2,1)S(1)} %get-tuple-element.72), channel_id=1, source_target_pairs={{0,4},{2,6},{4,0},{6,2},{1,5},{3,7},{5,1},{7,3},{8,12},{10,14},{12... | collective-permute-start | bytes 786440 | tf_op jit(solution)/shard_map/ppermute | solution.py:298
  12.3 11.9 %collective-permute-start.8 = (bf16[2,256,256]{2,1,0:T(8,128)(2,1)S(1)}, bf16[2,256,256]{2,1,0:T(8,128)(2,1)S(1)}, u32[]{:S(2)}, u32[]{:S(2)}) collective-permute-start(bf16[2,256,256]{2,1,0:T(8,128)(2,1)S(1)} %get-tuple-element.71), channel_id=1, source_target_pairs={{0,6},{2,0},{4,2},{6,4},{1,7},{3,1},{5,3},{7,5},{8,14},{10,8},{12,... | collective-permute-start | bytes 786440 | tf_op jit(solution)/shard_map/ppermute | solution.py:298
  29.2 30.4 %all-to-all-start.1 = ((bf16[128,2,8,256]{3,2,1,0:T(8,128)(2,1)}), bf16[128,2,8,256]{3,2,1,0:T(8,128)(2,1)S(1)}, u32[]{:S(2)}, u32[]{:S(2)}) async-start(bf16[128,2,8,256]{3,2,1,0:T(8,128)(2,1)} %bitcast.8), calls=%async_computation.1 | async-start | bytes 2097152 | tf_op jit(solution)/shard_map/all_to_all | solution.py:316
  59.6 18.5 %all-to-all-start = ((bf16[4,2,256,256]{3,2,1,0:T(8,128)(2,1)}), bf16[4,2,256,256]{3,2,1,0:T(8,128)(2,1)S(1)}, u32[]{:S(2)}, u32[]{:S(2)}) async-start(bf16[4,2,256,256]{3,2,1,0:T(8,128)(2,1)} %project_far.1), calls=%async_computation | async-start | bytes 2097152 | tf_op jit(solution)/shard_map/all_to_all | solution.py:323
  78.2 25.8 %collective-permute-start.11 = (bf16[4,2,256,256]{3,2,1,0:T(8,128)(2,1)S(1)}, bf16[4,2,256,256]{3,2,1,0:T(8,128)(2,1)S(1)}, u32[]{:S(2)}, u32[]{:S(2)}) collective-permute-start(bf16[4,2,256,256]{3,2,1,0:T(8,128)(2,1)S(1)} %pad_maximum_fusion.p0), channel_id=1, source_target_pairs={{0,64},{64,0},{1,65},{65,1},{2,66},{66,2},{3,67},{67,3},{4,68},{68... | collective-permute-start | bytes 3145736 | tf_op jit(solution)/shard_map/ppermute | solution.py:301
  90.2 13.8 %collective-permute-start.9 = (bf16[1,256,1024]{2,1,0:T(8,128)(2,1)}, bf16[1,256,1024]{2,1,0:T(8,128)(2,1)S(1)}, u32[]{:S(2)}, u32[]{:S(2)}) collective-permute-start(bf16[1,256,1024]{2,1,0:T(8,128)(2,1)} %get-tuple-element.52.refs_0_), channel_id=1, source_target_pairs={{0,2},{2,4},{4,6},{6,0},{1,3},{3,5},{5,7},{7,1},{8,10},{10,12},{12... | collective-permute-start | bytes 1572872 | tf_op jit(solution)/shard_map/ppermute | solution.py:298
  90.8 13.3 %collective-permute-start.10 = (bf16[1,256,1024]{2,1,0:T(8,128)(2,1)}, bf16[1,256,1024]{2,1,0:T(8,128)(2,1)S(1)}, u32[]{:S(2)}, u32[]{:S(2)}) collective-permute-start(bf16[1,256,1024]{2,1,0:T(8,128)(2,1)} %get-tuple-element.52.refs_0_), channel_id=1, source_target_pairs={{0,6},{2,0},{4,2},{6,4},{1,7},{3,1},{5,3},{7,5},{8,14},{10,8},{12,... | collective-permute-start | bytes 1572872 | tf_op jit(solution)/shard_map/ppermute | solution.py:298
  104.0 13.5 %collective-permute-start.14 = (bf16[4,2,256,256]{3,2,1,0:T(8,128)(2,1)S(1)}, bf16[4,2,256,256]{3,2,1,0:T(8,128)(2,1)S(1)}, u32[]{:S(2)}, u32[]{:S(2)}) collective-permute-start(bf16[4,2,256,256]{3,2,1,0:T(8,128)(2,1)S(1)} %pad_maximum_fusion.p0), channel_id=1, source_target_pairs={{0,32},{32,0},{1,33},{33,1},{2,34},{34,2},{3,35},{35,3},{4,36},{36... | collective-permute-start | bytes 3145736 | tf_op jit(solution)/shard_map/ppermute | solution.py:301
  104.1 13.4 %collective-permute-start.15 = (bf16[4,2,256,256]{3,2,1,0:T(8,128)(2,1)S(1)}, bf16[4,2,256,256]{3,2,1,0:T(8,128)(2,1)S(1)}, u32[]{:S(2)}, u32[]{:S(2)}) collective-permute-start(bf16[4,2,256,256]{3,2,1,0:T(8,128)(2,1)S(1)} %collective-permute-done.11.p2), channel_id=1, source_target_pairs={{0,32},{32,0},{1,33},{33,1},{2,34},{34,2},{3,35},{35,3},{4,36},{36... | collective-permute-start | bytes 3145736 | tf_op jit(solution)/shard_map/ppermute | solution.py:301
  104.7 9.6 %collective-permute-start.12 = (bf16[1,128,1024]{2,1,0:T(8,128)(2,1)S(1)}, bf16[1,128,1024]{2,1,0:T(8,128)(2,1)S(1)}, u32[]{:S(2)}, u32[]{:S(2)}) collective-permute-start(bf16[1,128,1024]{2,1,0:T(8,128)(2,1)S(1)} %slice.35), channel_id=1, source_target_pairs={{0,2},{2,4},{4,6},{6,0},{1,3},{3,5},{5,7},{7,1},{8,10},{10,12},{12... | collective-permute-start | bytes 786440 | tf_op jit(solution)/shard_map/ppermute | solution.py:298
  104.8 9.5 %collective-permute-start.13 = (bf16[1,128,1024]{2,1,0:T(8,128)(2,1)S(1)}, bf16[1,128,1024]{2,1,0:T(8,128)(2,1)S(1)}, u32[]{:S(2)}, u32[]{:S(2)}) collective-permute-start(bf16[1,128,1024]{2,1,0:T(8,128)(2,1)S(1)} %slice.36), channel_id=1, source_target_pairs={{0,6},{2,0},{4,2},{6,4},{1,7},{3,1},{5,3},{7,5},{8,14},{10,8},{12,... | collective-permute-start | bytes 786440 | tf_op jit(solution)/shard_map/ppermute | solution.py:298
  114.3 21.2 %collective-permute-start.16 = (bf16[1,256,1024]{2,1,0:T(8,128)(2,1)}, bf16[1,256,1024]{2,1,0:T(8,128)(2,1)}, u32[]{:S(2)}, u32[]{:S(2)}) collective-permute-start(bf16[1,256,1024]{2,1,0:T(8,128)(2,1)} %get-tuple-element.59.refs_0_), channel_id=1, source_target_pairs={{0,2},{2,4},{4,6},{6,0},{1,3},{3,5},{5,7},{7,1},{8,10},{10,12},{12... | collective-permute-start | bytes 1572872 | tf_op jit(solution)/shard_map/ppermute | solution.py:298
  115.4 20.1 %collective-permute-start.17 = (bf16[1,256,1024]{2,1,0:T(8,128)(2,1)}, bf16[1,256,1024]{2,1,0:T(8,128)(2,1)}, u32[]{:S(2)}, u32[]{:S(2)}) collective-permute-start(bf16[1,256,1024]{2,1,0:T(8,128)(2,1)} %get-tuple-element.59.refs_0_), channel_id=1, source_target_pairs={{0,6},{2,0},{4,2},{6,4},{1,7},{3,1},{5,3},{7,5},{8,14},{10,8},{12,... | collective-permute-start | bytes 1572872 | tf_op jit(solution)/shard_map/ppermute | solution.py:298
  131.8 29.7 %all-to-all-start.2 = ((bf16[8,1024,128]{2,1,0:T(8,128)(2,1)}), bf16[8,1024,128]{2,1,0:T(8,128)(2,1)S(1)}, u32[]{:S(2)}, u32[]{:S(2)}) async-start(bf16[8,1024,128]{2,1,0:T(8,128)(2,1)} %output_weight_terms.1), calls=%async_computation.2 | async-start | bytes 4194304 | tf_op jit(solution)/shard_map/all_to_all | solution.py:343
  162.6 33.8 %all-to-all-start.3 = ((bf16[128,2,8,256]{3,2,1,0:T(8,128)(2,1)}), bf16[128,2,8,256]{3,2,1,0:T(8,128)(2,1)S(1)}, u32[]{:S(2)}, u32[]{:S(2)}) async-start(bf16[128,2,8,256]{3,2,1,0:T(8,128)(2,1)} %pad_maximum_fusion.1), calls=%async_computation.3 | async-start | bytes 2097152 | tf_op jit(solution)/shard_map/all_to_all | solution.py:371
  167.8 27.7 %collective-permute-start.19 = (bf16[256,1024]{1,0:T(8,128)(2,1)S(1)}, bf16[256,1024]{1,0:T(8,128)(2,1)S(1)}, u32[]{:S(2)}, u32[]{:S(2)}) collective-permute-start(bf16[256,1024]{1,0:T(8,128)(2,1)S(1)} %fusion.2), channel_id=1, source_target_pairs={{0,64},{64,0},{1,65},{65,1},{2,66},{66,2},{3,67},{67,3},{4,68},{68... | collective-permute-start | bytes 1572872 | tf_op jit(solution)/shard_map/ppermute | solution.py:301
  172.3 15.1 %collective-permute-start.20 = (bf16[1,128,1024]{2,1,0:T(8,128)(2,1)S(1)}, bf16[1,128,1024]{2,1,0:T(8,128)(2,1)S(1)}, u32[]{:S(2)}, u32[]{:S(2)}) collective-permute-start(bf16[1,128,1024]{2,1,0:T(8,128)(2,1)S(1)} %slice.39), channel_id=1, source_target_pairs={{0,2},{2,4},{4,6},{6,0},{1,3},{3,5},{5,7},{7,1},{8,10},{10,12},{12... | collective-permute-start | bytes 786440 | tf_op jit(solution)/shard_map/ppermute | solution.py:298
  173.9 13.6 %collective-permute-start.21 = (bf16[1,128,1024]{2,1,0:T(8,128)(2,1)S(1)}, bf16[1,128,1024]{2,1,0:T(8,128)(2,1)S(1)}, u32[]{:S(2)}, u32[]{:S(2)}) collective-permute-start(bf16[1,128,1024]{2,1,0:T(8,128)(2,1)S(1)} %slice.40), channel_id=1, source_target_pairs={{0,6},{2,0},{4,2},{6,4},{1,7},{3,1},{5,3},{7,5},{8,14},{10,8},{12,... | collective-permute-start | bytes 786440 | tf_op jit(solution)/shard_map/ppermute | solution.py:298
  196.4 32.6 %all-to-all-start.4 = ((bf16[8,128,1024]{2,1,0:T(8,128)(2,1)}), bf16[8,128,1024]{2,1,0:T(8,128)(2,1)S(1)}, u32[]{:S(2)}, u32[]{:S(2)}) async-start(bf16[8,128,1024]{2,1,0:T(8,128)(2,1)} %bitcast.51), calls=%async_computation.4 | async-start | bytes 4194304 | tf_op jit(solution)/shard_map/all_to_all | solution.py:343
  (33 other events, 315.9 us)
